TPU v7x, 32 devices: a whole 2x2x4 slice. The times are simulated.
32 devices in a mesh: row: 4 (over z), col: 8 (over y, x, core).
Axes of the slice: x: 2, y: 2, z: 4, core: 2. Of those that a mesh axis runs over, the one named last changes fastest.
Arguments:
- block_values: bfloat16 [4, 8, 256, 128, 128], P('row', 'col'), may hold values from -1.2 to 1.2
- block_rows: int32 [4, 8, 256], P('row', 'col'), may hold values from 0 to 103, as said below
- block_cols: int32 [4, 8, 256], P('row', 'col'), may hold values from 0 to 51, as said below
- start_vectors: bfloat16 [53248, 256], P(('row', 'col')), may hold values from -6 to 6
- center: float32 [1], replicated, may hold values from -0.5 to -0.1
- half_width: float32 [1], replicated, may hold values from 0.9 to 1.3
- row_counts: int32 [32], replicated, may hold values from 7 to 19, as said below
Outputs:
- relaid: bfloat16 [77824, 256], P(('row', 'col'))
Inputs may be any that keep to these rules, and one draw needn't show every extreme that they name: `block_rows`: the first 13 entries of cell (r, c) are its diagonal blocks, at local row c * 13 + k; the rest are anywhere; positions may repeat, and repeated blocks add. `block_cols`: the first 13 entries of cell (r, c) are at local column r * 13 + k. `row_counts`: entries 2 i and 2 i + 1 sum to 26; entry 0 is larger than 13.
All inputs are finite; a program needn't handle non-finite values.
Results may differ from a plain program's by a relative error of at most 0.019.
Values may be sent and summed in bfloat16 or wider, within the bound.
No kernel may reach another device: no remote copies, remote signals or barrier semaphores. Data moves between devices by JAX's collectives and lax.ppermute only.
A program may use at most 192 MiB of HBM per device.

v0:
```python
import math

import jax
import jax.numpy as jnp
from jax import lax
from jax.sharding import PartitionSpec as P


def swapped(block, axis, bit):
    count = lax.axis_size(axis)
    route = []
    for low in range(count):
        high = low | 1 << bit
        if high != low and high < count:
            route += [(low, high), (high, low)]
    return lax.ppermute(block, axis, route)


def block_images(values, row_ids, col_ids, panel_rows, out_blocks):
    orbitals = values.shape[-1]
    vec_count = panel_rows.shape[-1]
    blocks = panel_rows.reshape(-1, orbitals, vec_count)
    block_count = values.shape[0]
    group_size = math.gcd(block_count, 64)

    def add_group(row_images, group_items):
        group_values, group_rows, group_cols = group_items
        picked = blocks[group_cols]
        images = jnp.einsum(
            "gij,gjv->giv", group_values, picked, preferred_element_type=jnp.float32
        )
        return (row_images.at[group_rows].add(images), None)

    initial = jnp.zeros((out_blocks, orbitals, vec_count), jnp.float32)
    turns = block_count // group_size
    group_items = (
        values.reshape(turns, group_size, orbitals, orbitals),
        row_ids.reshape(turns, group_size),
        col_ids.reshape(turns, group_size),
    )
    row_images, _ = lax.scan(add_group, initial, group_items)
    return row_images.reshape(out_blocks * orbitals, vec_count)


def on_device(block_values, block_rows, block_cols, start_vectors, center, half_width, row_counts):
    orbitals = block_values.shape[-1]
    values = block_values.reshape(-1, orbitals, orbitals)
    row_ids = block_rows.reshape(-1)
    col_ids = block_cols.reshape(-1)
    own_rows, vec_count = start_vectors.shape
    own_blocks = own_rows // orbitals
    col_count = lax.axis_size("col")
    center_value = center[0]
    width_value = half_width[0]

    def image_of(vectors):
        panel_rows = lax.all_gather(vectors, "row", axis=0, tiled=True)
        cell_terms = block_images(values, row_ids, col_ids, panel_rows, col_count * own_blocks)
        return lax.psum_scatter(
            cell_terms.astype(jnp.bfloat16), "col", scatter_dimension=0, tiled=True
        ).astype(jnp.float32)

    source = start_vectors.astype(jnp.float32)
    first_image = image_of(start_vectors)
    first_step = ((first_image - center_value * source) / width_value).astype(jnp.bfloat16)
    second_image = image_of(first_step)
    second = (
        2.0 * (second_image - center_value * first_step.astype(jnp.float32)) / width_value - source
    ).astype(jnp.bfloat16)
    device = lax.axis_index("row") * col_count + lax.axis_index("col")
    parity = device % 2
    even_count = row_counts[device - parity]
    own_count = row_counts[device]
    start_block = parity * even_count
    half_blocks = own_blocks // 2
    capacity = own_blocks + half_blocks
    edge_rows = jnp.where(
        parity == 0, second[own_rows - half_blocks * orbitals :], second[: half_blocks * orbitals]
    )
    partner = swapped(edge_rows, ("row", "col"), 0)
    window = jnp.where(
        parity == 0, jnp.concatenate([second, partner], 0), jnp.concatenate([partner, second], 0)
    )
    window_low = parity * (own_blocks - half_blocks)
    padded = jnp.concatenate([window, jnp.zeros((capacity * orbitals, vec_count), jnp.bfloat16)], 0)
    selected = lax.dynamic_slice_in_dim(
        padded, (start_block - window_low) * orbitals, capacity * orbitals, 0
    )
    live_rows = jnp.arange(capacity * orbitals, dtype=jnp.int32)[:, None] < own_count * orbitals
    return jnp.where(live_rows, selected, jnp.zeros_like(selected))


def solution(mesh):
    placed = (
        P("row", "col", None, None, None),
        P("row", "col", None),
        P("row", "col", None),
        P(("row", "col"), None),
        P(),
        P(),
        P(),
    )
    return jax.shard_map(
        on_device, mesh=mesh, in_specs=placed, out_specs=P(("row", "col"), None), check_vma=False
    )
```

profile of v0, /device:TPU:0, one launch (start us, length us, event | category | flops | bytes accessed | tf_op | source)
XLA Modules:
  0.0 559.5 jit_solution(15442905589920673264)
XLA Ops:
  10.8 68.7 %all-gather.3.cloned.1.call-done = bf16[6656,256]{1,0:T(8,128)(2,1)} async-done(((bf16[1664,256]{1,0:T(8,128)(2,1)}), bf16[6656,256]{1,0:T(8,128)(2,1)}) %all-gather.3.cloned.1.call-update) | async-done | bytes 3407888 | tf_op jit(solution)/shard_map/all_gather | solution.py:57
  79.5 6.6 %broadcast.88.clone = f32[104,128,256]{2,1,0:T(8,128)} broadcast(f32[]{:T(128)} %constant.62.clone.1), dimensions={} | broadcast | bytes 13631492 | tf_op jit(solution)/shard_map/broadcast.15
  86.1 119.1 %while.20 = (s32[]{:T(128)}, f32[104,128,256]{2,1,0:T(8,128)}, s32[4,64]{1,0:T(4,128)S(1)}, bf16[4,64,128,128]{3,2,1,0:T(8,128)(2,1)}, s32[4,64]{1,0:T(4,128)S(1)}, /*index=5*/bf16[52,128,256]{2,1,0:T(8,128)(2,1)S(1)}, s32[]{:T(128)}) while((s32[]{:T(128)}, f32[104,128,256]{2,1,0:T(8,128)}, s32[4,64]{1,0:T(4,128)S(1)}, ...), condition=%wide.region_2.3_spmd, body=%wide.region_0.2_spmd.sunk | while | flops 538969472 | bytes 48240976 | solution.py:41
  86.1 2.8 gather_fusion
  88.9 7.3 %fusion.35 = f32[64,128,256]{2,1,0:T(8,128)} fusion(bf16[64,128,256]{2,1,0:T(8,128)(2,1)} %gather_fusion, bf16[4,64,128,128]{3,2,1,0:T(8,128)(2,1)} %get-tuple-element.200, s32[]{:T(128)} %get-tuple-element.190), kind=kOutput, calls=%fused_computation.4.clone.1 | convolution fusion | flops 536870912 | bytes 14680576 | tf_op jit(solution)/shard_map/while/body/eval_jaxpr/gij,gjv->giv/dot_general | solution.py:29
  96.2 19.8 %scatter_fusion = f32[104,128,256]{2,1,0:T(8,128)} fusion(f32[104,128,256]{2,1,0:T(8,128)} %get-tuple-element.191, s32[64]{0:T(128)S(1)} %get-tuple-element.173, f32[64,128,256]{2,1,0:T(8,128)} %fusion.35), kind=kCustom, calls=%fused_computation.2.clone.1 | custom fusion | flops 2097152 | bytes 25166080 | tf_op jit(solution)/shard_map/while/body/eval_jaxpr/scatter-add | solution.py:32
  116.0 2.8 gather_fusion
  118.9 7.3 %fusion.35 = f32[64,128,256]{2,1,0:T(8,128)} fusion(bf16[64,128,256]{2,1,0:T(8,128)(2,1)} %gather_fusion, bf16[4,64,128,128]{3,2,1,0:T(8,128)(2,1)} %get-tuple-element.200, s32[]{:T(128)} %get-tuple-element.190), kind=kOutput, calls=%fused_computation.4.clone.1 | convolution fusion | flops 536870912 | bytes 14680576 | tf_op jit(solution)/shard_map/while/body/eval_jaxpr/gij,gjv->giv/dot_general | solution.py:29
  126.2 19.5 %scatter_fusion = f32[104,128,256]{2,1,0:T(8,128)} fusion(f32[104,128,256]{2,1,0:T(8,128)} %get-tuple-element.191, s32[64]{0:T(128)S(1)} %get-tuple-element.173, f32[64,128,256]{2,1,0:T(8,128)} %fusion.35), kind=kCustom, calls=%fused_computation.2.clone.1 | custom fusion | flops 2097152 | bytes 25166080 | tf_op jit(solution)/shard_map/while/body/eval_jaxpr/scatter-add | solution.py:32
  145.7 2.8 gather_fusion
  148.6 7.3 %fusion.35 = f32[64,128,256]{2,1,0:T(8,128)} fusion(bf16[64,128,256]{2,1,0:T(8,128)(2,1)} %gather_fusion, bf16[4,64,128,128]{3,2,1,0:T(8,128)(2,1)} %get-tuple-element.200, s32[]{:T(128)} %get-tuple-element.190), kind=kOutput, calls=%fused_computation.4.clone.1 | convolution fusion | flops 536870912 | bytes 14680576 | tf_op jit(solution)/shard_map/while/body/eval_jaxpr/gij,gjv->giv/dot_general | solution.py:29
  155.9 19.6 %scatter_fusion = f32[104,128,256]{2,1,0:T(8,128)} fusion(f32[104,128,256]{2,1,0:T(8,128)} %get-tuple-element.191, s32[64]{0:T(128)S(1)} %get-tuple-element.173, f32[64,128,256]{2,1,0:T(8,128)} %fusion.35), kind=kCustom, calls=%fused_computation.2.clone.1 | custom fusion | flops 2097152 | bytes 25166080 | tf_op jit(solution)/shard_map/while/body/eval_jaxpr/scatter-add | solution.py:32
  178.3 7.3 %fusion.35 = f32[64,128,256]{2,1,0:T(8,128)} fusion(bf16[64,128,256]{2,1,0:T(8,128)(2,1)} %gather_fusion, bf16[4,64,128,128]{3,2,1,0:T(8,128)(2,1)} %get-tuple-element.200, s32[]{:T(128)} %get-tuple-element.190), kind=kOutput, calls=%fused_computation.4.clone.1 | convolution fusion | flops 536870912 | bytes 14680576 | tf_op jit(solution)/shard_map/while/body/eval_jaxpr/gij,gjv->giv/dot_general | solution.py:29
  185.6 19.5 %scatter_fusion = f32[104,128,256]{2,1,0:T(8,128)} fusion(f32[104,128,256]{2,1,0:T(8,128)} %get-tuple-element.191, s32[64]{0:T(128)S(1)} %get-tuple-element.173, f32[64,128,256]{2,1,0:T(8,128)} %fusion.35), kind=kCustom, calls=%fused_computation.2.clone.1 | custom fusion | flops 2097152 | bytes 25166080 | tf_op jit(solution)/shard_map/while/body/eval_jaxpr/scatter-add | solution.py:32
  205.2 8.6 %convert_element_type.30 = bf16[104,128,256]{2,1,0:T(8,128)(2,1)} convert(f32[104,128,256]{2,1,0:T(8,128)} %get-tuple-element.69) | non-fusion elementwise | flops 3407872 | bytes 20447232 | tf_op jit(solution)/shard_map/convert_element_type | solution.py:60
  215.3 61.9 %reduce-scatter.3.cloned.1.call-done = bf16[1664,256]{1,0:T(8,128)(2,1)} async-done(((bf16[13312,256]{1,0:T(8,128)(2,1)}), bf16[1664,256]{1,0:T(8,128)(2,1)}) %reduce-scatter.3.cloned.1.call-update) | async-done | bytes 851984 | tf_op jit(solution)/shard_map/reduce_scatter | solution.py:59
  279.8 67.7 %all-gather.5.cloned.1.call-done = bf16[6656,256]{1,0:T(8,128)(2,1)} async-done(((bf16[1664,256]{1,0:T(8,128)(2,1)}), bf16[6656,256]{1,0:T(8,128)(2,1)}) %all-gather.5.cloned.1.call-update) | async-done | bytes 3407888 | tf_op jit(solution)/shard_map/all_gather | solution.py:57
  347.5 6.6 %broadcast.88 = f32[104,128,256]{2,1,0:T(8,128)} broadcast(f32[]{:T(128)} %constant.62.clone.1), dimensions={} | broadcast | bytes 13631492 | tf_op jit(solution)/shard_map/broadcast.15
  354.1 119.1 %while.21 = (s32[]{:T(128)}, f32[104,128,256]{2,1,0:T(8,128)}, s32[4,64]{1,0:T(4,128)S(1)}, bf16[4,64,128,128]{3,2,1,0:T(8,128)(2,1)}, s32[4,64]{1,0:T(4,128)S(1)}, /*index=5*/bf16[52,128,256]{2,1,0:T(8,128)(2,1)S(1)}, s32[]{:T(128)}) while((s32[]{:T(128)}, f32[104,128,256]{2,1,0:T(8,128)}, s32[4,64]{1,0:T(4,128)S(1)}, ...), condition=%wide.region_6.7_spmd, body=%wide.region_4.6_spmd.sunk | while | flops 538969472 | bytes 48240976 | solution.py:41
  354.1 2.8 gather_fusion.1
  357.0 7.3 %fusion.39 = f32[64,128,256]{2,1,0:T(8,128)} fusion(bf16[64,128,256]{2,1,0:T(8,128)(2,1)} %gather_fusion.1, bf16[4,64,128,128]{3,2,1,0:T(8,128)(2,1)} %get-tuple-element.221, s32[]{:T(128)} %get-tuple-element.211), kind=kOutput, calls=%fused_computation.17.clone.1 | convolution fusion | flops 536870912 | bytes 14680576 | tf_op jit(solution)/shard_map/while/body/eval_jaxpr/gij,gjv->giv/dot_general | solution.py:29
  364.3 19.8 %scatter_fusion.1 = f32[104,128,256]{2,1,0:T(8,128)} fusion(f32[104,128,256]{2,1,0:T(8,128)} %get-tuple-element.212, s32[64]{0:T(128)S(1)} %get-tuple-element.181, f32[64,128,256]{2,1,0:T(8,128)} %fusion.39), kind=kCustom, calls=%fused_computation.3.clone.1 | custom fusion | flops 2097152 | bytes 25166080 | tf_op jit(solution)/shard_map/while/body/eval_jaxpr/scatter-add | solution.py:32
  386.9 7.3 %fusion.39 = f32[64,128,256]{2,1,0:T(8,128)} fusion(bf16[64,128,256]{2,1,0:T(8,128)(2,1)} %gather_fusion.1, bf16[4,64,128,128]{3,2,1,0:T(8,128)(2,1)} %get-tuple-element.221, s32[]{:T(128)} %get-tuple-element.211), kind=kOutput, calls=%fused_computation.17.clone.1 | convolution fusion | flops 536870912 | bytes 14680576 | tf_op jit(solution)/shard_map/while/body/eval_jaxpr/gij,gjv->giv/dot_general | solution.py:29
  394.2 19.5 %scatter_fusion.1 = f32[104,128,256]{2,1,0:T(8,128)} fusion(f32[104,128,256]{2,1,0:T(8,128)} %get-tuple-element.212, s32[64]{0:T(128)S(1)} %get-tuple-element.181, f32[64,128,256]{2,1,0:T(8,128)} %fusion.39), kind=kCustom, calls=%fused_computation.3.clone.1 | custom fusion | flops 2097152 | bytes 25166080 | tf_op jit(solution)/shard_map/while/body/eval_jaxpr/scatter-add | solution.py:32
  413.8 2.8 gather_fusion.1
  416.6 7.3 %fusion.39 = f32[64,128,256]{2,1,0:T(8,128)} fusion(bf16[64,128,256]{2,1,0:T(8,128)(2,1)} %gather_fusion.1, bf16[4,64,128,128]{3,2,1,0:T(8,128)(2,1)} %get-tuple-element.221, s32[]{:T(128)} %get-tuple-element.211), kind=kOutput, calls=%fused_computation.17.clone.1 | convolution fusion | flops 536870912 | bytes 14680576 | tf_op jit(solution)/shard_map/while/body/eval_jaxpr/gij,gjv->giv/dot_general | solution.py:29
  423.9 19.6 %scatter_fusion.1 = f32[104,128,256]{2,1,0:T(8,128)} fusion(f32[104,128,256]{2,1,0:T(8,128)} %get-tuple-element.212, s32[64]{0:T(128)S(1)} %get-tuple-element.181, f32[64,128,256]{2,1,0:T(8,128)} %fusion.39), kind=kCustom, calls=%fused_computation.3.clone.1 | custom fusion | flops 2097152 | bytes 25166080 | tf_op jit(solution)/shard_map/while/body/eval_jaxpr/scatter-add | solution.py:32
  446.4 7.3 %fusion.39 = f32[64,128,256]{2,1,0:T(8,128)} fusion(bf16[64,128,256]{2,1,0:T(8,128)(2,1)} %gather_fusion.1, bf16[4,64,128,128]{3,2,1,0:T(8,128)(2,1)} %get-tuple-element.221, s32[]{:T(128)} %get-tuple-element.211), kind=kOutput, calls=%fused_computation.17.clone.1 | convolution fusion | flops 536870912 | bytes 14680576 | tf_op jit(solution)/shard_map/while/body/eval_jaxpr/gij,gjv->giv/dot_general | solution.py:29
  453.7 19.5 %scatter_fusion.1 = f32[104,128,256]{2,1,0:T(8,128)} fusion(f32[104,128,256]{2,1,0:T(8,128)} %get-tuple-element.212, s32[64]{0:T(128)S(1)} %get-tuple-element.181, f32[64,128,256]{2,1,0:T(8,128)} %fusion.39), kind=kCustom, calls=%fused_computation.3.clone.1 | custom fusion | flops 2097152 | bytes 25166080 | tf_op jit(solution)/shard_map/while/body/eval_jaxpr/scatter-add | solution.py:32
  473.2 8.6 %convert_element_type.35 = bf16[104,128,256]{2,1,0:T(8,128)(2,1)} convert(f32[104,128,256]{2,1,0:T(8,128)} %get-tuple-element.70) | non-fusion elementwise | flops 3407872 | bytes 20447232 | tf_op jit(solution)/shard_map/convert_element_type | solution.py:60
  481.9 63.3 %reduce-scatter.5.cloned.1.call-done = bf16[1664,256]{1,0:T(8,128)(2,1)} async-done(((bf16[13312,256]{1,0:T(8,128)(2,1)}), bf16[1664,256]{1,0:T(8,128)(2,1)}) %reduce-scatter.5.cloned.1.call-update) | async-done | bytes 851984 | tf_op jit(solution)/shard_map/reduce_scatter | solution.py:59
  549.8 3.1 fusion.20
  (52 shorter events, 18.8 us)
Async XLA Ops:
  6.5 73.0 %all-gather.3.cloned.1.call-start = ((), (), s32[]{:S(2)}) async-start(), calls=%async_computation.2 | async-start | bytes 4259840 | tf_op jit(solution)/shard_map/all_gather | solution.py:57
  7.3 269.9 %reduce-scatter.3.cloned.1.call-start = ((), (), s32[]{:S(2)}) async-start(), calls=%async_computation.3 | async-start | bytes 7667712 | tf_op jit(solution)/shard_map/reduce_scatter | solution.py:59
  79.5 6.6 %copy-start = (bf16[6656,256]{1,0:T(8,128)(2,1)S(1)}, bf16[6656,256]{1,0:T(8,128)(2,1)}, u32[]{:S(2)}) copy-start(bf16[6656,256]{1,0:T(8,128)(2,1)} %all-gather.3.cloned.1.call-done) | copy-start | bytes 10223620
  213.8 63.3 %copy-start.2 = (bf16[1664,256]{1,0:T(8,128)(2,1)S(1)}, bf16[1664,256]{1,0:T(8,128)(2,1)}, u32[]{:S(2)}) copy-start(bf16[1664,256]{1,0:T(8,128)(2,1)} %param.14) | copy-start | bytes 2555908
  213.9 133.7 %all-gather.5.cloned.1.call-start = ((), (), s32[]{:S(2)}) async-start(), calls=%async_computation.4 | async-start | bytes 4259840 | tf_op jit(solution)/shard_map/all_gather | solution.py:57
  279.6 265.7 %reduce-scatter.5.cloned.1.call-start = ((), (), s32[]{:S(2)}) async-start(), calls=%async_computation.5 | async-start | bytes 7667712 | tf_op jit(solution)/shard_map/reduce_scatter | solution.py:59
  347.5 6.6 %copy-start.1 = (bf16[6656,256]{1,0:T(8,128)(2,1)S(1)}, bf16[6656,256]{1,0:T(8,128)(2,1)}, u32[]{:S(2)}) copy-start(bf16[6656,256]{1,0:T(8,128)(2,1)} %all-gather.5.cloned.1.call-done) | copy-start | bytes 10223620
  481.9 63.3 %copy-start.3 = (bf16[1664,256]{1,0:T(8,128)(2,1)S(1)}, bf16[1664,256]{1,0:T(8,128)(2,1)}, u32[]{:S(2)}) copy-start(bf16[1664,256]{1,0:T(8,128)(2,1)} %param.14) | copy-start | bytes 2555908
  481.9 63.3 %copy-start.4 = (bf16[1664,256]{1,0:T(8,128)(2,1)S(1)}, bf16[1664,256]{1,0:T(8,128)(2,1)}, u32[]{:S(2)}) copy-start(bf16[1664,256]{1,0:T(8,128)(2,1)} %reduce-scatter.3.cloned.1.call-done) | copy-start | bytes 2555908
  481.9 65.4 %copy-start.5 = (s32[32]{0:T(128)S(1)}, s32[32]{0:T(128)}, u32[]{:S(2)}) copy-start(s32[32]{0:T(128)} %param.17) | copy-start | bytes 388
  547.2 2.1 collective-permute-start
Sparse Core Ops, SparseCore 0:
  8.9 70.5 all-gather.2
  214.0 63.1 reduce-scatter.2
  279.7 67.8 all-gather.4
  482.0 63.1 reduce-scatter.4
where the time goes:
time: 560 us; the launch traced here: 559 us
  waiting for transfers between devices  262 us (47%)
  other arithmetic  185 us (33%)
  matrix products  58.5 us (10%)
  local copies, waits for them, and re-layouts  37.2 us (7%)
  between operations  15.9 us (3%)
    scatter-add x8, other arithmetic, add_group(): return (row_images.at[group_rows].add(images), None)  157 us
    all_gather x2, waiting for transfers between devices, image_of(): panel_rows = lax.all_gather(vectors, 'row', axis=0, tiled=True)  136 us
    reduce_scatter x2, waiting for transfers between devices, image_of(): lax.psum_scatter(cell_terms.astype(jnp.bfloat16), 'col', scatter_dimensio...  125 us
    dot_general x8, matrix products, add_group(): jnp.einsum('gij,gjv->giv', group_values, picked, preferred_element_type=j...  58.5 us
    gather x8, local copies, waits for them, and re-layouts, add_group(): picked = blocks[group_cols]  22.6 us
    convert_element_type x2, other arithmetic, image_of(): cell_terms.astype(jnp.bfloat16)  17.3 us
    another operation x2, local copies, waits for them, and re-layouts  13.2 us
  transfers between devices with their start and end apart: 5, of which 4 were waited for; matrix products, arithmetic and copies ran while one was open for 1% of the time, Pallas kernels for 0%

commit v1 on v0

v1 whole, which is shorter than its diff:
```python
import functools
import math

import jax
import jax.numpy as jnp
from jax import lax
from jax.experimental import pallas as pl
from jax.experimental.pallas import tpu as pltpu
from jax.sharding import PartitionSpec as P

UNROLL = 8
DEPTH = 4
LANES = 128


def sort_values(order, values):
    count = values.shape[0]

    def kernel(order_ref, values_ref, sorted_ref, sem):
        def send(slot, carry):
            pltpu.make_async_copy(
                values_ref.at[order_ref[slot]], sorted_ref.at[slot], sem
            ).start()
            return carry

        lax.fori_loop(0, count, send, 0)
        pltpu.make_async_copy(values_ref, sorted_ref, sem).wait()

    size = values.size * values.dtype.itemsize
    return pl.pallas_call(
        kernel,
        out_shape=jax.ShapeDtypeStruct(values.shape, values.dtype),
        in_specs=[pl.BlockSpec(memory_space=pltpu.SMEM), pl.BlockSpec(memory_space=pl.ANY)],
        out_specs=pl.BlockSpec(memory_space=pl.ANY),
        scratch_shapes=[pltpu.SemaphoreType.DMA],
        cost_estimate=pl.CostEstimate(flops=0, bytes_accessed=2 * size, transcendentals=0),
        name="sort_values",
    )(order, values)


def columns_of(vectors, low, width, after=None):
    rows = vectors.shape[0]
    cut = rows // 2 if rows % 32 == 0 else rows
    sizes = [cut, rows - cut] if cut < rows else [rows]

    def kernel(vectors_ref, *refs):
        out_refs = refs[len(after) :]
        row = 0
        for size, out_ref in zip(sizes, out_refs):
            out_ref[...] = vectors_ref[pl.ds(row, size), pl.ds(low, width)]
            row += size

    after = [] if after is None else list(after)
    return pl.pallas_call(
        kernel,
        out_shape=[jax.ShapeDtypeStruct((size, width), vectors.dtype) for size in sizes],
        in_specs=[pl.BlockSpec(memory_space=pltpu.VMEM)]
        + [pl.BlockSpec(memory_space=pl.ANY)] * len(after),
        out_specs=[pl.BlockSpec(memory_space=pltpu.VMEM)] * len(sizes),
        name="columns_of",
    )(vectors, *after)


def image_kernel(shape, bounds, rows, cols, values, *refs):
    first_piece, pieces, part_count, own, orbitals = shape
    parts = refs[:part_count]
    outs = refs[part_count : part_count + 2 * pieces]
    total, panel, slots, part_sems, slot_sems = refs[part_count + 2 * pieces :]
    start = bounds[first_piece]
    end = bounds[first_piece + pieces]
    first_group = start // UNROLL
    groups = (end + UNROLL - 1) // UNROLL - first_group

    def load(turn, slot):
        return pltpu.make_async_copy(
            values.at[pl.ds((first_group + turn) * UNROLL, UNROLL)],
            slots.at[slot],
            slot_sems.at[slot],
        )

    copies = []
    low = 0
    for index, part in enumerate(parts):
        copy = pltpu.make_async_copy(
            part, panel.at[pl.ds(low, part.shape[0])], part_sems.at[index]
        )
        copy.start()
        copies.append(copy)
        low += part.shape[0]
    for turn in range(DEPTH):
        @pl.when(turn < groups)
        def _():
            load(turn, turn).start()

    base = first_piece * 2 * own
    trash = pieces * 2 * own
    total[...] = jnp.zeros_like(total)
    for copy in copies:
        copy.wait()

    def step(turn, carry):
        slot = lax.rem(turn, DEPTH)
        load(turn, slot).wait()
        images = []
        for lane in range(UNROLL):
            entry = (first_group + turn) * UNROLL + lane
            picked = panel[pl.ds(pl.multiple_of(cols[entry] * orbitals, orbitals), orbitals), :]
            images.append(
                jnp.dot(slots[slot, lane], picked, preferred_element_type=jnp.float32)
            )
        for lane in range(UNROLL):
            entry = (first_group + turn) * UNROLL + lane
            inside = jnp.logical_and(entry >= start, entry < end)
            row = jnp.where(inside, rows[entry] - base, trash)
            place = pl.ds(pl.multiple_of(row * orbitals, orbitals), orbitals)
            total[place, :] += images[lane]

        @pl.when(turn + DEPTH < groups)
        def _():
            load(turn + DEPTH, slot).start()

        return carry

    lax.fori_loop(0, groups, step, 0)
    height = own * orbitals
    for index, out in enumerate(outs):
        out[...] = total[index * height : (index + 1) * height, :].astype(out.dtype)


def images_of(first_piece, pieces, bounds, rows, cols, values, parts, own):
    orbitals = values.shape[-1]
    width = parts[0].shape[1]
    panel_rows = sum(part.shape[0] for part in parts)
    out = jax.ShapeDtypeStruct((own * orbitals, width), jnp.bfloat16)
    entries = values.shape[0] * pieces // (bounds.shape[0] - 1)
    kernel = functools.partial(image_kernel, (first_piece, pieces, len(parts), own, orbitals))
    return pl.pallas_call(
        kernel,
        out_shape=[out] * (2 * pieces),
        in_specs=[pl.BlockSpec(memory_space=pltpu.SMEM)] * 3
        + [pl.BlockSpec(memory_space=pl.ANY)] * (1 + len(parts)),
        out_specs=[pl.BlockSpec(memory_space=pltpu.VMEM)] * (2 * pieces),
        scratch_shapes=[
            pltpu.VMEM(((pieces * 2 * own + 1) * orbitals, width), jnp.float32),
            pltpu.VMEM((panel_rows, width), jnp.bfloat16),
            pltpu.VMEM((DEPTH, UNROLL, orbitals, orbitals), values.dtype),
            pltpu.SemaphoreType.DMA((len(parts),)),
            pltpu.SemaphoreType.DMA((DEPTH,)),
        ],
        compiler_params=pltpu.CompilerParams(vmem_limit_bytes=48 << 20),
        cost_estimate=pl.CostEstimate(
            flops=entries * 8 * orbitals * orbitals * width,
            bytes_accessed=2 * (entries * orbitals * orbitals + panel_rows * width),
            transcendentals=0,
        ),
        name="images_of",
    )(bounds, rows, cols, values, *parts)


def ring_order(count):
    return [i for i in range(count) if i == 0 or i % 2] + [
        i for i in range(count - 1, 0, -1) if i and i % 2 == 0
    ]


def on_device(block_values, block_rows, block_cols, start_vectors, center, half_width, row_counts):
    orbitals = block_values.shape[-1]
    values = block_values.reshape(-1, orbitals, orbitals)
    row_ids = block_rows.reshape(-1)
    col_ids = block_cols.reshape(-1)
    entry_count = values.shape[0]
    own_rows, vec_count = start_vectors.shape
    own = own_rows // orbitals
    row_count = lax.axis_size("row")
    col_count = lax.axis_size("col")
    my_row = lax.axis_index("row")
    my_col = lax.axis_index("col")
    center_value = center[0]
    width_value = half_width[0]
    chip_count = col_count // 2

    order = ring_order(row_count)
    route = [(order[i], order[(i + 1) % row_count]) for i in range(row_count)]
    place_of = [order.index(i) for i in range(row_count)]

    def looked_up(table, index):
        result = jnp.zeros_like(index)
        for at, value in enumerate(table):
            result = jnp.where(index == at, value, result)
        return result

    with jax.named_scope("entry_order"):
        arrival = lax.rem(
            looked_up(place_of, my_row) - looked_up(place_of, col_ids // own) + row_count, row_count
        )
        panel_cols = arrival * own + col_ids % own
        relative = (row_ids // own) ^ my_col
        piece = chip_count - 1 - relative // 2
        out_rows = (piece * 2 + 1 - relative % 2) * own + row_ids % own
        number = jnp.arange(entry_count, dtype=jnp.int32)
        before = (out_rows[None, :] < out_rows[:, None]) | (
            (out_rows[None, :] == out_rows[:, None]) & (number[None, :] < number[:, None])
        )
        rank = jnp.sum(before.astype(jnp.int32), 1)
        at_rank = rank[None, :] == number[:, None]

        def ordered(items):
            return jnp.sum(jnp.where(at_rank, items[None, :], 0), 1).astype(jnp.int32)

        entry_order, rows, cols = ordered(number), ordered(out_rows), ordered(panel_cols)
        limits = jnp.arange(chip_count + 1, dtype=jnp.int32) * (2 * own)
        bounds = jnp.sum((out_rows[None, :] < limits[:, None]).astype(jnp.int32), 1)
        bounds = bounds.astype(jnp.int32)
    values = sort_values(entry_order, values)

    other_core = [(i, i ^ 1) for i in range(col_count)]
    if chip_count >= 4:
        groups = [(0, 1), (1, chip_count - 2), (chip_count - 1, 1)]
    else:
        groups = [(0, chip_count)]

    def gathered(parts):
        held = list(parts)
        arrived = [held]
        for _ in range(row_count - 1):
            held = [lax.ppermute(part, "row", route) for part in held]
            arrived.append(held)
        return arrived

    def summed(arrived):
        parts = [part for step in arrived for part in step]
        terms = None
        for first_piece, pieces in groups:
            outs = images_of(first_piece, pieces, bounds, rows, cols, values, parts, own)
            for index in range(pieces):
                chip = chip_count - 1 - first_piece - index
                partner = lax.ppermute(outs[2 * index], "col", other_core)
                both = outs[2 * index + 1].astype(jnp.float32) + partner.astype(jnp.float32)
                if chip:
                    both = lax.ppermute(
                        both.astype(jnp.bfloat16), "col",
                        [(i, i ^ 2 * chip) for i in range(col_count)],
                    ).astype(jnp.float32)
                terms = both if terms is None else terms + both
        return terms

    def pieces_of(array):
        cut = own_rows // 2 if own_rows % 32 == 0 else own_rows
        return [array[:cut], array[cut:]] if cut < own_rows else [array]

    lows = range(0, vec_count, LANES)
    first_arrived = []
    after = None
    for low in lows:
        arrived = gathered(columns_of(start_vectors, low, LANES, after))
        first_arrived.append(arrived)
        after = arrived[-1]
    firsts = []
    for low, arrived in zip(lows, first_arrived):
        source = start_vectors[:, low : low + LANES].astype(jnp.float32)
        first = ((summed(arrived) - center_value * source) / width_value).astype(jnp.bfloat16)
        firsts.append(first)
    second_arrived = [gathered(pieces_of(first)) for first in firsts]
    seconds = []
    for low, arrived, first in zip(lows, second_arrived, firsts):
        source = start_vectors[:, low : low + LANES].astype(jnp.float32)
        second = (
            2.0 * (summed(arrived) - center_value * first.astype(jnp.float32)) / width_value
            - source
        ).astype(jnp.bfloat16)
        seconds.append(second)
    second = jnp.concatenate(seconds, 1)

    device = my_row * col_count + my_col
    parity = device % 2
    even_count = row_counts[device - parity]
    own_count = row_counts[device]
    start_block = parity * even_count
    half_blocks = own // 2
    capacity = own + half_blocks
    edge_rows = jnp.where(
        parity == 0, second[own_rows - half_blocks * orbitals :], second[: half_blocks * orbitals]
    )
    partner = lax.ppermute(edge_rows, "col", other_core)
    window = jnp.where(
        parity == 0, jnp.concatenate([second, partner], 0), jnp.concatenate([partner, second], 0)
    )
    window_low = parity * (own - half_blocks)
    padded = jnp.concatenate([window, jnp.zeros((capacity * orbitals, vec_count), jnp.bfloat16)], 0)
    selected = lax.dynamic_slice_in_dim(
        padded, (start_block - window_low) * orbitals, capacity * orbitals, 0
    )
    live_rows = jnp.arange(capacity * orbitals, dtype=jnp.int32)[:, None] < own_count * orbitals
    return jnp.where(live_rows, selected, jnp.zeros_like(selected))


def solution(mesh):
    placed = (
        P("row", "col", None, None, None),
        P("row", "col", None),
        P("row", "col", None),
        P(("row", "col"), None),
        P(),
        P(),
        P(),
    )
    return jax.shard_map(
        on_device, mesh=mesh, in_specs=placed, out_specs=P(("row", "col"), None), check_vma=False
    )
```

time: 560 us -> 518 us (0.925)
  Pallas kernels: 0 us -> 342 us
  other arithmetic: 185 us -> 14.1 us
  waiting for transfers between devices: 262 us -> 112 us
  matrix products: 58.5 us -> 0 us
  starting transfers between devices: 0.38 us -> 45.4 us
  local copies, waits for them, and re-layouts: 37.2 us -> 1.2 us
  between operations: 15.9 us -> 3.14 us
    pallas_call x0 -> x15, Pallas kernels: none -> 342 us  [the longest x1 256 us: sort_values(): pl.pallas_call(kernel, out_shape=jax.ShapeDtypeStruct(values.shape, value...]
    scatter-add x8 -> x0, other arithmetic: 157 us -> none  [add_group(): return (row_images.at[group_rows].add(images), None)]
    all_gather x2 -> x0, waiting for transfers between devices: 136 us -> none  [image_of(): panel_rows = lax.all_gather(vectors, 'row', axis=0, tiled=True)]
    reduce_scatter x2 -> x0, waiting for transfers between devices: 125 us -> none  [image_of(): lax.psum_scatter(cell_terms.astype(jnp.bfloat16), 'col', scatter_dimensio...]
    ppermute x1 -> x53, waiting for transfers between devices: 0.01 us -> 112 us  [the longest x24 72.6 us: gathered(): held = [lax.ppermute(part, 'row', route) for part in held]]
    dot_general x8 -> x0, matrix products: 58.5 us -> none  [add_group(): jnp.einsum('gij,gjv->giv', group_values, picked, preferred_element_type=j...]
    ppermute x1 -> x53, starting transfers between devices: 0.07 us -> 45.4 us  [the longest x24 23.4 us: gathered(): held = [lax.ppermute(part, 'row', route) for part in held]]
    gather x8 -> x0, local copies, waits for them, and re-layouts: 22.6 us -> none  [add_group(): picked = blocks[group_cols]]
  transfers between devices with their start and end apart: 5 -> 53, of which waited for: 4 -> 25; matrix products, arithmetic and copies ran while one was open for 1% -> 2% of each run, Pallas kernels for 0% -> 63%
where the time goes in v1:
time: 518 us
  Pallas kernels  342 us (66%)
  waiting for transfers between devices  112 us (22%)
  starting transfers between devices  45.4 us (9%)
  other arithmetic  14.1 us (3%)
    pallas_call x1, Pallas kernels, sort_values(): pl.pallas_call(kernel, out_shape=jax.ShapeDtypeStruct(values.shape, value...  256 us
    pallas_call x12, Pallas kernels, images_of(): pl.pallas_call(kernel, out_shape=[out] * (2 * pieces), in_specs=[pl.Block...  82.3 us
    ppermute x24, waiting for transfers between devices, gathered(): held = [lax.ppermute(part, 'row', route) for part in held]  72.6 us
    ppermute x12, waiting for transfers between devices, summed(): lax.ppermute(both.astype(jnp.bfloat16), 'col', [(i, i ^ 2 * chip) for i i...  36.3 us
    ppermute x24, starting transfers between devices, gathered(): held = [lax.ppermute(part, 'row', route) for part in held]  23.4 us
    ppermute x12, starting transfers between devices, summed(): lax.ppermute(both.astype(jnp.bfloat16), 'col', [(i, i ^ 2 * chip) for i i...  18.4 us
  transfers between devices with their start and end apart: 53, of which 25 were waited for; matrix products, arithmetic and copies ran while one was open for 2% of the time, Pallas kernels for 63%

profile of v1, /device:TPU:0, one launch (start us, length us, event | category | flops | bytes accessed | tf_op | source)
XLA Modules:
  0.0 518.2 jit_solution(383920754690790211)
XLA Ops:
  19.1 256.0 %sort_values.1.values = bf16[256,128,128]{2,1,0:T(8,128)(2,1)} custom-call(s32[256]{0:T(256)} %get-tuple-element.77.order_ref, bf16[256,128,128]{2,1,0:T(8,128)(2,1)} %bitcast.15), custom_call_target="tpu_custom_call" | custom-call | bytes 16777216 | tf_op jit(solution)/shard_map/sort_values/pallas_call | solution.py:30
  278.7 5.1 collective-permute-done.4.refs_6_.refs_0_
  286.1 5.9 %images_of.12 = (bf16[1664,128]{1,0:T(8,128)(2,1)S(1)}, bf16[1664,128]{1,0:T(8,128)(2,1)S(1)}) custom-call(s32[5]{0:T(128)S(1)} %convert_reduce_fusion.1.bounds, s32[256]{0:T(256)S(1)} %get-tuple-element.79.rows, s32[256]{0:T(256)S(1)} %get-tuple-element.78.cols, bf16[256,128,128]{2,1,0:T(8,128)(2,1)} %sort_values.1.values, bf16[832,128]{1,0:T(8,128)(2,1)S(1)} %copy-done.6, ...), custom_call_target="tpu_custom_call" | custom-call | flops 1073741824 | bytes 3801088 | tf_op jit(solution)/shard_map/images_of/pallas_call | solution.py:137
  297.5 7.9 %images_of.13 = (bf16[1664,128]{1,0:T(8,128)(2,1)S(1)}, bf16[1664,128]{1,0:T(8,128)(2,1)S(1)}, bf16[1664,128]{1,0:T(8,128)(2,1)S(1)}, bf16[1664,128]{1,0:T(8,128)(2,1)S(1)}) custom-call(s32[5]{0:T(128)S(1)} %convert_reduce_fusion.1.bounds, s32[256]{0:T(256)S(1)} %get-tuple-element.79.rows, s32[256]{0:T(256)S(1)} %get-tuple-element.78.cols, ...), custom_call_target="tpu_custom_call" | custom-call | flops 2147483648 | bytes 5898240 | tf_op jit(solution)/shard_map/images_of/pallas_call | solution.py:137
  305.9 6.7 %images_of.14 = (bf16[1664,128]{1,0:T(8,128)(2,1)S(1)}, bf16[1664,128]{1,0:T(8,128)(2,1)S(1)}) custom-call(s32[5]{0:T(128)S(1)} %convert_reduce_fusion.1.bounds, s32[256]{0:T(256)S(1)} %get-tuple-element.79.rows, s32[256]{0:T(256)S(1)} %get-tuple-element.78.cols, bf16[256,128,128]{2,1,0:T(8,128)(2,1)} %sort_values.1.values, bf16[832,128]{1,0:T(8,128)(2,1)S(1)} %copy-done.6, ...), custom_call_target="tpu_custom_call" | custom-call | flops 1073741824 | bytes 3801088 | tf_op jit(solution)/shard_map/images_of/pallas_call | solution.py:137
  317.1 4.7 collective-permute-done.28.refs_4_
  323.0 3.4 collective-permute-done.29.refs_5_
  326.9 3.6 collective-permute-done.30.refs_6_
  331.8 5.4 %collective-permute-done.31.refs_7_ = bf16[832,128]{1,0:T(8,128)(2,1)S(1)} collective-permute-done((bf16[832,128]{1,0:T(8,128)(2,1)S(1)}, bf16[832,128]{1,0:T(8,128)(2,1)S(1)}, u32[]{:S(2)}, u32[]{:S(2)}) %collective-permute-start.31) | collective-permute-done | bytes 213024 | tf_op jit(solution)/shard_map/ppermute | solution.py:226
  337.2 5.9 %images_of.18 = (bf16[1664,128]{1,0:T(8,128)(2,1)S(1)}, bf16[1664,128]{1,0:T(8,128)(2,1)S(1)}) custom-call(s32[5]{0:T(128)S(1)} %convert_reduce_fusion.1.bounds, s32[256]{0:T(256)S(1)} %get-tuple-element.79.rows, s32[256]{0:T(256)S(1)} %get-tuple-element.78.cols, bf16[256,128,128]{2,1,0:T(8,128)(2,1)} %sort_values.1.values, bf16[832,128]{1,0:T(8,128)(2,1)S(1)} %copy-done.4, ...), custom_call_target="tpu_custom_call" | custom-call | flops 1073741824 | bytes 3801088 | tf_op jit(solution)/shard_map/images_of/pallas_call | solution.py:137
  346.6 7.9 %images_of.19 = (bf16[1664,128]{1,0:T(8,128)(2,1)S(1)}, bf16[1664,128]{1,0:T(8,128)(2,1)S(1)}, bf16[1664,128]{1,0:T(8,128)(2,1)S(1)}, bf16[1664,128]{1,0:T(8,128)(2,1)S(1)}) custom-call(s32[5]{0:T(128)S(1)} %convert_reduce_fusion.1.bounds, s32[256]{0:T(256)S(1)} %get-tuple-element.79.rows, s32[256]{0:T(256)S(1)} %get-tuple-element.78.cols, ...), custom_call_target="tpu_custom_call" | custom-call | flops 2147483648 | bytes 5898240 | tf_op jit(solution)/shard_map/images_of/pallas_call | solution.py:137
  355.1 6.7 %images_of.20 = (bf16[1664,128]{1,0:T(8,128)(2,1)S(1)}, bf16[1664,128]{1,0:T(8,128)(2,1)S(1)}) custom-call(s32[5]{0:T(128)S(1)} %convert_reduce_fusion.1.bounds, s32[256]{0:T(256)S(1)} %get-tuple-element.79.rows, s32[256]{0:T(256)S(1)} %get-tuple-element.78.cols, bf16[256,128,128]{2,1,0:T(8,128)(2,1)} %sort_values.1.values, bf16[832,128]{1,0:T(8,128)(2,1)S(1)} %copy-done.4, ...), custom_call_target="tpu_custom_call" | custom-call | flops 1073741824 | bytes 3801088 | tf_op jit(solution)/shard_map/images_of/pallas_call | solution.py:137
  367.2 3.8 collective-permute-done.15.refs_4_
  371.0 4.6 collective-permute-done.16.refs_5_
  375.6 4.4 collective-permute-done.17.refs_6_
  384.2 5.9 %images_of.15 = (bf16[1664,128]{1,0:T(8,128)(2,1)S(1)}, bf16[1664,128]{1,0:T(8,128)(2,1)S(1)}) custom-call(s32[5]{0:T(128)S(1)} %convert_reduce_fusion.1.bounds, s32[256]{0:T(256)S(1)} %get-tuple-element.79.rows, s32[256]{0:T(256)S(1)} %get-tuple-element.78.cols, bf16[256,128,128]{2,1,0:T(8,128)(2,1)} %sort_values.1.values, ...), custom_call_target="tpu_custom_call" | custom-call | flops 1073741824 | bytes 3801088 | tf_op jit(solution)/shard_map/images_of/pallas_call | solution.py:137
  390.9 6.7 %images_of.17 = (bf16[1664,128]{1,0:T(8,128)(2,1)S(1)}, bf16[1664,128]{1,0:T(8,128)(2,1)S(1)}) custom-call(s32[5]{0:T(128)S(1)} %convert_reduce_fusion.1.bounds, s32[256]{0:T(256)S(1)} %get-tuple-element.79.rows, s32[256]{0:T(256)S(1)} %get-tuple-element.78.cols, bf16[256,128,128]{2,1,0:T(8,128)(2,1)} %sort_values.1.values, ...), custom_call_target="tpu_custom_call" | custom-call | flops 1073741824 | bytes 3801088 | tf_op jit(solution)/shard_map/images_of/pallas_call | solution.py:137
  397.7 7.9 %images_of.16 = (bf16[1664,128]{1,0:T(8,128)(2,1)S(1)}, bf16[1664,128]{1,0:T(8,128)(2,1)S(1)}, bf16[1664,128]{1,0:T(8,128)(2,1)S(1)}, bf16[1664,128]{1,0:T(8,128)(2,1)S(1)}) custom-call(s32[5]{0:T(128)S(1)} %convert_reduce_fusion.1.bounds, s32[256]{0:T(256)S(1)} %get-tuple-element.79.rows, s32[256]{0:T(256)S(1)} %get-tuple-element.78.cols, ...), custom_call_target="tpu_custom_call" | custom-call | flops 2147483648 | bytes 5898240 | tf_op jit(solution)/shard_map/images_of/pallas_call | solution.py:137
  409.5 4.0 collective-permute-start.20
  414.2 10.0 %collective-permute-done.20 = bf16[1664,128]{1,0:T(8,128)(2,1)S(1)} collective-permute-done((bf16[1664,128]{1,0:T(8,128)(2,1)S(1)}, bf16[1664,128]{1,0:T(8,128)(2,1)S(1)}, u32[]{:S(2)}, u32[]{:S(2)}) %collective-permute-start.20) | collective-permute-done | bytes 426016 | tf_op jit(solution)/shard_map/ppermute | solution.py:240
  424.3 8.8 %collective-permute-done.22 = bf16[1664,128]{1,0:T(8,128)(2,1)S(1)} collective-permute-done((bf16[1664,128]{1,0:T(8,128)(2,1)S(1)}, bf16[1664,128]{1,0:T(8,128)(2,1)S(1)}, u32[]{:S(2)}, u32[]{:S(2)}) %collective-permute-start.22) | collective-permute-done | bytes 426016 | tf_op jit(solution)/shard_map/ppermute | solution.py:240
  436.3 6.7 %collective-permute-done.39.refs_2_ = bf16[832,128]{1,0:T(8,128)(2,1)S(1)} collective-permute-done((bf16[832,128]{1,0:T(8,128)(2,1)S(1)}, bf16[832,128]{1,0:T(8,128)(2,1)S(1)}, u32[]{:S(2)}, u32[]{:S(2)}) %collective-permute-start.39) | collective-permute-done | bytes 213024 | tf_op jit(solution)/shard_map/ppermute | solution.py:226
  443.0 4.6 collective-permute-done.40.refs_3_
  447.6 4.6 collective-permute-done.41.refs_4_
  452.2 4.6 collective-permute-done.42.refs_5_
  456.7 4.6 collective-permute-done.43.refs_6_
  461.3 3.6 collective-permute-done.44.refs_7_
  464.9 5.9 %images_of.21 = (bf16[1664,128]{1,0:T(8,128)(2,1)S(1)}, bf16[1664,128]{1,0:T(8,128)(2,1)S(1)}) custom-call(s32[5]{0:T(128)S(1)} %convert_reduce_fusion.1.bounds, s32[256]{0:T(256)S(1)} %get-tuple-element.79.rows, s32[256]{0:T(256)S(1)} %get-tuple-element.78.cols, bf16[256,128,128]{2,1,0:T(8,128)(2,1)} %sort_values.1.values, ...), custom_call_target="tpu_custom_call" | custom-call | flops 1073741824 | bytes 3801088 | tf_op jit(solution)/shard_map/images_of/pallas_call | solution.py:137
  470.9 7.9 %images_of.22 = (bf16[1664,128]{1,0:T(8,128)(2,1)S(1)}, bf16[1664,128]{1,0:T(8,128)(2,1)S(1)}, bf16[1664,128]{1,0:T(8,128)(2,1)S(1)}, bf16[1664,128]{1,0:T(8,128)(2,1)S(1)}) custom-call(s32[5]{0:T(128)S(1)} %convert_reduce_fusion.1.bounds, s32[256]{0:T(256)S(1)} %get-tuple-element.79.rows, s32[256]{0:T(256)S(1)} %get-tuple-element.78.cols, ...), custom_call_target="tpu_custom_call" | custom-call | flops 2147483648 | bytes 5898240 | tf_op jit(solution)/shard_map/images_of/pallas_call | solution.py:137
  479.5 6.7 %images_of.23 = (bf16[1664,128]{1,0:T(8,128)(2,1)S(1)}, bf16[1664,128]{1,0:T(8,128)(2,1)S(1)}) custom-call(s32[5]{0:T(128)S(1)} %convert_reduce_fusion.1.bounds, s32[256]{0:T(256)S(1)} %get-tuple-element.79.rows, s32[256]{0:T(256)S(1)} %get-tuple-element.78.cols, bf16[256,128,128]{2,1,0:T(8,128)(2,1)} %sort_values.1.values, ...), custom_call_target="tpu_custom_call" | custom-call | flops 1073741824 | bytes 3801088 | tf_op jit(solution)/shard_map/images_of/pallas_call | solution.py:137
  492.9 8.6 %collective-permute-done.46 = bf16[1664,128]{1,0:T(8,128)(2,1)S(1)} collective-permute-done((bf16[1664,128]{1,0:T(8,128)(2,1)}, bf16[1664,128]{1,0:T(8,128)(2,1)S(1)}, u32[]{:S(2)}, u32[]{:S(2)}) %collective-permute-start.46) | collective-permute-done | bytes 426016 | tf_op jit(solution)/shard_map/ppermute | solution.py:240
  501.4 8.3 %collective-permute-done.48 = bf16[1664,128]{1,0:T(8,128)(2,1)} collective-permute-done((bf16[1664,128]{1,0:T(8,128)(2,1)}, bf16[1664,128]{1,0:T(8,128)(2,1)}, u32[]{:S(2)}, u32[]{:S(2)}) %collective-permute-start.48) | collective-permute-done | bytes 426016 | tf_op jit(solution)/shard_map/ppermute | solution.py:240
  (141 shorter events, 73.6 us)
Async XLA Ops:
  2.0 10.3 %collective-permute-start = (bf16[832,128]{1,0:T(8,128)(2,1)}, bf16[832,128]{1,0:T(8,128)(2,1)S(1)}, u32[]{:S(2)}, u32[]{:S(2)}) collective-permute-start(bf16[832,128]{1,0:T(8,128)(2,1)} %get-tuple-element.41.refs_0_), channel_id=1, source_target_pairs={{0,8},{8,24},{24,16},{16,0},{1,9},{9,25},{25,17},{17,1},{2,10},{10... | collective-permute-start | bytes 638984 | tf_op jit(solution)/shard_map/ppermute | solution.py:226
  5.0 11.9 %collective-permute-start.1 = (bf16[832,128]{1,0:T(8,128)(2,1)}, bf16[832,128]{1,0:T(8,128)(2,1)S(1)}, u32[]{:S(2)}, u32[]{:S(2)}) collective-permute-start(bf16[832,128]{1,0:T(8,128)(2,1)} %get-tuple-element.42.refs_1_), channel_id=1, source_target_pairs={{0,8},{8,24},{24,16},{16,0},{1,9},{9,25},{25,17},{17,1},{2,10},{10... | collective-permute-start | bytes 638984 | tf_op jit(solution)/shard_map/ppermute | solution.py:226
  12.3 262.8 %collective-permute-start.2 = (bf16[832,128]{1,0:T(8,128)(2,1)S(1)}, bf16[832,128]{1,0:T(8,128)(2,1)S(1)}, u32[]{:S(2)}, u32[]{:S(2)}) collective-permute-start(bf16[832,128]{1,0:T(8,128)(2,1)S(1)} %collective-permute-done.refs_2_), channel_id=1, source_target_pairs={{0,8},{8,24},{24,16},{16,0},{1,9},{9,25},{25,17},{17,1},{2,10},{10... | collective-permute-start | bytes 638984 | tf_op jit(solution)/shard_map/ppermute | solution.py:226
  16.9 261.6 %collective-permute-start.3 = (bf16[832,128]{1,0:T(8,128)(2,1)S(1)}, bf16[832,128]{1,0:T(8,128)(2,1)S(1)}, u32[]{:S(2)}, u32[]{:S(2)}) collective-permute-start(bf16[832,128]{1,0:T(8,128)(2,1)S(1)} %collective-permute-done.1.refs_3_), channel_id=1, source_target_pairs={{0,8},{8,24},{24,16},{16,0},{1,9},{9,25},{25,17},{17,1},{2,10},{10... | collective-permute-start | bytes 638984 | tf_op jit(solution)/shard_map/ppermute | solution.py:226
  292.1 20.8 %collective-permute-start.6 = (bf16[1664,128]{1,0:T(8,128)(2,1)S(1)}, bf16[1664,128]{1,0:T(8,128)(2,1)S(1)}, u32[]{:S(2)}, u32[]{:S(2)}) collective-permute-start(bf16[1664,128]{1,0:T(8,128)(2,1)S(1)} %get-tuple-element.44), channel_id=1, source_target_pairs={{0,1},{1,0},{2,3},{3,2},{4,5},{5,4},{6,7},{7,6},{8,9},{9,8},{10,11... | collective-permute-start | bytes 1277960 | tf_op jit(solution)/shard_map/ppermute | solution.py:237
  294.2 18.4 %collective-permute-start.26 = (bf16[832,128]{1,0:T(8,128)(2,1)}, bf16[832,128]{1,0:T(8,128)(2,1)S(1)}, u32[]{:S(2)}, u32[]{:S(2)}) collective-permute-start(bf16[832,128]{1,0:T(8,128)(2,1)} %get-tuple-element.59.refs_0_), channel_id=1, source_target_pairs={{0,8},{8,24},{24,16},{16,0},{1,9},{9,25},{25,17},{17,1},{2,10},{10... | collective-permute-start | bytes 638984 | tf_op jit(solution)/shard_map/ppermute | solution.py:226
  296.3 16.6 %collective-permute-start.27 = (bf16[832,128]{1,0:T(8,128)(2,1)}, bf16[832,128]{1,0:T(8,128)(2,1)S(1)}, u32[]{:S(2)}, u32[]{:S(2)}) collective-permute-start(bf16[832,128]{1,0:T(8,128)(2,1)} %get-tuple-element.60.refs_1_), channel_id=1, source_target_pairs={{0,8},{8,24},{24,16},{16,0},{1,9},{9,25},{25,17},{17,1},{2,10},{10... | collective-permute-start | bytes 638984 | tf_op jit(solution)/shard_map/ppermute | solution.py:226
  305.4 17.4 %collective-permute-start.10 = (bf16[1664,128]{1,0:T(8,128)(2,1)S(1)}, bf16[1664,128]{1,0:T(8,128)(2,1)S(1)}, u32[]{:S(2)}, u32[]{:S(2)}) collective-permute-start(bf16[1664,128]{1,0:T(8,128)(2,1)S(1)} %get-tuple-element.48), channel_id=1, source_target_pairs={{0,1},{1,0},{2,3},{3,2},{4,5},{5,4},{6,7},{7,6},{8,9},{9,8},{10,11... | collective-permute-start | bytes 1277960 | tf_op jit(solution)/shard_map/ppermute | solution.py:237
  312.7 30.5 %collective-permute-start.12 = (bf16[1664,128]{1,0:T(8,128)(2,1)S(1)}, bf16[1664,128]{1,0:T(8,128)(2,1)S(1)}, u32[]{:S(2)}, u32[]{:S(2)}) collective-permute-start(bf16[1664,128]{1,0:T(8,128)(2,1)S(1)} %get-tuple-element.50), channel_id=1, source_target_pairs={{0,1},{1,0},{2,3},{3,2},{4,5},{5,4},{6,7},{7,6},{8,9},{9,8},{10,11... | collective-permute-start | bytes 1277960 | tf_op jit(solution)/shard_map/ppermute | solution.py:237
  312.9 13.5 %collective-permute-start.29 = (bf16[832,128]{1,0:T(8,128)(2,1)S(1)}, bf16[832,128]{1,0:T(8,128)(2,1)S(1)}, u32[]{:S(2)}, u32[]{:S(2)}) collective-permute-start(bf16[832,128]{1,0:T(8,128)(2,1)S(1)} %collective-permute-done.27.refs_3_), channel_id=1, source_target_pairs={{0,8},{8,24},{24,16},{16,0},{1,9},{9,25},{25,17},{17,1},{2,10},{10... | collective-permute-start | bytes 638984 | tf_op jit(solution)/shard_map/ppermute | solution.py:226
  314.5 28.7 %collective-permute-start.7 = (bf16[1664,128]{1,0:T(8,128)(2,1)S(1)}, bf16[1664,128]{1,0:T(8,128)(2,1)S(1)}, u32[]{:S(2)}, u32[]{:S(2)}) collective-permute-start(bf16[1664,128]{1,0:T(8,128)(2,1)S(1)} %add_convert_fusion.11), channel_id=1, source_target_pairs={{0,6},{1,7},{2,4},{3,5},{4,2},{5,3},{6,0},{7,1},{8,14},{9,15},{10,... | collective-permute-start | bytes 1277960 | tf_op jit(solution)/shard_map/ppermute | solution.py:240
  321.8 21.4 %collective-permute-start.9 = (bf16[1664,128]{1,0:T(8,128)(2,1)S(1)}, bf16[1664,128]{1,0:T(8,128)(2,1)S(1)}, u32[]{:S(2)}, u32[]{:S(2)}) collective-permute-start(bf16[1664,128]{1,0:T(8,128)(2,1)S(1)} %add_convert_fusion.10), channel_id=1, source_target_pairs={{0,4},{1,5},{2,6},{3,7},{4,0},{5,1},{6,2},{7,3},{8,12},{9,13},{10,... | collective-permute-start | bytes 1277960 | tf_op jit(solution)/shard_map/ppermute | solution.py:240
  326.4 16.9 %collective-permute-start.11 = (bf16[1664,128]{1,0:T(8,128)(2,1)S(1)}, bf16[1664,128]{1,0:T(8,128)(2,1)S(1)}, u32[]{:S(2)}, u32[]{:S(2)}) collective-permute-start(bf16[1664,128]{1,0:T(8,128)(2,1)S(1)} %add_convert_fusion.9), channel_id=1, source_target_pairs={{0,2},{1,3},{2,0},{3,1},{4,6},{5,7},{6,4},{7,5},{8,10},{9,11},{10,... | collective-permute-start | bytes 1277960 | tf_op jit(solution)/shard_map/ppermute | solution.py:240
  343.1 18.7 %collective-permute-start.32 = (bf16[1664,128]{1,0:T(8,128)(2,1)S(1)}, bf16[1664,128]{1,0:T(8,128)(2,1)S(1)}, u32[]{:S(2)}, u32[]{:S(2)}) collective-permute-start(bf16[1664,128]{1,0:T(8,128)(2,1)S(1)} %get-tuple-element.62), channel_id=1, source_target_pairs={{0,1},{1,0},{2,3},{3,2},{4,5},{5,4},{6,7},{7,6},{8,9},{9,8},{10,11... | collective-permute-start | bytes 1277960 | tf_op jit(solution)/shard_map/ppermute | solution.py:237
  343.7 18.3 %collective-permute-start.13 = (bf16[832,128]{1,0:T(8,128)(2,1)S(1)}, bf16[832,128]{1,0:T(8,128)(2,1)S(1)}, u32[]{:S(2)}, u32[]{:S(2)}) collective-permute-start(bf16[832,128]{1,0:T(8,128)(2,1)S(1)} %get-tuple-element.83.refs_0_), channel_id=1, source_target_pairs={{0,8},{8,24},{24,16},{16,0},{1,9},{9,25},{25,17},{17,1},{2,10},{10... | collective-permute-start | bytes 638984 | tf_op jit(solution)/shard_map/ppermute | solution.py:226
  343.8 18.4 %collective-permute-start.14 = (bf16[832,128]{1,0:T(8,128)(2,1)S(1)}, bf16[832,128]{1,0:T(8,128)(2,1)S(1)}, u32[]{:S(2)}, u32[]{:S(2)}) collective-permute-start(bf16[832,128]{1,0:T(8,128)(2,1)S(1)} %get-tuple-element.82.refs_1_), channel_id=1, source_target_pairs={{0,8},{8,24},{24,16},{16,0},{1,9},{9,25},{25,17},{17,1},{2,10},{10... | collective-permute-start | bytes 638984 | tf_op jit(solution)/shard_map/ppermute | solution.py:226
  354.6 35.6 %collective-permute-start.36 = (bf16[1664,128]{1,0:T(8,128)(2,1)S(1)}, bf16[1664,128]{1,0:T(8,128)(2,1)S(1)}, u32[]{:S(2)}, u32[]{:S(2)}) collective-permute-start(bf16[1664,128]{1,0:T(8,128)(2,1)S(1)} %get-tuple-element.66), channel_id=1, source_target_pairs={{0,1},{1,0},{2,3},{3,2},{4,5},{5,4},{6,7},{7,6},{8,9},{9,8},{10,11... | collective-permute-start | bytes 1277960 | tf_op jit(solution)/shard_map/ppermute | solution.py:237
  361.9 47.7 %collective-permute-start.38 = (bf16[1664,128]{1,0:T(8,128)(2,1)S(1)}, bf16[1664,128]{1,0:T(8,128)(2,1)S(1)}, u32[]{:S(2)}, u32[]{:S(2)}) collective-permute-start(bf16[1664,128]{1,0:T(8,128)(2,1)S(1)} %get-tuple-element.68), channel_id=1, source_target_pairs={{0,1},{1,0},{2,3},{3,2},{4,5},{5,4},{6,7},{7,6},{8,9},{9,8},{10,11... | collective-permute-start | bytes 1277960 | tf_op jit(solution)/shard_map/ppermute | solution.py:237
  362.2 13.3 %collective-permute-start.16 = (bf16[832,128]{1,0:T(8,128)(2,1)S(1)}, bf16[832,128]{1,0:T(8,128)(2,1)S(1)}, u32[]{:S(2)}, u32[]{:S(2)}) collective-permute-start(bf16[832,128]{1,0:T(8,128)(2,1)S(1)} %collective-permute-done.14.refs_3_), channel_id=1, source_target_pairs={{0,8},{8,24},{24,16},{16,0},{1,9},{9,25},{25,17},{17,1},{2,10},{10... | collective-permute-start | bytes 638984 | tf_op jit(solution)/shard_map/ppermute | solution.py:226
  364.0 49.6 %collective-permute-start.33 = (bf16[1664,128]{1,0:T(8,128)(2,1)S(1)}, bf16[1664,128]{1,0:T(8,128)(2,1)S(1)}, u32[]{:S(2)}, u32[]{:S(2)}) collective-permute-start(bf16[1664,128]{1,0:T(8,128)(2,1)S(1)} %add_convert_fusion.5), channel_id=1, source_target_pairs={{0,6},{1,7},{2,4},{3,5},{4,2},{5,3},{6,0},{7,1},{8,14},{9,15},{10,... | collective-permute-start | bytes 1277960 | tf_op jit(solution)/shard_map/ppermute | solution.py:240
  380.1 33.5 %collective-permute-start.35 = (bf16[1664,128]{1,0:T(8,128)(2,1)S(1)}, bf16[1664,128]{1,0:T(8,128)(2,1)S(1)}, u32[]{:S(2)}, u32[]{:S(2)}) collective-permute-start(bf16[1664,128]{1,0:T(8,128)(2,1)S(1)} %add_convert_fusion.4), channel_id=1, source_target_pairs={{0,4},{1,5},{2,6},{3,7},{4,0},{5,1},{6,2},{7,3},{8,12},{9,13},{10,... | collective-permute-start | bytes 1277960 | tf_op jit(solution)/shard_map/ppermute | solution.py:240
  390.1 15.5 %collective-permute-start.19 = (bf16[1664,128]{1,0:T(8,128)(2,1)S(1)}, bf16[1664,128]{1,0:T(8,128)(2,1)S(1)}, u32[]{:S(2)}, u32[]{:S(2)}) collective-permute-start(bf16[1664,128]{1,0:T(8,128)(2,1)S(1)} %get-tuple-element.52), channel_id=1, source_target_pairs={{0,1},{1,0},{2,3},{3,2},{4,5},{5,4},{6,7},{7,6},{8,9},{9,8},{10,11... | collective-permute-start | bytes 1277960 | tf_op jit(solution)/shard_map/ppermute | solution.py:237
  390.3 23.9 %collective-permute-start.37 = (bf16[1664,128]{1,0:T(8,128)(2,1)S(1)}, bf16[1664,128]{1,0:T(8,128)(2,1)S(1)}, u32[]{:S(2)}, u32[]{:S(2)}) collective-permute-start(bf16[1664,128]{1,0:T(8,128)(2,1)S(1)} %add_convert_fusion.3), channel_id=1, source_target_pairs={{0,2},{1,3},{2,0},{3,1},{4,6},{5,7},{6,4},{7,5},{8,10},{9,11},{10,... | collective-permute-start | bytes 1277960 | tf_op jit(solution)/shard_map/ppermute | solution.py:240
  409.5 14.7 %collective-permute-start.20 = (bf16[1664,128]{1,0:T(8,128)(2,1)S(1)}, bf16[1664,128]{1,0:T(8,128)(2,1)S(1)}, u32[]{:S(2)}, u32[]{:S(2)}) collective-permute-start(bf16[1664,128]{1,0:T(8,128)(2,1)S(1)} %add_convert_fusion.8), channel_id=1, source_target_pairs={{0,6},{1,7},{2,4},{3,5},{4,2},{5,3},{6,0},{7,1},{8,14},{9,15},{10,... | collective-permute-start | bytes 1277960 | tf_op jit(solution)/shard_map/ppermute | solution.py:240
  413.6 19.5 %collective-permute-start.22 = (bf16[1664,128]{1,0:T(8,128)(2,1)S(1)}, bf16[1664,128]{1,0:T(8,128)(2,1)S(1)}, u32[]{:S(2)}, u32[]{:S(2)}) collective-permute-start(bf16[1664,128]{1,0:T(8,128)(2,1)S(1)} %add_convert_fusion.7), channel_id=1, source_target_pairs={{0,4},{1,5},{2,6},{3,7},{4,0},{5,1},{6,2},{7,3},{8,12},{9,13},{10,... | collective-permute-start | bytes 1277960 | tf_op jit(solution)/shard_map/ppermute | solution.py:240
  413.6 19.5 %collective-permute-start.24 = (bf16[1664,128]{1,0:T(8,128)(2,1)S(1)}, bf16[1664,128]{1,0:T(8,128)(2,1)S(1)}, u32[]{:S(2)}, u32[]{:S(2)}) collective-permute-start(bf16[1664,128]{1,0:T(8,128)(2,1)S(1)} %add_convert_fusion.6), channel_id=1, source_target_pairs={{0,2},{1,3},{2,0},{3,1},{4,6},{5,7},{6,4},{7,5},{8,10},{9,11},{10,... | collective-permute-start | bytes 1277960 | tf_op jit(solution)/shard_map/ppermute | solution.py:240
  434.0 13.6 %collective-permute-start.40 = (bf16[832,128]{1,0:T(8,128)(2,1)S(1)}, bf16[832,128]{1,0:T(8,128)(2,1)S(1)}, u32[]{:S(2)}, u32[]{:S(2)}) collective-permute-start(bf16[832,128]{1,0:T(8,128)(2,1)S(1)} %get-tuple-element.84.refs_1_), channel_id=1, source_target_pairs={{0,8},{8,24},{24,16},{16,0},{1,9},{9,25},{25,17},{17,1},{2,10},{10... | collective-permute-start | bytes 638984 | tf_op jit(solution)/shard_map/ppermute | solution.py:226
  470.9 15.9 %collective-permute-start.45 = (bf16[1664,128]{1,0:T(8,128)(2,1)S(1)}, bf16[1664,128]{1,0:T(8,128)(2,1)S(1)}, u32[]{:S(2)}, u32[]{:S(2)}) collective-permute-start(bf16[1664,128]{1,0:T(8,128)(2,1)S(1)} %get-tuple-element.70), channel_id=1, source_target_pairs={{0,1},{1,0},{2,3},{3,2},{4,5},{5,4},{6,7},{7,6},{8,9},{9,8},{10,11... | collective-permute-start | bytes 1277960 | tf_op jit(solution)/shard_map/ppermute | solution.py:237
  479.4 12.2 %collective-permute-start.49 = (bf16[1664,128]{1,0:T(8,128)(2,1)S(1)}, bf16[1664,128]{1,0:T(8,128)(2,1)S(1)}, u32[]{:S(2)}, u32[]{:S(2)}) collective-permute-start(bf16[1664,128]{1,0:T(8,128)(2,1)S(1)} %get-tuple-element.74), channel_id=1, source_target_pairs={{0,1},{1,0},{2,3},{3,2},{4,5},{5,4},{6,7},{7,6},{8,9},{9,8},{10,11... | collective-permute-start | bytes 1277960 | tf_op jit(solution)/shard_map/ppermute | solution.py:237
  487.6 13.8 %collective-permute-start.46 = (bf16[1664,128]{1,0:T(8,128)(2,1)}, bf16[1664,128]{1,0:T(8,128)(2,1)S(1)}, u32[]{:S(2)}, u32[]{:S(2)}) collective-permute-start(bf16[1664,128]{1,0:T(8,128)(2,1)} %add_convert_fusion.2), channel_id=1, source_target_pairs={{0,6},{1,7},{2,4},{3,5},{4,2},{5,3},{6,0},{7,1},{8,14},{9,15},{10,... | collective-permute-start | bytes 1277960 | tf_op jit(solution)/shard_map/ppermute | solution.py:240
  489.8 20.0 %collective-permute-start.48 = (bf16[1664,128]{1,0:T(8,128)(2,1)}, bf16[1664,128]{1,0:T(8,128)(2,1)}, u32[]{:S(2)}, u32[]{:S(2)}) collective-permute-start(bf16[1664,128]{1,0:T(8,128)(2,1)} %add_convert_fusion.1), channel_id=1, source_target_pairs={{0,4},{1,5},{2,6},{3,7},{4,0},{5,1},{6,2},{7,3},{8,12},{9,13},{10,... | collective-permute-start | bytes 1277960 | tf_op jit(solution)/shard_map/ppermute | solution.py:240
  492.5 17.9 %collective-permute-start.50 = (bf16[1664,128]{1,0:T(8,128)(2,1)}, bf16[1664,128]{1,0:T(8,128)(2,1)}, u32[]{:S(2)}, u32[]{:S(2)}) collective-permute-start(bf16[1664,128]{1,0:T(8,128)(2,1)} %add_convert_fusion), channel_id=1, source_target_pairs={{0,2},{1,3},{2,0},{3,1},{4,6},{5,7},{6,4},{7,5},{8,10},{9,11},{10,... | collective-permute-start | bytes 1277960 | tf_op jit(solution)/shard_map/ppermute | solution.py:240
  (31 other events, 769.0 us)

commit v2 on v1

v2 whole, which is shorter than its diff:
```python
import functools
import math

import jax
import jax.numpy as jnp
from jax import lax
from jax.experimental import pallas as pl
from jax.experimental.pallas import tpu as pltpu
from jax.sharding import PartitionSpec as P

UNROLL = 16
MIB = 1 << 20
VMEM = pl.BlockSpec(memory_space=pltpu.VMEM)
SMEM = pl.BlockSpec(memory_space=pltpu.SMEM)
ANY = pl.BlockSpec(memory_space=pl.ANY)


def bytes_of(*shapes):
    return sum(math.prod(s.shape) * jnp.dtype(s.dtype).itemsize for s in shapes)


def params(need):
    return pltpu.CompilerParams(vmem_limit_bytes=need + 3 * MIB)


def resident(values):
    def kernel(values_ref, held_ref, sem):
        copy = pltpu.make_async_copy(values_ref, held_ref, sem)
        copy.start()
        copy.wait()

    return pl.pallas_call(
        kernel,
        out_shape=pltpu.VMEM(values.shape, values.dtype),
        in_specs=[ANY],
        out_specs=VMEM,
        scratch_shapes=[pltpu.SemaphoreType.DMA],
        compiler_params=pltpu.CompilerParams(vmem_limit_bytes=MIB),
        cost_estimate=pl.CostEstimate(
            flops=0, bytes_accessed=bytes_of(values), transcendentals=0
        ),
        name="resident",
    )(values)


def columns_of(vectors, row, rows, low, width, after):
    def kernel(vectors_ref, *refs):
        out_ref, sem = refs[-2:]
        copy = pltpu.make_async_copy(
            vectors_ref.at[pl.ds(row, rows), pl.ds(low, width)], out_ref, sem
        )
        copy.start()
        copy.wait()

    out = jax.ShapeDtypeStruct((rows, width), vectors.dtype)
    return pl.pallas_call(
        kernel,
        out_shape=out,
        in_specs=[ANY] * (1 + len(after)),
        out_specs=VMEM,
        scratch_shapes=[pltpu.SemaphoreType.DMA],
        compiler_params=params(bytes_of(out)),
        cost_estimate=pl.CostEstimate(
            flops=0, bytes_accessed=2 * bytes_of(out), transcendentals=0
        ),
        name="columns_of",
    )(vectors, *after)


def image_kernel(shape, bounds, order, rows, cols, values, *refs):
    first_piece, pieces, part_count, own, orbitals = shape
    parts = refs[:part_count]
    outs = refs[part_count : part_count + 2 * pieces]
    total, panel = refs[part_count + 2 * pieces :]
    start = bounds[first_piece]
    end = bounds[first_piece + pieces]
    base = first_piece * 2 * own
    trash = pieces * 2 * own
    low = 0
    for part in parts:
        panel[low : low + part.shape[0], :] = part[...]
        low += part.shape[0]
    total[...] = jnp.zeros_like(total)

    def step(turn, carry):
        images = []
        for lane in range(UNROLL):
            entry = start + turn * UNROLL + lane
            picked = panel[pl.ds(pl.multiple_of(cols[entry] * orbitals, orbitals), orbitals), :]
            images.append(
                jnp.dot(values[order[entry]], picked, preferred_element_type=jnp.float32)
            )
        for lane in range(UNROLL):
            entry = start + turn * UNROLL + lane
            row = jnp.where(entry < end, rows[entry] - base, trash)
            place = pl.ds(pl.multiple_of(row * orbitals, orbitals), orbitals)
            total[place, :] += images[lane]
        return carry

    lax.fori_loop(0, (end - start + UNROLL - 1) // UNROLL, step, 0)
    height = own * orbitals
    for index, out in enumerate(outs):
        out[...] = total[index * height : (index + 1) * height, :].astype(out.dtype)


def images_of(first_piece, pieces, tables, values, parts, own):
    orbitals = values.shape[-1]
    width = parts[0].shape[1]
    panel_rows = sum(part.shape[0] for part in parts)
    out = jax.ShapeDtypeStruct((own * orbitals, width), jnp.bfloat16)
    total = jax.ShapeDtypeStruct(((pieces * 2 * own + 1) * orbitals, width), jnp.float32)
    entries = values.shape[0] * pieces // (tables[0].shape[0] - 1)
    kernel = functools.partial(image_kernel, (first_piece, pieces, len(parts), own, orbitals))
    return pl.pallas_call(
        kernel,
        out_shape=[out] * (2 * pieces),
        in_specs=[SMEM] * 4 + [VMEM] * (1 + len(parts)),
        out_specs=[VMEM] * (2 * pieces),
        scratch_shapes=[
            pltpu.VMEM(total.shape, total.dtype),
            pltpu.VMEM((panel_rows, width), jnp.bfloat16),
        ],
        compiler_params=params(bytes_of(total, *parts, *parts) + 2 * pieces * bytes_of(out)),
        cost_estimate=pl.CostEstimate(
            flops=entries * 8 * orbitals * orbitals * width,
            bytes_accessed=2 * (entries * orbitals * orbitals + panel_rows * width),
            transcendentals=0,
        ),
        name="images_of",
    )(*tables, values, *parts)


def added(kept, arrived):
    def kernel(kept_ref, arrived_ref, out_ref):
        out_ref[...] = (
            kept_ref[...].astype(jnp.float32) + arrived_ref[...].astype(jnp.float32)
        ).astype(out_ref.dtype)

    return pl.pallas_call(
        kernel,
        out_shape=jax.ShapeDtypeStruct(kept.shape, kept.dtype),
        in_specs=[VMEM] * 2,
        out_specs=VMEM,
        compiler_params=params(3 * bytes_of(kept)),
        cost_estimate=pl.CostEstimate(
            flops=kept.size, bytes_accessed=3 * bytes_of(kept), transcendentals=0
        ),
        name="added",
    )(kept, arrived)


def first_update(terms, vectors, low, center, half_width, sizes):
    width = terms[0].shape[1]

    def kernel(center_ref, width_ref, vectors_ref, *refs):
        term_refs, out_refs = refs[: len(terms)], refs[len(terms) :]
        row = 0
        for size, out_ref in zip(sizes, out_refs):
            span = slice(row, row + size)
            image = term_refs[0][span, :].astype(jnp.float32)
            for term_ref in term_refs[1:]:
                image += term_ref[span, :].astype(jnp.float32)
            source = vectors_ref[span, low : low + width].astype(jnp.float32)
            out_ref[...] = ((image - center_ref[0] * source) / width_ref[0]).astype(out_ref.dtype)
            row += size

    need = bytes_of(*terms, vectors) + bytes_of(terms[0])
    return pl.pallas_call(
        kernel,
        out_shape=[jax.ShapeDtypeStruct((size, width), jnp.bfloat16) for size in sizes],
        in_specs=[SMEM] * 2 + [VMEM] * (1 + len(terms)),
        out_specs=[VMEM] * len(sizes),
        compiler_params=params(need),
        cost_estimate=pl.CostEstimate(flops=0, bytes_accessed=need, transcendentals=0),
        name="first_update",
    )(center, half_width, vectors, *terms)


def second_update(terms, firsts, vectors, low, center, half_width, edges, edge_size):
    rows, width = terms[0].shape

    def kernel(edges_ref, center_ref, width_ref, vectors_ref, *refs):
        term_refs = refs[: len(terms)]
        first_refs = refs[len(terms) : len(terms) + len(firsts)]
        out_ref, edge_ref = refs[len(terms) + len(firsts) :]
        row = 0
        for first_ref in first_refs:
            span = slice(row, row + first_ref.shape[0])
            image = term_refs[0][span, :].astype(jnp.float32)
            for term_ref in term_refs[1:]:
                image += term_ref[span, :].astype(jnp.float32)
            source = vectors_ref[span, low : low + width].astype(jnp.float32)
            first = first_ref[...].astype(jnp.float32)
            out_ref[span, :] = (
                2.0 * (image - center_ref[0] * first) / width_ref[0] - source
            ).astype(out_ref.dtype)
            row += first_ref.shape[0]
        edge_ref[...] = out_ref[pl.ds(pl.multiple_of(edges_ref[0], 16), edge_size), :]

    need = bytes_of(*terms, *firsts, vectors) + 2 * bytes_of(terms[0])
    return pl.pallas_call(
        kernel,
        out_shape=[
            jax.ShapeDtypeStruct((rows, width), jnp.bfloat16),
            jax.ShapeDtypeStruct((edge_size, width), jnp.bfloat16),
        ],
        in_specs=[SMEM] * 3 + [VMEM] * (1 + len(terms) + len(firsts)),
        out_specs=[VMEM] * 2,
        compiler_params=params(need),
        cost_estimate=pl.CostEstimate(flops=0, bytes_accessed=need, transcendentals=0),
        name="second_update",
    )(edges, center, half_width, vectors, *terms, *firsts)


def relaid_rows(seconds, partners, edges, own, capacity, orbitals):
    width = seconds[0].shape[1]
    count = len(seconds)
    edge_size = partners[0].shape[0]

    def kernel(edges_ref, *refs):
        out_ref, window = refs[-2:]
        for index in range(count):
            window[pl.ds(pl.multiple_of(edges_ref[1], 16), own * orbitals), :] = refs[index][...]
            window[pl.ds(pl.multiple_of(edges_ref[2], 16), edge_size), :] = refs[count + index][...]
            for block in range(capacity):
                lane = slice(index * width, (index + 1) * width)
                span = slice(block * orbitals, (block + 1) * orbitals)

                @pl.when(block < edges_ref[4])
                def _():
                    row = pl.multiple_of(edges_ref[3] + block * orbitals, 16)
                    out_ref[span, lane] = window[pl.ds(row, orbitals), :]

                @pl.when(block >= edges_ref[4])
                def _():
                    out_ref[span, lane] = jnp.zeros((orbitals, width), out_ref.dtype)

    out = jax.ShapeDtypeStruct((capacity * orbitals, count * width), jnp.bfloat16)
    need = 2 * bytes_of(out) + bytes_of(*seconds, *partners)
    return pl.pallas_call(
        kernel,
        out_shape=out,
        in_specs=[SMEM] + [VMEM] * (2 * count),
        out_specs=VMEM,
        scratch_shapes=[pltpu.VMEM((own * orbitals + edge_size, width), jnp.bfloat16)],
        compiler_params=params(need),
        cost_estimate=pl.CostEstimate(flops=0, bytes_accessed=need, transcendentals=0),
        name="relaid_rows",
    )(edges, *seconds, *partners)


def ring_order(count):
    return [i for i in range(count) if i == 0 or i % 2] + [
        i for i in range(count - 1, 0, -1) if i and i % 2 == 0
    ]


def on_device(block_values, block_rows, block_cols, start_vectors, center, half_width, row_counts):
    orbitals = block_values.shape[-1]
    values = block_values.reshape(-1, orbitals, orbitals)
    row_ids = block_rows.reshape(-1)
    col_ids = block_cols.reshape(-1)
    entry_count = values.shape[0]
    own_rows, vec_count = start_vectors.shape
    own = own_rows // orbitals
    row_count = lax.axis_size("row")
    col_count = lax.axis_size("col")
    my_row = lax.axis_index("row")
    my_col = lax.axis_index("col")
    chip_count = col_count // 2

    order = ring_order(row_count)
    route = [(order[i], order[(i + 1) % row_count]) for i in range(row_count)]
    place_of = [order.index(i) for i in range(row_count)]

    def looked_up(table, index):
        result = jnp.zeros_like(index)
        for at, value in enumerate(table):
            result = jnp.where(index == at, value, result)
        return result

    with jax.named_scope("entry_order"):
        arrival = lax.rem(
            looked_up(place_of, my_row) - looked_up(place_of, col_ids // own) + row_count, row_count
        )
        panel_cols = arrival * own + col_ids % own
        relative = (row_ids // own) ^ my_col
        piece = chip_count - 1 - relative // 2
        out_rows = (piece * 2 + 1 - relative % 2) * own + row_ids % own
        number = jnp.arange(entry_count, dtype=jnp.int32)
        before = (out_rows[None, :] < out_rows[:, None]) | (
            (out_rows[None, :] == out_rows[:, None]) & (number[None, :] < number[:, None])
        )
        rank = jnp.sum(before.astype(jnp.int32), 1)
        at_rank = rank[None, :] == number[:, None]

        def ordered(items):
            return jnp.sum(jnp.where(at_rank, items[None, :], 0), 1).astype(jnp.int32)

        room = (0, UNROLL)
        entry_order = jnp.pad(ordered(number), room)
        rows = jnp.pad(ordered(out_rows), room)
        cols = jnp.pad(ordered(panel_cols), room)
        limits = jnp.arange(chip_count + 1, dtype=jnp.int32) * (2 * own)
        bounds = jnp.sum((out_rows[None, :] < limits[:, None]).astype(jnp.int32), 1)
        bounds = bounds.astype(jnp.int32)
        tables = (bounds, entry_order, rows, cols)
    values = resident(values)

    other_core = [(i, i ^ 1) for i in range(col_count)]
    if chip_count >= 4:
        groups = [(0, 1), (1, chip_count - 2), (chip_count - 1, 1)]
    else:
        groups = [(0, chip_count)]
    lanes = 128 if vec_count % 128 == 0 else vec_count
    lows = range(0, vec_count, lanes)
    cut = own_rows // 2 if own_rows % 32 == 0 else own_rows
    sizes = [cut, own_rows - cut] if cut < own_rows else [own_rows]

    def gathered(parts):
        held = list(parts)
        arrived = [held]
        for _ in range(row_count - 1):
            held = [lax.ppermute(part, "row", route) for part in held]
            arrived.append(held)
        return arrived

    def terms_of(arrived):
        parts = [part for step in arrived for part in step]
        terms = []
        for first_piece, pieces in groups:
            outs = images_of(first_piece, pieces, tables, values, parts, own)
            for index in range(pieces):
                chip = chip_count - 1 - first_piece - index
                kept = outs[2 * index + 1]
                partner = lax.ppermute(outs[2 * index], "col", other_core)
                if chip:
                    chips = [(i, i ^ 2 * chip) for i in range(col_count)]
                    terms.append(lax.ppermute(added(kept, partner), "col", chips))
                else:
                    terms += [kept, partner]
        return terms

    half_blocks = own // 2
    capacity = own + half_blocks
    edge_size = half_blocks * orbitals
    device = my_row * col_count + my_col
    parity = device % 2
    even_count = row_counts[device - parity]
    edges = jnp.stack(
        [
            (1 - parity) * (own_rows - edge_size),
            parity * edge_size,
            (1 - parity) * own_rows,
            parity * (even_count - (own - half_blocks)) * orbitals,
            row_counts[device],
        ]
    ).astype(jnp.int32)

    first_arrived = []
    after = [[] for _ in sizes]
    for low in lows:
        parts = [
            columns_of(start_vectors, index * cut, size, low, lanes, after[index])
            for index, size in enumerate(sizes)
        ]
        first_arrived.append(gathered(parts))
        after = [[part] for part in first_arrived[-1][-1]]
    firsts = [
        first_update(terms_of(arrived), start_vectors, low, center, half_width, sizes)
        for low, arrived in zip(lows, first_arrived)
    ]
    seconds, partners = [], []
    for low, first in zip(lows, firsts):
        terms = terms_of(gathered(first))
        second, edge = second_update(
            terms, first, start_vectors, low, center, half_width, edges, edge_size
        )
        seconds.append(second)
        partners.append(lax.ppermute(edge, "col", other_core))
    return relaid_rows(seconds, partners, edges, own, capacity, orbitals)


def solution(mesh):
    placed = (
        P("row", "col", None, None, None),
        P("row", "col", None),
        P("row", "col", None),
        P(("row", "col"), None),
        P(),
        P(),
        P(),
    )
    return jax.shard_map(
        on_device, mesh=mesh, in_specs=placed, out_specs=P(("row", "col"), None), check_vma=False
    )
```

time: 518 us -> 221 us (0.43)
  Pallas kernels: 342 us -> 42.7 us
  local copies, waits for them, and re-layouts: 1.2 us -> 15.2 us
  waiting for transfers between devices: 112 us -> 98.7 us
  starting transfers between devices: 45.4 us -> 57.5 us
  other arithmetic: 14.1 us -> 3.41 us
    pallas_call x15 -> x34, Pallas kernels: 342 us -> 42.7 us  [the longest x12 33.6 us: images_of(): pl.pallas_call(kernel, out_shape=[out] * (2 * pieces), in_specs=[SMEM] *...]
    ppermute x24, waiting for transfers between devices: 72.6 us -> 55.1 us  [gathered(): held = [lax.ppermute(part, 'row', route) for part in held]]
    unnamed x20 -> x30, local copies, waits for them, and re-layouts: 0.48 us -> 13.8 us
    ppermute x24, starting transfers between devices: 23.4 us -> 36.2 us  [gathered(): held = [lax.ppermute(part, 'row', route) for part in held]]
    convert_element_type x15 -> x0, other arithmetic: 6.53 us -> none  [the longest x12 3.65 us: summed(): both.astype(jnp.bfloat16)]
    ppermute x29 -> x30, waiting for transfers between devices: 39.3 us -> 43.6 us  [the longest x12 42.1 us: terms_of(): terms.append(lax.ppermute(added(kept, partner), 'col', chips))]
    ppermute x29 -> x30, starting transfers between devices: 22 us -> 21.4 us  [the longest x12 17.3 us: terms_of(): terms.append(lax.ppermute(added(kept, partner), 'col', chips))]
  transfers between devices with their start and end apart: 53 -> 54, of which waited for: 25 -> 26; matrix products, arithmetic and copies ran while one was open for 2% -> 2% of each run, Pallas kernels for 63% -> 18%
where the time goes in v2:
time: 221 us; the launch traced here: 220 us
  waiting for transfers between devices  98.7 us (45%)
  starting transfers between devices  57.5 us (26%)
  Pallas kernels  42.7 us (19%)
  local copies, waits for them, and re-layouts  15.2 us (7%)
  other arithmetic  3.41 us (2%)
  between operations  2.47 us (1%)
    ppermute x24, waiting for transfers between devices, gathered(): held = [lax.ppermute(part, 'row', route) for part in held]  55.1 us
    ppermute x12, waiting for transfers between devices, terms_of(): terms.append(lax.ppermute(added(kept, partner), 'col', chips))  42.1 us
    ppermute x24, starting transfers between devices, gathered(): held = [lax.ppermute(part, 'row', route) for part in held]  36.2 us
    pallas_call x12, Pallas kernels, images_of(): pl.pallas_call(kernel, out_shape=[out] * (2 * pieces), in_specs=[SMEM] *...  33.6 us
    ppermute x12, starting transfers between devices, terms_of(): terms.append(lax.ppermute(added(kept, partner), 'col', chips))  17.3 us
    unnamed x30, local copies, waits for them, and re-layouts  13.8 us
  transfers between devices with their start and end apart: 54, of which 26 were waited for; matrix products, arithmetic and copies ran while one was open for 2% of the time, Pallas kernels for 18%

profile of v2, /device:TPU:0, one launch (start us, length us, event | category | flops | bytes accessed | tf_op | source)
XLA Modules:
  0.0 220.0 jit_solution(9658837533977571787)
XLA Ops:
  1.2 3.1 %collective-permute-start = (bf16[832,128]{1,0:T(8,128)(2,1)S(1)}, bf16[832,128]{1,0:T(8,128)(2,1)S(1)}, u32[]{:S(2)}, u32[]{:S(2)}) collective-permute-start(bf16[832,128]{1,0:T(8,128)(2,1)S(1)} %columns_of.4.refs_0_), channel_id=1, source_target_pairs={{0,8},{8,24},{24,16},{16,0},{1,9},{9,25},{25,17},{17,1},{2,10},{10... | collective-permute-start | bytes 638984 | tf_op jit(solution)/shard_map/ppermute | solution.py:324
  4.3 2.6 %collective-permute-start.1 = (bf16[832,128]{1,0:T(8,128)(2,1)S(1)}, bf16[832,128]{1,0:T(8,128)(2,1)S(1)}, u32[]{:S(2)}, u32[]{:S(2)}) collective-permute-start(bf16[832,128]{1,0:T(8,128)(2,1)S(1)} %columns_of.5.refs_1_), channel_id=1, source_target_pairs={{0,8},{8,24},{24,16},{16,0},{1,9},{9,25},{25,17},{17,1},{2,10},{10... | collective-permute-start | bytes 638984 | tf_op jit(solution)/shard_map/ppermute | solution.py:324
  12.5 3.4 %collective-permute-done.1.refs_3_ = bf16[832,128]{1,0:T(8,128)(2,1)S(1)} collective-permute-done((bf16[832,128]{1,0:T(8,128)(2,1)S(1)}, bf16[832,128]{1,0:T(8,128)(2,1)S(1)}, u32[]{:S(2)}, u32[]{:S(2)}) %collective-permute-start.1) | collective-permute-done | bytes 213024 | tf_op jit(solution)/shard_map/ppermute | solution.py:324
  17.8 2.7 %collective-permute-done.2.refs_4_ = bf16[832,128]{1,0:T(8,128)(2,1)S(1)} collective-permute-done((bf16[832,128]{1,0:T(8,128)(2,1)S(1)}, bf16[832,128]{1,0:T(8,128)(2,1)S(1)}, u32[]{:S(2)}, u32[]{:S(2)}) %collective-permute-start.2) | collective-permute-done | bytes 213024 | tf_op jit(solution)/shard_map/ppermute | solution.py:324
  21.7 3.4 %collective-permute-done.3.refs_5_ = bf16[832,128]{1,0:T(8,128)(2,1)S(1)} collective-permute-done((bf16[832,128]{1,0:T(8,128)(2,1)S(1)}, bf16[832,128]{1,0:T(8,128)(2,1)S(1)}, u32[]{:S(2)}, u32[]{:S(2)}) %collective-permute-start.3) | collective-permute-done | bytes 213024 | tf_op jit(solution)/shard_map/ppermute | solution.py:324
  26.2 3.4 %collective-permute-done.4.refs_6_.refs_0_ = bf16[832,128]{1,0:T(8,128)(2,1)S(1)} collective-permute-done((bf16[832,128]{1,0:T(8,128)(2,1)S(1)}, bf16[832,128]{1,0:T(8,128)(2,1)S(1)}, u32[]{:S(2)}, u32[]{:S(2)}) %collective-permute-start.4) | collective-permute-done | bytes 213024 | tf_op jit(solution)/shard_map/ppermute | solution.py:324
  36.0 3.4 %copy-done.3 = bf16[1,1,256,128,128]{4,3,2,1,0:T(8,128)(2,1)S(1)} copy-done((bf16[1,1,256,128,128]{4,3,2,1,0:T(8,128)(2,1)S(1)}, bf16[1,1,256,128,128]{4,3,2,1,0:T(8,128)(2,1)}, u32[]{:S(2)}) %copy-start.3) | copy-done | bytes 8388632
  40.0 3.0 %collective-permute-start.28 = (bf16[832,128]{1,0:T(8,128)(2,1)S(1)}, bf16[832,128]{1,0:T(8,128)(2,1)S(1)}, u32[]{:S(2)}, u32[]{:S(2)}) collective-permute-start(bf16[832,128]{1,0:T(8,128)(2,1)S(1)} %collective-permute-done.26.refs_2_), channel_id=1, source_target_pairs={{0,8},{8,24},{24,16},{16,0},{1,9},{9,25},{25,17},{17,1},{2,10},{10... | collective-permute-start | bytes 638984 | tf_op jit(solution)/shard_map/ppermute | solution.py:324
  45.6 3.5 %collective-permute-done.28.refs_4_ = bf16[832,128]{1,0:T(8,128)(2,1)S(1)} collective-permute-done((bf16[832,128]{1,0:T(8,128)(2,1)S(1)}, bf16[832,128]{1,0:T(8,128)(2,1)S(1)}, u32[]{:S(2)}, u32[]{:S(2)}) %collective-permute-start.28) | collective-permute-done | bytes 213024 | tf_op jit(solution)/shard_map/ppermute | solution.py:324
  51.1 2.5 %collective-permute-done.29.refs_5_ = bf16[832,128]{1,0:T(8,128)(2,1)S(1)} collective-permute-done((bf16[832,128]{1,0:T(8,128)(2,1)S(1)}, bf16[832,128]{1,0:T(8,128)(2,1)S(1)}, u32[]{:S(2)}, u32[]{:S(2)}) %collective-permute-start.29) | collective-permute-done | bytes 213024 | tf_op jit(solution)/shard_map/ppermute | solution.py:324
  57.9 3.6 %images_of.13 = (bf16[1664,128]{1,0:T(8,128)(2,1)S(1)}, bf16[1664,128]{1,0:T(8,128)(2,1)S(1)}, bf16[1664,128]{1,0:T(8,128)(2,1)S(1)}, bf16[1664,128]{1,0:T(8,128)(2,1)S(1)}) custom-call(s32[5]{0:T(128)S(1)} %convert_reduce_fusion.1.bounds, s32[272]{0:T(512)S(1)} %pad.10.order, s32[272]{0:T(512)S(1)} %pad.11.rows, s32[272]{0:T(512)S(1)} %pad.12.cols, ...), custom_call_target="tpu_custom_call" | custom-call | flops 2147483648 | bytes 5898240 | tf_op jit(solution)/shard_map/images_of/pallas_call | solution.py:114
  65.2 3.6 %images_of.19 = (bf16[1664,128]{1,0:T(8,128)(2,1)S(1)}, bf16[1664,128]{1,0:T(8,128)(2,1)S(1)}, bf16[1664,128]{1,0:T(8,128)(2,1)S(1)}, bf16[1664,128]{1,0:T(8,128)(2,1)S(1)}) custom-call(s32[5]{0:T(128)S(1)} %convert_reduce_fusion.1.bounds, s32[272]{0:T(512)S(1)} %pad.10.order, s32[272]{0:T(512)S(1)} %pad.11.rows, s32[272]{0:T(512)S(1)} %pad.12.cols, ...), custom_call_target="tpu_custom_call" | custom-call | flops 2147483648 | bytes 5898240 | tf_op jit(solution)/shard_map/images_of/pallas_call | solution.py:114
  72.1 2.9 %collective-permute-start.7 = (bf16[1664,128]{1,0:T(8,128)(2,1)S(1)}, bf16[1664,128]{1,0:T(8,128)(2,1)S(1)}, u32[]{:S(2)}, u32[]{:S(2)}) collective-permute-start(bf16[1664,128]{1,0:T(8,128)(2,1)S(1)} %added.12), channel_id=1, source_target_pairs={{0,6},{1,7},{2,4},{3,5},{4,2},{5,3},{6,0},{7,1},{8,14},{9,15},{10,... | collective-permute-start | bytes 1277960 | tf_op jit(solution)/shard_map/ppermute | solution.py:339
  78.7 2.6 %collective-permute-start.33 = (bf16[1664,128]{1,0:T(8,128)(2,1)S(1)}, bf16[1664,128]{1,0:T(8,128)(2,1)S(1)}, u32[]{:S(2)}, u32[]{:S(2)}) collective-permute-start(bf16[1664,128]{1,0:T(8,128)(2,1)S(1)} %added.18), channel_id=1, source_target_pairs={{0,6},{1,7},{2,4},{3,5},{4,2},{5,3},{6,0},{7,1},{8,14},{9,15},{10,... | collective-permute-start | bytes 1277960 | tf_op jit(solution)/shard_map/ppermute | solution.py:339
  81.3 4.4 %collective-permute-done.7.refs_0_ = bf16[1664,128]{1,0:T(8,128)(2,1)S(1)} collective-permute-done((bf16[1664,128]{1,0:T(8,128)(2,1)S(1)}, bf16[1664,128]{1,0:T(8,128)(2,1)S(1)}, u32[]{:S(2)}, u32[]{:S(2)}) %collective-permute-start.7) | collective-permute-done | bytes 426016 | tf_op jit(solution)/shard_map/ppermute | solution.py:339
  87.0 7.9 %collective-permute-done.9.refs_1_ = bf16[1664,128]{1,0:T(8,128)(2,1)S(1)} collective-permute-done((bf16[1664,128]{1,0:T(8,128)(2,1)S(1)}, bf16[1664,128]{1,0:T(8,128)(2,1)S(1)}, u32[]{:S(2)}, u32[]{:S(2)}) %collective-permute-start.9) | collective-permute-done | bytes 426016 | tf_op jit(solution)/shard_map/ppermute | solution.py:339
  101.1 2.9 %collective-permute-done.33.refs_0_ = bf16[1664,128]{1,0:T(8,128)(2,1)S(1)} collective-permute-done((bf16[1664,128]{1,0:T(8,128)(2,1)S(1)}, bf16[1664,128]{1,0:T(8,128)(2,1)S(1)}, u32[]{:S(2)}, u32[]{:S(2)}) %collective-permute-start.33) | collective-permute-done | bytes 426016 | tf_op jit(solution)/shard_map/ppermute | solution.py:339
  104.0 8.6 %collective-permute-done.35.refs_1_ = bf16[1664,128]{1,0:T(8,128)(2,1)S(1)} collective-permute-done((bf16[1664,128]{1,0:T(8,128)(2,1)S(1)}, bf16[1664,128]{1,0:T(8,128)(2,1)S(1)}, u32[]{:S(2)}, u32[]{:S(2)}) %collective-permute-start.35) | collective-permute-done | bytes 426016 | tf_op jit(solution)/shard_map/ppermute | solution.py:339
  118.0 4.1 %collective-permute-done.39.refs_2_ = bf16[832,128]{1,0:T(8,128)(2,1)S(1)} collective-permute-done((bf16[832,128]{1,0:T(8,128)(2,1)S(1)}, bf16[832,128]{1,0:T(8,128)(2,1)S(1)}, u32[]{:S(2)}, u32[]{:S(2)}) %collective-permute-start.39) | collective-permute-done | bytes 213024 | tf_op jit(solution)/shard_map/ppermute | solution.py:324
  123.2 3.5 %collective-permute-done.40.refs_3_ = bf16[832,128]{1,0:T(8,128)(2,1)S(1)} collective-permute-done((bf16[832,128]{1,0:T(8,128)(2,1)S(1)}, bf16[832,128]{1,0:T(8,128)(2,1)S(1)}, u32[]{:S(2)}, u32[]{:S(2)}) %collective-permute-start.40) | collective-permute-done | bytes 213024 | tf_op jit(solution)/shard_map/ppermute | solution.py:324
  127.8 3.5 %collective-permute-done.15.refs_4_ = bf16[832,128]{1,0:T(8,128)(2,1)S(1)} collective-permute-done((bf16[832,128]{1,0:T(8,128)(2,1)S(1)}, bf16[832,128]{1,0:T(8,128)(2,1)S(1)}, u32[]{:S(2)}, u32[]{:S(2)}) %collective-permute-start.15) | collective-permute-done | bytes 213024 | tf_op jit(solution)/shard_map/ppermute | solution.py:324
  132.3 3.5 %collective-permute-done.16.refs_5_ = bf16[832,128]{1,0:T(8,128)(2,1)S(1)} collective-permute-done((bf16[832,128]{1,0:T(8,128)(2,1)S(1)}, bf16[832,128]{1,0:T(8,128)(2,1)S(1)}, u32[]{:S(2)}, u32[]{:S(2)}) %collective-permute-start.16) | collective-permute-done | bytes 213024 | tf_op jit(solution)/shard_map/ppermute | solution.py:324
  136.9 3.5 %collective-permute-done.41.refs_4_ = bf16[832,128]{1,0:T(8,128)(2,1)S(1)} collective-permute-done((bf16[832,128]{1,0:T(8,128)(2,1)S(1)}, bf16[832,128]{1,0:T(8,128)(2,1)S(1)}, u32[]{:S(2)}, u32[]{:S(2)}) %collective-permute-start.41) | collective-permute-done | bytes 213024 | tf_op jit(solution)/shard_map/ppermute | solution.py:324
  141.4 3.5 %collective-permute-done.42.refs_5_ = bf16[832,128]{1,0:T(8,128)(2,1)S(1)} collective-permute-done((bf16[832,128]{1,0:T(8,128)(2,1)S(1)}, bf16[832,128]{1,0:T(8,128)(2,1)S(1)}, u32[]{:S(2)}, u32[]{:S(2)}) %collective-permute-start.42) | collective-permute-done | bytes 213024 | tf_op jit(solution)/shard_map/ppermute | solution.py:324
  146.0 3.5 %collective-permute-done.17.refs_6_ = bf16[832,128]{1,0:T(8,128)(2,1)S(1)} collective-permute-done((bf16[832,128]{1,0:T(8,128)(2,1)S(1)}, bf16[832,128]{1,0:T(8,128)(2,1)S(1)}, u32[]{:S(2)}, u32[]{:S(2)}) %collective-permute-start.17) | collective-permute-done | bytes 213024 | tf_op jit(solution)/shard_map/ppermute | solution.py:324
  149.5 4.6 %collective-permute-done.18.refs_7_ = bf16[832,128]{1,0:T(8,128)(2,1)S(1)} collective-permute-done((bf16[832,128]{1,0:T(8,128)(2,1)S(1)}, bf16[832,128]{1,0:T(8,128)(2,1)S(1)}, u32[]{:S(2)}, u32[]{:S(2)}) %collective-permute-start.18) | collective-permute-done | bytes 213024 | tf_op jit(solution)/shard_map/ppermute | solution.py:324
  156.3 3.7 %images_of.16 = (bf16[1664,128]{1,0:T(8,128)(2,1)S(1)}, bf16[1664,128]{1,0:T(8,128)(2,1)S(1)}, bf16[1664,128]{1,0:T(8,128)(2,1)S(1)}, bf16[1664,128]{1,0:T(8,128)(2,1)S(1)}) custom-call(s32[5]{0:T(128)S(1)} %convert_reduce_fusion.1.bounds, s32[272]{0:T(512)S(1)} %pad.10.order, s32[272]{0:T(512)S(1)} %pad.11.rows, s32[272]{0:T(512)S(1)} %pad.12.cols, ...), custom_call_target="tpu_custom_call" | custom-call | flops 2147483648 | bytes 5898240 | tf_op jit(solution)/shard_map/images_of/pallas_call | solution.py:114
  167.7 3.6 %images_of.22 = (bf16[1664,128]{1,0:T(8,128)(2,1)S(1)}, bf16[1664,128]{1,0:T(8,128)(2,1)S(1)}, bf16[1664,128]{1,0:T(8,128)(2,1)S(1)}, bf16[1664,128]{1,0:T(8,128)(2,1)S(1)}) custom-call(s32[5]{0:T(128)S(1)} %convert_reduce_fusion.1.bounds, s32[272]{0:T(512)S(1)} %pad.10.order, s32[272]{0:T(512)S(1)} %pad.11.rows, s32[272]{0:T(512)S(1)} %pad.12.cols, ...), custom_call_target="tpu_custom_call" | custom-call | flops 2147483648 | bytes 5898240 | tf_op jit(solution)/shard_map/images_of/pallas_call | solution.py:114
  175.3 3.2 %images_of.23 = (bf16[1664,128]{1,0:T(8,128)(2,1)}, bf16[1664,128]{1,0:T(8,128)(2,1)S(1)}) custom-call(s32[5]{0:T(128)S(1)} %convert_reduce_fusion.1.bounds, s32[272]{0:T(512)S(1)} %pad.10.order, s32[272]{0:T(512)S(1)} %pad.11.rows, s32[272]{0:T(512)S(1)} %pad.12.cols, bf16[256,128,128]{2,1,0:T(8,128)(2,1)S(1)} %resident.1.values, ...), custom_call_target="tpu_custom_call" | custom-call | flops 1073741824 | bytes 3801088 | tf_op jit(solution)/shard_map/images_of/pallas_call | solution.py:114
  182.3 3.7 %collective-permute-done.20.refs_0_ = bf16[1664,128]{1,0:T(8,128)(2,1)S(1)} collective-permute-done((bf16[1664,128]{1,0:T(8,128)(2,1)S(1)}, bf16[1664,128]{1,0:T(8,128)(2,1)S(1)}, u32[]{:S(2)}, u32[]{:S(2)}) %collective-permute-start.20) | collective-permute-done | bytes 426016 | tf_op jit(solution)/shard_map/ppermute | solution.py:339
  188.3 6.9 %collective-permute-done.22.refs_1_ = bf16[1664,128]{1,0:T(8,128)(2,1)S(1)} collective-permute-done((bf16[1664,128]{1,0:T(8,128)(2,1)S(1)}, bf16[1664,128]{1,0:T(8,128)(2,1)S(1)}, u32[]{:S(2)}, u32[]{:S(2)}) %collective-permute-start.22) | collective-permute-done | bytes 426016 | tf_op jit(solution)/shard_map/ppermute | solution.py:339
  205.2 7.6 %collective-permute-done.48.refs_1_ = bf16[1664,128]{1,0:T(8,128)(2,1)} collective-permute-done((bf16[1664,128]{1,0:T(8,128)(2,1)S(1)}, bf16[1664,128]{1,0:T(8,128)(2,1)}, u32[]{:S(2)}, u32[]{:S(2)}) %collective-permute-start.48) | collective-permute-done | bytes 426016 | tf_op jit(solution)/shard_map/ppermute | solution.py:339
  (155 shorter events, 91.8 us)
Async XLA Ops:
  4.3 11.6 %collective-permute-start.1 = (bf16[832,128]{1,0:T(8,128)(2,1)S(1)}, bf16[832,128]{1,0:T(8,128)(2,1)S(1)}, u32[]{:S(2)}, u32[]{:S(2)}) collective-permute-start(bf16[832,128]{1,0:T(8,128)(2,1)S(1)} %columns_of.5.refs_1_), channel_id=1, source_target_pairs={{0,8},{8,24},{24,16},{16,0},{1,9},{9,25},{25,17},{17,1},{2,10},{10... | collective-permute-start | bytes 638984 | tf_op jit(solution)/shard_map/ppermute | solution.py:324
  49.1 13.1 %collective-permute-start.30 = (bf16[832,128]{1,0:T(8,128)(2,1)S(1)}, bf16[832,128]{1,0:T(8,128)(2,1)S(1)}, u32[]{:S(2)}, u32[]{:S(2)}) collective-permute-start(bf16[832,128]{1,0:T(8,128)(2,1)S(1)} %collective-permute-done.28.refs_4_), channel_id=1, source_target_pairs={{0,8},{8,24},{24,16},{16,0},{1,9},{9,25},{25,17},{17,1},{2,10},{10... | collective-permute-start | bytes 638984 | tf_op jit(solution)/shard_map/ppermute | solution.py:324
  57.9 11.0 %collective-permute-start.6 = (bf16[1664,128]{1,0:T(8,128)(2,1)S(1)}, bf16[1664,128]{1,0:T(8,128)(2,1)S(1)}, u32[]{:S(2)}, u32[]{:S(2)}) collective-permute-start(bf16[1664,128]{1,0:T(8,128)(2,1)S(1)} %get-tuple-element.46), channel_id=1, source_target_pairs={{0,1},{1,0},{2,3},{3,2},{4,5},{5,4},{6,7},{7,6},{8,9},{9,8},{10,11... | collective-permute-start | bytes 1277960 | tf_op jit(solution)/shard_map/ppermute | solution.py:336
  72.1 13.6 %collective-permute-start.7 = (bf16[1664,128]{1,0:T(8,128)(2,1)S(1)}, bf16[1664,128]{1,0:T(8,128)(2,1)S(1)}, u32[]{:S(2)}, u32[]{:S(2)}) collective-permute-start(bf16[1664,128]{1,0:T(8,128)(2,1)S(1)} %added.12), channel_id=1, source_target_pairs={{0,6},{1,7},{2,4},{3,5},{4,2},{5,3},{6,0},{7,1},{8,14},{9,15},{10,... | collective-permute-start | bytes 1277960 | tf_op jit(solution)/shard_map/ppermute | solution.py:339
  75.0 19.9 %collective-permute-start.9 = (bf16[1664,128]{1,0:T(8,128)(2,1)S(1)}, bf16[1664,128]{1,0:T(8,128)(2,1)S(1)}, u32[]{:S(2)}, u32[]{:S(2)}) collective-permute-start(bf16[1664,128]{1,0:T(8,128)(2,1)S(1)} %added.13), channel_id=1, source_target_pairs={{0,4},{1,5},{2,6},{3,7},{4,0},{5,1},{6,2},{7,3},{8,12},{9,13},{10,... | collective-permute-start | bytes 1277960 | tf_op jit(solution)/shard_map/ppermute | solution.py:339
  75.2 22.5 %collective-permute-start.11 = (bf16[1664,128]{1,0:T(8,128)(2,1)S(1)}, bf16[1664,128]{1,0:T(8,128)(2,1)S(1)}, u32[]{:S(2)}, u32[]{:S(2)}) collective-permute-start(bf16[1664,128]{1,0:T(8,128)(2,1)S(1)} %added.14), channel_id=1, source_target_pairs={{0,2},{1,3},{2,0},{3,1},{4,6},{5,7},{6,4},{7,5},{8,10},{9,11},{10,... | collective-permute-start | bytes 1277960 | tf_op jit(solution)/shard_map/ppermute | solution.py:339
  78.3 22.1 %collective-permute-start.38 = (bf16[1664,128]{1,0:T(8,128)(2,1)S(1)}, bf16[1664,128]{1,0:T(8,128)(2,1)S(1)}, u32[]{:S(2)}, u32[]{:S(2)}) collective-permute-start(bf16[1664,128]{1,0:T(8,128)(2,1)S(1)} %get-tuple-element.71), channel_id=1, source_target_pairs={{0,1},{1,0},{2,3},{3,2},{4,5},{5,4},{6,7},{7,6},{8,9},{9,8},{10,11... | collective-permute-start | bytes 1277960 | tf_op jit(solution)/shard_map/ppermute | solution.py:336
  78.7 25.3 %collective-permute-start.33 = (bf16[1664,128]{1,0:T(8,128)(2,1)S(1)}, bf16[1664,128]{1,0:T(8,128)(2,1)S(1)}, u32[]{:S(2)}, u32[]{:S(2)}) collective-permute-start(bf16[1664,128]{1,0:T(8,128)(2,1)S(1)} %added.18), channel_id=1, source_target_pairs={{0,6},{1,7},{2,4},{3,5},{4,2},{5,3},{6,0},{7,1},{8,14},{9,15},{10,... | collective-permute-start | bytes 1277960 | tf_op jit(solution)/shard_map/ppermute | solution.py:339
  85.7 26.9 %collective-permute-start.35 = (bf16[1664,128]{1,0:T(8,128)(2,1)S(1)}, bf16[1664,128]{1,0:T(8,128)(2,1)S(1)}, u32[]{:S(2)}, u32[]{:S(2)}) collective-permute-start(bf16[1664,128]{1,0:T(8,128)(2,1)S(1)} %added.19), channel_id=1, source_target_pairs={{0,4},{1,5},{2,6},{3,7},{4,0},{5,1},{6,2},{7,3},{8,12},{9,13},{10,... | collective-permute-start | bytes 1277960 | tf_op jit(solution)/shard_map/ppermute | solution.py:339
  94.9 17.8 %collective-permute-start.37 = (bf16[1664,128]{1,0:T(8,128)(2,1)S(1)}, bf16[1664,128]{1,0:T(8,128)(2,1)S(1)}, u32[]{:S(2)}, u32[]{:S(2)}) collective-permute-start(bf16[1664,128]{1,0:T(8,128)(2,1)S(1)} %added.20), channel_id=1, source_target_pairs={{0,2},{1,3},{2,0},{3,1},{4,6},{5,7},{6,4},{7,5},{8,10},{9,11},{10,... | collective-permute-start | bytes 1277960 | tf_op jit(solution)/shard_map/ppermute | solution.py:339
  98.1 17.6 %collective-permute-start.13 = (bf16[832,128]{1,0:T(8,128)(2,1)S(1)}, bf16[832,128]{1,0:T(8,128)(2,1)S(1)}, u32[]{:S(2)}, u32[]{:S(2)}) collective-permute-start(bf16[832,128]{1,0:T(8,128)(2,1)S(1)} %get-tuple-element.53.refs_0_.refs_5_), channel_id=1, source_target_pairs={{0,8},{8,24},{24,16},{16,0},{1,9},{9,25},{25,17},{17,1},{2,10},{10... | collective-permute-start | bytes 638984 | tf_op jit(solution)/shard_map/ppermute | solution.py:324
  100.4 16.3 %collective-permute-start.14 = (bf16[832,128]{1,0:T(8,128)(2,1)S(1)}, bf16[832,128]{1,0:T(8,128)(2,1)S(1)}, u32[]{:S(2)}, u32[]{:S(2)}) collective-permute-start(bf16[832,128]{1,0:T(8,128)(2,1)S(1)} %get-tuple-element.54.refs_1_.refs_6_), channel_id=1, source_target_pairs={{0,8},{8,24},{24,16},{16,0},{1,9},{9,25},{25,17},{17,1},{2,10},{10... | collective-permute-start | bytes 638984 | tf_op jit(solution)/shard_map/ppermute | solution.py:324
  115.1 11.6 %collective-permute-start.40 = (bf16[832,128]{1,0:T(8,128)(2,1)S(1)}, bf16[832,128]{1,0:T(8,128)(2,1)S(1)}, u32[]{:S(2)}, u32[]{:S(2)}) collective-permute-start(bf16[832,128]{1,0:T(8,128)(2,1)S(1)} %get-tuple-element.73.refs_1_.refs_6_), channel_id=1, source_target_pairs={{0,8},{8,24},{24,16},{16,0},{1,9},{9,25},{25,17},{17,1},{2,10},{10... | collective-permute-start | bytes 638984 | tf_op jit(solution)/shard_map/ppermute | solution.py:324
  115.7 15.5 %collective-permute-start.15 = (bf16[832,128]{1,0:T(8,128)(2,1)S(1)}, bf16[832,128]{1,0:T(8,128)(2,1)S(1)}, u32[]{:S(2)}, u32[]{:S(2)}) collective-permute-start(bf16[832,128]{1,0:T(8,128)(2,1)S(1)} %collective-permute-done.13.refs_2_), channel_id=1, source_target_pairs={{0,8},{8,24},{24,16},{16,0},{1,9},{9,25},{25,17},{17,1},{2,10},{10... | collective-permute-start | bytes 638984 | tf_op jit(solution)/shard_map/ppermute | solution.py:324
  116.7 19.1 %collective-permute-start.16 = (bf16[832,128]{1,0:T(8,128)(2,1)S(1)}, bf16[832,128]{1,0:T(8,128)(2,1)S(1)}, u32[]{:S(2)}, u32[]{:S(2)}) collective-permute-start(bf16[832,128]{1,0:T(8,128)(2,1)S(1)} %collective-permute-done.14.refs_3_), channel_id=1, source_target_pairs={{0,8},{8,24},{24,16},{16,0},{1,9},{9,25},{25,17},{17,1},{2,10},{10... | collective-permute-start | bytes 638984 | tf_op jit(solution)/shard_map/ppermute | solution.py:324
  122.1 18.3 %collective-permute-start.41 = (bf16[832,128]{1,0:T(8,128)(2,1)S(1)}, bf16[832,128]{1,0:T(8,128)(2,1)S(1)}, u32[]{:S(2)}, u32[]{:S(2)}) collective-permute-start(bf16[832,128]{1,0:T(8,128)(2,1)S(1)} %collective-permute-done.39.refs_2_), channel_id=1, source_target_pairs={{0,8},{8,24},{24,16},{16,0},{1,9},{9,25},{25,17},{17,1},{2,10},{10... | collective-permute-start | bytes 638984 | tf_op jit(solution)/shard_map/ppermute | solution.py:324
  126.7 18.3 %collective-permute-start.42 = (bf16[832,128]{1,0:T(8,128)(2,1)S(1)}, bf16[832,128]{1,0:T(8,128)(2,1)S(1)}, u32[]{:S(2)}, u32[]{:S(2)}) collective-permute-start(bf16[832,128]{1,0:T(8,128)(2,1)S(1)} %collective-permute-done.40.refs_3_), channel_id=1, source_target_pairs={{0,8},{8,24},{24,16},{16,0},{1,9},{9,25},{25,17},{17,1},{2,10},{10... | collective-permute-start | bytes 638984 | tf_op jit(solution)/shard_map/ppermute | solution.py:324
  131.2 18.3 %collective-permute-start.17 = (bf16[832,128]{1,0:T(8,128)(2,1)S(1)}, bf16[832,128]{1,0:T(8,128)(2,1)S(1)}, u32[]{:S(2)}, u32[]{:S(2)}) collective-permute-start(bf16[832,128]{1,0:T(8,128)(2,1)S(1)} %collective-permute-done.15.refs_4_), channel_id=1, source_target_pairs={{0,8},{8,24},{24,16},{16,0},{1,9},{9,25},{25,17},{17,1},{2,10},{10... | collective-permute-start | bytes 638984 | tf_op jit(solution)/shard_map/ppermute | solution.py:324
  135.8 18.3 %collective-permute-start.18 = (bf16[832,128]{1,0:T(8,128)(2,1)S(1)}, bf16[832,128]{1,0:T(8,128)(2,1)S(1)}, u32[]{:S(2)}, u32[]{:S(2)}) collective-permute-start(bf16[832,128]{1,0:T(8,128)(2,1)S(1)} %collective-permute-done.16.refs_5_), channel_id=1, source_target_pairs={{0,8},{8,24},{24,16},{16,0},{1,9},{9,25},{25,17},{17,1},{2,10},{10... | collective-permute-start | bytes 638984 | tf_op jit(solution)/shard_map/ppermute | solution.py:324
  140.4 20.3 %collective-permute-start.43 = (bf16[832,128]{1,0:T(8,128)(2,1)S(1)}, bf16[832,128]{1,0:T(8,128)(2,1)S(1)}, u32[]{:S(2)}, u32[]{:S(2)}) collective-permute-start(bf16[832,128]{1,0:T(8,128)(2,1)S(1)} %collective-permute-done.41.refs_4_), channel_id=1, source_target_pairs={{0,8},{8,24},{24,16},{16,0},{1,9},{9,25},{25,17},{17,1},{2,10},{10... | collective-permute-start | bytes 638984 | tf_op jit(solution)/shard_map/ppermute | solution.py:324
  144.9 17.3 %collective-permute-start.44 = (bf16[832,128]{1,0:T(8,128)(2,1)S(1)}, bf16[832,128]{1,0:T(8,128)(2,1)S(1)}, u32[]{:S(2)}, u32[]{:S(2)}) collective-permute-start(bf16[832,128]{1,0:T(8,128)(2,1)S(1)} %collective-permute-done.42.refs_5_), channel_id=1, source_target_pairs={{0,8},{8,24},{24,16},{16,0},{1,9},{9,25},{25,17},{17,1},{2,10},{10... | collective-permute-start | bytes 638984 | tf_op jit(solution)/shard_map/ppermute | solution.py:324
  156.2 15.3 %collective-permute-start.19 = (bf16[1664,128]{1,0:T(8,128)(2,1)S(1)}, bf16[1664,128]{1,0:T(8,128)(2,1)S(1)}, u32[]{:S(2)}, u32[]{:S(2)}) collective-permute-start(bf16[1664,128]{1,0:T(8,128)(2,1)S(1)} %get-tuple-element.56), channel_id=1, source_target_pairs={{0,1},{1,0},{2,3},{3,2},{4,5},{5,4},{6,7},{7,6},{8,9},{9,8},{10,11... | collective-permute-start | bytes 1277960 | tf_op jit(solution)/shard_map/ppermute | solution.py:336
  160.0 12.0 %collective-permute-start.21 = (bf16[1664,128]{1,0:T(8,128)(2,1)S(1)}, bf16[1664,128]{1,0:T(8,128)(2,1)S(1)}, u32[]{:S(2)}, u32[]{:S(2)}) collective-permute-start(bf16[1664,128]{1,0:T(8,128)(2,1)S(1)} %get-tuple-element.58), channel_id=1, source_target_pairs={{0,1},{1,0},{2,3},{3,2},{4,5},{5,4},{6,7},{7,6},{8,9},{9,8},{10,11... | collective-permute-start | bytes 1277960 | tf_op jit(solution)/shard_map/ppermute | solution.py:336
  160.6 11.7 %collective-permute-start.23 = (bf16[1664,128]{1,0:T(8,128)(2,1)S(1)}, bf16[1664,128]{1,0:T(8,128)(2,1)S(1)}, u32[]{:S(2)}, u32[]{:S(2)}) collective-permute-start(bf16[1664,128]{1,0:T(8,128)(2,1)S(1)} %get-tuple-element.60), channel_id=1, source_target_pairs={{0,1},{1,0},{2,3},{3,2},{4,5},{5,4},{6,7},{7,6},{8,9},{9,8},{10,11... | collective-permute-start | bytes 1277960 | tf_op jit(solution)/shard_map/ppermute | solution.py:336
  172.3 13.6 %collective-permute-start.20 = (bf16[1664,128]{1,0:T(8,128)(2,1)S(1)}, bf16[1664,128]{1,0:T(8,128)(2,1)S(1)}, u32[]{:S(2)}, u32[]{:S(2)}) collective-permute-start(bf16[1664,128]{1,0:T(8,128)(2,1)S(1)} %added.15), channel_id=1, source_target_pairs={{0,6},{1,7},{2,4},{3,5},{4,2},{5,3},{6,0},{7,1},{8,14},{9,15},{10,... | collective-permute-start | bytes 1277960 | tf_op jit(solution)/shard_map/ppermute | solution.py:339
  174.2 21.0 %collective-permute-start.22 = (bf16[1664,128]{1,0:T(8,128)(2,1)S(1)}, bf16[1664,128]{1,0:T(8,128)(2,1)S(1)}, u32[]{:S(2)}, u32[]{:S(2)}) collective-permute-start(bf16[1664,128]{1,0:T(8,128)(2,1)S(1)} %added.16), channel_id=1, source_target_pairs={{0,4},{1,5},{2,6},{3,7},{4,0},{5,1},{6,2},{7,3},{8,12},{9,13},{10,... | collective-permute-start | bytes 1277960 | tf_op jit(solution)/shard_map/ppermute | solution.py:339
  178.7 20.7 %collective-permute-start.24 = (bf16[1664,128]{1,0:T(8,128)(2,1)S(1)}, bf16[1664,128]{1,0:T(8,128)(2,1)}, u32[]{:S(2)}, u32[]{:S(2)}) collective-permute-start(bf16[1664,128]{1,0:T(8,128)(2,1)S(1)} %added.17), channel_id=1, source_target_pairs={{0,2},{1,3},{2,0},{3,1},{4,6},{5,7},{6,4},{7,5},{8,10},{9,11},{10,... | collective-permute-start | bytes 1277960 | tf_op jit(solution)/shard_map/ppermute | solution.py:339
  179.2 26.0 %collective-permute-start.51 = (bf16[1664,128]{1,0:T(8,128)(2,1)}, bf16[1664,128]{1,0:T(8,128)(2,1)}, u32[]{:S(2)}, u32[]{:S(2)}) collective-permute-start(bf16[1664,128]{1,0:T(8,128)(2,1)} %get-tuple-element.81), channel_id=1, source_target_pairs={{0,1},{1,0},{2,3},{3,2},{4,5},{5,4},{6,7},{7,6},{8,9},{9,8},{10,11... | collective-permute-start | bytes 1277960 | tf_op jit(solution)/shard_map/ppermute | solution.py:336
  180.2 25.1 %collective-permute-start.46 = (bf16[1664,128]{1,0:T(8,128)(2,1)S(1)}, bf16[1664,128]{1,0:T(8,128)(2,1)}, u32[]{:S(2)}, u32[]{:S(2)}) collective-permute-start(bf16[1664,128]{1,0:T(8,128)(2,1)S(1)} %added.21), channel_id=1, source_target_pairs={{0,6},{1,7},{2,4},{3,5},{4,2},{5,3},{6,0},{7,1},{8,14},{9,15},{10,... | collective-permute-start | bytes 1277960 | tf_op jit(solution)/shard_map/ppermute | solution.py:339
  186.8 26.1 %collective-permute-start.48 = (bf16[1664,128]{1,0:T(8,128)(2,1)S(1)}, bf16[1664,128]{1,0:T(8,128)(2,1)}, u32[]{:S(2)}, u32[]{:S(2)}) collective-permute-start(bf16[1664,128]{1,0:T(8,128)(2,1)S(1)} %added.22), channel_id=1, source_target_pairs={{0,4},{1,5},{2,6},{3,7},{4,0},{5,1},{6,2},{7,3},{8,12},{9,13},{10,... | collective-permute-start | bytes 1277960 | tf_op jit(solution)/shard_map/ppermute | solution.py:339
  195.9 16.9 %collective-permute-start.50 = (bf16[1664,128]{1,0:T(8,128)(2,1)S(1)}, bf16[1664,128]{1,0:T(8,128)(2,1)}, u32[]{:S(2)}, u32[]{:S(2)}) collective-permute-start(bf16[1664,128]{1,0:T(8,128)(2,1)S(1)} %added.23), channel_id=1, source_target_pairs={{0,2},{1,3},{2,0},{3,1},{4,6},{5,7},{6,4},{7,5},{8,10},{9,11},{10,... | collective-permute-start | bytes 1277960 | tf_op jit(solution)/shard_map/ppermute | solution.py:339
  205.1 10.9 %collective-permute-start.52 = (bf16[768,128]{1,0:T(8,128)(2,1)S(1)}, bf16[768,128]{1,0:T(8,128)(2,1)S(1)}, u32[]{:S(2)}, u32[]{:S(2)}) collective-permute-start(bf16[768,128]{1,0:T(8,128)(2,1)S(1)} %get-tuple-element.83), channel_id=1, source_target_pairs={{0,1},{1,0},{2,3},{3,2},{4,5},{5,4},{6,7},{7,6},{8,9},{9,8},{10,11... | collective-permute-start | bytes 589832 | tf_op jit(solution)/shard_map/ppermute | solution.py:380
  (37 other events, 271.1 us)

commit v3 on v2

v3 whole, which is shorter than its diff:
```python
import functools
import math

import jax
import jax.numpy as jnp
from jax import lax
from jax.experimental import pallas as pl
from jax.experimental.pallas import tpu as pltpu
from jax.sharding import PartitionSpec as P

UNROLL = 32
EDGES = 5
MIB = 1 << 20
VMEM = pl.BlockSpec(memory_space=pltpu.VMEM)
SMEM = pl.BlockSpec(memory_space=pltpu.SMEM)
ANY = pl.BlockSpec(memory_space=pl.ANY)
HBM = pl.BlockSpec(memory_space=pltpu.HBM)


def bytes_of(*shapes):
    return sum(math.prod(s.shape) * jnp.dtype(s.dtype).itemsize for s in shapes)


def params(need):
    return pltpu.CompilerParams(vmem_limit_bytes=need + 3 * MIB)


def resident(values, after):
    def kernel(values_ref, *refs):
        held_ref, sem = refs[-2:]
        copy = pltpu.make_async_copy(values_ref, held_ref, sem)
        copy.start()
        copy.wait()

    return pl.pallas_call(
        kernel,
        out_shape=pltpu.VMEM(values.shape, values.dtype),
        in_specs=[HBM] + [ANY] * len(after),
        out_specs=VMEM,
        scratch_shapes=[pltpu.SemaphoreType.DMA],
        compiler_params=pltpu.CompilerParams(vmem_limit_bytes=MIB),
        cost_estimate=pl.CostEstimate(
            flops=0, bytes_accessed=bytes_of(values), transcendentals=0
        ),
        name="resident",
    )(values, *after)


def columns_of(vectors, row, rows, low, width, after):
    def kernel(vectors_ref, *refs):
        out_ref, sem = refs[-2:]
        copy = pltpu.make_async_copy(
            vectors_ref.at[pl.ds(row, rows), pl.ds(low, width)], out_ref, sem
        )
        copy.start()
        copy.wait()

    out = jax.ShapeDtypeStruct((rows, width), vectors.dtype)
    return pl.pallas_call(
        kernel,
        out_shape=out,
        in_specs=[HBM] + [ANY] * len(after),
        out_specs=VMEM,
        scratch_shapes=[pltpu.SemaphoreType.DMA],
        compiler_params=params(bytes_of(out)),
        cost_estimate=pl.CostEstimate(
            flops=0, bytes_accessed=2 * bytes_of(out), transcendentals=0
        ),
        name="columns_of",
    )(vectors, *after)


def add_images(bounds, order, rows, cols, values, panel, total, phase, low_col):
    orbitals = values.shape[-1]
    trash = total.shape[0] // orbitals - 1
    start = bounds[EDGES + phase]
    end = bounds[EDGES + phase + 1]

    def step(turn, carry):
        images = []
        for lane in range(UNROLL):
            entry = start + turn * UNROLL + lane
            col = jnp.where(entry < end, cols[entry] - low_col, 0)
            picked = panel[pl.ds(pl.multiple_of(col * orbitals, orbitals), orbitals), :]
            images.append(
                jnp.dot(values[order[entry]], picked, preferred_element_type=jnp.float32)
            )
        for lane in range(UNROLL):
            entry = start + turn * UNROLL + lane
            row = jnp.where(entry < end, rows[entry], trash)
            place = pl.ds(pl.multiple_of(row * orbitals, orbitals), orbitals)
            total[place, :] += images[lane]
        return carry

    lax.fori_loop(0, (end - start + UNROLL - 1) // UNROLL, step, 0)


def fill(panel, parts):
    low = 0
    for part in parts:
        panel[low : low + part.shape[0], :] = part[...]
        low += part.shape[0]


def early_images(out_blocks, tables, values, parts):
    orbitals = values.shape[-1]
    width = parts[0].shape[1]
    panel_rows = sum(part.shape[0] for part in parts)
    total = ((out_blocks + 1) * orbitals, width)

    def kernel(bounds, order, rows, cols, values, *refs):
        total_ref, panel = refs[-2:]
        fill(panel, refs[:-2])
        total_ref[...] = jnp.zeros_like(total_ref)
        add_images(bounds, order, rows, cols, values, panel, total_ref, 0, 0)

    return pl.pallas_call(
        kernel,
        out_shape=pltpu.VMEM(total, jnp.float32),
        in_specs=[SMEM] * 4 + [VMEM] * (1 + len(parts)),
        out_specs=VMEM,
        scratch_shapes=[pltpu.VMEM((panel_rows, width), jnp.bfloat16)],
        compiler_params=params(bytes_of(*parts, *parts)),
        name="early_images",
    )(*tables, values, *parts)


def last_images(counts, low_col, tables, values, early, parts):
    orbitals = values.shape[-1]
    width = parts[0].shape[1]
    panel_rows = sum(part.shape[0] for part in parts)
    height = (early.shape[0] - orbitals) // (2 * sum(counts))
    outs = [
        jax.ShapeDtypeStruct((count * height, width), jnp.bfloat16)
        for count in counts
        for _ in range(2)
    ]

    def kernel(bounds, order, rows, cols, values, early, *refs):
        part_refs, out_refs = refs[: len(parts)], refs[len(parts) + 1 : -1]
        total, panel = refs[len(parts)], refs[-1]
        fill(panel, part_refs)
        add_images(bounds, order, rows, cols, values, panel, total, 1, low_col)
        low = 0
        for count, *pair in zip(counts, out_refs[::2], out_refs[1::2]):
            for piece in range(count):
                for out in pair:
                    out[piece * height : (piece + 1) * height, :] = total[
                        low : low + height, :
                    ].astype(out.dtype)
                    low += height

    return pl.pallas_call(
        kernel,
        out_shape=[pltpu.VMEM(early.shape, jnp.float32), *outs],
        in_specs=[SMEM] * 4 + [VMEM] * (2 + len(parts)),
        out_specs=[VMEM] * (1 + len(outs)),
        scratch_shapes=[pltpu.VMEM((panel_rows, width), jnp.bfloat16)],
        input_output_aliases={5: 0},
        compiler_params=params(bytes_of(*parts, *parts, *outs)),
        name="last_images",
    )(*tables, values, early, *parts)[1:]


def summed(specs):
    flat = [array for segments in specs for _, pairs in segments for array, _ in pairs]

    def kernel(*refs):
        out_refs = refs[len(flat) :]
        at = 0
        for segments, out_ref in zip(specs, out_refs):
            row = 0
            for size, pairs in segments:
                total = image_rows(refs[at : at + len(pairs)], pairs, size)
                at += len(pairs)
                out_ref[row : row + size, :] = total.astype(out_ref.dtype)
                row += size

    width = flat[0].shape[1]
    outs = [
        jax.ShapeDtypeStruct((sum(size for size, _ in segments), width), flat[0].dtype)
        for segments in specs
    ]
    need = bytes_of(*flat, *outs)
    return pl.pallas_call(
        kernel,
        out_shape=outs,
        in_specs=[VMEM] * len(flat),
        out_specs=[VMEM] * len(outs),
        compiler_params=params(need),
        cost_estimate=pl.CostEstimate(flops=0, bytes_accessed=need, transcendentals=0),
        name="summed",
    )(*flat)


def image_rows(refs, pairs, size):
    image = None
    for ref, (_, low) in zip(refs, pairs):
        term = ref[low : low + size, :].astype(jnp.float32)
        image = term if image is None else image + term
    return image


def first_update(terms, vectors, low, center, half_width):
    flat = [array for _, pairs in terms for array, _ in pairs]
    width = flat[0].shape[1]

    def kernel(center_ref, width_ref, vectors_ref, *refs):
        out_refs = refs[len(flat) :]
        row, at = 0, 0
        for (size, pairs), out_ref in zip(terms, out_refs):
            image = image_rows(refs[at : at + len(pairs)], pairs, size)
            at += len(pairs)
            source = vectors_ref[row : row + size, low : low + width].astype(jnp.float32)
            out_ref[...] = ((image - center_ref[0] * source) / width_ref[0]).astype(out_ref.dtype)
            row += size

    need = bytes_of(*flat, vectors)
    return pl.pallas_call(
        kernel,
        out_shape=[jax.ShapeDtypeStruct((size, width), jnp.bfloat16) for size, _ in terms],
        in_specs=[SMEM] * 2 + [VMEM] * (1 + len(flat)),
        out_specs=[VMEM] * len(terms),
        compiler_params=params(need),
        cost_estimate=pl.CostEstimate(flops=0, bytes_accessed=need, transcendentals=0),
        name="first_update",
    )(center, half_width, vectors, *flat)


def second_update(terms, firsts, vectors, low, center, half_width, tables, edge_size):
    flat = [array for _, pairs in terms for array, _ in pairs]
    rows = sum(size for size, _ in terms)
    width = flat[0].shape[1]

    def kernel(edges_ref, center_ref, width_ref, vectors_ref, *refs):
        first_refs = refs[len(flat) : len(flat) + len(firsts)]
        out_ref, edge_ref = refs[-2:]
        row, at = 0, 0
        for (size, pairs), first_ref in zip(terms, first_refs):
            image = image_rows(refs[at : at + len(pairs)], pairs, size)
            at += len(pairs)
            source = vectors_ref[row : row + size, low : low + width].astype(jnp.float32)
            first = first_ref[...].astype(jnp.float32)
            out_ref[row : row + size, :] = (
                2.0 * (image - center_ref[0] * first) / width_ref[0] - source
            ).astype(out_ref.dtype)
            row += size
        edge_ref[...] = out_ref[pl.ds(pl.multiple_of(edges_ref[0], 16), edge_size), :]

    need = bytes_of(*flat, *firsts, vectors) + 4 * rows * width
    return pl.pallas_call(
        kernel,
        out_shape=[
            jax.ShapeDtypeStruct((rows, width), jnp.bfloat16),
            jax.ShapeDtypeStruct((edge_size, width), jnp.bfloat16),
        ],
        in_specs=[SMEM] * 3 + [VMEM] * (1 + len(flat) + len(firsts)),
        out_specs=[VMEM] * 2,
        compiler_params=params(need),
        cost_estimate=pl.CostEstimate(flops=0, bytes_accessed=need, transcendentals=0),
        name="second_update",
    )(tables[0], center, half_width, vectors, *flat, *firsts)


def relaid_half(relaid, second, partner, edges, low, shape, own, orbitals):
    width = second.shape[1]
    edge_size = partner.shape[0]
    capacity = shape[0] // orbitals
    given = [] if relaid is None else [relaid]

    def kernel(edges_ref, second_ref, partner_ref, *refs):
        out_ref, window, block_rows, sem = refs[-4:]
        window[pl.ds(pl.multiple_of(edges_ref[1], 16), own * orbitals), :] = second_ref[...]
        window[pl.ds(pl.multiple_of(edges_ref[2], 16), edge_size), :] = partner_ref[...]
        for block in range(capacity):
            span = slice(block * orbitals, (block + 1) * orbitals)

            @pl.when(block < edges_ref[4])
            def _():
                row = pl.multiple_of(edges_ref[3] + block * orbitals, 16)
                block_rows[span, :] = window[pl.ds(row, orbitals), :]

            @pl.when(block >= edges_ref[4])
            def _():
                block_rows[span, :] = jnp.zeros((orbitals, width), block_rows.dtype)

        copy = pltpu.make_async_copy(block_rows, out_ref.at[:, pl.ds(low, width)], sem)
        copy.start()
        copy.wait()

    out = jax.ShapeDtypeStruct(shape, jnp.bfloat16)
    return pl.pallas_call(
        kernel,
        out_shape=out,
        in_specs=[SMEM] + [VMEM] * 2 + [HBM] * len(given),
        out_specs=HBM,
        scratch_shapes=[
            pltpu.VMEM((own * orbitals + edge_size, width), jnp.bfloat16),
            pltpu.VMEM((shape[0], width), jnp.bfloat16),
            pltpu.SemaphoreType.DMA,
        ],
        input_output_aliases={3: 0} if given else {},
        compiler_params=params(bytes_of(out) + 2 * bytes_of(second)),
        name="relaid_half",
    )(edges, second, partner, *given)


def ring_order(count):
    return [i for i in range(count) if i == 0 or i % 2] + [
        i for i in range(count - 1, 0, -1) if i and i % 2 == 0
    ]


def on_device(block_values, block_rows, block_cols, start_vectors, center, half_width, row_counts):
    orbitals = block_values.shape[-1]
    values = block_values.reshape(-1, orbitals, orbitals)
    row_ids = block_rows.reshape(-1)
    col_ids = block_cols.reshape(-1)
    entry_count = values.shape[0]
    own_rows, vec_count = start_vectors.shape
    own = own_rows // orbitals
    row_count = lax.axis_size("row")
    col_count = lax.axis_size("col")
    my_row = lax.axis_index("row")
    my_col = lax.axis_index("col")
    chip_count = col_count // 2

    order = ring_order(row_count)
    route = [(order[i], order[(i + 1) % row_count]) for i in range(row_count)]
    place_of = [order.index(i) for i in range(row_count)]

    def looked_up(table, index):
        result = jnp.zeros_like(index)
        for at, value in enumerate(table):
            result = jnp.where(index == at, value, result)
        return result

    half_blocks = own // 2
    capacity = own + half_blocks
    edge_size = half_blocks * orbitals
    parity = my_col % 2
    device = my_row * col_count + my_col
    even_count = row_counts[device - parity]
    edges = [
        (1 - parity) * (own_rows - edge_size),
        parity * edge_size,
        (1 - parity) * own_rows,
        parity * (even_count - (own - half_blocks)) * orbitals,
        row_counts[device],
    ]

    with jax.named_scope("entry_order"):
        arrival = lax.rem(
            looked_up(place_of, my_row) - looked_up(place_of, col_ids // own) + row_count, row_count
        )
        panel_cols = arrival * own + col_ids % own
        relative = (row_ids // own) ^ my_col
        piece = chip_count - 1 - relative // 2
        out_rows = (piece * 2 + 1 - relative % 2) * own + row_ids % own
        number = jnp.arange(entry_count, dtype=jnp.int32)
        is_last = (arrival == row_count - 1).astype(jnp.int32)
        key = is_last * (2 * chip_count * own) + out_rows
        before = (key[None, :] < key[:, None]) | (
            (key[None, :] == key[:, None]) & (number[None, :] < number[:, None])
        )
        rank = jnp.sum(before.astype(jnp.int32), 1)
        at_rank = rank[None, :] == number[:, None]

        def ordered(items):
            return jnp.sum(jnp.where(at_rank, items[None, :], 0), 1).astype(jnp.int32)

        room = (0, UNROLL)
        entry_order = jnp.pad(ordered(number), room)
        rows = jnp.pad(ordered(out_rows), room)
        cols = jnp.pad(ordered(panel_cols), room)
        bounds = jnp.stack([0, entry_count - jnp.sum(is_last), entry_count])
        bounds = jnp.concatenate([jnp.stack(edges), bounds]).astype(jnp.int32)
        tables = (bounds, entry_order, rows, cols)
    values = resident(values, tables)

    other_core = [(i, i ^ 1) for i in range(col_count)]
    lanes = 128 if vec_count % 128 == 0 else vec_count
    lows = list(range(0, vec_count, lanes))
    cut = own_rows // 2 if own_rows % 32 == 0 else own_rows
    sizes = [cut, own_rows - cut] if cut < own_rows else [own_rows]
    crossed = chip_count == 4 and len(sizes) == 2

    def along_row(array):
        return lax.ppermute(array, "row", route)

    def to_core(array):
        return lax.ppermute(array, "col", other_core)

    def to_chip(array, chip):
        return lax.ppermute(array, "col", [(i, i ^ 2 * chip) for i in range(col_count)])

    class Gather:
        def __init__(self, parts):
            self.arrived = [list(parts)]

        def step(self, ties):
            held = self.arrived[-1]
            if len(self.arrived) < row_count:
                self.arrived.append(
                    [along_row(tied(part, tie)) for part, tie in zip(held, ties)]
                )

    def tied(array, tokens):
        tokens = list(tokens)
        return lax.optimization_barrier((array, *tokens))[0] if tokens else array

    def terms_of(gather, following, tokens):
        none = [[] for _ in sizes]
        counts = (1, 3) if crossed else (1,) * chip_count
        parts = [part for step in gather.arrived[:-1] for part in step]
        parts[0] = tied(parts[0], tokens)
        early = early_images(2 * chip_count * own, tables, values, parts)
        last = gather.arrived[-1]
        outs = last_images(counts, (row_count - 1) * own, tables, values, early, last)

        def go_on(*ties):
            if following is not None:
                following.step(ties)

        if not crossed:
            kept = partner = None
            arrived = []
            for piece in range(chip_count):
                chip = chip_count - 1 - piece
                sent, kept = outs[2 * piece], outs[2 * piece + 1]
                partner = to_core(sent)
                if chip:
                    (both,) = summed([[(own_rows, [(kept, 0), (partner, 0)])]])
                    arrived.append(to_chip(both, chip))
            for _ in range(row_count):
                go_on(*none)
            low, terms = 0, []
            for size in sizes:
                pairs = [(array, low) for array in [kept, partner, *arrived]]
                terms.append((size, pairs))
                low += size
            return terms

        top, rest = sizes
        sent, kept, sent_others, others = outs
        if following is not None:
            sent = tied(sent, following.arrived[-1][:1])
        partner = to_core(sent)
        partners = to_core(tied(sent_others, [partner]))
        corner = summed(
            [[(top, [(kept, 0), (partner, 0)])], [(rest, [(kept, top), (partner, top)])]]
        )
        by_x, by_y = to_chip(corner[0], 1), to_chip(corner[1], 2)
        go_on([sent], corner)

        def both(low, *more):
            return [(others, low), (partners, low), *more]

        y, x, mine = 0, own_rows, 2 * own_rows
        sides = summed(
            [
                [(top, both(x)), (rest, both(x + top, (by_y, 0)))],
                [(top, both(y, (by_x, 0))), (rest, both(y + top))],
            ]
        )
        from_x, from_y = to_chip(sides[0], 1), to_chip(sides[1], 2)
        go_on(corner, sides)
        for _ in range(row_count):
            go_on(*none)
        return [
            (top, both(mine, (from_x, 0), (from_y, 0))),
            (rest, both(mine + top, (from_x, top), (from_y, top))),
        ]

    none = [[] for _ in sizes]
    gathers = []
    for low in lows:
        after = [[] for _ in sizes]
        if gathers:
            before = gathers[-1].arrived
            after = [[before[-2 if row_count > 1 else -1][i]] for i in range(len(sizes))]
        gather = Gather(
            columns_of(start_vectors, i * cut, size, low, lanes, after[i])
            for i, size in enumerate(sizes)
        )
        if not gathers:
            gather.step(none)
            gather.step([tables, *none[1:]])
            gather.step([*none[1:], [values]])
            for _ in range(row_count):
                gather.step(none)
        else:
            gather.step(none)
        gathers.append(gather)
    firsts = []
    count = len(lows)
    for turn in range(count):
        if turn:
            following = Gather(firsts[-1])
            following.step(none)
            gathers.append(following)
        following = gathers[turn + 1] if turn + 1 < len(gathers) else None
        terms = terms_of(gathers[turn], following, firsts[-1] if turn else [])
        firsts.append(first_update(terms, start_vectors, lows[turn], center, half_width))
    if count == 1:
        gathers.append(Gather(firsts[0]))
        for _ in range(row_count):
            gathers[-1].step(none)
    seconds = []
    relaid = None
    for turn in range(count):
        following = None
        if turn + 1 < count:
            if count + turn + 1 == len(gathers):
                gathers.append(Gather(firsts[turn + 1]))
                gathers[-1].step(none)
            following = gathers[count + turn + 1]
        tokens = seconds[-1:] if turn else firsts[-1]
        terms = terms_of(gathers[count + turn], following, tokens)
        if relaid is not None:
            size, ((array, row), *more) = terms[0]
            terms = [(size, [(tied(array, [relaid]), row), *more]), *terms[1:]]
        second, edge = second_update(
            terms, firsts[turn], start_vectors, lows[turn], center, half_width, tables, edge_size
        )
        seconds.append(second)
        shape = (capacity * orbitals, vec_count)
        relaid = relaid_half(
            relaid, second, to_core(edge), tables[0], lows[turn], shape, own, orbitals
        )
    return relaid


def solution(mesh):
    placed = (
        P("row", "col", None, None, None),
        P("row", "col", None),
        P("row", "col", None),
        P(("row", "col"), None),
        P(),
        P(),
        P(),
    )
    return jax.shard_map(
        on_device, mesh=mesh, in_specs=placed, out_specs=P(("row", "col"), None), check_vma=False
    )
```

time: 221 us -> 176 us (0.80)
  waiting for transfers between devices: 98.7 us -> 71.9 us
  local copies, waits for them, and re-layouts: 15.2 us -> 5.79 us
  Pallas kernels: 42.7 us -> 34.4 us
  starting transfers between devices: 57.5 us -> 59.9 us
  other arithmetic: 3.41 us -> 1.19 us
    ppermute x54 -> x50, waiting for transfers between devices: 98.7 us -> 71.9 us  [the longest x24 36.8 us: along_row(): return lax.ppermute(array, 'row', route)]
    unnamed x30 -> x12, local copies, waits for them, and re-layouts: 13.8 us -> 4.55 us
    pallas_call x29 -> x22, Pallas kernels: 37.5 us -> 30.8 us  [the longest x4 16 us: early_images(): pl.pallas_call(kernel, out_shape=pltpu.VMEM(total, jnp.float32), in_specs...]
    ppermute x54 -> x50, starting transfers between devices: 57.5 us -> 59.9 us  [the longest x24 41.5 us: along_row(): return lax.ppermute(array, 'row', route)]
  transfers between devices with their start and end apart: 54 -> 50, of which waited for: 26 -> 31; matrix products, arithmetic and copies ran while one was open for 2% -> 1% of each run, Pallas kernels for 18% -> 16%
where the time goes in v3:
time: 176 us
  waiting for transfers between devices  71.9 us (41%)
  starting transfers between devices  59.9 us (34%)
  Pallas kernels  34.4 us (20%)
  local copies, waits for them, and re-layouts  5.79 us (3%)
  between operations  3.17 us (2%)
    ppermute x24, starting transfers between devices, along_row(): return lax.ppermute(array, 'row', route)  41.5 us
    ppermute x24, waiting for transfers between devices, along_row(): return lax.ppermute(array, 'row', route)  36.8 us
    ppermute x16, waiting for transfers between devices, to_chip(): lax.ppermute(array, 'col', [(i, i ^ 2 * chip) for i in range(col_count)])  25.2 us
    ppermute x16, starting transfers between devices, to_chip(): lax.ppermute(array, 'col', [(i, i ^ 2 * chip) for i in range(col_count)])  17.5 us
    pallas_call x4, Pallas kernels, early_images(): pl.pallas_call(kernel, out_shape=pltpu.VMEM(total, jnp.float32), in_specs...  16 us
    ppermute x10, waiting for transfers between devices, to_core(): return lax.ppermute(array, 'col', other_core)  9.91 us
    pallas_call x4, Pallas kernels, last_images(): pl.pallas_call(kernel, out_shape=[pltpu.VMEM(early.shape, jnp.float32), *...  9.62 us
    unnamed x12, local copies, waits for them, and re-layouts  4.55 us
  transfers between devices with their start and end apart: 50, of which 31 were waited for; matrix products, arithmetic and copies ran while one was open for 1% of the time, Pallas kernels for 16%

profile of v3, /device:TPU:0, one launch (start us, length us, event | category | flops | bytes accessed | tf_op | source)
XLA Modules:
  0.0 176.3 jit_solution(2607702752751288323)
XLA Ops:
  1.2 3.1 %collective-permute-start = (bf16[832,128]{1,0:T(8,128)(2,1)S(1)}, bf16[832,128]{1,0:T(8,128)(2,1)S(1)}, u32[]{:S(2)}, u32[]{:S(2)}) collective-permute-start(bf16[832,128]{1,0:T(8,128)(2,1)S(1)} %columns_of.4.refs_0_), channel_id=1, source_target_pairs={{0,8},{8,24},{24,16},{16,0},{1,9},{9,25},{25,17},{17,1},{2,10},{10... | collective-permute-start | bytes 638984 | tf_op jit(solution)/shard_map/ppermute | solution.py:389
  4.4 2.6 %collective-permute-start.2 = (bf16[832,128]{1,0:T(8,128)(2,1)S(1)}, bf16[832,128]{1,0:T(8,128)(2,1)S(1)}, u32[]{:S(2)}, u32[]{:S(2)}) collective-permute-start(bf16[832,128]{1,0:T(8,128)(2,1)S(1)} %columns_of.6.refs_1_), channel_id=1, source_target_pairs={{0,8},{8,24},{24,16},{16,0},{1,9},{9,25},{25,17},{17,1},{2,10},{10... | collective-permute-start | bytes 638984 | tf_op jit(solution)/shard_map/ppermute | solution.py:389
  10.9 4.3 %collective-permute-done.2.refs_3_ = bf16[832,128]{1,0:T(8,128)(2,1)S(1)} collective-permute-done((bf16[832,128]{1,0:T(8,128)(2,1)S(1)}, bf16[832,128]{1,0:T(8,128)(2,1)S(1)}, u32[]{:S(2)}, u32[]{:S(2)}) %collective-permute-start.2) | collective-permute-done | bytes 213024 | tf_op jit(solution)/shard_map/ppermute | solution.py:389
  16.0 3.4 %collective-permute-start.1 = (bf16[832,128]{1,0:T(8,128)(2,1)S(1)}, bf16[832,128]{1,0:T(8,128)(2,1)S(1)}, u32[]{:S(2)}, u32[]{:S(2)}) collective-permute-start(bf16[832,128]{1,0:T(8,128)(2,1)S(1)} %collective-permute-done.refs_2_), channel_id=1, source_target_pairs={{0,8},{8,24},{24,16},{16,0},{1,9},{9,25},{25,17},{17,1},{2,10},{10... | collective-permute-start | bytes 638984 | tf_op jit(solution)/shard_map/ppermute | solution.py:389
  19.3 3.4 %copy-done.2 = bf16[1,1,256,128,128]{4,3,2,1,0:T(8,128)(2,1)S(1)} copy-done((bf16[1,1,256,128,128]{4,3,2,1,0:T(8,128)(2,1)S(1)}, bf16[1,1,256,128,128]{4,3,2,1,0:T(8,128)(2,1)}, u32[]{:S(2)}) %copy-start.2) | copy-done | bytes 8388632
  25.0 3.7 %collective-permute-done.1.refs_0_.refs_4_ = bf16[832,128]{1,0:T(8,128)(2,1)S(1)} collective-permute-done((bf16[832,128]{1,0:T(8,128)(2,1)S(1)}, bf16[832,128]{1,0:T(8,128)(2,1)S(1)}, u32[]{:S(2)}, u32[]{:S(2)}) %collective-permute-start.1) | collective-permute-done | bytes 213024 | tf_op jit(solution)/shard_map/ppermute | solution.py:389
  29.7 3.4 %collective-permute-start.6 = (bf16[832,128]{1,0:T(8,128)(2,1)S(1)}, bf16[832,128]{1,0:T(8,128)(2,1)S(1)}, u32[]{:S(2)}, u32[]{:S(2)}) collective-permute-start(bf16[832,128]{1,0:T(8,128)(2,1)S(1)} %columns_of.5.refs_0_), channel_id=1, source_target_pairs={{0,8},{8,24},{24,16},{16,0},{1,9},{9,25},{25,17},{17,1},{2,10},{10... | collective-permute-start | bytes 638984 | tf_op jit(solution)/shard_map/ppermute | solution.py:389
  33.1 4.0 %early_images.4.early = f32[13440,128]{1,0:T(8,128)S(1)} custom-call(s32[8]{0:T(128)S(1)} %concatenate.3.refs_0_.bounds.edges_ref, s32[288]{0:T(512)S(1)} %pad.10.refs_1_.order, s32[288]{0:T(512)S(1)} %pad.11.refs_2_.rows, s32[288]{0:T(512)S(1)} %pad.12.refs_3_.cols, bf16[256,128,128]{2,1,0:T(8,128)(2,1)S(1)} %resident.1.values, ...), custom_call_target="tpu_custom_call" | custom-call | tf_op jit(solution)/shard_map/early_images/pallas_call | solution.py:117
  37.9 2.4 %last_images.4 = (f32[13440,128]{1,0:T(8,128)S(1)}, bf16[1664,128]{1,0:T(8,128)(2,1)S(1)}, bf16[1664,128]{1,0:T(8,128)(2,1)S(1)}, bf16[4992,128]{1,0:T(8,128)(2,1)S(1)}, bf16[4992,128]{1,0:T(8,128)(2,1)S(1)}) custom-call(s32[8]{0:T(128)S(1)} %concatenate.3.refs_0_.bounds.edges_ref, s32[288]{0:T(512)S(1)} %pad.10.refs_1_.order, ...), custom_call_target="tpu_custom_call", output_to_operand_aliasing={{0}: (5, {})} | custom-call | tf_op jit(solution)/shard_map/last_images/pallas_call | solution.py:153
  46.4 3.9 %collective-permute-done.10.refs_7_ = bf16[832,128]{1,0:T(8,128)(2,1)S(1)} collective-permute-done((bf16[832,128]{1,0:T(8,128)(2,1)S(1)}, bf16[832,128]{1,0:T(8,128)(2,1)S(1)}, u32[]{:S(2)}, u32[]{:S(2)}) %collective-permute-start.10) | collective-permute-done | bytes 213024 | tf_op jit(solution)/shard_map/ppermute | solution.py:395
  54.4 3.4 %collective-permute-start.15 = (bf16[832,128]{1,0:T(8,128)(2,1)S(1)}, bf16[832,128]{1,0:T(8,128)(2,1)S(1)}, u32[]{:S(2)}, u32[]{:S(2)}) collective-permute-start(bf16[832,128]{1,0:T(8,128)(2,1)S(1)} %collective-permute-done.13.refs_3_), channel_id=1, source_target_pairs={{0,8},{8,24},{24,16},{16,0},{1,9},{9,25},{25,17},{17,1},{2,10},{10... | collective-permute-start | bytes 638984 | tf_op jit(solution)/shard_map/ppermute | solution.py:389
  59.1 3.6 %collective-permute-done.14.refs_4_ = bf16[832,128]{1,0:T(8,128)(2,1)S(1)} collective-permute-done((bf16[832,128]{1,0:T(8,128)(2,1)S(1)}, bf16[832,128]{1,0:T(8,128)(2,1)S(1)}, u32[]{:S(2)}, u32[]{:S(2)}) %collective-permute-start.14) | collective-permute-done | bytes 213024 | tf_op jit(solution)/shard_map/ppermute | solution.py:389
  63.5 3.8 %collective-permute-done.15.refs_5_ = bf16[832,128]{1,0:T(8,128)(2,1)S(1)} collective-permute-done((bf16[832,128]{1,0:T(8,128)(2,1)S(1)}, bf16[832,128]{1,0:T(8,128)(2,1)S(1)}, u32[]{:S(2)}, u32[]{:S(2)}) %collective-permute-start.15) | collective-permute-done | bytes 213024 | tf_op jit(solution)/shard_map/ppermute | solution.py:389
  68.4 3.4 %collective-permute-start.18 = (bf16[832,128]{1,0:T(8,128)(2,1)S(1)}, bf16[832,128]{1,0:T(8,128)(2,1)S(1)}, u32[]{:S(2)}, u32[]{:S(2)}) collective-permute-start(bf16[832,128]{1,0:T(8,128)(2,1)S(1)} %get-tuple-element.101.refs_0_.refs_8_), channel_id=1, source_target_pairs={{0,8},{8,24},{24,16},{16,0},{1,9},{9,25},{25,17},{17,1},{2,10},{10... | collective-permute-start | bytes 638984 | tf_op jit(solution)/shard_map/ppermute | solution.py:389
  71.9 4.0 %early_images.5.early = f32[13440,128]{1,0:T(8,128)S(1)} custom-call(s32[8]{0:T(128)S(1)} %concatenate.3.refs_0_.bounds.edges_ref, s32[288]{0:T(512)S(1)} %pad.10.refs_1_.order, s32[288]{0:T(512)S(1)} %pad.11.refs_2_.rows, s32[288]{0:T(512)S(1)} %pad.12.refs_3_.cols, bf16[256,128,128]{2,1,0:T(8,128)(2,1)S(1)} %resident.1.values, ...), custom_call_target="tpu_custom_call" | custom-call | tf_op jit(solution)/shard_map/early_images/pallas_call | solution.py:117
  76.4 2.4 %last_images.5 = (f32[13440,128]{1,0:T(8,128)S(1)}, bf16[1664,128]{1,0:T(8,128)(2,1)S(1)}, bf16[1664,128]{1,0:T(8,128)(2,1)S(1)}, bf16[4992,128]{1,0:T(8,128)(2,1)S(1)}, bf16[4992,128]{1,0:T(8,128)(2,1)S(1)}) custom-call(s32[8]{0:T(128)S(1)} %concatenate.3.refs_0_.bounds.edges_ref, s32[288]{0:T(512)S(1)} %pad.10.refs_1_.order, ...), custom_call_target="tpu_custom_call", output_to_operand_aliasing={{0}: (5, {})} | custom-call | tf_op jit(solution)/shard_map/last_images/pallas_call | solution.py:153
  83.5 5.0 %collective-permute-done.21.refs_4_ = bf16[832,128]{1,0:T(8,128)(2,1)S(1)} collective-permute-done((bf16[832,128]{1,0:T(8,128)(2,1)S(1)}, bf16[832,128]{1,0:T(8,128)(2,1)S(1)}, u32[]{:S(2)}, u32[]{:S(2)}) %collective-permute-start.21) | collective-permute-done | bytes 213024 | tf_op jit(solution)/shard_map/ppermute | solution.py:395
  92.6 3.4 %collective-permute-start.27 = (bf16[832,128]{1,0:T(8,128)(2,1)S(1)}, bf16[832,128]{1,0:T(8,128)(2,1)S(1)}, u32[]{:S(2)}, u32[]{:S(2)}) collective-permute-start(bf16[832,128]{1,0:T(8,128)(2,1)S(1)} %collective-permute-done.25.refs_3_), channel_id=1, source_target_pairs={{0,8},{8,24},{24,16},{16,0},{1,9},{9,25},{25,17},{17,1},{2,10},{10... | collective-permute-start | bytes 638984 | tf_op jit(solution)/shard_map/ppermute | solution.py:389
  96.0 4.9 %collective-permute-done.26.refs_4_ = bf16[832,128]{1,0:T(8,128)(2,1)S(1)} collective-permute-done((bf16[832,128]{1,0:T(8,128)(2,1)S(1)}, bf16[832,128]{1,0:T(8,128)(2,1)S(1)}, u32[]{:S(2)}, u32[]{:S(2)}) %collective-permute-start.26) | collective-permute-done | bytes 213024 | tf_op jit(solution)/shard_map/ppermute | solution.py:389
  101.7 3.8 %collective-permute-done.27.refs_5_ = bf16[832,128]{1,0:T(8,128)(2,1)S(1)} collective-permute-done((bf16[832,128]{1,0:T(8,128)(2,1)S(1)}, bf16[832,128]{1,0:T(8,128)(2,1)S(1)}, u32[]{:S(2)}, u32[]{:S(2)}) %collective-permute-start.27) | collective-permute-done | bytes 213024 | tf_op jit(solution)/shard_map/ppermute | solution.py:389
  106.6 3.4 %collective-permute-start.30 = (bf16[832,128]{1,0:T(8,128)(2,1)S(1)}, bf16[832,128]{1,0:T(8,128)(2,1)S(1)}, u32[]{:S(2)}, u32[]{:S(2)}) collective-permute-start(bf16[832,128]{1,0:T(8,128)(2,1)S(1)} %get-tuple-element.117.refs_0_.refs_8_), channel_id=1, source_target_pairs={{0,8},{8,24},{24,16},{16,0},{1,9},{9,25},{25,17},{17,1},{2,10},{10... | collective-permute-start | bytes 638984 | tf_op jit(solution)/shard_map/ppermute | solution.py:389
  110.0 4.0 %early_images.6.early = f32[13440,128]{1,0:T(8,128)S(1)} custom-call(s32[8]{0:T(128)S(1)} %concatenate.3.refs_0_.bounds.edges_ref, s32[288]{0:T(512)S(1)} %pad.10.refs_1_.order, s32[288]{0:T(512)S(1)} %pad.11.refs_2_.rows, s32[288]{0:T(512)S(1)} %pad.12.refs_3_.cols, bf16[256,128,128]{2,1,0:T(8,128)(2,1)S(1)} %resident.1.values, ...), custom_call_target="tpu_custom_call" | custom-call | tf_op jit(solution)/shard_map/early_images/pallas_call | solution.py:117
  114.5 2.4 %last_images.6 = (f32[13440,128]{1,0:T(8,128)S(1)}, bf16[1664,128]{1,0:T(8,128)(2,1)S(1)}, bf16[1664,128]{1,0:T(8,128)(2,1)S(1)}, bf16[4992,128]{1,0:T(8,128)(2,1)S(1)}, bf16[4992,128]{1,0:T(8,128)(2,1)S(1)}) custom-call(s32[8]{0:T(128)S(1)} %concatenate.3.refs_0_.bounds.edges_ref, s32[288]{0:T(512)S(1)} %pad.10.refs_1_.order, ...), custom_call_target="tpu_custom_call", output_to_operand_aliasing={{0}: (5, {})} | custom-call | tf_op jit(solution)/shard_map/last_images/pallas_call | solution.py:153
  121.1 3.4 %collective-permute-start.38 = (bf16[832,128]{1,0:T(8,128)(2,1)S(1)}, bf16[832,128]{1,0:T(8,128)(2,1)S(1)}, u32[]{:S(2)}, u32[]{:S(2)}) collective-permute-start(bf16[832,128]{1,0:T(8,128)(2,1)S(1)} %collective-permute-done.30.refs_2_), channel_id=1, source_target_pairs={{0,8},{8,24},{24,16},{16,0},{1,9},{9,25},{25,17},{17,1},{2,10},{10... | collective-permute-start | bytes 638984 | tf_op jit(solution)/shard_map/ppermute | solution.py:389
  124.5 2.2 %collective-permute-done.33.refs_4_ = bf16[832,128]{1,0:T(8,128)(2,1)S(1)} collective-permute-done((bf16[832,128]{1,0:T(8,128)(2,1)S(1)}, bf16[832,128]{1,0:T(8,128)(2,1)S(1)}, u32[]{:S(2)}, u32[]{:S(2)}) %collective-permute-start.33) | collective-permute-done | bytes 213024 | tf_op jit(solution)/shard_map/ppermute | solution.py:395
  130.1 3.8 %collective-permute-done.38.refs_4_ = bf16[832,128]{1,0:T(8,128)(2,1)S(1)} collective-permute-done((bf16[832,128]{1,0:T(8,128)(2,1)S(1)}, bf16[832,128]{1,0:T(8,128)(2,1)S(1)}, u32[]{:S(2)}, u32[]{:S(2)}) %collective-permute-start.38) | collective-permute-done | bytes 213024 | tf_op jit(solution)/shard_map/ppermute | solution.py:389
  134.7 3.8 %collective-permute-done.39.refs_5_ = bf16[832,128]{1,0:T(8,128)(2,1)S(1)} collective-permute-done((bf16[832,128]{1,0:T(8,128)(2,1)S(1)}, bf16[832,128]{1,0:T(8,128)(2,1)S(1)}, u32[]{:S(2)}, u32[]{:S(2)}) %collective-permute-start.39) | collective-permute-done | bytes 213024 | tf_op jit(solution)/shard_map/ppermute | solution.py:389
  140.5 4.0 %early_images.7.early = f32[13440,128]{1,0:T(8,128)S(1)} custom-call(s32[8]{0:T(128)S(1)} %concatenate.3.refs_0_.bounds.edges_ref, s32[288]{0:T(512)S(1)} %pad.10.refs_1_.order, s32[288]{0:T(512)S(1)} %pad.11.refs_2_.rows, s32[288]{0:T(512)S(1)} %pad.12.refs_3_.cols, bf16[256,128,128]{2,1,0:T(8,128)(2,1)S(1)} %resident.1.values, ...), custom_call_target="tpu_custom_call" | custom-call | tf_op jit(solution)/shard_map/early_images/pallas_call | solution.py:117
  144.5 1.9 %collective-permute-done.41.refs_1_ = bf16[832,128]{1,0:T(8,128)(2,1)S(1)} collective-permute-done((bf16[832,128]{1,0:T(8,128)(2,1)S(1)}, bf16[832,128]{1,0:T(8,128)(2,1)S(1)}, u32[]{:S(2)}, u32[]{:S(2)}) %collective-permute-start.41) | collective-permute-done | bytes 213024 | tf_op jit(solution)/shard_map/ppermute | solution.py:389
  146.4 2.4 %last_images.7 = (f32[13440,128]{1,0:T(8,128)S(1)}, bf16[1664,128]{1,0:T(8,128)(2,1)S(1)}, bf16[1664,128]{1,0:T(8,128)(2,1)S(1)}, bf16[4992,128]{1,0:T(8,128)(2,1)S(1)}, bf16[4992,128]{1,0:T(8,128)(2,1)S(1)}) custom-call(s32[8]{0:T(128)S(1)} %concatenate.3.refs_0_.bounds.edges_ref, s32[288]{0:T(512)S(1)} %pad.10.refs_1_.order, ...), custom_call_target="tpu_custom_call", output_to_operand_aliasing={{0}: (5, {})} | custom-call | tf_op jit(solution)/shard_map/last_images/pallas_call | solution.py:153
  153.4 5.1 %collective-permute-done.45.refs_4_ = bf16[832,128]{1,0:T(8,128)(2,1)S(1)} collective-permute-done((bf16[832,128]{1,0:T(8,128)(2,1)S(1)}, bf16[832,128]{1,0:T(8,128)(2,1)S(1)}, u32[]{:S(2)}, u32[]{:S(2)}) %collective-permute-start.45) | collective-permute-done | bytes 213024 | tf_op jit(solution)/shard_map/ppermute | solution.py:395
  164.5 5.9 %collective-permute-done.47.refs_2_.refs_6_ = bf16[1664,128]{1,0:T(8,128)(2,1)S(1)} collective-permute-done((bf16[1664,128]{1,0:T(8,128)(2,1)S(1)}, bf16[1664,128]{1,0:T(8,128)(2,1)S(1)}, u32[]{:S(2)}, u32[]{:S(2)}) %collective-permute-start.47) | collective-permute-done | bytes 426016 | tf_op jit(solution)/shard_map/ppermute | solution.py:395
  (119 shorter events, 58.9 us)
Async XLA Ops:
  1.2 14.7 %collective-permute-start = (bf16[832,128]{1,0:T(8,128)(2,1)S(1)}, bf16[832,128]{1,0:T(8,128)(2,1)S(1)}, u32[]{:S(2)}, u32[]{:S(2)}) collective-permute-start(bf16[832,128]{1,0:T(8,128)(2,1)S(1)} %columns_of.4.refs_0_), channel_id=1, source_target_pairs={{0,8},{8,24},{24,16},{16,0},{1,9},{9,25},{25,17},{17,1},{2,10},{10... | collective-permute-start | bytes 638984 | tf_op jit(solution)/shard_map/ppermute | solution.py:389
  4.4 10.8 %collective-permute-start.2 = (bf16[832,128]{1,0:T(8,128)(2,1)S(1)}, bf16[832,128]{1,0:T(8,128)(2,1)S(1)}, u32[]{:S(2)}, u32[]{:S(2)}) collective-permute-start(bf16[832,128]{1,0:T(8,128)(2,1)S(1)} %columns_of.6.refs_1_), channel_id=1, source_target_pairs={{0,8},{8,24},{24,16},{16,0},{1,9},{9,25},{25,17},{17,1},{2,10},{10... | collective-permute-start | bytes 638984 | tf_op jit(solution)/shard_map/ppermute | solution.py:389
  15.1 9.1 %collective-permute-start.3 = (bf16[832,128]{1,0:T(8,128)(2,1)S(1)}, bf16[832,128]{1,0:T(8,128)(2,1)S(1)}, u32[]{:S(2)}, u32[]{:S(2)}) collective-permute-start(bf16[832,128]{1,0:T(8,128)(2,1)S(1)} %collective-permute-done.2.refs_3_), channel_id=1, source_target_pairs={{0,8},{8,24},{24,16},{16,0},{1,9},{9,25},{25,17},{17,1},{2,10},{10... | collective-permute-start | bytes 638984 | tf_op jit(solution)/shard_map/ppermute | solution.py:389
  16.0 12.8 %collective-permute-start.1 = (bf16[832,128]{1,0:T(8,128)(2,1)S(1)}, bf16[832,128]{1,0:T(8,128)(2,1)S(1)}, u32[]{:S(2)}, u32[]{:S(2)}) collective-permute-start(bf16[832,128]{1,0:T(8,128)(2,1)S(1)} %collective-permute-done.refs_2_), channel_id=1, source_target_pairs={{0,8},{8,24},{24,16},{16,0},{1,9},{9,25},{25,17},{17,1},{2,10},{10... | collective-permute-start | bytes 638984 | tf_op jit(solution)/shard_map/ppermute | solution.py:389
  24.2 12.9 %collective-permute-start.5 = (bf16[832,128]{1,0:T(8,128)(2,1)S(1)}, bf16[832,128]{1,0:T(8,128)(2,1)S(1)}, u32[]{:S(2)}, u32[]{:S(2)}) collective-permute-start(bf16[832,128]{1,0:T(8,128)(2,1)S(1)} %collective-permute-done.3.refs_5_.refs_0_), channel_id=1, source_target_pairs={{0,8},{8,24},{24,16},{16,0},{1,9},{9,25},{25,17},{17,1},{2,10},{10... | collective-permute-start | bytes 638984 | tf_op jit(solution)/shard_map/ppermute | solution.py:389
  28.8 9.1 %collective-permute-start.4 = (bf16[832,128]{1,0:T(8,128)(2,1)S(1)}, bf16[832,128]{1,0:T(8,128)(2,1)S(1)}, u32[]{:S(2)}, u32[]{:S(2)}) collective-permute-start(bf16[832,128]{1,0:T(8,128)(2,1)S(1)} %collective-permute-done.1.refs_0_.refs_4_), channel_id=1, source_target_pairs={{0,8},{8,24},{24,16},{16,0},{1,9},{9,25},{25,17},{17,1},{2,10},{10... | collective-permute-start | bytes 638984 | tf_op jit(solution)/shard_map/ppermute | solution.py:389
  29.7 11.0 %collective-permute-start.6 = (bf16[832,128]{1,0:T(8,128)(2,1)S(1)}, bf16[832,128]{1,0:T(8,128)(2,1)S(1)}, u32[]{:S(2)}, u32[]{:S(2)}) collective-permute-start(bf16[832,128]{1,0:T(8,128)(2,1)S(1)} %columns_of.5.refs_0_), channel_id=1, source_target_pairs={{0,8},{8,24},{24,16},{16,0},{1,9},{9,25},{25,17},{17,1},{2,10},{10... | collective-permute-start | bytes 638984 | tf_op jit(solution)/shard_map/ppermute | solution.py:389
  42.5 8.8 %collective-permute-start.8 = (bf16[4992,128]{1,0:T(8,128)(2,1)S(1)}, bf16[4992,128]{1,0:T(8,128)(2,1)S(1)}, u32[]{:S(2)}, u32[]{:S(2)}) collective-permute-start(bf16[4992,128]{1,0:T(8,128)(2,1)S(1)} %get-tuple-element.76), channel_id=1, source_target_pairs={{0,1},{1,0},{2,3},{3,2},{4,5},{5,4},{6,7},{7,6},{8,9},{9,8},{10,11... | collective-permute-start | bytes 3833864 | tf_op jit(solution)/shard_map/ppermute | solution.py:392
  45.6 8.8 %collective-permute-start.13 = (bf16[832,128]{1,0:T(8,128)(2,1)S(1)}, bf16[832,128]{1,0:T(8,128)(2,1)S(1)}, u32[]{:S(2)}, u32[]{:S(2)}) collective-permute-start(bf16[832,128]{1,0:T(8,128)(2,1)S(1)} %columns_of.7.refs_1_), channel_id=1, source_target_pairs={{0,8},{8,24},{24,16},{16,0},{1,9},{9,25},{25,17},{17,1},{2,10},{10... | collective-permute-start | bytes 638984 | tf_op jit(solution)/shard_map/ppermute | solution.py:389
  51.5 16.6 %collective-permute-start.11 = (bf16[1664,128]{1,0:T(8,128)(2,1)S(1)}, bf16[1664,128]{1,0:T(8,128)(2,1)S(1)}, u32[]{:S(2)}, u32[]{:S(2)}) collective-permute-start(bf16[1664,128]{1,0:T(8,128)(2,1)S(1)} %get-tuple-element.80), channel_id=1, source_target_pairs={{0,2},{1,3},{2,0},{3,1},{4,6},{5,7},{6,4},{7,5},{8,10},{9,11},{10,... | collective-permute-start | bytes 1277960 | tf_op jit(solution)/shard_map/ppermute | solution.py:395
  52.4 15.7 %collective-permute-start.12 = (bf16[1664,128]{1,0:T(8,128)(2,1)S(1)}, bf16[1664,128]{1,0:T(8,128)(2,1)S(1)}, u32[]{:S(2)}, u32[]{:S(2)}) collective-permute-start(bf16[1664,128]{1,0:T(8,128)(2,1)S(1)} %get-tuple-element.81), channel_id=1, source_target_pairs={{0,4},{1,5},{2,6},{3,7},{4,0},{5,1},{6,2},{7,3},{8,12},{9,13},{10,... | collective-permute-start | bytes 1277960 | tf_op jit(solution)/shard_map/ppermute | solution.py:395
  53.6 9.1 %collective-permute-start.14 = (bf16[832,128]{1,0:T(8,128)(2,1)S(1)}, bf16[832,128]{1,0:T(8,128)(2,1)S(1)}, u32[]{:S(2)}, u32[]{:S(2)}) collective-permute-start(bf16[832,128]{1,0:T(8,128)(2,1)S(1)} %collective-permute-done.6.refs_2_), channel_id=1, source_target_pairs={{0,8},{8,24},{24,16},{16,0},{1,9},{9,25},{25,17},{17,1},{2,10},{10... | collective-permute-start | bytes 638984 | tf_op jit(solution)/shard_map/ppermute | solution.py:389
  54.4 12.9 %collective-permute-start.15 = (bf16[832,128]{1,0:T(8,128)(2,1)S(1)}, bf16[832,128]{1,0:T(8,128)(2,1)S(1)}, u32[]{:S(2)}, u32[]{:S(2)}) collective-permute-start(bf16[832,128]{1,0:T(8,128)(2,1)S(1)} %collective-permute-done.13.refs_3_), channel_id=1, source_target_pairs={{0,8},{8,24},{24,16},{16,0},{1,9},{9,25},{25,17},{17,1},{2,10},{10... | collective-permute-start | bytes 638984 | tf_op jit(solution)/shard_map/ppermute | solution.py:389
  62.7 13.1 %collective-permute-start.16 = (bf16[832,128]{1,0:T(8,128)(2,1)S(1)}, bf16[832,128]{1,0:T(8,128)(2,1)S(1)}, u32[]{:S(2)}, u32[]{:S(2)}) collective-permute-start(bf16[832,128]{1,0:T(8,128)(2,1)S(1)} %collective-permute-done.14.refs_4_), channel_id=1, source_target_pairs={{0,8},{8,24},{24,16},{16,0},{1,9},{9,25},{25,17},{17,1},{2,10},{10... | collective-permute-start | bytes 638984 | tf_op jit(solution)/shard_map/ppermute | solution.py:389
  67.3 9.1 %collective-permute-start.17 = (bf16[832,128]{1,0:T(8,128)(2,1)S(1)}, bf16[832,128]{1,0:T(8,128)(2,1)S(1)}, u32[]{:S(2)}, u32[]{:S(2)}) collective-permute-start(bf16[832,128]{1,0:T(8,128)(2,1)S(1)} %collective-permute-done.15.refs_5_), channel_id=1, source_target_pairs={{0,8},{8,24},{24,16},{16,0},{1,9},{9,25},{25,17},{17,1},{2,10},{10... | collective-permute-start | bytes 638984 | tf_op jit(solution)/shard_map/ppermute | solution.py:389
  68.4 10.4 %collective-permute-start.18 = (bf16[832,128]{1,0:T(8,128)(2,1)S(1)}, bf16[832,128]{1,0:T(8,128)(2,1)S(1)}, u32[]{:S(2)}, u32[]{:S(2)}) collective-permute-start(bf16[832,128]{1,0:T(8,128)(2,1)S(1)} %get-tuple-element.101.refs_0_.refs_8_), channel_id=1, source_target_pairs={{0,8},{8,24},{24,16},{16,0},{1,9},{9,25},{25,17},{17,1},{2,10},{10... | collective-permute-start | bytes 638984 | tf_op jit(solution)/shard_map/ppermute | solution.py:389
  82.7 9.9 %collective-permute-start.25 = (bf16[832,128]{1,0:T(8,128)(2,1)S(1)}, bf16[832,128]{1,0:T(8,128)(2,1)S(1)}, u32[]{:S(2)}, u32[]{:S(2)}) collective-permute-start(bf16[832,128]{1,0:T(8,128)(2,1)S(1)} %get-tuple-element.83.refs_1_.refs_9_), channel_id=1, source_target_pairs={{0,8},{8,24},{24,16},{16,0},{1,9},{9,25},{25,17},{17,1},{2,10},{10... | collective-permute-start | bytes 638984 | tf_op jit(solution)/shard_map/ppermute | solution.py:389
  89.0 17.2 %collective-permute-start.23 = (bf16[1664,128]{1,0:T(8,128)(2,1)S(1)}, bf16[1664,128]{1,0:T(8,128)(2,1)S(1)}, u32[]{:S(2)}, u32[]{:S(2)}) collective-permute-start(bf16[1664,128]{1,0:T(8,128)(2,1)S(1)} %get-tuple-element.97), channel_id=1, source_target_pairs={{0,2},{1,3},{2,0},{3,1},{4,6},{5,7},{6,4},{7,5},{8,10},{9,11},{10,... | collective-permute-start | bytes 1277960 | tf_op jit(solution)/shard_map/ppermute | solution.py:395
  90.3 16.0 %collective-permute-start.24 = (bf16[1664,128]{1,0:T(8,128)(2,1)S(1)}, bf16[1664,128]{1,0:T(8,128)(2,1)S(1)}, u32[]{:S(2)}, u32[]{:S(2)}) collective-permute-start(bf16[1664,128]{1,0:T(8,128)(2,1)S(1)} %get-tuple-element.98), channel_id=1, source_target_pairs={{0,4},{1,5},{2,6},{3,7},{4,0},{5,1},{6,2},{7,3},{8,12},{9,13},{10,... | collective-permute-start | bytes 1277960 | tf_op jit(solution)/shard_map/ppermute | solution.py:395
  91.8 9.1 %collective-permute-start.26 = (bf16[832,128]{1,0:T(8,128)(2,1)S(1)}, bf16[832,128]{1,0:T(8,128)(2,1)S(1)}, u32[]{:S(2)}, u32[]{:S(2)}) collective-permute-start(bf16[832,128]{1,0:T(8,128)(2,1)S(1)} %collective-permute-done.18.refs_2_), channel_id=1, source_target_pairs={{0,8},{8,24},{24,16},{16,0},{1,9},{9,25},{25,17},{17,1},{2,10},{10... | collective-permute-start | bytes 638984 | tf_op jit(solution)/shard_map/ppermute | solution.py:389
  92.6 12.9 %collective-permute-start.27 = (bf16[832,128]{1,0:T(8,128)(2,1)S(1)}, bf16[832,128]{1,0:T(8,128)(2,1)S(1)}, u32[]{:S(2)}, u32[]{:S(2)}) collective-permute-start(bf16[832,128]{1,0:T(8,128)(2,1)S(1)} %collective-permute-done.25.refs_3_), channel_id=1, source_target_pairs={{0,8},{8,24},{24,16},{16,0},{1,9},{9,25},{25,17},{17,1},{2,10},{10... | collective-permute-start | bytes 638984 | tf_op jit(solution)/shard_map/ppermute | solution.py:389
  100.9 13.1 %collective-permute-start.28 = (bf16[832,128]{1,0:T(8,128)(2,1)S(1)}, bf16[832,128]{1,0:T(8,128)(2,1)S(1)}, u32[]{:S(2)}, u32[]{:S(2)}) collective-permute-start(bf16[832,128]{1,0:T(8,128)(2,1)S(1)} %collective-permute-done.26.refs_4_), channel_id=1, source_target_pairs={{0,8},{8,24},{24,16},{16,0},{1,9},{9,25},{25,17},{17,1},{2,10},{10... | collective-permute-start | bytes 638984 | tf_op jit(solution)/shard_map/ppermute | solution.py:389
  105.5 9.1 %collective-permute-start.29 = (bf16[832,128]{1,0:T(8,128)(2,1)S(1)}, bf16[832,128]{1,0:T(8,128)(2,1)S(1)}, u32[]{:S(2)}, u32[]{:S(2)}) collective-permute-start(bf16[832,128]{1,0:T(8,128)(2,1)S(1)} %collective-permute-done.27.refs_5_), channel_id=1, source_target_pairs={{0,8},{8,24},{24,16},{16,0},{1,9},{9,25},{25,17},{17,1},{2,10},{10... | collective-permute-start | bytes 638984 | tf_op jit(solution)/shard_map/ppermute | solution.py:389
  106.6 10.4 %collective-permute-start.30 = (bf16[832,128]{1,0:T(8,128)(2,1)S(1)}, bf16[832,128]{1,0:T(8,128)(2,1)S(1)}, u32[]{:S(2)}, u32[]{:S(2)}) collective-permute-start(bf16[832,128]{1,0:T(8,128)(2,1)S(1)} %get-tuple-element.117.refs_0_.refs_8_), channel_id=1, source_target_pairs={{0,8},{8,24},{24,16},{16,0},{1,9},{9,25},{25,17},{17,1},{2,10},{10... | collective-permute-start | bytes 638984 | tf_op jit(solution)/shard_map/ppermute | solution.py:389
  120.3 9.0 %collective-permute-start.37 = (bf16[832,128]{1,0:T(8,128)(2,1)S(1)}, bf16[832,128]{1,0:T(8,128)(2,1)S(1)}, u32[]{:S(2)}, u32[]{:S(2)}) collective-permute-start(bf16[832,128]{1,0:T(8,128)(2,1)S(1)} %get-tuple-element.100.refs_1_.refs_9_), channel_id=1, source_target_pairs={{0,8},{8,24},{24,16},{16,0},{1,9},{9,25},{25,17},{17,1},{2,10},{10... | collective-permute-start | bytes 638984 | tf_op jit(solution)/shard_map/ppermute | solution.py:389
  121.1 12.8 %collective-permute-start.38 = (bf16[832,128]{1,0:T(8,128)(2,1)S(1)}, bf16[832,128]{1,0:T(8,128)(2,1)S(1)}, u32[]{:S(2)}, u32[]{:S(2)}) collective-permute-start(bf16[832,128]{1,0:T(8,128)(2,1)S(1)} %collective-permute-done.30.refs_2_), channel_id=1, source_target_pairs={{0,8},{8,24},{24,16},{16,0},{1,9},{9,25},{25,17},{17,1},{2,10},{10... | collective-permute-start | bytes 638984 | tf_op jit(solution)/shard_map/ppermute | solution.py:389
  127.0 12.3 %collective-permute-start.35 = (bf16[1664,128]{1,0:T(8,128)(2,1)S(1)}, bf16[1664,128]{1,0:T(8,128)(2,1)S(1)}, u32[]{:S(2)}, u32[]{:S(2)}) collective-permute-start(bf16[1664,128]{1,0:T(8,128)(2,1)S(1)} %get-tuple-element.114), channel_id=1, source_target_pairs={{0,2},{1,3},{2,0},{3,1},{4,6},{5,7},{6,4},{7,5},{8,10},{9,11},{10,... | collective-permute-start | bytes 1277960 | tf_op jit(solution)/shard_map/ppermute | solution.py:395
  127.9 11.4 %collective-permute-start.36 = (bf16[1664,128]{1,0:T(8,128)(2,1)S(1)}, bf16[1664,128]{1,0:T(8,128)(2,1)S(1)}, u32[]{:S(2)}, u32[]{:S(2)}) collective-permute-start(bf16[1664,128]{1,0:T(8,128)(2,1)S(1)} %get-tuple-element.115), channel_id=1, source_target_pairs={{0,4},{1,5},{2,6},{3,7},{4,0},{5,1},{6,2},{7,3},{8,12},{9,13},{10,... | collective-permute-start | bytes 1277960 | tf_op jit(solution)/shard_map/ppermute | solution.py:395
  129.3 9.1 %collective-permute-start.39 = (bf16[832,128]{1,0:T(8,128)(2,1)S(1)}, bf16[832,128]{1,0:T(8,128)(2,1)S(1)}, u32[]{:S(2)}, u32[]{:S(2)}) collective-permute-start(bf16[832,128]{1,0:T(8,128)(2,1)S(1)} %collective-permute-done.37.refs_3_), channel_id=1, source_target_pairs={{0,8},{8,24},{24,16},{16,0},{1,9},{9,25},{25,17},{17,1},{2,10},{10... | collective-permute-start | bytes 638984 | tf_op jit(solution)/shard_map/ppermute | solution.py:389
  133.9 10.6 %collective-permute-start.40 = (bf16[832,128]{1,0:T(8,128)(2,1)S(1)}, bf16[832,128]{1,0:T(8,128)(2,1)S(1)}, u32[]{:S(2)}, u32[]{:S(2)}) collective-permute-start(bf16[832,128]{1,0:T(8,128)(2,1)S(1)} %collective-permute-done.38.refs_4_), channel_id=1, source_target_pairs={{0,8},{8,24},{24,16},{16,0},{1,9},{9,25},{25,17},{17,1},{2,10},{10... | collective-permute-start | bytes 638984 | tf_op jit(solution)/shard_map/ppermute | solution.py:389
  159.4 11.0 %collective-permute-start.47 = (bf16[1664,128]{1,0:T(8,128)(2,1)S(1)}, bf16[1664,128]{1,0:T(8,128)(2,1)S(1)}, u32[]{:S(2)}, u32[]{:S(2)}) collective-permute-start(bf16[1664,128]{1,0:T(8,128)(2,1)S(1)} %get-tuple-element.131), channel_id=1, source_target_pairs={{0,2},{1,3},{2,0},{3,1},{4,6},{5,7},{6,4},{7,5},{8,10},{9,11},{10,... | collective-permute-start | bytes 1277960 | tf_op jit(solution)/shard_map/ppermute | solution.py:395
  160.9 10.7 %collective-permute-start.48 = (bf16[1664,128]{1,0:T(8,128)(2,1)S(1)}, bf16[1664,128]{1,0:T(8,128)(2,1)S(1)}, u32[]{:S(2)}, u32[]{:S(2)}) collective-permute-start(bf16[1664,128]{1,0:T(8,128)(2,1)S(1)} %get-tuple-element.132), channel_id=1, source_target_pairs={{0,4},{1,5},{2,6},{3,7},{4,0},{5,1},{6,2},{7,3},{8,12},{9,13},{10,... | collective-permute-start | bytes 1277960 | tf_op jit(solution)/shard_map/ppermute | solution.py:395
  (24 other events, 131.0 us)

commit v4 on v3

--- a/solution.py
+++ b/solution.py
@@ -68,6 +68,21 @@
         ),
         name="columns_of",
     )(vectors, *after)
+
+
+def rows_of(array, low, size):
+    def kernel(array_ref, out_ref):
+        out_ref[...] = array_ref[low : low + size, :]
+
+    out = jax.ShapeDtypeStruct((size, array.shape[1]), array.dtype)
+    return pl.pallas_call(
+        kernel,
+        out_shape=out,
+        in_specs=[VMEM],
+        out_specs=VMEM,
+        compiler_params=params(bytes_of(array, out)),
+        name="rows_of",
+    )(array)
 
 
 def add_images(bounds, order, rows, cols, values, panel, total, phase, low_col):
@@ -201,26 +216,29 @@
     return image
 
 
-def first_update(terms, vectors, low, center, half_width):
+def first_update(terms, vectors, low, center, half_width, top):
     flat = [array for _, pairs in terms for array, _ in pairs]
     width = flat[0].shape[1]
 
     def kernel(center_ref, width_ref, vectors_ref, *refs):
-        out_refs = refs[len(flat) :]
-        row, at = 0, 0
-        for (size, pairs), out_ref in zip(terms, out_refs):
-            image = image_rows(refs[at : at + len(pairs)], pairs, size)
-            at += len(pairs)
-            source = vectors_ref[row : row + size, low : low + width].astype(jnp.float32)
-            out_ref[...] = ((image - center_ref[0] * source) / width_ref[0]).astype(out_ref.dtype)
-            row += size
-
+        full_ref, upper_ref, lower_ref = refs[len(flat) :]
+        ((size, pairs),) = terms
+        image = image_rows(refs[: len(flat)], pairs, size)
+        source = vectors_ref[:, low : low + width].astype(jnp.float32)
+        step = ((image - center_ref[0] * source) / width_ref[0]).astype(full_ref.dtype)
+        full_ref[...] = step
+        upper_ref[...] = step[:top]
+        lower_ref[...] = step[top:]
+
+    rows = terms[0][0]
     need = bytes_of(*flat, vectors)
     return pl.pallas_call(
         kernel,
-        out_shape=[jax.ShapeDtypeStruct((size, width), jnp.bfloat16) for size, _ in terms],
+        out_shape=[
+            jax.ShapeDtypeStruct((size, width), jnp.bfloat16) for size in (rows, top, rows - top)
+        ],
         in_specs=[SMEM] * 2 + [VMEM] * (1 + len(flat)),
-        out_specs=[VMEM] * len(terms),
+        out_specs=[VMEM] * 3,
         compiler_params=params(need),
         cost_estimate=pl.CostEstimate(flops=0, bytes_accessed=need, transcendentals=0),
         name="first_update",
@@ -329,6 +347,9 @@
     route = [(order[i], order[(i + 1) % row_count]) for i in range(row_count)]
     place_of = [order.index(i) for i in range(row_count)]
 
+    back_route = [(target, source) for source, target in route]
+    both_ways = row_count == 4
+
     def looked_up(table, index):
         result = jnp.zeros_like(index)
         for at, value in enumerate(table):
@@ -353,6 +374,8 @@
         arrival = lax.rem(
             looked_up(place_of, my_row) - looked_up(place_of, col_ids // own) + row_count, row_count
         )
+        if both_ways:
+            arrival = looked_up([0, 1, 3, 2], arrival)
         panel_cols = arrival * own + col_ids % own
         relative = (row_ids // own) ^ my_col
         piece = chip_count - 1 - relative // 2
@@ -381,147 +404,103 @@
     other_core = [(i, i ^ 1) for i in range(col_count)]
     lanes = 128 if vec_count % 128 == 0 else vec_count
     lows = list(range(0, vec_count, lanes))
-    cut = own_rows // 2 if own_rows % 32 == 0 else own_rows
-    sizes = [cut, own_rows - cut] if cut < own_rows else [own_rows]
-    crossed = chip_count == 4 and len(sizes) == 2
-
-    def along_row(array):
-        return lax.ppermute(array, "row", route)
+    top = own_rows // 32 * 16
 
     def to_core(array):
         return lax.ppermute(array, "col", other_core)
 
     def to_chip(array, chip):
         return lax.ppermute(array, "col", [(i, i ^ 2 * chip) for i in range(col_count)])
-
-    class Gather:
-        def __init__(self, parts):
-            self.arrived = [list(parts)]
-
-        def step(self, ties):
-            held = self.arrived[-1]
-            if len(self.arrived) < row_count:
-                self.arrived.append(
-                    [along_row(tied(part, tie)) for part, tie in zip(held, ties)]
-                )
 
     def tied(array, tokens):
         tokens = list(tokens)
         return lax.optimization_barrier((array, *tokens))[0] if tokens else array
 
-    def terms_of(gather, following, tokens):
-        none = [[] for _ in sizes]
-        counts = (1, 3) if crossed else (1,) * chip_count
-        parts = [part for step in gather.arrived[:-1] for part in step]
-        parts[0] = tied(parts[0], tokens)
-        early = early_images(2 * chip_count * own, tables, values, parts)
-        last = gather.arrived[-1]
+    class Gather:
+        def __init__(self, part, upper, lower):
+            if both_ways:
+                upper, lower = (lax.ppermute(half, "row", route) for half in (upper, lower))
+                self.early = [part, upper, lower, lax.ppermute(part, "row", back_route)]
+            else:
+                self.early = [part, lax.ppermute(part, "row", route)]
+
+        def finish(self, tokens):
+            self.send_last(tokens)
+            self.images = early_images(2 * chip_count * own, tables, values, self.early)
+
+        def send_last(self, tokens):
+            if both_ways:
+                _, upper, _, behind = self.early
+                lower = rows_of(tied(behind, tokens), top, own_rows - top)
+                self.last = [
+                    lax.ppermute(tied(upper, tokens), "row", route),
+                    lax.ppermute(lower, "row", back_route),
+                ]
+                return
+            while len(self.early) < row_count:
+                self.early.append(lax.ppermute(self.early[-1], "row", route))
+            self.last = [self.early.pop()]
+
+    def image_terms(gather, following, tokens):
+        counts = (1, chip_count - 1) if chip_count > 1 else (1,)
+        early = gather.images
+        last = [tied(gather.last[0], tokens), *gather.last[1:]]
         outs = last_images(counts, (row_count - 1) * own, tables, values, early, last)
-
-        def go_on(*ties):
-            if following is not None:
-                following.step(ties)
-
-        if not crossed:
-            kept = partner = None
-            arrived = []
-            for piece in range(chip_count):
-                chip = chip_count - 1 - piece
-                sent, kept = outs[2 * piece], outs[2 * piece + 1]
-                partner = to_core(sent)
-                if chip:
-                    (both,) = summed([[(own_rows, [(kept, 0), (partner, 0)])]])
-                    arrived.append(to_chip(both, chip))
-            for _ in range(row_count):
-                go_on(*none)
-            low, terms = 0, []
-            for size in sizes:
-                pairs = [(array, low) for array in [kept, partner, *arrived]]
-                terms.append((size, pairs))
-                low += size
-            return terms
-
-        top, rest = sizes
-        sent, kept, sent_others, others = outs
+        pairs = []
+        for sent, kept in zip(outs[::2], outs[1::2]):
+            if pairs:
+                sent = tied(sent, [pairs[-1][1]])
+            elif following is not None and both_ways:
+                sent = tied(sent, following.early[1:2])
+            pairs.append((kept, to_core(sent)))
+        terms, arrived, chip = [], [], chip_count - 1
+        for count, (kept, partner) in zip(counts, pairs):
+            places = [[(kept, i * own_rows), (partner, i * own_rows)] for i in range(count)]
+            if chip < count:
+                terms = places.pop()
+            sums = summed([[(own_rows, place)] for place in places]) if places else []
+            for array in sums:
+                arrived.append((to_chip(array, chip), 0))
+                chip -= 1
         if following is not None:
-            sent = tied(sent, following.arrived[-1][:1])
-        partner = to_core(sent)
-        partners = to_core(tied(sent_others, [partner]))
-        corner = summed(
-            [[(top, [(kept, 0), (partner, 0)])], [(rest, [(kept, top), (partner, top)])]]
-        )
-        by_x, by_y = to_chip(corner[0], 1), to_chip(corner[1], 2)
-        go_on([sent], corner)
-
-        def both(low, *more):
-            return [(others, low), (partners, low), *more]
-
-        y, x, mine = 0, own_rows, 2 * own_rows
-        sides = summed(
-            [
-                [(top, both(x)), (rest, both(x + top, (by_y, 0)))],
-                [(top, both(y, (by_x, 0))), (rest, both(y + top))],
-            ]
-        )
-        from_x, from_y = to_chip(sides[0], 1), to_chip(sides[1], 2)
-        go_on(corner, sides)
-        for _ in range(row_count):
-            go_on(*none)
-        return [
-            (top, both(mine, (from_x, 0), (from_y, 0))),
-            (rest, both(mine + top, (from_x, top), (from_y, top))),
-        ]
-
-    none = [[] for _ in sizes]
+            following.finish(sums)
+        return [(own_rows, [*terms, *arrived])]
+
     gathers = []
     for low in lows:
-        after = [[] for _ in sizes]
-        if gathers:
-            before = gathers[-1].arrived
-            after = [[before[-2 if row_count > 1 else -1][i]] for i in range(len(sizes))]
-        gather = Gather(
-            columns_of(start_vectors, i * cut, size, low, lanes, after[i])
-            for i, size in enumerate(sizes)
+        after = [gathers[-1].images] if len(gathers) == 1 else []
+        cuts = [(0, own_rows), (0, top), (top, own_rows - top)]
+        gathers.append(
+            Gather(*[columns_of(start_vectors, *cut, low, lanes, after) for cut in cuts])
         )
-        if not gathers:
-            gather.step(none)
-            gather.step([tables, *none[1:]])
-            gather.step([*none[1:], [values]])
-            for _ in range(row_count):
-                gather.step(none)
-        else:
-            gather.step(none)
-        gathers.append(gather)
+        if len(gathers) == 1:
+            gathers[0].finish([*tables, values, gathers[0].early[2 if both_ways else 1]])
     firsts = []
     count = len(lows)
     for turn in range(count):
         if turn:
-            following = Gather(firsts[-1])
-            following.step(none)
-            gathers.append(following)
+            gathers.append(Gather(*firsts[-1]))
         following = gathers[turn + 1] if turn + 1 < len(gathers) else None
-        terms = terms_of(gathers[turn], following, firsts[-1] if turn else [])
-        firsts.append(first_update(terms, start_vectors, lows[turn], center, half_width))
+        terms = image_terms(gathers[turn], following, firsts[-1] if turn else [])
+        firsts.append(first_update(terms, start_vectors, lows[turn], center, half_width, top))
     if count == 1:
-        gathers.append(Gather(firsts[0]))
-        for _ in range(row_count):
-            gathers[-1].step(none)
+        gathers.append(Gather(*firsts[0]))
+        gathers[-1].finish([])
+    relaid = None
     seconds = []
-    relaid = None
     for turn in range(count):
         following = None
         if turn + 1 < count:
             if count + turn + 1 == len(gathers):
-                gathers.append(Gather(firsts[turn + 1]))
-                gathers[-1].step(none)
+                gathers.append(Gather(*firsts[turn + 1]))
             following = gathers[count + turn + 1]
         tokens = seconds[-1:] if turn else firsts[-1]
-        terms = terms_of(gathers[count + turn], following, tokens)
+        terms = image_terms(gathers[count + turn], following, tokens)
         if relaid is not None:
-            size, ((array, row), *more) = terms[0]
-            terms = [(size, [(tied(array, [relaid]), row), *more]), *terms[1:]]
+            ((size, ((array, row), *more)),) = terms
+            terms = [(size, [(tied(array, [relaid]), row), *more])]
         second, edge = second_update(
-            terms, firsts[turn], start_vectors, lows[turn], center, half_width, tables, edge_size
+            terms, firsts[turn][:1], start_vectors, lows[turn], center, half_width, tables, edge_size
         )
         seconds.append(second)
         shape = (capacity * orbitals, vec_count)

time: 176 us -> 171 us (0.972)
  starting transfers between devices: 59.9 us -> 50.8 us
  waiting for transfers between devices: 71.9 us -> 74.6 us
    ppermute x24 -> x20, starting transfers between devices: 41.5 us -> 29.2 us  [the longest x4 10.6 us: send_last(): lax.ppermute(lower, 'row', back_route)]
    ppermute x24 -> x20, waiting for transfers between devices: 36.8 us -> 40.7 us  [the longest x8 17.3 us: __init__(): upper, lower = (lax.ppermute(half, 'row', route) for half in (upper, lower))]
    ppermute x16 -> x12, starting transfers between devices: 17.5 us -> 20 us  [to_chip(): lax.ppermute(array, 'col', [(i, i ^ 2 * chip) for i in range(col_count)])]
    pallas_call x4, Pallas kernels: 9.62 us -> 7.7 us  [last_images(): pl.pallas_call(kernel, out_shape=[pltpu.VMEM(early.shape, jnp.float32), *...]
    pallas_call x4, Pallas kernels: 16 us -> 17.9 us  [early_images(): pl.pallas_call(kernel, out_shape=pltpu.VMEM(total, jnp.float32), in_specs...]
    ppermute x16 -> x12, waiting for transfers between devices: 25.2 us -> 24.1 us  [to_chip(): lax.ppermute(array, 'col', [(i, i ^ 2 * chip) for i in range(col_count)])]
  transfers between devices with their start and end apart: 50 -> 42, of which waited for: 31 -> 28; matrix products, arithmetic and copies ran while one was open for 1% -> 1% of each run, Pallas kernels for 16% -> 17%
where the time goes in v4:
time: 171 us; the launch traced here: 170 us
  waiting for transfers between devices  74.6 us (44%)
  starting transfers between devices  50.8 us (30%)
  Pallas kernels  34.9 us (20%)
  local copies, waits for them, and re-layouts  5.8 us (3%)
  between operations  3.15 us (2%)
    ppermute x12, waiting for transfers between devices, to_chip(): lax.ppermute(array, 'col', [(i, i ^ 2 * chip) for i in range(col_count)])  24.1 us
    ppermute x12, starting transfers between devices, to_chip(): lax.ppermute(array, 'col', [(i, i ^ 2 * chip) for i in range(col_count)])  20 us
    pallas_call x4, Pallas kernels, early_images(): pl.pallas_call(kernel, out_shape=pltpu.VMEM(total, jnp.float32), in_specs...  17.9 us
    ppermute x8, waiting for transfers between devices, __init__(): upper, lower = (lax.ppermute(half, 'row', route) for half in (upper, lower))  17.3 us
    ppermute x4, waiting for transfers between devices, __init__(): self.early = [part, upper, lower, lax.ppermute(part, 'row', back_route)]  16.3 us
    ppermute x4, starting transfers between devices, send_last(): lax.ppermute(lower, 'row', back_route)  10.6 us
    ppermute x10, waiting for transfers between devices, to_core(): return lax.ppermute(array, 'col', other_core)  9.84 us
    pallas_call x4, Pallas kernels, last_images(): pl.pallas_call(kernel, out_shape=[pltpu.VMEM(early.shape, jnp.float32), *...  7.7 us
  transfers between devices with their start and end apart: 42, of which 28 were waited for; matrix products, arithmetic and copies ran while one was open for 1% of the time, Pallas kernels for 17%

profile of v4, /device:TPU:0, one launch (start us, length us, event | category | flops | bytes accessed | tf_op | source)
XLA Modules:
  0.0 170.4 jit_solution(8554214172927224108)
XLA Ops:
  1.3 4.1 %collective-permute-start.2 = (bf16[1664,128]{1,0:T(8,128)(2,1)S(1)}, bf16[1664,128]{1,0:T(8,128)(2,1)S(1)}, u32[]{:S(2)}, u32[]{:S(2)}) collective-permute-start(bf16[1664,128]{1,0:T(8,128)(2,1)S(1)} %columns_of.6.refs_0_), channel_id=1, source_target_pairs={{8,0},{24,8},{16,24},{0,16},{9,1},{25,9},{17,25},{1,17},{10,2},{26... | collective-permute-start | bytes 1277960 | tf_op jit(solution)/shard_map/ppermute | solution.py:423
  5.6 2.6 %collective-permute-start = (bf16[832,128]{1,0:T(8,128)(2,1)S(1)}, bf16[832,128]{1,0:T(8,128)(2,1)S(1)}, u32[]{:S(2)}, u32[]{:S(2)}) collective-permute-start(bf16[832,128]{1,0:T(8,128)(2,1)S(1)} %columns_of.7), channel_id=1, source_target_pairs={{0,8},{8,24},{24,16},{16,0},{1,9},{9,25},{25,17},{17,1},{2,10},{10... | collective-permute-start | bytes 638984 | tf_op jit(solution)/shard_map/ppermute | solution.py:422
  11.9 3.4 %copy-done.2 = bf16[1,1,256,128,128]{4,3,2,1,0:T(8,128)(2,1)S(1)} copy-done((bf16[1,1,256,128,128]{4,3,2,1,0:T(8,128)(2,1)S(1)}, bf16[1,1,256,128,128]{4,3,2,1,0:T(8,128)(2,1)}, u32[]{:S(2)}) %copy-start.2) | copy-done | bytes 8388632
  15.9 5.1 %collective-permute-done.1.refs_2_ = bf16[832,128]{1,0:T(8,128)(2,1)S(1)} collective-permute-done((bf16[832,128]{1,0:T(8,128)(2,1)S(1)}, bf16[832,128]{1,0:T(8,128)(2,1)S(1)}, u32[]{:S(2)}, u32[]{:S(2)}) %collective-permute-start.1) | collective-permute-done | bytes 213024 | tf_op jit(solution)/shard_map/ppermute | solution.py:422
  20.9 4.5 %collective-permute-done.refs_1_ = bf16[832,128]{1,0:T(8,128)(2,1)S(1)} collective-permute-done((bf16[832,128]{1,0:T(8,128)(2,1)S(1)}, bf16[832,128]{1,0:T(8,128)(2,1)S(1)}, u32[]{:S(2)}, u32[]{:S(2)}) %collective-permute-start) | collective-permute-done | bytes 213024 | tf_op jit(solution)/shard_map/ppermute | solution.py:422
  26.1 2.3 %collective-permute-start.7 = (bf16[832,128]{1,0:T(8,128)(2,1)S(1)}, bf16[832,128]{1,0:T(8,128)(2,1)S(1)}, u32[]{:S(2)}, u32[]{:S(2)}) collective-permute-start(bf16[832,128]{1,0:T(8,128)(2,1)S(1)} %rows_of.4), channel_id=1, source_target_pairs={{8,0},{24,8},{16,24},{0,16},{9,1},{25,9},{17,25},{1,17},{10,2},{26... | collective-permute-start | bytes 638984 | tf_op jit(solution)/shard_map/ppermute | solution.py:437
  28.4 4.5 %early_images.4.refs_0_.early = f32[13440,128]{1,0:T(8,128)S(1)} custom-call(s32[8]{0:T(128)S(1)} %concatenate.3.refs_0_.bounds.edges_ref, s32[288]{0:T(512)S(1)} %pad.10.refs_1_.order, s32[288]{0:T(512)S(1)} %pad.11.refs_2_.rows, s32[288]{0:T(512)S(1)} %pad.12.refs_3_.cols, bf16[256,128,128]{2,1,0:T(8,128)(2,1)S(1)} %resident.1.values, ...), custom_call_target="tpu_custom_call" | custom-call | tf_op jit(solution)/shard_map/early_images/pallas_call | solution.py:132
  33.2 4.4 %collective-permute-done.6.refs_0_ = bf16[832,128]{1,0:T(8,128)(2,1)S(1)} collective-permute-done((bf16[832,128]{1,0:T(8,128)(2,1)S(1)}, bf16[832,128]{1,0:T(8,128)(2,1)S(1)}, u32[]{:S(2)}, u32[]{:S(2)}) %collective-permute-start.6) | collective-permute-done | bytes 213024 | tf_op jit(solution)/shard_map/ppermute | solution.py:436
  38.4 1.9 %last_images.4 = (f32[13440,128]{1,0:T(8,128)S(1)}, bf16[1664,128]{1,0:T(8,128)(2,1)S(1)}, bf16[1664,128]{1,0:T(8,128)(2,1)S(1)}, bf16[4992,128]{1,0:T(8,128)(2,1)S(1)}, bf16[4992,128]{1,0:T(8,128)(2,1)S(1)}) custom-call(s32[8]{0:T(128)S(1)} %concatenate.3.refs_0_.bounds.edges_ref, s32[288]{0:T(512)S(1)} %pad.10.refs_1_.order, ...), custom_call_target="tpu_custom_call", output_to_operand_aliasing={{0}: (5, {})} | custom-call | tf_op jit(solution)/shard_map/last_images/pallas_call | solution.py:168
  40.4 2.3 %collective-permute-done.3.refs_1_ = bf16[832,128]{1,0:T(8,128)(2,1)S(1)} collective-permute-done((bf16[832,128]{1,0:T(8,128)(2,1)S(1)}, bf16[832,128]{1,0:T(8,128)(2,1)S(1)}, u32[]{:S(2)}, u32[]{:S(2)}) %collective-permute-start.3) | collective-permute-done | bytes 213024 | tf_op jit(solution)/shard_map/ppermute | solution.py:422
  45.1 2.5 %collective-permute-start.11 = (bf16[1664,128]{1,0:T(8,128)(2,1)S(1)}, bf16[1664,128]{1,0:T(8,128)(2,1)S(1)}, u32[]{:S(2)}, u32[]{:S(2)}) collective-permute-start(bf16[1664,128]{1,0:T(8,128)(2,1)S(1)} %summed.9), channel_id=1, source_target_pairs={{0,6},{1,7},{2,4},{3,5},{4,2},{5,3},{6,0},{7,1},{8,14},{9,15},{10,... | collective-permute-start | bytes 1277960 | tf_op jit(solution)/shard_map/ppermute | solution.py:413
  52.0 4.7 %collective-permute-done.5.refs_3_.array_ref = bf16[1664,128]{1,0:T(8,128)(2,1)S(1)} collective-permute-done((bf16[1664,128]{1,0:T(8,128)(2,1)S(1)}, bf16[1664,128]{1,0:T(8,128)(2,1)S(1)}, u32[]{:S(2)}, u32[]{:S(2)}) %collective-permute-start.5) | collective-permute-done | bytes 426016 | tf_op jit(solution)/shard_map/ppermute | solution.py:423
  58.7 5.4 %collective-permute-start.14 = (bf16[832,128]{1,0:T(8,128)(2,1)S(1)}, bf16[832,128]{1,0:T(8,128)(2,1)S(1)}, u32[]{:S(2)}, u32[]{:S(2)}) collective-permute-start(bf16[832,128]{1,0:T(8,128)(2,1)S(1)} %rows_of.5), channel_id=1, source_target_pairs={{8,0},{24,8},{16,24},{0,16},{9,1},{25,9},{17,25},{1,17},{10,2},{26... | collective-permute-start | bytes 638984 | tf_op jit(solution)/shard_map/ppermute | solution.py:437
  64.2 2.8 %collective-permute-done.12.refs_3_ = bf16[1664,128]{1,0:T(8,128)(2,1)S(1)} collective-permute-done((bf16[1664,128]{1,0:T(8,128)(2,1)S(1)}, bf16[1664,128]{1,0:T(8,128)(2,1)S(1)}, u32[]{:S(2)}, u32[]{:S(2)}) %collective-permute-start.12) | collective-permute-done | bytes 426016 | tf_op jit(solution)/shard_map/ppermute | solution.py:413
  69.1 4.5 %early_images.5.early = f32[13440,128]{1,0:T(8,128)S(1)} custom-call(s32[8]{0:T(128)S(1)} %concatenate.3.refs_0_.bounds.edges_ref, s32[288]{0:T(512)S(1)} %pad.10.refs_1_.order, s32[288]{0:T(512)S(1)} %pad.11.refs_2_.rows, s32[288]{0:T(512)S(1)} %pad.12.refs_3_.cols, bf16[256,128,128]{2,1,0:T(8,128)(2,1)S(1)} %resident.1.values, ...), custom_call_target="tpu_custom_call" | custom-call | tf_op jit(solution)/shard_map/early_images/pallas_call | solution.py:132
  73.6 1.9 %last_images.5 = (f32[13440,128]{1,0:T(8,128)S(1)}, bf16[1664,128]{1,0:T(8,128)(2,1)S(1)}, bf16[1664,128]{1,0:T(8,128)(2,1)S(1)}, bf16[4992,128]{1,0:T(8,128)(2,1)S(1)}, bf16[4992,128]{1,0:T(8,128)(2,1)S(1)}) custom-call(s32[8]{0:T(128)S(1)} %concatenate.3.refs_0_.bounds.edges_ref, s32[288]{0:T(512)S(1)} %pad.10.refs_1_.order, ...), custom_call_target="tpu_custom_call", output_to_operand_aliasing={{0}: (5, {})} | custom-call | tf_op jit(solution)/shard_map/last_images/pallas_call | solution.py:168
  75.6 1.9 %collective-permute-done.15.refs_1_ = bf16[832,128]{1,0:T(8,128)(2,1)S(1)} collective-permute-done((bf16[832,128]{1,0:T(8,128)(2,1)S(1)}, bf16[832,128]{1,0:T(8,128)(2,1)S(1)}, u32[]{:S(2)}, u32[]{:S(2)}) %collective-permute-start.15) | collective-permute-done | bytes 213024 | tf_op jit(solution)/shard_map/ppermute | solution.py:422
  80.1 2.5 %collective-permute-start.18 = (bf16[1664,128]{1,0:T(8,128)(2,1)S(1)}, bf16[1664,128]{1,0:T(8,128)(2,1)S(1)}, u32[]{:S(2)}, u32[]{:S(2)}) collective-permute-start(bf16[1664,128]{1,0:T(8,128)(2,1)S(1)} %summed.10), channel_id=1, source_target_pairs={{0,6},{1,7},{2,4},{3,5},{4,2},{5,3},{6,0},{7,1},{8,14},{9,15},{10,... | collective-permute-start | bytes 1277960 | tf_op jit(solution)/shard_map/ppermute | solution.py:413
  85.5 6.2 %collective-permute-done.25.refs_3_.array_ref = bf16[1664,128]{1,0:T(8,128)(2,1)S(1)} collective-permute-done((bf16[1664,128]{1,0:T(8,128)(2,1)S(1)}, bf16[1664,128]{1,0:T(8,128)(2,1)S(1)}, u32[]{:S(2)}, u32[]{:S(2)}) %collective-permute-start.25) | collective-permute-done | bytes 426016 | tf_op jit(solution)/shard_map/ppermute | solution.py:423
  95.6 6.3 %collective-permute-done.19.refs_3_ = bf16[1664,128]{1,0:T(8,128)(2,1)S(1)} collective-permute-done((bf16[1664,128]{1,0:T(8,128)(2,1)S(1)}, bf16[1664,128]{1,0:T(8,128)(2,1)S(1)}, u32[]{:S(2)}, u32[]{:S(2)}) %collective-permute-start.19) | collective-permute-done | bytes 426016 | tf_op jit(solution)/shard_map/ppermute | solution.py:413
  104.0 4.5 %early_images.7.early = f32[13440,128]{1,0:T(8,128)S(1)} custom-call(s32[8]{0:T(128)S(1)} %concatenate.3.refs_0_.bounds.edges_ref, s32[288]{0:T(512)S(1)} %pad.10.refs_1_.order, s32[288]{0:T(512)S(1)} %pad.11.refs_2_.rows, s32[288]{0:T(512)S(1)} %pad.12.refs_3_.cols, bf16[256,128,128]{2,1,0:T(8,128)(2,1)S(1)} %resident.1.values, ...), custom_call_target="tpu_custom_call" | custom-call | tf_op jit(solution)/shard_map/early_images/pallas_call | solution.py:132
  108.5 1.9 %last_images.6 = (f32[13440,128]{1,0:T(8,128)S(1)}, bf16[1664,128]{1,0:T(8,128)(2,1)S(1)}, bf16[1664,128]{1,0:T(8,128)(2,1)S(1)}, bf16[4992,128]{1,0:T(8,128)(2,1)S(1)}, bf16[4992,128]{1,0:T(8,128)(2,1)S(1)}) custom-call(s32[8]{0:T(128)S(1)} %concatenate.3.refs_0_.bounds.edges_ref, s32[288]{0:T(512)S(1)} %pad.10.refs_1_.order, ...), custom_call_target="tpu_custom_call", output_to_operand_aliasing={{0}: (5, {})} | custom-call | tf_op jit(solution)/shard_map/last_images/pallas_call | solution.py:168
  114.0 2.4 %collective-permute-start.31 = (bf16[1664,128]{1,0:T(8,128)(2,1)S(1)}, bf16[1664,128]{1,0:T(8,128)(2,1)S(1)}, u32[]{:S(2)}, u32[]{:S(2)}) collective-permute-start(bf16[1664,128]{1,0:T(8,128)(2,1)S(1)} %summed.13), channel_id=1, source_target_pairs={{0,6},{1,7},{2,4},{3,5},{4,2},{5,3},{6,0},{7,1},{8,14},{9,15},{10,... | collective-permute-start | bytes 1277960 | tf_op jit(solution)/shard_map/ppermute | solution.py:413
  119.2 5.4 %collective-permute-done.23.refs_3_.array_ref = bf16[1664,128]{1,0:T(8,128)(2,1)S(1)} collective-permute-done((bf16[1664,128]{1,0:T(8,128)(2,1)S(1)}, bf16[1664,128]{1,0:T(8,128)(2,1)S(1)}, u32[]{:S(2)}, u32[]{:S(2)}) %collective-permute-start.23) | collective-permute-done | bytes 426016 | tf_op jit(solution)/shard_map/ppermute | solution.py:423
  124.6 2.1 %collective-permute-start.30 = (bf16[832,128]{1,0:T(8,128)(2,1)S(1)}, bf16[832,128]{1,0:T(8,128)(2,1)S(1)}, u32[]{:S(2)}, u32[]{:S(2)}) collective-permute-start(bf16[832,128]{1,0:T(8,128)(2,1)S(1)} %collective-permute-done.21.refs_1_), channel_id=1, source_target_pairs={{0,8},{8,24},{24,16},{16,0},{1,9},{9,25},{25,17},{17,1},{2,10},{10... | collective-permute-start | bytes 638984 | tf_op jit(solution)/shard_map/ppermute | solution.py:436
  126.7 3.5 %collective-permute-done.22.refs_2_ = bf16[832,128]{1,0:T(8,128)(2,1)S(1)} collective-permute-done((bf16[832,128]{1,0:T(8,128)(2,1)S(1)}, bf16[832,128]{1,0:T(8,128)(2,1)S(1)}, u32[]{:S(2)}, u32[]{:S(2)}) %collective-permute-start.22) | collective-permute-done | bytes 213024 | tf_op jit(solution)/shard_map/ppermute | solution.py:422
  131.3 4.5 %early_images.6.early = f32[13440,128]{1,0:T(8,128)S(1)} custom-call(s32[8]{0:T(128)S(1)} %concatenate.3.refs_0_.bounds.edges_ref, s32[288]{0:T(512)S(1)} %pad.10.refs_1_.order, s32[288]{0:T(512)S(1)} %pad.11.refs_2_.rows, s32[288]{0:T(512)S(1)} %pad.12.refs_3_.cols, bf16[256,128,128]{2,1,0:T(8,128)(2,1)S(1)} %resident.1.values, ...), custom_call_target="tpu_custom_call" | custom-call | tf_op jit(solution)/shard_map/early_images/pallas_call | solution.py:132
  137.3 2.0 %collective-permute-done.34.refs_1_ = bf16[832,128]{1,0:T(8,128)(2,1)S(1)} collective-permute-done((bf16[832,128]{1,0:T(8,128)(2,1)S(1)}, bf16[832,128]{1,0:T(8,128)(2,1)S(1)}, u32[]{:S(2)}, u32[]{:S(2)}) %collective-permute-start.34) | collective-permute-done | bytes 213024 | tf_op jit(solution)/shard_map/ppermute | solution.py:437
  139.2 1.9 %last_images.7 = (f32[13440,128]{1,0:T(8,128)S(1)}, bf16[1664,128]{1,0:T(8,128)(2,1)S(1)}, bf16[1664,128]{1,0:T(8,128)(2,1)S(1)}, bf16[4992,128]{1,0:T(8,128)(2,1)S(1)}, bf16[4992,128]{1,0:T(8,128)(2,1)S(1)}) custom-call(s32[8]{0:T(128)S(1)} %concatenate.3.refs_0_.bounds.edges_ref, s32[288]{0:T(512)S(1)} %pad.10.refs_1_.order, ...), custom_call_target="tpu_custom_call", output_to_operand_aliasing={{0}: (5, {})} | custom-call | tf_op jit(solution)/shard_map/last_images/pallas_call | solution.py:168
  143.6 2.1 %collective-permute-start.38 = (bf16[1664,128]{1,0:T(8,128)(2,1)S(1)}, bf16[1664,128]{1,0:T(8,128)(2,1)S(1)}, u32[]{:S(2)}, u32[]{:S(2)}) collective-permute-start(bf16[1664,128]{1,0:T(8,128)(2,1)S(1)} %summed.14), channel_id=1, source_target_pairs={{0,6},{1,7},{2,4},{3,5},{4,2},{5,3},{6,0},{7,1},{8,14},{9,15},{10,... | collective-permute-start | bytes 1277960 | tf_op jit(solution)/shard_map/ppermute | solution.py:413
  152.5 4.8 %collective-permute-done.38.refs_2_ = bf16[1664,128]{1,0:T(8,128)(2,1)S(1)} collective-permute-done((bf16[1664,128]{1,0:T(8,128)(2,1)S(1)}, bf16[1664,128]{1,0:T(8,128)(2,1)S(1)}, u32[]{:S(2)}, u32[]{:S(2)}) %collective-permute-start.38) | collective-permute-done | bytes 426016 | tf_op jit(solution)/shard_map/ppermute | solution.py:413
  157.3 8.3 %collective-permute-done.39.refs_3_ = bf16[1664,128]{1,0:T(8,128)(2,1)S(1)} collective-permute-done((bf16[1664,128]{1,0:T(8,128)(2,1)S(1)}, bf16[1664,128]{1,0:T(8,128)(2,1)S(1)}, u32[]{:S(2)}, u32[]{:S(2)}) %collective-permute-start.39) | collective-permute-done | bytes 426016 | tf_op jit(solution)/shard_map/ppermute | solution.py:413
  (109 shorter events, 50.2 us)
Async XLA Ops:
  1.3 24.8 %collective-permute-start.2 = (bf16[1664,128]{1,0:T(8,128)(2,1)S(1)}, bf16[1664,128]{1,0:T(8,128)(2,1)S(1)}, u32[]{:S(2)}, u32[]{:S(2)}) collective-permute-start(bf16[1664,128]{1,0:T(8,128)(2,1)S(1)} %columns_of.6.refs_0_), channel_id=1, source_target_pairs={{8,0},{24,8},{16,24},{0,16},{9,1},{25,9},{17,25},{1,17},{10,2},{26... | collective-permute-start | bytes 1277960 | tf_op jit(solution)/shard_map/ppermute | solution.py:423
  5.4 15.5 %collective-permute-start.1 = (bf16[832,128]{1,0:T(8,128)(2,1)S(1)}, bf16[832,128]{1,0:T(8,128)(2,1)S(1)}, u32[]{:S(2)}, u32[]{:S(2)}) collective-permute-start(bf16[832,128]{1,0:T(8,128)(2,1)S(1)} %columns_of.8), channel_id=1, source_target_pairs={{0,8},{8,24},{24,16},{16,0},{1,9},{9,25},{25,17},{17,1},{2,10},{10... | collective-permute-start | bytes 638984 | tf_op jit(solution)/shard_map/ppermute | solution.py:422
  5.6 19.8 %collective-permute-start = (bf16[832,128]{1,0:T(8,128)(2,1)S(1)}, bf16[832,128]{1,0:T(8,128)(2,1)S(1)}, u32[]{:S(2)}, u32[]{:S(2)}) collective-permute-start(bf16[832,128]{1,0:T(8,128)(2,1)S(1)} %columns_of.7), channel_id=1, source_target_pairs={{0,8},{8,24},{24,16},{16,0},{1,9},{9,25},{25,17},{17,1},{2,10},{10... | collective-permute-start | bytes 638984 | tf_op jit(solution)/shard_map/ppermute | solution.py:422
  25.4 12.3 %collective-permute-start.6 = (bf16[832,128]{1,0:T(8,128)(2,1)S(1)}, bf16[832,128]{1,0:T(8,128)(2,1)S(1)}, u32[]{:S(2)}, u32[]{:S(2)}) collective-permute-start(bf16[832,128]{1,0:T(8,128)(2,1)S(1)} %collective-permute-done.refs_1_), channel_id=1, source_target_pairs={{0,8},{8,24},{24,16},{16,0},{1,9},{9,25},{25,17},{17,1},{2,10},{10... | collective-permute-start | bytes 638984 | tf_op jit(solution)/shard_map/ppermute | solution.py:436
  26.1 12.3 %collective-permute-start.7 = (bf16[832,128]{1,0:T(8,128)(2,1)S(1)}, bf16[832,128]{1,0:T(8,128)(2,1)S(1)}, u32[]{:S(2)}, u32[]{:S(2)}) collective-permute-start(bf16[832,128]{1,0:T(8,128)(2,1)S(1)} %rows_of.4), channel_id=1, source_target_pairs={{8,0},{24,8},{16,24},{0,16},{9,1},{25,9},{17,25},{1,17},{10,2},{26... | collective-permute-start | bytes 638984 | tf_op jit(solution)/shard_map/ppermute | solution.py:437
  32.9 9.7 %collective-permute-start.3 = (bf16[832,128]{1,0:T(8,128)(2,1)S(1)}, bf16[832,128]{1,0:T(8,128)(2,1)S(1)}, u32[]{:S(2)}, u32[]{:S(2)}) collective-permute-start(bf16[832,128]{1,0:T(8,128)(2,1)S(1)} %columns_of.10), channel_id=1, source_target_pairs={{0,8},{8,24},{24,16},{16,0},{1,9},{9,25},{25,17},{17,1},{2,10},{10... | collective-permute-start | bytes 638984 | tf_op jit(solution)/shard_map/ppermute | solution.py:422
  44.5 12.2 %collective-permute-start.5 = (bf16[1664,128]{1,0:T(8,128)(2,1)S(1)}, bf16[1664,128]{1,0:T(8,128)(2,1)S(1)}, u32[]{:S(2)}, u32[]{:S(2)}) collective-permute-start(bf16[1664,128]{1,0:T(8,128)(2,1)S(1)} %columns_of.9.refs_0_), channel_id=1, source_target_pairs={{8,0},{24,8},{16,24},{0,16},{9,1},{25,9},{17,25},{1,17},{10,2},{26... | collective-permute-start | bytes 1277960 | tf_op jit(solution)/shard_map/ppermute | solution.py:423
  45.1 13.7 %collective-permute-start.11 = (bf16[1664,128]{1,0:T(8,128)(2,1)S(1)}, bf16[1664,128]{1,0:T(8,128)(2,1)S(1)}, u32[]{:S(2)}, u32[]{:S(2)}) collective-permute-start(bf16[1664,128]{1,0:T(8,128)(2,1)S(1)} %summed.9), channel_id=1, source_target_pairs={{0,6},{1,7},{2,4},{3,5},{4,2},{5,3},{6,0},{7,1},{8,14},{9,15},{10,... | collective-permute-start | bytes 1277960 | tf_op jit(solution)/shard_map/ppermute | solution.py:413
  47.8 19.2 %collective-permute-start.12 = (bf16[1664,128]{1,0:T(8,128)(2,1)S(1)}, bf16[1664,128]{1,0:T(8,128)(2,1)S(1)}, u32[]{:S(2)}, u32[]{:S(2)}) collective-permute-start(bf16[1664,128]{1,0:T(8,128)(2,1)S(1)} %get-tuple-element.65), channel_id=1, source_target_pairs={{0,4},{1,5},{2,6},{3,7},{4,0},{5,1},{6,2},{7,3},{8,12},{9,13},{10,... | collective-permute-start | bytes 1277960 | tf_op jit(solution)/shard_map/ppermute | solution.py:413
  49.2 17.9 %collective-permute-start.13 = (bf16[1664,128]{1,0:T(8,128)(2,1)S(1)}, bf16[1664,128]{1,0:T(8,128)(2,1)S(1)}, u32[]{:S(2)}, u32[]{:S(2)}) collective-permute-start(bf16[1664,128]{1,0:T(8,128)(2,1)S(1)} %get-tuple-element.66), channel_id=1, source_target_pairs={{0,2},{1,3},{2,0},{3,1},{4,6},{5,7},{6,4},{7,5},{8,10},{9,11},{10,... | collective-permute-start | bytes 1277960 | tf_op jit(solution)/shard_map/ppermute | solution.py:413
  52.0 17.2 %collective-permute-start.4 = (bf16[832,128]{1,0:T(8,128)(2,1)S(1)}, bf16[832,128]{1,0:T(8,128)(2,1)S(1)}, u32[]{:S(2)}, u32[]{:S(2)}) collective-permute-start(bf16[832,128]{1,0:T(8,128)(2,1)S(1)} %columns_of.11), channel_id=1, source_target_pairs={{0,8},{8,24},{24,16},{16,0},{1,9},{9,25},{25,17},{17,1},{2,10},{10... | collective-permute-start | bytes 638984 | tf_op jit(solution)/shard_map/ppermute | solution.py:422
  56.7 16.9 %collective-permute-start.10 = (bf16[832,128]{1,0:T(8,128)(2,1)S(1)}, bf16[832,128]{1,0:T(8,128)(2,1)S(1)}, u32[]{:S(2)}, u32[]{:S(2)}) collective-permute-start(bf16[832,128]{1,0:T(8,128)(2,1)S(1)} %collective-permute-done.3.refs_1_), channel_id=1, source_target_pairs={{0,8},{8,24},{24,16},{16,0},{1,9},{9,25},{25,17},{17,1},{2,10},{10... | collective-permute-start | bytes 638984 | tf_op jit(solution)/shard_map/ppermute | solution.py:436
  58.7 14.9 %collective-permute-start.14 = (bf16[832,128]{1,0:T(8,128)(2,1)S(1)}, bf16[832,128]{1,0:T(8,128)(2,1)S(1)}, u32[]{:S(2)}, u32[]{:S(2)}) collective-permute-start(bf16[832,128]{1,0:T(8,128)(2,1)S(1)} %rows_of.5), channel_id=1, source_target_pairs={{8,0},{24,8},{16,24},{0,16},{9,1},{25,9},{17,25},{1,17},{10,2},{26... | collective-permute-start | bytes 638984 | tf_op jit(solution)/shard_map/ppermute | solution.py:437
  67.4 10.0 %collective-permute-start.15 = (bf16[832,128]{1,0:T(8,128)(2,1)S(1)}, bf16[832,128]{1,0:T(8,128)(2,1)S(1)}, u32[]{:S(2)}, u32[]{:S(2)}) collective-permute-start(bf16[832,128]{1,0:T(8,128)(2,1)S(1)} %get-tuple-element.70), channel_id=1, source_target_pairs={{0,8},{8,24},{24,16},{16,0},{1,9},{9,25},{25,17},{17,1},{2,10},{10... | collective-permute-start | bytes 638984 | tf_op jit(solution)/shard_map/ppermute | solution.py:422
  79.4 12.3 %collective-permute-start.25 = (bf16[1664,128]{1,0:T(8,128)(2,1)S(1)}, bf16[1664,128]{1,0:T(8,128)(2,1)S(1)}, u32[]{:S(2)}, u32[]{:S(2)}) collective-permute-start(bf16[1664,128]{1,0:T(8,128)(2,1)S(1)} %get-tuple-element.69.refs_0_.refs_5_), channel_id=1, source_target_pairs={{8,0},{24,8},{16,24},{0,16},{9,1},{25,9},{17,25},{1,17},{10,2},{26... | collective-permute-start | bytes 1277960 | tf_op jit(solution)/shard_map/ppermute | solution.py:423
  80.1 13.7 %collective-permute-start.18 = (bf16[1664,128]{1,0:T(8,128)(2,1)S(1)}, bf16[1664,128]{1,0:T(8,128)(2,1)S(1)}, u32[]{:S(2)}, u32[]{:S(2)}) collective-permute-start(bf16[1664,128]{1,0:T(8,128)(2,1)S(1)} %summed.10), channel_id=1, source_target_pairs={{0,6},{1,7},{2,4},{3,5},{4,2},{5,3},{6,0},{7,1},{8,14},{9,15},{10,... | collective-permute-start | bytes 1277960 | tf_op jit(solution)/shard_map/ppermute | solution.py:413
  82.8 19.2 %collective-permute-start.19 = (bf16[1664,128]{1,0:T(8,128)(2,1)S(1)}, bf16[1664,128]{1,0:T(8,128)(2,1)S(1)}, u32[]{:S(2)}, u32[]{:S(2)}) collective-permute-start(bf16[1664,128]{1,0:T(8,128)(2,1)S(1)} %get-tuple-element.80), channel_id=1, source_target_pairs={{0,4},{1,5},{2,6},{3,7},{4,0},{5,1},{6,2},{7,3},{8,12},{9,13},{10,... | collective-permute-start | bytes 1277960 | tf_op jit(solution)/shard_map/ppermute | solution.py:413
  84.0 18.0 %collective-permute-start.20 = (bf16[1664,128]{1,0:T(8,128)(2,1)S(1)}, bf16[1664,128]{1,0:T(8,128)(2,1)S(1)}, u32[]{:S(2)}, u32[]{:S(2)}) collective-permute-start(bf16[1664,128]{1,0:T(8,128)(2,1)S(1)} %get-tuple-element.81), channel_id=1, source_target_pairs={{0,2},{1,3},{2,0},{3,1},{4,6},{5,7},{6,4},{7,5},{8,10},{9,11},{10,... | collective-permute-start | bytes 1277960 | tf_op jit(solution)/shard_map/ppermute | solution.py:413
  85.5 18.5 %collective-permute-start.24 = (bf16[832,128]{1,0:T(8,128)(2,1)S(1)}, bf16[832,128]{1,0:T(8,128)(2,1)S(1)}, u32[]{:S(2)}, u32[]{:S(2)}) collective-permute-start(bf16[832,128]{1,0:T(8,128)(2,1)S(1)} %get-tuple-element.71), channel_id=1, source_target_pairs={{0,8},{8,24},{24,16},{16,0},{1,9},{9,25},{25,17},{17,1},{2,10},{10... | collective-permute-start | bytes 638984 | tf_op jit(solution)/shard_map/ppermute | solution.py:422
  91.7 16.8 %collective-permute-start.26 = (bf16[832,128]{1,0:T(8,128)(2,1)S(1)}, bf16[832,128]{1,0:T(8,128)(2,1)S(1)}, u32[]{:S(2)}, u32[]{:S(2)}) collective-permute-start(bf16[832,128]{1,0:T(8,128)(2,1)S(1)} %collective-permute-done.15.refs_1_), channel_id=1, source_target_pairs={{0,8},{8,24},{24,16},{16,0},{1,9},{9,25},{25,17},{17,1},{2,10},{10... | collective-permute-start | bytes 638984 | tf_op jit(solution)/shard_map/ppermute | solution.py:436
  93.7 14.7 %collective-permute-start.27 = (bf16[832,128]{1,0:T(8,128)(2,1)S(1)}, bf16[832,128]{1,0:T(8,128)(2,1)S(1)}, u32[]{:S(2)}, u32[]{:S(2)}) collective-permute-start(bf16[832,128]{1,0:T(8,128)(2,1)S(1)} %rows_of.6), channel_id=1, source_target_pairs={{8,0},{24,8},{16,24},{0,16},{9,1},{25,9},{17,25},{1,17},{10,2},{26... | collective-permute-start | bytes 638984 | tf_op jit(solution)/shard_map/ppermute | solution.py:437
  102.4 8.0 %collective-permute-start.21 = (bf16[832,128]{1,0:T(8,128)(2,1)S(1)}, bf16[832,128]{1,0:T(8,128)(2,1)S(1)}, u32[]{:S(2)}, u32[]{:S(2)}) collective-permute-start(bf16[832,128]{1,0:T(8,128)(2,1)S(1)} %get-tuple-element.83), channel_id=1, source_target_pairs={{0,8},{8,24},{24,16},{16,0},{1,9},{9,25},{25,17},{17,1},{2,10},{10... | collective-permute-start | bytes 638984 | tf_op jit(solution)/shard_map/ppermute | solution.py:422
  112.4 12.2 %collective-permute-start.23 = (bf16[1664,128]{1,0:T(8,128)(2,1)S(1)}, bf16[1664,128]{1,0:T(8,128)(2,1)S(1)}, u32[]{:S(2)}, u32[]{:S(2)}) collective-permute-start(bf16[1664,128]{1,0:T(8,128)(2,1)S(1)} %get-tuple-element.82.refs_0_.refs_5_), channel_id=1, source_target_pairs={{8,0},{24,8},{16,24},{0,16},{9,1},{25,9},{17,25},{1,17},{10,2},{26... | collective-permute-start | bytes 1277960 | tf_op jit(solution)/shard_map/ppermute | solution.py:423
  114.0 21.8 %collective-permute-start.31 = (bf16[1664,128]{1,0:T(8,128)(2,1)S(1)}, bf16[1664,128]{1,0:T(8,128)(2,1)S(1)}, u32[]{:S(2)}, u32[]{:S(2)}) collective-permute-start(bf16[1664,128]{1,0:T(8,128)(2,1)S(1)} %summed.13), channel_id=1, source_target_pairs={{0,6},{1,7},{2,4},{3,5},{4,2},{5,3},{6,0},{7,1},{8,14},{9,15},{10,... | collective-permute-start | bytes 1277960 | tf_op jit(solution)/shard_map/ppermute | solution.py:413
  116.6 19.2 %collective-permute-start.32 = (bf16[1664,128]{1,0:T(8,128)(2,1)S(1)}, bf16[1664,128]{1,0:T(8,128)(2,1)S(1)}, u32[]{:S(2)}, u32[]{:S(2)}) collective-permute-start(bf16[1664,128]{1,0:T(8,128)(2,1)S(1)} %get-tuple-element.93), channel_id=1, source_target_pairs={{0,4},{1,5},{2,6},{3,7},{4,0},{5,1},{6,2},{7,3},{8,12},{9,13},{10,... | collective-permute-start | bytes 1277960 | tf_op jit(solution)/shard_map/ppermute | solution.py:413
  117.2 18.6 %collective-permute-start.33 = (bf16[1664,128]{1,0:T(8,128)(2,1)S(1)}, bf16[1664,128]{1,0:T(8,128)(2,1)S(1)}, u32[]{:S(2)}, u32[]{:S(2)}) collective-permute-start(bf16[1664,128]{1,0:T(8,128)(2,1)S(1)} %get-tuple-element.94), channel_id=1, source_target_pairs={{0,2},{1,3},{2,0},{3,1},{4,6},{5,7},{6,4},{7,5},{8,10},{9,11},{10,... | collective-permute-start | bytes 1277960 | tf_op jit(solution)/shard_map/ppermute | solution.py:413
  118.5 11.7 %collective-permute-start.22 = (bf16[832,128]{1,0:T(8,128)(2,1)S(1)}, bf16[832,128]{1,0:T(8,128)(2,1)S(1)}, u32[]{:S(2)}, u32[]{:S(2)}) collective-permute-start(bf16[832,128]{1,0:T(8,128)(2,1)S(1)} %get-tuple-element.84), channel_id=1, source_target_pairs={{0,8},{8,24},{24,16},{16,0},{1,9},{9,25},{25,17},{17,1},{2,10},{10... | collective-permute-start | bytes 638984 | tf_op jit(solution)/shard_map/ppermute | solution.py:422
  124.6 12.7 %collective-permute-start.30 = (bf16[832,128]{1,0:T(8,128)(2,1)S(1)}, bf16[832,128]{1,0:T(8,128)(2,1)S(1)}, u32[]{:S(2)}, u32[]{:S(2)}) collective-permute-start(bf16[832,128]{1,0:T(8,128)(2,1)S(1)} %collective-permute-done.21.refs_1_), channel_id=1, source_target_pairs={{0,8},{8,24},{24,16},{16,0},{1,9},{9,25},{25,17},{17,1},{2,10},{10... | collective-permute-start | bytes 638984 | tf_op jit(solution)/shard_map/ppermute | solution.py:436
  130.2 9.0 %collective-permute-start.34 = (bf16[832,128]{1,0:T(8,128)(2,1)S(1)}, bf16[832,128]{1,0:T(8,128)(2,1)S(1)}, u32[]{:S(2)}, u32[]{:S(2)}) collective-permute-start(bf16[832,128]{1,0:T(8,128)(2,1)S(1)} %rows_of.7), channel_id=1, source_target_pairs={{8,0},{24,8},{16,24},{0,16},{9,1},{25,9},{17,25},{1,17},{10,2},{26... | collective-permute-start | bytes 638984 | tf_op jit(solution)/shard_map/ppermute | solution.py:437
  143.6 13.7 %collective-permute-start.38 = (bf16[1664,128]{1,0:T(8,128)(2,1)S(1)}, bf16[1664,128]{1,0:T(8,128)(2,1)S(1)}, u32[]{:S(2)}, u32[]{:S(2)}) collective-permute-start(bf16[1664,128]{1,0:T(8,128)(2,1)S(1)} %summed.14), channel_id=1, source_target_pairs={{0,6},{1,7},{2,4},{3,5},{4,2},{5,3},{6,0},{7,1},{8,14},{9,15},{10,... | collective-permute-start | bytes 1277960 | tf_op jit(solution)/shard_map/ppermute | solution.py:413
  146.4 19.2 %collective-permute-start.39 = (bf16[1664,128]{1,0:T(8,128)(2,1)S(1)}, bf16[1664,128]{1,0:T(8,128)(2,1)S(1)}, u32[]{:S(2)}, u32[]{:S(2)}) collective-permute-start(bf16[1664,128]{1,0:T(8,128)(2,1)S(1)} %get-tuple-element.107), channel_id=1, source_target_pairs={{0,4},{1,5},{2,6},{3,7},{4,0},{5,1},{6,2},{7,3},{8,12},{9,13},{10,... | collective-permute-start | bytes 1277960 | tf_op jit(solution)/shard_map/ppermute | solution.py:413
  147.7 17.9 %collective-permute-start.40 = (bf16[1664,128]{1,0:T(8,128)(2,1)S(1)}, bf16[1664,128]{1,0:T(8,128)(2,1)S(1)}, u32[]{:S(2)}, u32[]{:S(2)}) collective-permute-start(bf16[1664,128]{1,0:T(8,128)(2,1)S(1)} %get-tuple-element.108), channel_id=1, source_target_pairs={{0,2},{1,3},{2,0},{3,1},{4,6},{5,7},{6,4},{7,5},{8,10},{9,11},{10,... | collective-permute-start | bytes 1277960 | tf_op jit(solution)/shard_map/ppermute | solution.py:413
  (16 other events, 53.4 us)

commit v5 on v4

--- a/solution.py
+++ b/solution.py
@@ -269,7 +269,7 @@
     return pl.pallas_call(
         kernel,
         out_shape=[
-            jax.ShapeDtypeStruct((rows, width), jnp.bfloat16),
+            pltpu.VMEM((rows, width), jnp.bfloat16),
             jax.ShapeDtypeStruct((edge_size, width), jnp.bfloat16),
         ],
         in_specs=[SMEM] * 3 + [VMEM] * (1 + len(flat) + len(firsts)),
@@ -441,6 +441,29 @@
                 self.early.append(lax.ppermute(self.early[-1], "row", route))
             self.last = [self.early.pop()]
 
+    def crossed_terms(pairs):
+        (kept, partner), (others, partners) = pairs
+        rest = own_rows - top
+        y, x, mine = 0, own_rows, 2 * own_rows
+
+        def both(low, *more):
+            return [(others, low), (partners, low), *more]
+
+        corner = summed(
+            [[(top, [(kept, 0), (partner, 0)])], [(rest, [(kept, top), (partner, top)])]]
+        )
+        by_x, by_y = to_chip(corner[0], 1), to_chip(corner[1], 2)
+        sides = summed([[(top, both(x))], [(rest, both(y + top))]])
+        x_top, y_rest = to_chip(sides[0], 1), to_chip(sides[1], 2)
+        joined = summed(
+            [[(rest, both(x + top, (by_y, 0)))], [(top, both(y, (by_x, 0)))]]
+        )
+        x_rest, y_top = to_chip(joined[0], 1), to_chip(joined[1], 2)
+        return [
+            (top, both(mine, (x_top, 0), (y_top, 0))),
+            (rest, both(mine + top, (x_rest, 0), (y_rest, 0))),
+        ]
+
     def image_terms(gather, following, tokens):
         counts = (1, chip_count - 1) if chip_count > 1 else (1,)
         early = gather.images
@@ -453,6 +476,8 @@
             elif following is not None and both_ways:
                 sent = tied(sent, following.early[1:2])
             pairs.append((kept, to_core(sent)))
+        if following is None and chip_count == 4:
+            return crossed_terms(pairs)
         terms, arrived, chip = [], [], chip_count - 1
         for count, (kept, partner) in zip(counts, pairs):
             places = [[(kept, i * own_rows), (partner, i * own_rows)] for i in range(count)]
@@ -497,10 +522,10 @@
         tokens = seconds[-1:] if turn else firsts[-1]
         terms = image_terms(gathers[count + turn], following, tokens)
         if relaid is not None:
-            ((size, ((array, row), *more)),) = terms
-            terms = [(size, [(tied(array, [relaid]), row), *more])]
+            (size, ((array, row), *more)), *others = terms
+            terms = [(size, [(tied(array, [relaid]), row), *more]), *others]
         second, edge = second_update(
-            terms, firsts[turn][:1], start_vectors, lows[turn], center, half_width, tables, edge_size
+            terms, firsts[turn][len(terms) - 1 :][: len(terms)], start_vectors, lows[turn], center, half_width, tables, edge_size
         )
         seconds.append(second)
         shape = (capacity * orbitals, vec_count)

time: 171 us -> 169 us (0.988)
  waiting for transfers between devices: 74.6 us -> 71.4 us
    ppermute x12 -> x15, waiting for transfers between devices: 24.1 us -> 21.5 us  [to_chip(): lax.ppermute(array, 'col', [(i, i ^ 2 * chip) for i in range(col_count)])]
    pallas_call x4, Pallas kernels: 7.7 us -> 9.64 us  [last_images(): pl.pallas_call(kernel, out_shape=[pltpu.VMEM(early.shape, jnp.float32), *...]
    pallas_call x4, Pallas kernels: 17.9 us -> 16 us  [early_images(): pl.pallas_call(kernel, out_shape=pltpu.VMEM(total, jnp.float32), in_specs...]
    ppermute x12 -> x15, starting transfers between devices: 20 us -> 21.7 us  [to_chip(): lax.ppermute(array, 'col', [(i, i ^ 2 * chip) for i in range(col_count)])]
  transfers between devices with their start and end apart: 42 -> 45, of which waited for: 28 -> 30; matrix products, arithmetic and copies ran while one was open for 1% -> 1% of each run, Pallas kernels for 17% -> 17%
where the time goes in v5:
time: 169 us
  waiting for transfers between devices  71.4 us (42%)
  starting transfers between devices  52.3 us (31%)
  Pallas kernels  34.8 us (21%)
  local copies, waits for them, and re-layouts  5.81 us (3%)
  between operations  3.2 us (2%)
    ppermute x15, starting transfers between devices, to_chip(): lax.ppermute(array, 'col', [(i, i ^ 2 * chip) for i in range(col_count)])  21.7 us
    ppermute x15, waiting for transfers between devices, to_chip(): lax.ppermute(array, 'col', [(i, i ^ 2 * chip) for i in range(col_count)])  21.5 us
    ppermute x8, waiting for transfers between devices, __init__(): upper, lower = (lax.ppermute(half, 'row', route) for half in (upper, lower))  16.7 us
    ppermute x4, waiting for transfers between devices, __init__(): self.early = [part, upper, lower, lax.ppermute(part, 'row', back_route)]  16.2 us
    pallas_call x4, Pallas kernels, early_images(): pl.pallas_call(kernel, out_shape=pltpu.VMEM(total, jnp.float32), in_specs...  16 us
    ppermute x4, starting transfers between devices, send_last(): lax.ppermute(lower, 'row', back_route)  10.6 us
    ppermute x10, waiting for transfers between devices, to_core(): return lax.ppermute(array, 'col', other_core)  9.85 us
    pallas_call x4, Pallas kernels, last_images(): pl.pallas_call(kernel, out_shape=[pltpu.VMEM(early.shape, jnp.float32), *...  9.64 us
  transfers between devices with their start and end apart: 45, of which 30 were waited for; matrix products, arithmetic and copies ran while one was open for 1% of the time, Pallas kernels for 17%

profile of v5, /device:TPU:0, one launch (start us, length us, event | category | flops | bytes accessed | tf_op | source)
XLA Modules:
  0.0 168.7 jit_solution(3419003175458105352)
XLA Ops:
  1.3 4.1 %collective-permute-start.2 = (bf16[1664,128]{1,0:T(8,128)(2,1)S(1)}, bf16[1664,128]{1,0:T(8,128)(2,1)S(1)}, u32[]{:S(2)}, u32[]{:S(2)}) collective-permute-start(bf16[1664,128]{1,0:T(8,128)(2,1)S(1)} %columns_of.6.refs_0_), channel_id=1, source_target_pairs={{8,0},{24,8},{16,24},{0,16},{9,1},{25,9},{17,25},{1,17},{10,2},{26... | collective-permute-start | bytes 1277960 | tf_op jit(solution)/shard_map/ppermute | solution.py:423
  5.6 2.6 %collective-permute-start = (bf16[832,128]{1,0:T(8,128)(2,1)S(1)}, bf16[832,128]{1,0:T(8,128)(2,1)S(1)}, u32[]{:S(2)}, u32[]{:S(2)}) collective-permute-start(bf16[832,128]{1,0:T(8,128)(2,1)S(1)} %columns_of.7), channel_id=1, source_target_pairs={{0,8},{8,24},{24,16},{16,0},{1,9},{9,25},{25,17},{17,1},{2,10},{10... | collective-permute-start | bytes 638984 | tf_op jit(solution)/shard_map/ppermute | solution.py:422
  12.0 3.4 %copy-done.2 = bf16[1,1,256,128,128]{4,3,2,1,0:T(8,128)(2,1)S(1)} copy-done((bf16[1,1,256,128,128]{4,3,2,1,0:T(8,128)(2,1)S(1)}, bf16[1,1,256,128,128]{4,3,2,1,0:T(8,128)(2,1)}, u32[]{:S(2)}) %copy-start.2) | copy-done | bytes 8388632
  15.9 5.0 %collective-permute-done.1.refs_2_ = bf16[832,128]{1,0:T(8,128)(2,1)S(1)} collective-permute-done((bf16[832,128]{1,0:T(8,128)(2,1)S(1)}, bf16[832,128]{1,0:T(8,128)(2,1)S(1)}, u32[]{:S(2)}, u32[]{:S(2)}) %collective-permute-start.1) | collective-permute-done | bytes 213024 | tf_op jit(solution)/shard_map/ppermute | solution.py:422
  20.9 4.5 %collective-permute-done.refs_1_ = bf16[832,128]{1,0:T(8,128)(2,1)S(1)} collective-permute-done((bf16[832,128]{1,0:T(8,128)(2,1)S(1)}, bf16[832,128]{1,0:T(8,128)(2,1)S(1)}, u32[]{:S(2)}, u32[]{:S(2)}) %collective-permute-start) | collective-permute-done | bytes 213024 | tf_op jit(solution)/shard_map/ppermute | solution.py:422
  26.1 2.3 %collective-permute-start.7 = (bf16[832,128]{1,0:T(8,128)(2,1)S(1)}, bf16[832,128]{1,0:T(8,128)(2,1)S(1)}, u32[]{:S(2)}, u32[]{:S(2)}) collective-permute-start(bf16[832,128]{1,0:T(8,128)(2,1)S(1)} %rows_of.4), channel_id=1, source_target_pairs={{8,0},{24,8},{16,24},{0,16},{9,1},{25,9},{17,25},{1,17},{10,2},{26... | collective-permute-start | bytes 638984 | tf_op jit(solution)/shard_map/ppermute | solution.py:437
  28.4 4.0 %early_images.4.refs_0_.early = f32[13440,128]{1,0:T(8,128)S(1)} custom-call(s32[8]{0:T(128)S(1)} %concatenate.3.refs_0_.bounds.edges_ref, s32[288]{0:T(512)S(1)} %pad.10.refs_1_.order, s32[288]{0:T(512)S(1)} %pad.11.refs_2_.rows, s32[288]{0:T(512)S(1)} %pad.12.refs_3_.cols, bf16[256,128,128]{2,1,0:T(8,128)(2,1)S(1)} %resident.1.values, ...), custom_call_target="tpu_custom_call" | custom-call | tf_op jit(solution)/shard_map/early_images/pallas_call | solution.py:132
  33.3 4.4 %collective-permute-done.6.refs_0_ = bf16[832,128]{1,0:T(8,128)(2,1)S(1)} collective-permute-done((bf16[832,128]{1,0:T(8,128)(2,1)S(1)}, bf16[832,128]{1,0:T(8,128)(2,1)S(1)}, u32[]{:S(2)}, u32[]{:S(2)}) %collective-permute-start.6) | collective-permute-done | bytes 213024 | tf_op jit(solution)/shard_map/ppermute | solution.py:436
  38.4 2.4 %last_images.4 = (f32[13440,128]{1,0:T(8,128)S(1)}, bf16[1664,128]{1,0:T(8,128)(2,1)S(1)}, bf16[1664,128]{1,0:T(8,128)(2,1)S(1)}, bf16[4992,128]{1,0:T(8,128)(2,1)S(1)}, bf16[4992,128]{1,0:T(8,128)(2,1)S(1)}) custom-call(s32[8]{0:T(128)S(1)} %concatenate.3.refs_0_.bounds.edges_ref, s32[288]{0:T(512)S(1)} %pad.10.refs_1_.order, ...), custom_call_target="tpu_custom_call", output_to_operand_aliasing={{0}: (5, {})} | custom-call | tf_op jit(solution)/shard_map/last_images/pallas_call | solution.py:168
  40.8 1.8 %collective-permute-done.3.refs_1_ = bf16[832,128]{1,0:T(8,128)(2,1)S(1)} collective-permute-done((bf16[832,128]{1,0:T(8,128)(2,1)S(1)}, bf16[832,128]{1,0:T(8,128)(2,1)S(1)}, u32[]{:S(2)}, u32[]{:S(2)}) %collective-permute-start.3) | collective-permute-done | bytes 213024 | tf_op jit(solution)/shard_map/ppermute | solution.py:422
  45.1 2.5 %collective-permute-start.11 = (bf16[1664,128]{1,0:T(8,128)(2,1)S(1)}, bf16[1664,128]{1,0:T(8,128)(2,1)S(1)}, u32[]{:S(2)}, u32[]{:S(2)}) collective-permute-start(bf16[1664,128]{1,0:T(8,128)(2,1)S(1)} %summed.10), channel_id=1, source_target_pairs={{0,6},{1,7},{2,4},{3,5},{4,2},{5,3},{6,0},{7,1},{8,14},{9,15},{10,... | collective-permute-start | bytes 1277960 | tf_op jit(solution)/shard_map/ppermute | solution.py:413
  52.0 4.7 %collective-permute-done.5.refs_3_.array_ref = bf16[1664,128]{1,0:T(8,128)(2,1)S(1)} collective-permute-done((bf16[1664,128]{1,0:T(8,128)(2,1)S(1)}, bf16[1664,128]{1,0:T(8,128)(2,1)S(1)}, u32[]{:S(2)}, u32[]{:S(2)}) %collective-permute-start.5) | collective-permute-done | bytes 426016 | tf_op jit(solution)/shard_map/ppermute | solution.py:423
  58.7 5.4 %collective-permute-start.14 = (bf16[832,128]{1,0:T(8,128)(2,1)S(1)}, bf16[832,128]{1,0:T(8,128)(2,1)S(1)}, u32[]{:S(2)}, u32[]{:S(2)}) collective-permute-start(bf16[832,128]{1,0:T(8,128)(2,1)S(1)} %rows_of.5), channel_id=1, source_target_pairs={{8,0},{24,8},{16,24},{0,16},{9,1},{25,9},{17,25},{1,17},{10,2},{26... | collective-permute-start | bytes 638984 | tf_op jit(solution)/shard_map/ppermute | solution.py:437
  64.2 2.8 %collective-permute-done.12.refs_3_ = bf16[1664,128]{1,0:T(8,128)(2,1)S(1)} collective-permute-done((bf16[1664,128]{1,0:T(8,128)(2,1)S(1)}, bf16[1664,128]{1,0:T(8,128)(2,1)S(1)}, u32[]{:S(2)}, u32[]{:S(2)}) %collective-permute-start.12) | collective-permute-done | bytes 426016 | tf_op jit(solution)/shard_map/ppermute | solution.py:413
  69.1 4.0 %early_images.5.early = f32[13440,128]{1,0:T(8,128)S(1)} custom-call(s32[8]{0:T(128)S(1)} %concatenate.3.refs_0_.bounds.edges_ref, s32[288]{0:T(512)S(1)} %pad.10.refs_1_.order, s32[288]{0:T(512)S(1)} %pad.11.refs_2_.rows, s32[288]{0:T(512)S(1)} %pad.12.refs_3_.cols, bf16[256,128,128]{2,1,0:T(8,128)(2,1)S(1)} %resident.1.values, ...), custom_call_target="tpu_custom_call" | custom-call | tf_op jit(solution)/shard_map/early_images/pallas_call | solution.py:132
  73.2 2.4 %last_images.5 = (f32[13440,128]{1,0:T(8,128)S(1)}, bf16[1664,128]{1,0:T(8,128)(2,1)S(1)}, bf16[1664,128]{1,0:T(8,128)(2,1)S(1)}, bf16[4992,128]{1,0:T(8,128)(2,1)S(1)}, bf16[4992,128]{1,0:T(8,128)(2,1)S(1)}) custom-call(s32[8]{0:T(128)S(1)} %concatenate.3.refs_0_.bounds.edges_ref, s32[288]{0:T(512)S(1)} %pad.10.refs_1_.order, ...), custom_call_target="tpu_custom_call", output_to_operand_aliasing={{0}: (5, {})} | custom-call | tf_op jit(solution)/shard_map/last_images/pallas_call | solution.py:168
  75.6 1.9 %collective-permute-done.15.refs_1_ = bf16[832,128]{1,0:T(8,128)(2,1)S(1)} collective-permute-done((bf16[832,128]{1,0:T(8,128)(2,1)S(1)}, bf16[832,128]{1,0:T(8,128)(2,1)S(1)}, u32[]{:S(2)}, u32[]{:S(2)}) %collective-permute-start.15) | collective-permute-done | bytes 213024 | tf_op jit(solution)/shard_map/ppermute | solution.py:422
  80.1 2.5 %collective-permute-start.18 = (bf16[1664,128]{1,0:T(8,128)(2,1)S(1)}, bf16[1664,128]{1,0:T(8,128)(2,1)S(1)}, u32[]{:S(2)}, u32[]{:S(2)}) collective-permute-start(bf16[1664,128]{1,0:T(8,128)(2,1)S(1)} %summed.11), channel_id=1, source_target_pairs={{0,6},{1,7},{2,4},{3,5},{4,2},{5,3},{6,0},{7,1},{8,14},{9,15},{10,... | collective-permute-start | bytes 1277960 | tf_op jit(solution)/shard_map/ppermute | solution.py:413
  85.5 6.2 %collective-permute-done.25.refs_3_.array_ref = bf16[1664,128]{1,0:T(8,128)(2,1)S(1)} collective-permute-done((bf16[1664,128]{1,0:T(8,128)(2,1)S(1)}, bf16[1664,128]{1,0:T(8,128)(2,1)S(1)}, u32[]{:S(2)}, u32[]{:S(2)}) %collective-permute-start.25) | collective-permute-done | bytes 426016 | tf_op jit(solution)/shard_map/ppermute | solution.py:423
  93.7 1.9 %collective-permute-start.27 = (bf16[832,128]{1,0:T(8,128)(2,1)S(1)}, bf16[832,128]{1,0:T(8,128)(2,1)S(1)}, u32[]{:S(2)}, u32[]{:S(2)}) collective-permute-start(bf16[832,128]{1,0:T(8,128)(2,1)S(1)} %rows_of.6), channel_id=1, source_target_pairs={{8,0},{24,8},{16,24},{0,16},{9,1},{25,9},{17,25},{1,17},{10,2},{26... | collective-permute-start | bytes 638984 | tf_op jit(solution)/shard_map/ppermute | solution.py:437
  95.6 6.3 %collective-permute-done.19.refs_3_ = bf16[1664,128]{1,0:T(8,128)(2,1)S(1)} collective-permute-done((bf16[1664,128]{1,0:T(8,128)(2,1)S(1)}, bf16[1664,128]{1,0:T(8,128)(2,1)S(1)}, u32[]{:S(2)}, u32[]{:S(2)}) %collective-permute-start.19) | collective-permute-done | bytes 426016 | tf_op jit(solution)/shard_map/ppermute | solution.py:413
  104.0 4.0 %early_images.7.early = f32[13440,128]{1,0:T(8,128)S(1)} custom-call(s32[8]{0:T(128)S(1)} %concatenate.3.refs_0_.bounds.edges_ref, s32[288]{0:T(512)S(1)} %pad.10.refs_1_.order, s32[288]{0:T(512)S(1)} %pad.11.refs_2_.rows, s32[288]{0:T(512)S(1)} %pad.12.refs_3_.cols, bf16[256,128,128]{2,1,0:T(8,128)(2,1)S(1)} %resident.1.values, ...), custom_call_target="tpu_custom_call" | custom-call | tf_op jit(solution)/shard_map/early_images/pallas_call | solution.py:132
  108.0 2.4 %last_images.6 = (f32[13440,128]{1,0:T(8,128)S(1)}, bf16[1664,128]{1,0:T(8,128)(2,1)S(1)}, bf16[1664,128]{1,0:T(8,128)(2,1)S(1)}, bf16[4992,128]{1,0:T(8,128)(2,1)S(1)}, bf16[4992,128]{1,0:T(8,128)(2,1)S(1)}) custom-call(s32[8]{0:T(128)S(1)} %concatenate.3.refs_0_.bounds.edges_ref, s32[288]{0:T(512)S(1)} %pad.10.refs_1_.order, ...), custom_call_target="tpu_custom_call", output_to_operand_aliasing={{0}: (5, {})} | custom-call | tf_op jit(solution)/shard_map/last_images/pallas_call | solution.py:168
  114.0 2.4 %collective-permute-start.31 = (bf16[1664,128]{1,0:T(8,128)(2,1)S(1)}, bf16[1664,128]{1,0:T(8,128)(2,1)S(1)}, u32[]{:S(2)}, u32[]{:S(2)}) collective-permute-start(bf16[1664,128]{1,0:T(8,128)(2,1)S(1)} %summed.14), channel_id=1, source_target_pairs={{0,6},{1,7},{2,4},{3,5},{4,2},{5,3},{6,0},{7,1},{8,14},{9,15},{10,... | collective-permute-start | bytes 1277960 | tf_op jit(solution)/shard_map/ppermute | solution.py:413
  119.2 5.4 %collective-permute-done.23.refs_3_.array_ref = bf16[1664,128]{1,0:T(8,128)(2,1)S(1)} collective-permute-done((bf16[1664,128]{1,0:T(8,128)(2,1)S(1)}, bf16[1664,128]{1,0:T(8,128)(2,1)S(1)}, u32[]{:S(2)}, u32[]{:S(2)}) %collective-permute-start.23) | collective-permute-done | bytes 426016 | tf_op jit(solution)/shard_map/ppermute | solution.py:423
  124.6 2.2 %collective-permute-start.30 = (bf16[832,128]{1,0:T(8,128)(2,1)S(1)}, bf16[832,128]{1,0:T(8,128)(2,1)S(1)}, u32[]{:S(2)}, u32[]{:S(2)}) collective-permute-start(bf16[832,128]{1,0:T(8,128)(2,1)S(1)} %collective-permute-done.21.refs_1_), channel_id=1, source_target_pairs={{0,8},{8,24},{24,16},{16,0},{1,9},{9,25},{25,17},{17,1},{2,10},{10... | collective-permute-start | bytes 638984 | tf_op jit(solution)/shard_map/ppermute | solution.py:436
  126.8 3.5 %collective-permute-done.22.refs_2_ = bf16[832,128]{1,0:T(8,128)(2,1)S(1)} collective-permute-done((bf16[832,128]{1,0:T(8,128)(2,1)S(1)}, bf16[832,128]{1,0:T(8,128)(2,1)S(1)}, u32[]{:S(2)}, u32[]{:S(2)}) %collective-permute-start.22) | collective-permute-done | bytes 213024 | tf_op jit(solution)/shard_map/ppermute | solution.py:422
  131.3 4.0 %early_images.6.early = f32[13440,128]{1,0:T(8,128)S(1)} custom-call(s32[8]{0:T(128)S(1)} %concatenate.3.refs_0_.bounds.edges_ref, s32[288]{0:T(512)S(1)} %pad.10.refs_1_.order, s32[288]{0:T(512)S(1)} %pad.11.refs_2_.rows, s32[288]{0:T(512)S(1)} %pad.12.refs_3_.cols, bf16[256,128,128]{2,1,0:T(8,128)(2,1)S(1)} %resident.1.values, ...), custom_call_target="tpu_custom_call" | custom-call | tf_op jit(solution)/shard_map/early_images/pallas_call | solution.py:132
  137.3 2.0 %collective-permute-done.34.refs_1_ = bf16[832,128]{1,0:T(8,128)(2,1)S(1)} collective-permute-done((bf16[832,128]{1,0:T(8,128)(2,1)S(1)}, bf16[832,128]{1,0:T(8,128)(2,1)S(1)}, u32[]{:S(2)}, u32[]{:S(2)}) %collective-permute-start.34) | collective-permute-done | bytes 213024 | tf_op jit(solution)/shard_map/ppermute | solution.py:437
  139.3 2.4 %last_images.7 = (f32[13440,128]{1,0:T(8,128)S(1)}, bf16[1664,128]{1,0:T(8,128)(2,1)S(1)}, bf16[1664,128]{1,0:T(8,128)(2,1)S(1)}, bf16[4992,128]{1,0:T(8,128)(2,1)S(1)}, bf16[4992,128]{1,0:T(8,128)(2,1)S(1)}) custom-call(s32[8]{0:T(128)S(1)} %concatenate.3.refs_0_.bounds.edges_ref, s32[288]{0:T(512)S(1)} %pad.10.refs_1_.order, ...), custom_call_target="tpu_custom_call", output_to_operand_aliasing={{0}: (5, {})} | custom-call | tf_op jit(solution)/shard_map/last_images/pallas_call | solution.py:168
  146.3 5.1 %collective-permute-done.39.refs_2_ = bf16[832,128]{1,0:T(8,128)(2,1)S(1)} collective-permute-done((bf16[832,128]{1,0:T(8,128)(2,1)S(1)}, bf16[832,128]{1,0:T(8,128)(2,1)S(1)}, u32[]{:S(2)}, u32[]{:S(2)}) %collective-permute-start.39) | collective-permute-done | bytes 213024 | tf_op jit(solution)/shard_map/ppermute | solution.py:413
  161.5 2.5 %collective-permute-done.38.refs_2_ = bf16[832,128]{1,0:T(8,128)(2,1)S(1)} collective-permute-done((bf16[832,128]{1,0:T(8,128)(2,1)S(1)}, bf16[832,128]{1,0:T(8,128)(2,1)S(1)}, u32[]{:S(2)}, u32[]{:S(2)}) %collective-permute-start.38) | collective-permute-done | bytes 213024 | tf_op jit(solution)/shard_map/ppermute | solution.py:413
  (116 shorter events, 54.8 us)
Async XLA Ops:
  1.3 24.8 %collective-permute-start.2 = (bf16[1664,128]{1,0:T(8,128)(2,1)S(1)}, bf16[1664,128]{1,0:T(8,128)(2,1)S(1)}, u32[]{:S(2)}, u32[]{:S(2)}) collective-permute-start(bf16[1664,128]{1,0:T(8,128)(2,1)S(1)} %columns_of.6.refs_0_), channel_id=1, source_target_pairs={{8,0},{24,8},{16,24},{0,16},{9,1},{25,9},{17,25},{1,17},{10,2},{26... | collective-permute-start | bytes 1277960 | tf_op jit(solution)/shard_map/ppermute | solution.py:423
  5.4 15.5 %collective-permute-start.1 = (bf16[832,128]{1,0:T(8,128)(2,1)S(1)}, bf16[832,128]{1,0:T(8,128)(2,1)S(1)}, u32[]{:S(2)}, u32[]{:S(2)}) collective-permute-start(bf16[832,128]{1,0:T(8,128)(2,1)S(1)} %columns_of.8), channel_id=1, source_target_pairs={{0,8},{8,24},{24,16},{16,0},{1,9},{9,25},{25,17},{17,1},{2,10},{10... | collective-permute-start | bytes 638984 | tf_op jit(solution)/shard_map/ppermute | solution.py:422
  5.6 19.8 %collective-permute-start = (bf16[832,128]{1,0:T(8,128)(2,1)S(1)}, bf16[832,128]{1,0:T(8,128)(2,1)S(1)}, u32[]{:S(2)}, u32[]{:S(2)}) collective-permute-start(bf16[832,128]{1,0:T(8,128)(2,1)S(1)} %columns_of.7), channel_id=1, source_target_pairs={{0,8},{8,24},{24,16},{16,0},{1,9},{9,25},{25,17},{17,1},{2,10},{10... | collective-permute-start | bytes 638984 | tf_op jit(solution)/shard_map/ppermute | solution.py:422
  25.4 12.3 %collective-permute-start.6 = (bf16[832,128]{1,0:T(8,128)(2,1)S(1)}, bf16[832,128]{1,0:T(8,128)(2,1)S(1)}, u32[]{:S(2)}, u32[]{:S(2)}) collective-permute-start(bf16[832,128]{1,0:T(8,128)(2,1)S(1)} %collective-permute-done.refs_1_), channel_id=1, source_target_pairs={{0,8},{8,24},{24,16},{16,0},{1,9},{9,25},{25,17},{17,1},{2,10},{10... | collective-permute-start | bytes 638984 | tf_op jit(solution)/shard_map/ppermute | solution.py:436
  26.1 12.3 %collective-permute-start.7 = (bf16[832,128]{1,0:T(8,128)(2,1)S(1)}, bf16[832,128]{1,0:T(8,128)(2,1)S(1)}, u32[]{:S(2)}, u32[]{:S(2)}) collective-permute-start(bf16[832,128]{1,0:T(8,128)(2,1)S(1)} %rows_of.4), channel_id=1, source_target_pairs={{8,0},{24,8},{16,24},{0,16},{9,1},{25,9},{17,25},{1,17},{10,2},{26... | collective-permute-start | bytes 638984 | tf_op jit(solution)/shard_map/ppermute | solution.py:437
  32.4 10.2 %collective-permute-start.3 = (bf16[832,128]{1,0:T(8,128)(2,1)S(1)}, bf16[832,128]{1,0:T(8,128)(2,1)S(1)}, u32[]{:S(2)}, u32[]{:S(2)}) collective-permute-start(bf16[832,128]{1,0:T(8,128)(2,1)S(1)} %columns_of.10), channel_id=1, source_target_pairs={{0,8},{8,24},{24,16},{16,0},{1,9},{9,25},{25,17},{17,1},{2,10},{10... | collective-permute-start | bytes 638984 | tf_op jit(solution)/shard_map/ppermute | solution.py:422
  44.5 12.2 %collective-permute-start.5 = (bf16[1664,128]{1,0:T(8,128)(2,1)S(1)}, bf16[1664,128]{1,0:T(8,128)(2,1)S(1)}, u32[]{:S(2)}, u32[]{:S(2)}) collective-permute-start(bf16[1664,128]{1,0:T(8,128)(2,1)S(1)} %columns_of.9.refs_0_), channel_id=1, source_target_pairs={{8,0},{24,8},{16,24},{0,16},{9,1},{25,9},{17,25},{1,17},{10,2},{26... | collective-permute-start | bytes 1277960 | tf_op jit(solution)/shard_map/ppermute | solution.py:423
  45.1 13.7 %collective-permute-start.11 = (bf16[1664,128]{1,0:T(8,128)(2,1)S(1)}, bf16[1664,128]{1,0:T(8,128)(2,1)S(1)}, u32[]{:S(2)}, u32[]{:S(2)}) collective-permute-start(bf16[1664,128]{1,0:T(8,128)(2,1)S(1)} %summed.10), channel_id=1, source_target_pairs={{0,6},{1,7},{2,4},{3,5},{4,2},{5,3},{6,0},{7,1},{8,14},{9,15},{10,... | collective-permute-start | bytes 1277960 | tf_op jit(solution)/shard_map/ppermute | solution.py:413
  47.8 19.2 %collective-permute-start.12 = (bf16[1664,128]{1,0:T(8,128)(2,1)S(1)}, bf16[1664,128]{1,0:T(8,128)(2,1)S(1)}, u32[]{:S(2)}, u32[]{:S(2)}) collective-permute-start(bf16[1664,128]{1,0:T(8,128)(2,1)S(1)} %get-tuple-element.69), channel_id=1, source_target_pairs={{0,4},{1,5},{2,6},{3,7},{4,0},{5,1},{6,2},{7,3},{8,12},{9,13},{10,... | collective-permute-start | bytes 1277960 | tf_op jit(solution)/shard_map/ppermute | solution.py:413
  49.2 17.9 %collective-permute-start.13 = (bf16[1664,128]{1,0:T(8,128)(2,1)S(1)}, bf16[1664,128]{1,0:T(8,128)(2,1)S(1)}, u32[]{:S(2)}, u32[]{:S(2)}) collective-permute-start(bf16[1664,128]{1,0:T(8,128)(2,1)S(1)} %get-tuple-element.70), channel_id=1, source_target_pairs={{0,2},{1,3},{2,0},{3,1},{4,6},{5,7},{6,4},{7,5},{8,10},{9,11},{10,... | collective-permute-start | bytes 1277960 | tf_op jit(solution)/shard_map/ppermute | solution.py:413
  52.0 17.2 %collective-permute-start.4 = (bf16[832,128]{1,0:T(8,128)(2,1)S(1)}, bf16[832,128]{1,0:T(8,128)(2,1)S(1)}, u32[]{:S(2)}, u32[]{:S(2)}) collective-permute-start(bf16[832,128]{1,0:T(8,128)(2,1)S(1)} %columns_of.11), channel_id=1, source_target_pairs={{0,8},{8,24},{24,16},{16,0},{1,9},{9,25},{25,17},{17,1},{2,10},{10... | collective-permute-start | bytes 638984 | tf_op jit(solution)/shard_map/ppermute | solution.py:422
  56.7 16.4 %collective-permute-start.10 = (bf16[832,128]{1,0:T(8,128)(2,1)S(1)}, bf16[832,128]{1,0:T(8,128)(2,1)S(1)}, u32[]{:S(2)}, u32[]{:S(2)}) collective-permute-start(bf16[832,128]{1,0:T(8,128)(2,1)S(1)} %collective-permute-done.3.refs_1_), channel_id=1, source_target_pairs={{0,8},{8,24},{24,16},{16,0},{1,9},{9,25},{25,17},{17,1},{2,10},{10... | collective-permute-start | bytes 638984 | tf_op jit(solution)/shard_map/ppermute | solution.py:436
  58.7 14.4 %collective-permute-start.14 = (bf16[832,128]{1,0:T(8,128)(2,1)S(1)}, bf16[832,128]{1,0:T(8,128)(2,1)S(1)}, u32[]{:S(2)}, u32[]{:S(2)}) collective-permute-start(bf16[832,128]{1,0:T(8,128)(2,1)S(1)} %rows_of.5), channel_id=1, source_target_pairs={{8,0},{24,8},{16,24},{0,16},{9,1},{25,9},{17,25},{1,17},{10,2},{26... | collective-permute-start | bytes 638984 | tf_op jit(solution)/shard_map/ppermute | solution.py:437
  67.4 10.0 %collective-permute-start.15 = (bf16[832,128]{1,0:T(8,128)(2,1)S(1)}, bf16[832,128]{1,0:T(8,128)(2,1)S(1)}, u32[]{:S(2)}, u32[]{:S(2)}) collective-permute-start(bf16[832,128]{1,0:T(8,128)(2,1)S(1)} %get-tuple-element.74), channel_id=1, source_target_pairs={{0,8},{8,24},{24,16},{16,0},{1,9},{9,25},{25,17},{17,1},{2,10},{10... | collective-permute-start | bytes 638984 | tf_op jit(solution)/shard_map/ppermute | solution.py:422
  79.4 12.3 %collective-permute-start.25 = (bf16[1664,128]{1,0:T(8,128)(2,1)S(1)}, bf16[1664,128]{1,0:T(8,128)(2,1)S(1)}, u32[]{:S(2)}, u32[]{:S(2)}) collective-permute-start(bf16[1664,128]{1,0:T(8,128)(2,1)S(1)} %get-tuple-element.73.refs_0_.refs_5_), channel_id=1, source_target_pairs={{8,0},{24,8},{16,24},{0,16},{9,1},{25,9},{17,25},{1,17},{10,2},{26... | collective-permute-start | bytes 1277960 | tf_op jit(solution)/shard_map/ppermute | solution.py:423
  80.1 13.7 %collective-permute-start.18 = (bf16[1664,128]{1,0:T(8,128)(2,1)S(1)}, bf16[1664,128]{1,0:T(8,128)(2,1)S(1)}, u32[]{:S(2)}, u32[]{:S(2)}) collective-permute-start(bf16[1664,128]{1,0:T(8,128)(2,1)S(1)} %summed.11), channel_id=1, source_target_pairs={{0,6},{1,7},{2,4},{3,5},{4,2},{5,3},{6,0},{7,1},{8,14},{9,15},{10,... | collective-permute-start | bytes 1277960 | tf_op jit(solution)/shard_map/ppermute | solution.py:413
  82.8 19.2 %collective-permute-start.19 = (bf16[1664,128]{1,0:T(8,128)(2,1)S(1)}, bf16[1664,128]{1,0:T(8,128)(2,1)S(1)}, u32[]{:S(2)}, u32[]{:S(2)}) collective-permute-start(bf16[1664,128]{1,0:T(8,128)(2,1)S(1)} %get-tuple-element.84), channel_id=1, source_target_pairs={{0,4},{1,5},{2,6},{3,7},{4,0},{5,1},{6,2},{7,3},{8,12},{9,13},{10,... | collective-permute-start | bytes 1277960 | tf_op jit(solution)/shard_map/ppermute | solution.py:413
  84.0 18.0 %collective-permute-start.20 = (bf16[1664,128]{1,0:T(8,128)(2,1)S(1)}, bf16[1664,128]{1,0:T(8,128)(2,1)S(1)}, u32[]{:S(2)}, u32[]{:S(2)}) collective-permute-start(bf16[1664,128]{1,0:T(8,128)(2,1)S(1)} %get-tuple-element.85), channel_id=1, source_target_pairs={{0,2},{1,3},{2,0},{3,1},{4,6},{5,7},{6,4},{7,5},{8,10},{9,11},{10,... | collective-permute-start | bytes 1277960 | tf_op jit(solution)/shard_map/ppermute | solution.py:413
  85.5 18.5 %collective-permute-start.24 = (bf16[832,128]{1,0:T(8,128)(2,1)S(1)}, bf16[832,128]{1,0:T(8,128)(2,1)S(1)}, u32[]{:S(2)}, u32[]{:S(2)}) collective-permute-start(bf16[832,128]{1,0:T(8,128)(2,1)S(1)} %get-tuple-element.75), channel_id=1, source_target_pairs={{0,8},{8,24},{24,16},{16,0},{1,9},{9,25},{25,17},{17,1},{2,10},{10... | collective-permute-start | bytes 638984 | tf_op jit(solution)/shard_map/ppermute | solution.py:422
  91.7 16.3 %collective-permute-start.26 = (bf16[832,128]{1,0:T(8,128)(2,1)S(1)}, bf16[832,128]{1,0:T(8,128)(2,1)S(1)}, u32[]{:S(2)}, u32[]{:S(2)}) collective-permute-start(bf16[832,128]{1,0:T(8,128)(2,1)S(1)} %collective-permute-done.15.refs_1_), channel_id=1, source_target_pairs={{0,8},{8,24},{24,16},{16,0},{1,9},{9,25},{25,17},{17,1},{2,10},{10... | collective-permute-start | bytes 638984 | tf_op jit(solution)/shard_map/ppermute | solution.py:436
  93.7 14.2 %collective-permute-start.27 = (bf16[832,128]{1,0:T(8,128)(2,1)S(1)}, bf16[832,128]{1,0:T(8,128)(2,1)S(1)}, u32[]{:S(2)}, u32[]{:S(2)}) collective-permute-start(bf16[832,128]{1,0:T(8,128)(2,1)S(1)} %rows_of.6), channel_id=1, source_target_pairs={{8,0},{24,8},{16,24},{0,16},{9,1},{25,9},{17,25},{1,17},{10,2},{26... | collective-permute-start | bytes 638984 | tf_op jit(solution)/shard_map/ppermute | solution.py:437
  112.4 12.2 %collective-permute-start.23 = (bf16[1664,128]{1,0:T(8,128)(2,1)S(1)}, bf16[1664,128]{1,0:T(8,128)(2,1)S(1)}, u32[]{:S(2)}, u32[]{:S(2)}) collective-permute-start(bf16[1664,128]{1,0:T(8,128)(2,1)S(1)} %get-tuple-element.86.refs_0_), channel_id=1, source_target_pairs={{8,0},{24,8},{16,24},{0,16},{9,1},{25,9},{17,25},{1,17},{10,2},{26... | collective-permute-start | bytes 1277960 | tf_op jit(solution)/shard_map/ppermute | solution.py:423
  114.0 21.3 %collective-permute-start.31 = (bf16[1664,128]{1,0:T(8,128)(2,1)S(1)}, bf16[1664,128]{1,0:T(8,128)(2,1)S(1)}, u32[]{:S(2)}, u32[]{:S(2)}) collective-permute-start(bf16[1664,128]{1,0:T(8,128)(2,1)S(1)} %summed.14), channel_id=1, source_target_pairs={{0,6},{1,7},{2,4},{3,5},{4,2},{5,3},{6,0},{7,1},{8,14},{9,15},{10,... | collective-permute-start | bytes 1277960 | tf_op jit(solution)/shard_map/ppermute | solution.py:413
  116.6 19.3 %collective-permute-start.32 = (bf16[1664,128]{1,0:T(8,128)(2,1)S(1)}, bf16[1664,128]{1,0:T(8,128)(2,1)S(1)}, u32[]{:S(2)}, u32[]{:S(2)}) collective-permute-start(bf16[1664,128]{1,0:T(8,128)(2,1)S(1)} %get-tuple-element.97), channel_id=1, source_target_pairs={{0,4},{1,5},{2,6},{3,7},{4,0},{5,1},{6,2},{7,3},{8,12},{9,13},{10,... | collective-permute-start | bytes 1277960 | tf_op jit(solution)/shard_map/ppermute | solution.py:413
  117.3 18.6 %collective-permute-start.33 = (bf16[1664,128]{1,0:T(8,128)(2,1)S(1)}, bf16[1664,128]{1,0:T(8,128)(2,1)S(1)}, u32[]{:S(2)}, u32[]{:S(2)}) collective-permute-start(bf16[1664,128]{1,0:T(8,128)(2,1)S(1)} %get-tuple-element.98), channel_id=1, source_target_pairs={{0,2},{1,3},{2,0},{3,1},{4,6},{5,7},{6,4},{7,5},{8,10},{9,11},{10,... | collective-permute-start | bytes 1277960 | tf_op jit(solution)/shard_map/ppermute | solution.py:413
  118.5 11.7 %collective-permute-start.22 = (bf16[832,128]{1,0:T(8,128)(2,1)S(1)}, bf16[832,128]{1,0:T(8,128)(2,1)S(1)}, u32[]{:S(2)}, u32[]{:S(2)}) collective-permute-start(bf16[832,128]{1,0:T(8,128)(2,1)S(1)} %get-tuple-element.88.refs_9_), channel_id=1, source_target_pairs={{0,8},{8,24},{24,16},{16,0},{1,9},{9,25},{25,17},{17,1},{2,10},{10... | collective-permute-start | bytes 638984 | tf_op jit(solution)/shard_map/ppermute | solution.py:422
  124.6 12.7 %collective-permute-start.30 = (bf16[832,128]{1,0:T(8,128)(2,1)S(1)}, bf16[832,128]{1,0:T(8,128)(2,1)S(1)}, u32[]{:S(2)}, u32[]{:S(2)}) collective-permute-start(bf16[832,128]{1,0:T(8,128)(2,1)S(1)} %collective-permute-done.21.refs_1_), channel_id=1, source_target_pairs={{0,8},{8,24},{24,16},{16,0},{1,9},{9,25},{25,17},{17,1},{2,10},{10... | collective-permute-start | bytes 638984 | tf_op jit(solution)/shard_map/ppermute | solution.py:436
  130.2 9.0 %collective-permute-start.34 = (bf16[832,128]{1,0:T(8,128)(2,1)S(1)}, bf16[832,128]{1,0:T(8,128)(2,1)S(1)}, u32[]{:S(2)}, u32[]{:S(2)}) collective-permute-start(bf16[832,128]{1,0:T(8,128)(2,1)S(1)} %rows_of.7), channel_id=1, source_target_pairs={{8,0},{24,8},{16,24},{0,16},{9,1},{25,9},{17,25},{1,17},{10,2},{26... | collective-permute-start | bytes 638984 | tf_op jit(solution)/shard_map/ppermute | solution.py:437
  143.5 8.4 %collective-permute-start.37 = (bf16[4992,128]{1,0:T(8,128)(2,1)S(1)}, bf16[4992,128]{1,0:T(8,128)(2,1)S(1)}, u32[]{:S(2)}, u32[]{:S(2)}) collective-permute-start(bf16[4992,128]{1,0:T(8,128)(2,1)S(1)} %get-tuple-element.109), channel_id=1, source_target_pairs={{0,1},{1,0},{2,3},{3,2},{4,5},{5,4},{6,7},{7,6},{8,9},{9,8},{10,11... | collective-permute-start | bytes 3833864 | tf_op jit(solution)/shard_map/ppermute | solution.py:410
  152.1 8.3 %collective-permute-start.41 = (bf16[832,128]{1,0:T(8,128)(2,1)S(1)}, bf16[832,128]{1,0:T(8,128)(2,1)S(1)}, u32[]{:S(2)}, u32[]{:S(2)}) collective-permute-start(bf16[832,128]{1,0:T(8,128)(2,1)S(1)} %get-tuple-element.114), channel_id=1, source_target_pairs={{0,4},{1,5},{2,6},{3,7},{4,0},{5,1},{6,2},{7,3},{8,12},{9,13},{10,... | collective-permute-start | bytes 638984 | tf_op jit(solution)/shard_map/ppermute | solution.py:413
  154.5 9.5 %collective-permute-start.38 = (bf16[832,128]{1,0:T(8,128)(2,1)S(1)}, bf16[832,128]{1,0:T(8,128)(2,1)S(1)}, u32[]{:S(2)}, u32[]{:S(2)}) collective-permute-start(bf16[832,128]{1,0:T(8,128)(2,1)S(1)} %get-tuple-element.110), channel_id=1, source_target_pairs={{0,2},{1,3},{2,0},{3,1},{4,6},{5,7},{6,4},{7,5},{8,10},{9,11},{10,... | collective-permute-start | bytes 638984 | tf_op jit(solution)/shard_map/ppermute | solution.py:413
  155.5 8.5 %collective-permute-start.43 = (bf16[832,128]{1,0:T(8,128)(2,1)S(1)}, bf16[832,128]{1,0:T(8,128)(2,1)S(1)}, u32[]{:S(2)}, u32[]{:S(2)}) collective-permute-start(bf16[832,128]{1,0:T(8,128)(2,1)S(1)} %get-tuple-element.116), channel_id=1, source_target_pairs={{0,4},{1,5},{2,6},{3,7},{4,0},{5,1},{6,2},{7,3},{8,12},{9,13},{10,... | collective-permute-start | bytes 638984 | tf_op jit(solution)/shard_map/ppermute | solution.py:413
  (19 other events, 81.3 us)

commit v6 on v5

--- a/solution.py
+++ b/solution.py
@@ -140,6 +140,27 @@
     )(*tables, values, *parts)
 
 
+def middle_images(low_col, tables, values, early, parts):
+    width = parts[0].shape[1]
+    panel_rows = sum(part.shape[0] for part in parts)
+
+    def kernel(bounds, order, rows, cols, values, early, *refs):
+        total, panel = refs[-2:]
+        fill(panel, refs[:-2])
+        add_images(bounds, order, rows, cols, values, panel, total, 1, low_col)
+
+    return pl.pallas_call(
+        kernel,
+        out_shape=pltpu.VMEM(early.shape, jnp.float32),
+        in_specs=[SMEM] * 4 + [VMEM] * (2 + len(parts)),
+        out_specs=VMEM,
+        scratch_shapes=[pltpu.VMEM((panel_rows, width), jnp.bfloat16)],
+        input_output_aliases={5: 0},
+        compiler_params=params(bytes_of(*parts, *parts)),
+        name="middle_images",
+    )(*tables, values, early, *parts)
+
+
 def last_images(counts, low_col, tables, values, early, parts):
     orbitals = values.shape[-1]
     width = parts[0].shape[1]
@@ -155,7 +176,7 @@
         part_refs, out_refs = refs[: len(parts)], refs[len(parts) + 1 : -1]
         total, panel = refs[len(parts)], refs[-1]
         fill(panel, part_refs)
-        add_images(bounds, order, rows, cols, values, panel, total, 1, low_col)
+        add_images(bounds, order, rows, cols, values, panel, total, 2, low_col)
         low = 0
         for count, *pair in zip(counts, out_refs[::2], out_refs[1::2]):
             for piece in range(count):
@@ -381,8 +402,9 @@
         piece = chip_count - 1 - relative // 2
         out_rows = (piece * 2 + 1 - relative % 2) * own + row_ids % own
         number = jnp.arange(entry_count, dtype=jnp.int32)
+        is_own = (arrival == 0).astype(jnp.int32)
         is_last = (arrival == row_count - 1).astype(jnp.int32)
-        key = is_last * (2 * chip_count * own) + out_rows
+        key = (1 - is_own + is_last) * (2 * chip_count * own) + out_rows
         before = (key[None, :] < key[:, None]) | (
             (key[None, :] == key[:, None]) & (number[None, :] < number[:, None])
         )
@@ -396,7 +418,9 @@
         entry_order = jnp.pad(ordered(number), room)
         rows = jnp.pad(ordered(out_rows), room)
         cols = jnp.pad(ordered(panel_cols), room)
-        bounds = jnp.stack([0, entry_count - jnp.sum(is_last), entry_count])
+        bounds = jnp.stack(
+            [0, jnp.sum(is_own), entry_count - jnp.sum(is_last), entry_count]
+        )
         bounds = jnp.concatenate([jnp.stack(edges), bounds]).astype(jnp.int32)
         tables = (bounds, entry_order, rows, cols)
     values = resident(values, tables)
@@ -426,7 +450,10 @@
 
         def finish(self, tokens):
             self.send_last(tokens)
-            self.images = early_images(2 * chip_count * own, tables, values, self.early)
+            self.own_images = early_images(2 * chip_count * own, tables, values, self.early[:1])
+            self.images = self.own_images
+            if self.early[1:]:
+                self.images = middle_images(own, tables, values, self.images, self.early[1:])
 
         def send_last(self, tokens):
             if both_ways:
@@ -489,6 +516,8 @@
                 chip -= 1
         if following is not None:
             following.finish(sums)
+            (array, row), *terms = terms
+            terms = [(tied(array, [following.own_images]), row), *terms]
         return [(own_rows, [*terms, *arrived])]
 
     gathers = []

time: 169 us -> 168 us (level)
  waiting for transfers between devices: 71.4 us -> 64.9 us
  Pallas kernels: 34.8 us -> 37.4 us
  local copies, waits for them, and re-layouts: 5.81 us -> 8.29 us
  other arithmetic: 1.17 us -> 3.23 us
    pallas_call x0 -> x4, Pallas kernels: none -> 10.3 us  [middle_images(): pl.pallas_call(kernel, out_shape=pltpu.VMEM(early.shape, jnp.float32), in...]
    ppermute x4, waiting for transfers between devices: 16.2 us -> 9.6 us  [__init__(): self.early = [part, upper, lower, lax.ppermute(part, 'row', back_route)]]
    pallas_call x4, Pallas kernels: 16 us -> 10 us  [early_images(): pl.pallas_call(kernel, out_shape=pltpu.VMEM(total, jnp.float32), in_specs...]
    ppermute x8, waiting for transfers between devices: 16.7 us -> 13 us  [__init__(): upper, lower = (lax.ppermute(half, 'row', route) for half in (upper, lower))]
    ppermute x15, waiting for transfers between devices: 21.5 us -> 24.4 us  [to_chip(): lax.ppermute(array, 'col', [(i, i ^ 2 * chip) for i in range(col_count)])]
    ppermute x4, starting transfers between devices: 10.6 us -> 7.88 us  [send_last(): lax.ppermute(lower, 'row', back_route)]
    ppermute x15, starting transfers between devices: 21.7 us -> 23.5 us  [to_chip(): lax.ppermute(array, 'col', [(i, i ^ 2 * chip) for i in range(col_count)])]
    pallas_call x4, Pallas kernels: 9.64 us -> 7.9 us  [last_images(): pl.pallas_call(kernel, out_shape=[pltpu.VMEM(early.shape, jnp.float32), *...]
  transfers between devices with their start and end apart: 45 -> 45, of which waited for: 30 -> 27; matrix products, arithmetic and copies ran while one was open for 1% -> 3% of each run, Pallas kernels for 17% -> 19%
where the time goes in v6:
time: 168 us
  waiting for transfers between devices  64.9 us (39%)
  starting transfers between devices  50.7 us (30%)
  Pallas kernels  37.4 us (22%)
  local copies, waits for them, and re-layouts  8.29 us (5%)
  other arithmetic  3.23 us (2%)
  between operations  3.19 us (2%)
    ppermute x15, waiting for transfers between devices, to_chip(): lax.ppermute(array, 'col', [(i, i ^ 2 * chip) for i in range(col_count)])  24.4 us
    ppermute x15, starting transfers between devices, to_chip(): lax.ppermute(array, 'col', [(i, i ^ 2 * chip) for i in range(col_count)])  23.5 us
    ppermute x8, waiting for transfers between devices, __init__(): upper, lower = (lax.ppermute(half, 'row', route) for half in (upper, lower))  13 us
    pallas_call x4, Pallas kernels, middle_images(): pl.pallas_call(kernel, out_shape=pltpu.VMEM(early.shape, jnp.float32), in...  10.3 us
    pallas_call x4, Pallas kernels, early_images(): pl.pallas_call(kernel, out_shape=pltpu.VMEM(total, jnp.float32), in_specs...  10 us
    ppermute x10, waiting for transfers between devices, to_core(): return lax.ppermute(array, 'col', other_core)  9.87 us
    ppermute x4, waiting for transfers between devices, __init__(): self.early = [part, upper, lower, lax.ppermute(part, 'row', back_route)]  9.6 us
    pallas_call x4, Pallas kernels, last_images(): pl.pallas_call(kernel, out_shape=[pltpu.VMEM(early.shape, jnp.float32), *...  7.9 us
  transfers between devices with their start and end apart: 45, of which 27 were waited for; matrix products, arithmetic and copies ran while one was open for 3% of the time, Pallas kernels for 19%

profile of v6, /device:TPU:0, one launch (start us, length us, event | category | flops | bytes accessed | tf_op | source)
XLA Modules:
  0.0 167.8 jit_solution(3195158778977032604)
XLA Ops:
  1.2 4.1 %collective-permute-start.2 = (bf16[1664,128]{1,0:T(8,128)(2,1)S(1)}, bf16[1664,128]{1,0:T(8,128)(2,1)S(1)}, u32[]{:S(2)}, u32[]{:S(2)}) collective-permute-start(bf16[1664,128]{1,0:T(8,128)(2,1)S(1)} %columns_of.6.refs_0_), channel_id=1, source_target_pairs={{8,0},{24,8},{16,24},{0,16},{9,1},{25,9},{17,25},{1,17},{10,2},{26... | collective-permute-start | bytes 1277960 | tf_op jit(solution)/shard_map/ppermute | solution.py:447
  6.7 1.9 %collective-permute-start = (bf16[832,128]{1,0:T(8,128)(2,1)S(1)}, bf16[832,128]{1,0:T(8,128)(2,1)S(1)}, u32[]{:S(2)}, u32[]{:S(2)}) collective-permute-start(bf16[832,128]{1,0:T(8,128)(2,1)S(1)} %columns_of.7), channel_id=1, source_target_pairs={{0,8},{8,24},{24,16},{16,0},{1,9},{9,25},{25,17},{17,1},{2,10},{10... | collective-permute-start | bytes 638984 | tf_op jit(solution)/shard_map/ppermute | solution.py:446
  15.8 3.4 %copy-done.3 = bf16[1,1,256,128,128]{4,3,2,1,0:T(8,128)(2,1)S(1)} copy-done((bf16[1,1,256,128,128]{4,3,2,1,0:T(8,128)(2,1)S(1)}, bf16[1,1,256,128,128]{4,3,2,1,0:T(8,128)(2,1)}, u32[]{:S(2)}) %copy-start.3) | copy-done | bytes 8388632
  19.7 2.5 %early_images.4.early = f32[13440,128]{1,0:T(8,128)S(1)} custom-call(s32[9]{0:T(128)S(1)} %concatenate.3.refs_0_.bounds.edges_ref, s32[288]{0:T(512)S(1)} %pad.10.refs_1_.order, s32[288]{0:T(512)S(1)} %pad.11.refs_2_.rows, s32[288]{0:T(512)S(1)} %pad.12.refs_3_.cols, bf16[256,128,128]{2,1,0:T(8,128)(2,1)S(1)} %resident.1.values, ...), custom_call_target="tpu_custom_call" | custom-call | tf_op jit(solution)/shard_map/early_images/pallas_call | solution.py:132
  22.3 3.1 %collective-permute-done.refs_0_ = bf16[832,128]{1,0:T(8,128)(2,1)S(1)} collective-permute-done((bf16[832,128]{1,0:T(8,128)(2,1)S(1)}, bf16[832,128]{1,0:T(8,128)(2,1)S(1)}, u32[]{:S(2)}, u32[]{:S(2)}) %collective-permute-start) | collective-permute-done | bytes 213024 | tf_op jit(solution)/shard_map/ppermute | solution.py:446
  26.1 2.3 %collective-permute-start.7 = (bf16[832,128]{1,0:T(8,128)(2,1)S(1)}, bf16[832,128]{1,0:T(8,128)(2,1)S(1)}, u32[]{:S(2)}, u32[]{:S(2)}) collective-permute-start(bf16[832,128]{1,0:T(8,128)(2,1)S(1)} %rows_of.4), channel_id=1, source_target_pairs={{8,0},{24,8},{16,24},{0,16},{9,1},{25,9},{17,25},{1,17},{10,2},{26... | collective-permute-start | bytes 638984 | tf_op jit(solution)/shard_map/ppermute | solution.py:464
  28.4 2.6 %middle_images.4.refs_0_.early = f32[13440,128]{1,0:T(8,128)S(1)} custom-call(s32[9]{0:T(128)S(1)} %concatenate.3.refs_0_.bounds.edges_ref, s32[288]{0:T(512)S(1)} %pad.10.refs_1_.order, s32[288]{0:T(512)S(1)} %pad.11.refs_2_.rows, s32[288]{0:T(512)S(1)} %pad.12.refs_3_.cols, ...), custom_call_target="tpu_custom_call", output_to_operand_aliasing={{}: (5, {})} | custom-call | tf_op jit(solution)/shard_map/middle_images/pallas_call | solution.py:152
  31.8 5.8 %collective-permute-done.6.refs_0_ = bf16[832,128]{1,0:T(8,128)(2,1)S(1)} collective-permute-done((bf16[832,128]{1,0:T(8,128)(2,1)S(1)}, bf16[832,128]{1,0:T(8,128)(2,1)S(1)}, u32[]{:S(2)}, u32[]{:S(2)}) %collective-permute-start.6) | collective-permute-done | bytes 213024 | tf_op jit(solution)/shard_map/ppermute | solution.py:463
  40.3 2.3 %collective-permute-done.3.refs_0_ = bf16[832,128]{1,0:T(8,128)(2,1)S(1)} collective-permute-done((bf16[832,128]{1,0:T(8,128)(2,1)S(1)}, bf16[832,128]{1,0:T(8,128)(2,1)S(1)}, u32[]{:S(2)}, u32[]{:S(2)}) %collective-permute-start.3) | collective-permute-done | bytes 213024 | tf_op jit(solution)/shard_map/ppermute | solution.py:446
  45.0 2.5 %collective-permute-start.11 = (bf16[1664,128]{1,0:T(8,128)(2,1)S(1)}, bf16[1664,128]{1,0:T(8,128)(2,1)S(1)}, u32[]{:S(2)}, u32[]{:S(2)}) collective-permute-start(bf16[1664,128]{1,0:T(8,128)(2,1)S(1)} %summed.10), channel_id=1, source_target_pairs={{0,6},{1,7},{2,4},{3,5},{4,2},{5,3},{6,0},{7,1},{8,14},{9,15},{10,... | collective-permute-start | bytes 1277960 | tf_op jit(solution)/shard_map/ppermute | solution.py:437
  51.9 2.5 %early_images.5.early = f32[13440,128]{1,0:T(8,128)S(1)} custom-call(s32[9]{0:T(128)S(1)} %concatenate.3.refs_0_.bounds.edges_ref, s32[288]{0:T(512)S(1)} %pad.10.refs_1_.order, s32[288]{0:T(512)S(1)} %pad.11.refs_2_.rows, s32[288]{0:T(512)S(1)} %pad.12.refs_3_.cols, bf16[256,128,128]{2,1,0:T(8,128)(2,1)S(1)} %resident.1.values, ...), custom_call_target="tpu_custom_call" | custom-call | tf_op jit(solution)/shard_map/early_images/pallas_call | solution.py:132
  54.5 2.1 %collective-permute-done.5.refs_2_.array_ref = bf16[1664,128]{1,0:T(8,128)(2,1)S(1)} collective-permute-done((bf16[1664,128]{1,0:T(8,128)(2,1)S(1)}, bf16[1664,128]{1,0:T(8,128)(2,1)S(1)}, u32[]{:S(2)}, u32[]{:S(2)}) %collective-permute-start.5) | collective-permute-done | bytes 426016 | tf_op jit(solution)/shard_map/ppermute | solution.py:447
  58.7 2.6 %collective-permute-start.14 = (bf16[832,128]{1,0:T(8,128)(2,1)S(1)}, bf16[832,128]{1,0:T(8,128)(2,1)S(1)}, u32[]{:S(2)}, u32[]{:S(2)}) collective-permute-start(bf16[832,128]{1,0:T(8,128)(2,1)S(1)} %rows_of.5), channel_id=1, source_target_pairs={{8,0},{24,8},{16,24},{0,16},{9,1},{25,9},{17,25},{1,17},{10,2},{26... | collective-permute-start | bytes 638984 | tf_op jit(solution)/shard_map/ppermute | solution.py:464
  61.3 5.6 %collective-permute-done.12.refs_3_ = bf16[1664,128]{1,0:T(8,128)(2,1)S(1)} collective-permute-done((bf16[1664,128]{1,0:T(8,128)(2,1)S(1)}, bf16[1664,128]{1,0:T(8,128)(2,1)S(1)}, u32[]{:S(2)}, u32[]{:S(2)}) %collective-permute-start.12) | collective-permute-done | bytes 426016 | tf_op jit(solution)/shard_map/ppermute | solution.py:437
  69.1 2.6 %middle_images.5.early = f32[13440,128]{1,0:T(8,128)S(1)} custom-call(s32[9]{0:T(128)S(1)} %concatenate.3.refs_0_.bounds.edges_ref, s32[288]{0:T(512)S(1)} %pad.10.refs_1_.order, s32[288]{0:T(512)S(1)} %pad.11.refs_2_.rows, s32[288]{0:T(512)S(1)} %pad.12.refs_3_.cols, bf16[256,128,128]{2,1,0:T(8,128)(2,1)S(1)} %resident.1.values, ...), custom_call_target="tpu_custom_call", output_to_operand_aliasing={{}: (5, {})} | custom-call | tf_op jit(solution)/shard_map/middle_images/pallas_call | solution.py:152
  73.6 2.3 %collective-permute-done.15.refs_0_ = bf16[832,128]{1,0:T(8,128)(2,1)S(1)} collective-permute-done((bf16[832,128]{1,0:T(8,128)(2,1)S(1)}, bf16[832,128]{1,0:T(8,128)(2,1)S(1)}, u32[]{:S(2)}, u32[]{:S(2)}) %collective-permute-start.15) | collective-permute-done | bytes 213024 | tf_op jit(solution)/shard_map/ppermute | solution.py:446
  79.2 3.3 %collective-permute-start.18 = (bf16[1664,128]{1,0:T(8,128)(2,1)S(1)}, bf16[1664,128]{1,0:T(8,128)(2,1)S(1)}, u32[]{:S(2)}, u32[]{:S(2)}) collective-permute-start(bf16[1664,128]{1,0:T(8,128)(2,1)S(1)} %summed.11), channel_id=1, source_target_pairs={{0,6},{1,7},{2,4},{3,5},{4,2},{5,3},{6,0},{7,1},{8,14},{9,15},{10,... | collective-permute-start | bytes 1277960 | tf_op jit(solution)/shard_map/ppermute | solution.py:437
  82.8 2.7 %collective-permute-start.20 = (bf16[1664,128]{1,0:T(8,128)(2,1)S(1)}, bf16[1664,128]{1,0:T(8,128)(2,1)S(1)}, u32[]{:S(2)}, u32[]{:S(2)}) collective-permute-start(bf16[1664,128]{1,0:T(8,128)(2,1)S(1)} %get-tuple-element.90), channel_id=1, source_target_pairs={{0,2},{1,3},{2,0},{3,1},{4,6},{5,7},{6,4},{7,5},{8,10},{9,11},{10,... | collective-permute-start | bytes 1277960 | tf_op jit(solution)/shard_map/ppermute | solution.py:437
  85.5 2.5 %early_images.6.early = f32[13440,128]{1,0:T(8,128)S(1)} custom-call(s32[9]{0:T(128)S(1)} %concatenate.3.refs_0_.bounds.edges_ref, s32[288]{0:T(512)S(1)} %pad.10.refs_1_.order, s32[288]{0:T(512)S(1)} %pad.11.refs_2_.rows, s32[288]{0:T(512)S(1)} %pad.12.refs_3_.cols, bf16[256,128,128]{2,1,0:T(8,128)(2,1)S(1)} %resident.1.values, ...), custom_call_target="tpu_custom_call" | custom-call | tf_op jit(solution)/shard_map/early_images/pallas_call | solution.py:132
  95.1 6.6 %collective-permute-done.19.refs_3_ = bf16[1664,128]{1,0:T(8,128)(2,1)S(1)} collective-permute-done((bf16[1664,128]{1,0:T(8,128)(2,1)S(1)}, bf16[1664,128]{1,0:T(8,128)(2,1)S(1)}, u32[]{:S(2)}, u32[]{:S(2)}) %collective-permute-start.19) | collective-permute-done | bytes 426016 | tf_op jit(solution)/shard_map/ppermute | solution.py:437
  103.6 2.6 %middle_images.7.early = f32[13440,128]{1,0:T(8,128)S(1)} custom-call(s32[9]{0:T(128)S(1)} %concatenate.3.refs_0_.bounds.edges_ref, s32[288]{0:T(512)S(1)} %pad.10.refs_1_.order, s32[288]{0:T(512)S(1)} %pad.11.refs_2_.rows, s32[288]{0:T(512)S(1)} %pad.12.refs_3_.cols, bf16[256,128,128]{2,1,0:T(8,128)(2,1)S(1)} %resident.1.values, ...), custom_call_target="tpu_custom_call", output_to_operand_aliasing={{}: (5, {})} | custom-call | tf_op jit(solution)/shard_map/middle_images/pallas_call | solution.py:152
  106.2 2.1 %last_images.6 = (f32[13440,128]{1,0:T(8,128)S(1)}, bf16[1664,128]{1,0:T(8,128)(2,1)S(1)}, bf16[1664,128]{1,0:T(8,128)(2,1)S(1)}, bf16[4992,128]{1,0:T(8,128)(2,1)S(1)}, bf16[4992,128]{1,0:T(8,128)(2,1)S(1)}) custom-call(s32[9]{0:T(128)S(1)} %concatenate.3.refs_0_.bounds.edges_ref, s32[288]{0:T(512)S(1)} %pad.10.refs_1_.order, ...), custom_call_target="tpu_custom_call", output_to_operand_aliasing={{0}: (5, {})} | custom-call | tf_op jit(solution)/shard_map/last_images/pallas_call | solution.py:189
  113.3 2.7 %collective-permute-start.31 = (bf16[1664,128]{1,0:T(8,128)(2,1)S(1)}, bf16[1664,128]{1,0:T(8,128)(2,1)S(1)}, u32[]{:S(2)}, u32[]{:S(2)}) collective-permute-start(bf16[1664,128]{1,0:T(8,128)(2,1)S(1)} %summed.14), channel_id=1, source_target_pairs={{0,6},{1,7},{2,4},{3,5},{4,2},{5,3},{6,0},{7,1},{8,14},{9,15},{10,... | collective-permute-start | bytes 1277960 | tf_op jit(solution)/shard_map/ppermute | solution.py:437
  116.3 2.2 %collective-permute-start.33 = (bf16[1664,128]{1,0:T(8,128)(2,1)S(1)}, bf16[1664,128]{1,0:T(8,128)(2,1)S(1)}, u32[]{:S(2)}, u32[]{:S(2)}) collective-permute-start(bf16[1664,128]{1,0:T(8,128)(2,1)S(1)} %get-tuple-element.103), channel_id=1, source_target_pairs={{0,2},{1,3},{2,0},{3,1},{4,6},{5,7},{6,4},{7,5},{8,10},{9,11},{10,... | collective-permute-start | bytes 1277960 | tf_op jit(solution)/shard_map/ppermute | solution.py:437
  118.7 5.7 %collective-permute-done.23.refs_2_.array_ref = bf16[1664,128]{1,0:T(8,128)(2,1)S(1)} collective-permute-done((bf16[1664,128]{1,0:T(8,128)(2,1)S(1)}, bf16[1664,128]{1,0:T(8,128)(2,1)S(1)}, u32[]{:S(2)}, u32[]{:S(2)}) %collective-permute-start.23) | collective-permute-done | bytes 426016 | tf_op jit(solution)/shard_map/ppermute | solution.py:447
  124.3 2.0 %collective-permute-start.30 = (bf16[832,128]{1,0:T(8,128)(2,1)S(1)}, bf16[832,128]{1,0:T(8,128)(2,1)S(1)}, u32[]{:S(2)}, u32[]{:S(2)}) collective-permute-start(bf16[832,128]{1,0:T(8,128)(2,1)S(1)} %collective-permute-done.21.refs_0_), channel_id=1, source_target_pairs={{0,8},{8,24},{24,16},{16,0},{1,9},{9,25},{25,17},{17,1},{2,10},{10... | collective-permute-start | bytes 638984 | tf_op jit(solution)/shard_map/ppermute | solution.py:463
  126.3 3.5 %collective-permute-done.22.refs_1_ = bf16[832,128]{1,0:T(8,128)(2,1)S(1)} collective-permute-done((bf16[832,128]{1,0:T(8,128)(2,1)S(1)}, bf16[832,128]{1,0:T(8,128)(2,1)S(1)}, u32[]{:S(2)}, u32[]{:S(2)}) %collective-permute-start.22) | collective-permute-done | bytes 213024 | tf_op jit(solution)/shard_map/ppermute | solution.py:446
  130.9 2.5 %early_images.7.early = f32[13440,128]{1,0:T(8,128)S(1)} custom-call(s32[9]{0:T(128)S(1)} %concatenate.3.refs_0_.bounds.edges_ref, s32[288]{0:T(512)S(1)} %pad.10.refs_1_.order, s32[288]{0:T(512)S(1)} %pad.11.refs_2_.rows, s32[288]{0:T(512)S(1)} %pad.12.refs_3_.cols, bf16[256,128,128]{2,1,0:T(8,128)(2,1)S(1)} %resident.1.values, ...), custom_call_target="tpu_custom_call" | custom-call | tf_op jit(solution)/shard_map/early_images/pallas_call | solution.py:132
  133.4 2.6 %middle_images.6.early = f32[13440,128]{1,0:T(8,128)S(1)} custom-call(s32[9]{0:T(128)S(1)} %concatenate.3.refs_0_.bounds.edges_ref, s32[288]{0:T(512)S(1)} %pad.10.refs_1_.order, s32[288]{0:T(512)S(1)} %pad.11.refs_2_.rows, s32[288]{0:T(512)S(1)} %pad.12.refs_3_.cols, bf16[256,128,128]{2,1,0:T(8,128)(2,1)S(1)} %resident.1.values, ...), custom_call_target="tpu_custom_call", output_to_operand_aliasing={{}: (5, {})} | custom-call | tf_op jit(solution)/shard_map/middle_images/pallas_call | solution.py:152
  143.1 2.7 %collective-permute-start.40 = (bf16[832,128]{1,0:T(8,128)(2,1)S(1)}, bf16[832,128]{1,0:T(8,128)(2,1)S(1)}, u32[]{:S(2)}, u32[]{:S(2)}) collective-permute-start(bf16[832,128]{1,0:T(8,128)(2,1)S(1)} %get-tuple-element.119), channel_id=1, source_target_pairs={{0,2},{1,3},{2,0},{3,1},{4,6},{5,7},{6,4},{7,5},{8,10},{9,11},{10,... | collective-permute-start | bytes 638984 | tf_op jit(solution)/shard_map/ppermute | solution.py:437
  145.8 4.7 %collective-permute-done.39.refs_2_ = bf16[832,128]{1,0:T(8,128)(2,1)S(1)} collective-permute-done((bf16[832,128]{1,0:T(8,128)(2,1)S(1)}, bf16[832,128]{1,0:T(8,128)(2,1)S(1)}, u32[]{:S(2)}, u32[]{:S(2)}) %collective-permute-start.39) | collective-permute-done | bytes 213024 | tf_op jit(solution)/shard_map/ppermute | solution.py:437
  160.6 2.5 %collective-permute-done.38.refs_2_ = bf16[832,128]{1,0:T(8,128)(2,1)S(1)} collective-permute-done((bf16[832,128]{1,0:T(8,128)(2,1)S(1)}, bf16[832,128]{1,0:T(8,128)(2,1)S(1)}, u32[]{:S(2)}, u32[]{:S(2)}) %collective-permute-start.38) | collective-permute-done | bytes 213024 | tf_op jit(solution)/shard_map/ppermute | solution.py:437
  (116 shorter events, 65.7 us)
Async XLA Ops:
  1.2 24.8 %collective-permute-start.2 = (bf16[1664,128]{1,0:T(8,128)(2,1)S(1)}, bf16[1664,128]{1,0:T(8,128)(2,1)S(1)}, u32[]{:S(2)}, u32[]{:S(2)}) collective-permute-start(bf16[1664,128]{1,0:T(8,128)(2,1)S(1)} %columns_of.6.refs_0_), channel_id=1, source_target_pairs={{8,0},{24,8},{16,24},{0,16},{9,1},{25,9},{17,25},{1,17},{10,2},{26... | collective-permute-start | bytes 1277960 | tf_op jit(solution)/shard_map/ppermute | solution.py:447
  6.6 15.7 %collective-permute-start.1 = (bf16[832,128]{1,0:T(8,128)(2,1)S(1)}, bf16[832,128]{1,0:T(8,128)(2,1)S(1)}, u32[]{:S(2)}, u32[]{:S(2)}) collective-permute-start(bf16[832,128]{1,0:T(8,128)(2,1)S(1)} %columns_of.8), channel_id=1, source_target_pairs={{0,8},{8,24},{24,16},{16,0},{1,9},{9,25},{25,17},{17,1},{2,10},{10... | collective-permute-start | bytes 638984 | tf_op jit(solution)/shard_map/ppermute | solution.py:446
  6.7 18.7 %collective-permute-start = (bf16[832,128]{1,0:T(8,128)(2,1)S(1)}, bf16[832,128]{1,0:T(8,128)(2,1)S(1)}, u32[]{:S(2)}, u32[]{:S(2)}) collective-permute-start(bf16[832,128]{1,0:T(8,128)(2,1)S(1)} %columns_of.7), channel_id=1, source_target_pairs={{0,8},{8,24},{24,16},{16,0},{1,9},{9,25},{25,17},{17,1},{2,10},{10... | collective-permute-start | bytes 638984 | tf_op jit(solution)/shard_map/ppermute | solution.py:446
  25.3 12.3 %collective-permute-start.6 = (bf16[832,128]{1,0:T(8,128)(2,1)S(1)}, bf16[832,128]{1,0:T(8,128)(2,1)S(1)}, u32[]{:S(2)}, u32[]{:S(2)}) collective-permute-start(bf16[832,128]{1,0:T(8,128)(2,1)S(1)} %collective-permute-done.refs_0_), channel_id=1, source_target_pairs={{0,8},{8,24},{24,16},{16,0},{1,9},{9,25},{25,17},{17,1},{2,10},{10... | collective-permute-start | bytes 638984 | tf_op jit(solution)/shard_map/ppermute | solution.py:463
  26.1 12.3 %collective-permute-start.7 = (bf16[832,128]{1,0:T(8,128)(2,1)S(1)}, bf16[832,128]{1,0:T(8,128)(2,1)S(1)}, u32[]{:S(2)}, u32[]{:S(2)}) collective-permute-start(bf16[832,128]{1,0:T(8,128)(2,1)S(1)} %rows_of.4), channel_id=1, source_target_pairs={{8,0},{24,8},{16,24},{0,16},{9,1},{25,9},{17,25},{1,17},{10,2},{26... | collective-permute-start | bytes 638984 | tf_op jit(solution)/shard_map/ppermute | solution.py:464
  31.0 11.6 %collective-permute-start.3 = (bf16[832,128]{1,0:T(8,128)(2,1)S(1)}, bf16[832,128]{1,0:T(8,128)(2,1)S(1)}, u32[]{:S(2)}, u32[]{:S(2)}) collective-permute-start(bf16[832,128]{1,0:T(8,128)(2,1)S(1)} %columns_of.10), channel_id=1, source_target_pairs={{0,8},{8,24},{24,16},{16,0},{1,9},{9,25},{25,17},{17,1},{2,10},{10... | collective-permute-start | bytes 638984 | tf_op jit(solution)/shard_map/ppermute | solution.py:446
  44.5 12.1 %collective-permute-start.5 = (bf16[1664,128]{1,0:T(8,128)(2,1)S(1)}, bf16[1664,128]{1,0:T(8,128)(2,1)S(1)}, u32[]{:S(2)}, u32[]{:S(2)}) collective-permute-start(bf16[1664,128]{1,0:T(8,128)(2,1)S(1)} %columns_of.9.refs_0_), channel_id=1, source_target_pairs={{8,0},{24,8},{16,24},{0,16},{9,1},{25,9},{17,25},{1,17},{10,2},{26... | collective-permute-start | bytes 1277960 | tf_op jit(solution)/shard_map/ppermute | solution.py:447
  45.0 13.7 %collective-permute-start.11 = (bf16[1664,128]{1,0:T(8,128)(2,1)S(1)}, bf16[1664,128]{1,0:T(8,128)(2,1)S(1)}, u32[]{:S(2)}, u32[]{:S(2)}) collective-permute-start(bf16[1664,128]{1,0:T(8,128)(2,1)S(1)} %summed.10), channel_id=1, source_target_pairs={{0,6},{1,7},{2,4},{3,5},{4,2},{5,3},{6,0},{7,1},{8,14},{9,15},{10,... | collective-permute-start | bytes 1277960 | tf_op jit(solution)/shard_map/ppermute | solution.py:437
  47.7 19.2 %collective-permute-start.12 = (bf16[1664,128]{1,0:T(8,128)(2,1)S(1)}, bf16[1664,128]{1,0:T(8,128)(2,1)S(1)}, u32[]{:S(2)}, u32[]{:S(2)}) collective-permute-start(bf16[1664,128]{1,0:T(8,128)(2,1)S(1)} %get-tuple-element.72), channel_id=1, source_target_pairs={{0,4},{1,5},{2,6},{3,7},{4,0},{5,1},{6,2},{7,3},{8,12},{9,13},{10,... | collective-permute-start | bytes 1277960 | tf_op jit(solution)/shard_map/ppermute | solution.py:437
  49.1 17.9 %collective-permute-start.13 = (bf16[1664,128]{1,0:T(8,128)(2,1)S(1)}, bf16[1664,128]{1,0:T(8,128)(2,1)S(1)}, u32[]{:S(2)}, u32[]{:S(2)}) collective-permute-start(bf16[1664,128]{1,0:T(8,128)(2,1)S(1)} %get-tuple-element.73), channel_id=1, source_target_pairs={{0,2},{1,3},{2,0},{3,1},{4,6},{5,7},{6,4},{7,5},{8,10},{9,11},{10,... | collective-permute-start | bytes 1277960 | tf_op jit(solution)/shard_map/ppermute | solution.py:437
  54.5 14.6 %collective-permute-start.4 = (bf16[832,128]{1,0:T(8,128)(2,1)S(1)}, bf16[832,128]{1,0:T(8,128)(2,1)S(1)}, u32[]{:S(2)}, u32[]{:S(2)}) collective-permute-start(bf16[832,128]{1,0:T(8,128)(2,1)S(1)} %columns_of.11), channel_id=1, source_target_pairs={{0,8},{8,24},{24,16},{16,0},{1,9},{9,25},{25,17},{17,1},{2,10},{10... | collective-permute-start | bytes 638984 | tf_op jit(solution)/shard_map/ppermute | solution.py:446
  56.6 15.1 %collective-permute-start.10 = (bf16[832,128]{1,0:T(8,128)(2,1)S(1)}, bf16[832,128]{1,0:T(8,128)(2,1)S(1)}, u32[]{:S(2)}, u32[]{:S(2)}) collective-permute-start(bf16[832,128]{1,0:T(8,128)(2,1)S(1)} %collective-permute-done.3.refs_0_), channel_id=1, source_target_pairs={{0,8},{8,24},{24,16},{16,0},{1,9},{9,25},{25,17},{17,1},{2,10},{10... | collective-permute-start | bytes 638984 | tf_op jit(solution)/shard_map/ppermute | solution.py:463
  58.7 13.0 %collective-permute-start.14 = (bf16[832,128]{1,0:T(8,128)(2,1)S(1)}, bf16[832,128]{1,0:T(8,128)(2,1)S(1)}, u32[]{:S(2)}, u32[]{:S(2)}) collective-permute-start(bf16[832,128]{1,0:T(8,128)(2,1)S(1)} %rows_of.5), channel_id=1, source_target_pairs={{8,0},{24,8},{16,24},{0,16},{9,1},{25,9},{17,25},{1,17},{10,2},{26... | collective-permute-start | bytes 638984 | tf_op jit(solution)/shard_map/ppermute | solution.py:464
  67.4 8.5 %collective-permute-start.15 = (bf16[832,128]{1,0:T(8,128)(2,1)S(1)}, bf16[832,128]{1,0:T(8,128)(2,1)S(1)}, u32[]{:S(2)}, u32[]{:S(2)}) collective-permute-start(bf16[832,128]{1,0:T(8,128)(2,1)S(1)} %get-tuple-element.78), channel_id=1, source_target_pairs={{0,8},{8,24},{24,16},{16,0},{1,9},{9,25},{25,17},{17,1},{2,10},{10... | collective-permute-start | bytes 638984 | tf_op jit(solution)/shard_map/ppermute | solution.py:446
  77.8 12.1 %collective-permute-start.25 = (bf16[1664,128]{1,0:T(8,128)(2,1)S(1)}, bf16[1664,128]{1,0:T(8,128)(2,1)S(1)}, u32[]{:S(2)}, u32[]{:S(2)}) collective-permute-start(bf16[1664,128]{1,0:T(8,128)(2,1)S(1)} %get-tuple-element.77.refs_0_.refs_5_), channel_id=1, source_target_pairs={{8,0},{24,8},{16,24},{0,16},{9,1},{25,9},{17,25},{1,17},{10,2},{26... | collective-permute-start | bytes 1277960 | tf_op jit(solution)/shard_map/ppermute | solution.py:447
  79.2 14.0 %collective-permute-start.18 = (bf16[1664,128]{1,0:T(8,128)(2,1)S(1)}, bf16[1664,128]{1,0:T(8,128)(2,1)S(1)}, u32[]{:S(2)}, u32[]{:S(2)}) collective-permute-start(bf16[1664,128]{1,0:T(8,128)(2,1)S(1)} %summed.11), channel_id=1, source_target_pairs={{0,6},{1,7},{2,4},{3,5},{4,2},{5,3},{6,0},{7,1},{8,14},{9,15},{10,... | collective-permute-start | bytes 1277960 | tf_op jit(solution)/shard_map/ppermute | solution.py:437
  82.7 19.0 %collective-permute-start.19 = (bf16[1664,128]{1,0:T(8,128)(2,1)S(1)}, bf16[1664,128]{1,0:T(8,128)(2,1)S(1)}, u32[]{:S(2)}, u32[]{:S(2)}) collective-permute-start(bf16[1664,128]{1,0:T(8,128)(2,1)S(1)} %get-tuple-element.89), channel_id=1, source_target_pairs={{0,4},{1,5},{2,6},{3,7},{4,0},{5,1},{6,2},{7,3},{8,12},{9,13},{10,... | collective-permute-start | bytes 1277960 | tf_op jit(solution)/shard_map/ppermute | solution.py:437
  82.8 18.9 %collective-permute-start.20 = (bf16[1664,128]{1,0:T(8,128)(2,1)S(1)}, bf16[1664,128]{1,0:T(8,128)(2,1)S(1)}, u32[]{:S(2)}, u32[]{:S(2)}) collective-permute-start(bf16[1664,128]{1,0:T(8,128)(2,1)S(1)} %get-tuple-element.90), channel_id=1, source_target_pairs={{0,2},{1,3},{2,0},{3,1},{4,6},{5,7},{6,4},{7,5},{8,10},{9,11},{10,... | collective-permute-start | bytes 1277960 | tf_op jit(solution)/shard_map/ppermute | solution.py:437
  88.0 15.7 %collective-permute-start.24 = (bf16[832,128]{1,0:T(8,128)(2,1)S(1)}, bf16[832,128]{1,0:T(8,128)(2,1)S(1)}, u32[]{:S(2)}, u32[]{:S(2)}) collective-permute-start(bf16[832,128]{1,0:T(8,128)(2,1)S(1)} %get-tuple-element.79), channel_id=1, source_target_pairs={{0,8},{8,24},{24,16},{16,0},{1,9},{9,25},{25,17},{17,1},{2,10},{10... | collective-permute-start | bytes 638984 | tf_op jit(solution)/shard_map/ppermute | solution.py:446
  89.9 16.3 %collective-permute-start.26 = (bf16[832,128]{1,0:T(8,128)(2,1)S(1)}, bf16[832,128]{1,0:T(8,128)(2,1)S(1)}, u32[]{:S(2)}, u32[]{:S(2)}) collective-permute-start(bf16[832,128]{1,0:T(8,128)(2,1)S(1)} %collective-permute-done.15.refs_0_), channel_id=1, source_target_pairs={{0,8},{8,24},{24,16},{16,0},{1,9},{9,25},{25,17},{17,1},{2,10},{10... | collective-permute-start | bytes 638984 | tf_op jit(solution)/shard_map/ppermute | solution.py:463
  93.2 13.0 %collective-permute-start.27 = (bf16[832,128]{1,0:T(8,128)(2,1)S(1)}, bf16[832,128]{1,0:T(8,128)(2,1)S(1)}, u32[]{:S(2)}, u32[]{:S(2)}) collective-permute-start(bf16[832,128]{1,0:T(8,128)(2,1)S(1)} %rows_of.6), channel_id=1, source_target_pairs={{8,0},{24,8},{16,24},{0,16},{9,1},{25,9},{17,25},{1,17},{10,2},{26... | collective-permute-start | bytes 638984 | tf_op jit(solution)/shard_map/ppermute | solution.py:464
  112.1 12.2 %collective-permute-start.23 = (bf16[1664,128]{1,0:T(8,128)(2,1)S(1)}, bf16[1664,128]{1,0:T(8,128)(2,1)S(1)}, u32[]{:S(2)}, u32[]{:S(2)}) collective-permute-start(bf16[1664,128]{1,0:T(8,128)(2,1)S(1)} %get-tuple-element.91.refs_0_), channel_id=1, source_target_pairs={{8,0},{24,8},{16,24},{0,16},{9,1},{25,9},{17,25},{1,17},{10,2},{26... | collective-permute-start | bytes 1277960 | tf_op jit(solution)/shard_map/ppermute | solution.py:447
  113.3 22.7 %collective-permute-start.31 = (bf16[1664,128]{1,0:T(8,128)(2,1)S(1)}, bf16[1664,128]{1,0:T(8,128)(2,1)S(1)}, u32[]{:S(2)}, u32[]{:S(2)}) collective-permute-start(bf16[1664,128]{1,0:T(8,128)(2,1)S(1)} %summed.14), channel_id=1, source_target_pairs={{0,6},{1,7},{2,4},{3,5},{4,2},{5,3},{6,0},{7,1},{8,14},{9,15},{10,... | collective-permute-start | bytes 1277960 | tf_op jit(solution)/shard_map/ppermute | solution.py:437
  116.2 19.8 %collective-permute-start.32 = (bf16[1664,128]{1,0:T(8,128)(2,1)S(1)}, bf16[1664,128]{1,0:T(8,128)(2,1)S(1)}, u32[]{:S(2)}, u32[]{:S(2)}) collective-permute-start(bf16[1664,128]{1,0:T(8,128)(2,1)S(1)} %get-tuple-element.102), channel_id=1, source_target_pairs={{0,4},{1,5},{2,6},{3,7},{4,0},{5,1},{6,2},{7,3},{8,12},{9,13},{10,... | collective-permute-start | bytes 1277960 | tf_op jit(solution)/shard_map/ppermute | solution.py:437
  116.3 19.7 %collective-permute-start.33 = (bf16[1664,128]{1,0:T(8,128)(2,1)S(1)}, bf16[1664,128]{1,0:T(8,128)(2,1)S(1)}, u32[]{:S(2)}, u32[]{:S(2)}) collective-permute-start(bf16[1664,128]{1,0:T(8,128)(2,1)S(1)} %get-tuple-element.103), channel_id=1, source_target_pairs={{0,2},{1,3},{2,0},{3,1},{4,6},{5,7},{6,4},{7,5},{8,10},{9,11},{10,... | collective-permute-start | bytes 1277960 | tf_op jit(solution)/shard_map/ppermute | solution.py:437
  118.5 11.3 %collective-permute-start.22 = (bf16[832,128]{1,0:T(8,128)(2,1)S(1)}, bf16[832,128]{1,0:T(8,128)(2,1)S(1)}, u32[]{:S(2)}, u32[]{:S(2)}) collective-permute-start(bf16[832,128]{1,0:T(8,128)(2,1)S(1)} %get-tuple-element.93.refs_9_), channel_id=1, source_target_pairs={{0,8},{8,24},{24,16},{16,0},{1,9},{9,25},{25,17},{17,1},{2,10},{10... | collective-permute-start | bytes 638984 | tf_op jit(solution)/shard_map/ppermute | solution.py:446
  124.3 13.1 %collective-permute-start.30 = (bf16[832,128]{1,0:T(8,128)(2,1)S(1)}, bf16[832,128]{1,0:T(8,128)(2,1)S(1)}, u32[]{:S(2)}, u32[]{:S(2)}) collective-permute-start(bf16[832,128]{1,0:T(8,128)(2,1)S(1)} %collective-permute-done.21.refs_0_), channel_id=1, source_target_pairs={{0,8},{8,24},{24,16},{16,0},{1,9},{9,25},{25,17},{17,1},{2,10},{10... | collective-permute-start | bytes 638984 | tf_op jit(solution)/shard_map/ppermute | solution.py:463
  129.8 9.0 %collective-permute-start.34 = (bf16[832,128]{1,0:T(8,128)(2,1)S(1)}, bf16[832,128]{1,0:T(8,128)(2,1)S(1)}, u32[]{:S(2)}, u32[]{:S(2)}) collective-permute-start(bf16[832,128]{1,0:T(8,128)(2,1)S(1)} %rows_of.7), channel_id=1, source_target_pairs={{8,0},{24,8},{16,24},{0,16},{9,1},{25,9},{17,25},{1,17},{10,2},{26... | collective-permute-start | bytes 638984 | tf_op jit(solution)/shard_map/ppermute | solution.py:464
  142.6 8.6 %collective-permute-start.37 = (bf16[4992,128]{1,0:T(8,128)(2,1)S(1)}, bf16[4992,128]{1,0:T(8,128)(2,1)S(1)}, u32[]{:S(2)}, u32[]{:S(2)}) collective-permute-start(bf16[4992,128]{1,0:T(8,128)(2,1)S(1)} %get-tuple-element.115), channel_id=1, source_target_pairs={{0,1},{1,0},{2,3},{3,2},{4,5},{5,4},{6,7},{7,6},{8,9},{9,8},{10,11... | collective-permute-start | bytes 3833864 | tf_op jit(solution)/shard_map/ppermute | solution.py:434
  151.4 8.2 %collective-permute-start.41 = (bf16[832,128]{1,0:T(8,128)(2,1)S(1)}, bf16[832,128]{1,0:T(8,128)(2,1)S(1)}, u32[]{:S(2)}, u32[]{:S(2)}) collective-permute-start(bf16[832,128]{1,0:T(8,128)(2,1)S(1)} %get-tuple-element.120), channel_id=1, source_target_pairs={{0,4},{1,5},{2,6},{3,7},{4,0},{5,1},{6,2},{7,3},{8,12},{9,13},{10,... | collective-permute-start | bytes 638984 | tf_op jit(solution)/shard_map/ppermute | solution.py:437
  153.7 9.4 %collective-permute-start.38 = (bf16[832,128]{1,0:T(8,128)(2,1)S(1)}, bf16[832,128]{1,0:T(8,128)(2,1)S(1)}, u32[]{:S(2)}, u32[]{:S(2)}) collective-permute-start(bf16[832,128]{1,0:T(8,128)(2,1)S(1)} %get-tuple-element.116), channel_id=1, source_target_pairs={{0,2},{1,3},{2,0},{3,1},{4,6},{5,7},{6,4},{7,5},{8,10},{9,11},{10,... | collective-permute-start | bytes 638984 | tf_op jit(solution)/shard_map/ppermute | solution.py:437
  154.6 8.5 %collective-permute-start.43 = (bf16[832,128]{1,0:T(8,128)(2,1)S(1)}, bf16[832,128]{1,0:T(8,128)(2,1)S(1)}, u32[]{:S(2)}, u32[]{:S(2)}) collective-permute-start(bf16[832,128]{1,0:T(8,128)(2,1)S(1)} %get-tuple-element.122), channel_id=1, source_target_pairs={{0,4},{1,5},{2,6},{3,7},{4,0},{5,1},{6,2},{7,3},{8,12},{9,13},{10,... | collective-permute-start | bytes 638984 | tf_op jit(solution)/shard_map/ppermute | solution.py:437
  (17 other events, 64.8 us)

commit v7 on v6

--- a/solution.py
+++ b/solution.py
@@ -482,6 +482,7 @@
         by_x, by_y = to_chip(corner[0], 1), to_chip(corner[1], 2)
         sides = summed([[(top, both(x))], [(rest, both(y + top))]])
         x_top, y_rest = to_chip(sides[0], 1), to_chip(sides[1], 2)
+        by_y = tied(by_y, [x_top])
         joined = summed(
             [[(rest, both(x + top, (by_y, 0)))], [(top, both(y, (by_x, 0)))]]
         )

time: 168 us -> 171 us (1.018)
  waiting for transfers between devices: 64.9 us -> 68.1 us
    ppermute x10, waiting for transfers between devices: 9.87 us -> 12.5 us  [to_core(): return lax.ppermute(array, 'col', other_core)]
    pallas_call x4, Pallas kernels: 10 us -> 8.13 us  [early_images(): pl.pallas_call(kernel, out_shape=pltpu.VMEM(total, jnp.float32), in_specs...]
    pallas_call x4, Pallas kernels: 7.9 us -> 9.8 us  [last_images(): pl.pallas_call(kernel, out_shape=[pltpu.VMEM(early.shape, jnp.float32), *...]
  transfers between devices with their start and end apart: 45 -> 45, of which waited for: 27 -> 28; matrix products, arithmetic and copies ran while one was open for 3% -> 3% of each run, Pallas kernels for 19% -> 19%
where the time goes in v7:
time: 171 us
  waiting for transfers between devices  68.1 us (40%)
  starting transfers between devices  50.3 us (29%)
  Pallas kernels  37.4 us (22%)
  local copies, waits for them, and re-layouts  8.29 us (5%)
  other arithmetic  3.23 us (2%)
  between operations  3.19 us (2%)
    ppermute x15, waiting for transfers between devices, to_chip(): lax.ppermute(array, 'col', [(i, i ^ 2 * chip) for i in range(col_count)])  25 us
    ppermute x15, starting transfers between devices, to_chip(): lax.ppermute(array, 'col', [(i, i ^ 2 * chip) for i in range(col_count)])  22.4 us
    ppermute x10, waiting for transfers between devices, to_core(): return lax.ppermute(array, 'col', other_core)  12.5 us
    ppermute x8, waiting for transfers between devices, __init__(): upper, lower = (lax.ppermute(half, 'row', route) for half in (upper, lower))  11.8 us
    pallas_call x4, Pallas kernels, middle_images(): pl.pallas_call(kernel, out_shape=pltpu.VMEM(early.shape, jnp.float32), in...  10.3 us
    ppermute x4, waiting for transfers between devices, __init__(): self.early = [part, upper, lower, lax.ppermute(part, 'row', back_route)]  9.82 us
    pallas_call x4, Pallas kernels, last_images(): pl.pallas_call(kernel, out_shape=[pltpu.VMEM(early.shape, jnp.float32), *...  9.8 us
    pallas_call x4, Pallas kernels, early_images(): pl.pallas_call(kernel, out_shape=pltpu.VMEM(total, jnp.float32), in_specs...  8.13 us
  transfers between devices with their start and end apart: 45, of which 28 were waited for; matrix products, arithmetic and copies ran while one was open for 3% of the time, Pallas kernels for 19%

profile of v7, /device:TPU:0, one launch (start us, length us, event | category | flops | bytes accessed | tf_op | source)
XLA Modules:
  0.0 170.6 jit_solution(319363808093312550)
XLA Ops:
  1.2 4.1 %collective-permute-start.2 = (bf16[1664,128]{1,0:T(8,128)(2,1)S(1)}, bf16[1664,128]{1,0:T(8,128)(2,1)S(1)}, u32[]{:S(2)}, u32[]{:S(2)}) collective-permute-start(bf16[1664,128]{1,0:T(8,128)(2,1)S(1)} %columns_of.6.refs_0_), channel_id=1, source_target_pairs={{8,0},{24,8},{16,24},{0,16},{9,1},{25,9},{17,25},{1,17},{10,2},{26... | collective-permute-start | bytes 1277960 | tf_op jit(solution)/shard_map/ppermute | solution.py:447
  15.8 3.4 %copy-done.3 = bf16[1,1,256,128,128]{4,3,2,1,0:T(8,128)(2,1)S(1)} copy-done((bf16[1,1,256,128,128]{4,3,2,1,0:T(8,128)(2,1)S(1)}, bf16[1,1,256,128,128]{4,3,2,1,0:T(8,128)(2,1)}, u32[]{:S(2)}) %copy-start.3) | copy-done | bytes 8388632
  19.7 2.0 %early_images.4.early = f32[13440,128]{1,0:T(8,128)S(1)} custom-call(s32[9]{0:T(128)S(1)} %concatenate.3.refs_0_.bounds.edges_ref, s32[288]{0:T(512)S(1)} %pad.10.refs_1_.order, s32[288]{0:T(512)S(1)} %pad.11.refs_2_.rows, s32[288]{0:T(512)S(1)} %pad.12.refs_3_.cols, bf16[256,128,128]{2,1,0:T(8,128)(2,1)S(1)} %resident.1.values, ...), custom_call_target="tpu_custom_call" | custom-call | tf_op jit(solution)/shard_map/early_images/pallas_call | solution.py:132
  21.8 3.6 %collective-permute-done.refs_0_ = bf16[832,128]{1,0:T(8,128)(2,1)S(1)} collective-permute-done((bf16[832,128]{1,0:T(8,128)(2,1)S(1)}, bf16[832,128]{1,0:T(8,128)(2,1)S(1)}, u32[]{:S(2)}, u32[]{:S(2)}) %collective-permute-start) | collective-permute-done | bytes 213024 | tf_op jit(solution)/shard_map/ppermute | solution.py:446
  26.1 2.3 %collective-permute-start.7 = (bf16[832,128]{1,0:T(8,128)(2,1)S(1)}, bf16[832,128]{1,0:T(8,128)(2,1)S(1)}, u32[]{:S(2)}, u32[]{:S(2)}) collective-permute-start(bf16[832,128]{1,0:T(8,128)(2,1)S(1)} %rows_of.4), channel_id=1, source_target_pairs={{8,0},{24,8},{16,24},{0,16},{9,1},{25,9},{17,25},{1,17},{10,2},{26... | collective-permute-start | bytes 638984 | tf_op jit(solution)/shard_map/ppermute | solution.py:464
  28.4 2.6 %middle_images.4.refs_0_.early = f32[13440,128]{1,0:T(8,128)S(1)} custom-call(s32[9]{0:T(128)S(1)} %concatenate.3.refs_0_.bounds.edges_ref, s32[288]{0:T(512)S(1)} %pad.10.refs_1_.order, s32[288]{0:T(512)S(1)} %pad.11.refs_2_.rows, s32[288]{0:T(512)S(1)} %pad.12.refs_3_.cols, ...), custom_call_target="tpu_custom_call", output_to_operand_aliasing={{}: (5, {})} | custom-call | tf_op jit(solution)/shard_map/middle_images/pallas_call | solution.py:152
  31.4 6.3 %collective-permute-done.6.refs_0_ = bf16[832,128]{1,0:T(8,128)(2,1)S(1)} collective-permute-done((bf16[832,128]{1,0:T(8,128)(2,1)S(1)}, bf16[832,128]{1,0:T(8,128)(2,1)S(1)}, u32[]{:S(2)}, u32[]{:S(2)}) %collective-permute-start.6) | collective-permute-done | bytes 213024 | tf_op jit(solution)/shard_map/ppermute | solution.py:463
  38.4 2.4 %last_images.4 = (f32[13440,128]{1,0:T(8,128)S(1)}, bf16[1664,128]{1,0:T(8,128)(2,1)S(1)}, bf16[1664,128]{1,0:T(8,128)(2,1)S(1)}, bf16[4992,128]{1,0:T(8,128)(2,1)S(1)}, bf16[4992,128]{1,0:T(8,128)(2,1)S(1)}) custom-call(s32[9]{0:T(128)S(1)} %concatenate.3.refs_0_.bounds.edges_ref, s32[288]{0:T(512)S(1)} %pad.10.refs_1_.order, ...), custom_call_target="tpu_custom_call", output_to_operand_aliasing={{0}: (5, {})} | custom-call | tf_op jit(solution)/shard_map/last_images/pallas_call | solution.py:189
  45.0 2.5 %collective-permute-start.11 = (bf16[1664,128]{1,0:T(8,128)(2,1)S(1)}, bf16[1664,128]{1,0:T(8,128)(2,1)S(1)}, u32[]{:S(2)}, u32[]{:S(2)}) collective-permute-start(bf16[1664,128]{1,0:T(8,128)(2,1)S(1)} %summed.10), channel_id=1, source_target_pairs={{0,6},{1,7},{2,4},{3,5},{4,2},{5,3},{6,0},{7,1},{8,14},{9,15},{10,... | collective-permute-start | bytes 1277960 | tf_op jit(solution)/shard_map/ppermute | solution.py:437
  51.9 2.0 %early_images.5.early = f32[13440,128]{1,0:T(8,128)S(1)} custom-call(s32[9]{0:T(128)S(1)} %concatenate.3.refs_0_.bounds.edges_ref, s32[288]{0:T(512)S(1)} %pad.10.refs_1_.order, s32[288]{0:T(512)S(1)} %pad.11.refs_2_.rows, s32[288]{0:T(512)S(1)} %pad.12.refs_3_.cols, bf16[256,128,128]{2,1,0:T(8,128)(2,1)S(1)} %resident.1.values, ...), custom_call_target="tpu_custom_call" | custom-call | tf_op jit(solution)/shard_map/early_images/pallas_call | solution.py:132
  54.3 2.3 %collective-permute-done.5.refs_2_.array_ref = bf16[1664,128]{1,0:T(8,128)(2,1)S(1)} collective-permute-done((bf16[1664,128]{1,0:T(8,128)(2,1)S(1)}, bf16[1664,128]{1,0:T(8,128)(2,1)S(1)}, u32[]{:S(2)}, u32[]{:S(2)}) %collective-permute-start.5) | collective-permute-done | bytes 426016 | tf_op jit(solution)/shard_map/ppermute | solution.py:447
  58.7 2.6 %collective-permute-start.14 = (bf16[832,128]{1,0:T(8,128)(2,1)S(1)}, bf16[832,128]{1,0:T(8,128)(2,1)S(1)}, u32[]{:S(2)}, u32[]{:S(2)}) collective-permute-start(bf16[832,128]{1,0:T(8,128)(2,1)S(1)} %rows_of.5), channel_id=1, source_target_pairs={{8,0},{24,8},{16,24},{0,16},{9,1},{25,9},{17,25},{1,17},{10,2},{26... | collective-permute-start | bytes 638984 | tf_op jit(solution)/shard_map/ppermute | solution.py:464
  61.3 5.6 %collective-permute-done.12.refs_3_ = bf16[1664,128]{1,0:T(8,128)(2,1)S(1)} collective-permute-done((bf16[1664,128]{1,0:T(8,128)(2,1)S(1)}, bf16[1664,128]{1,0:T(8,128)(2,1)S(1)}, u32[]{:S(2)}, u32[]{:S(2)}) %collective-permute-start.12) | collective-permute-done | bytes 426016 | tf_op jit(solution)/shard_map/ppermute | solution.py:437
  69.1 2.6 %middle_images.5.early = f32[13440,128]{1,0:T(8,128)S(1)} custom-call(s32[9]{0:T(128)S(1)} %concatenate.3.refs_0_.bounds.edges_ref, s32[288]{0:T(512)S(1)} %pad.10.refs_1_.order, s32[288]{0:T(512)S(1)} %pad.11.refs_2_.rows, s32[288]{0:T(512)S(1)} %pad.12.refs_3_.cols, bf16[256,128,128]{2,1,0:T(8,128)(2,1)S(1)} %resident.1.values, ...), custom_call_target="tpu_custom_call", output_to_operand_aliasing={{}: (5, {})} | custom-call | tf_op jit(solution)/shard_map/middle_images/pallas_call | solution.py:152
  71.7 2.4 %last_images.5 = (f32[13440,128]{1,0:T(8,128)S(1)}, bf16[1664,128]{1,0:T(8,128)(2,1)S(1)}, bf16[1664,128]{1,0:T(8,128)(2,1)S(1)}, bf16[4992,128]{1,0:T(8,128)(2,1)S(1)}, bf16[4992,128]{1,0:T(8,128)(2,1)S(1)}) custom-call(s32[9]{0:T(128)S(1)} %concatenate.3.refs_0_.bounds.edges_ref, s32[288]{0:T(512)S(1)} %pad.10.refs_1_.order, ...), custom_call_target="tpu_custom_call", output_to_operand_aliasing={{0}: (5, {})} | custom-call | tf_op jit(solution)/shard_map/last_images/pallas_call | solution.py:189
  79.2 3.3 %collective-permute-start.18 = (bf16[1664,128]{1,0:T(8,128)(2,1)S(1)}, bf16[1664,128]{1,0:T(8,128)(2,1)S(1)}, u32[]{:S(2)}, u32[]{:S(2)}) collective-permute-start(bf16[1664,128]{1,0:T(8,128)(2,1)S(1)} %summed.11), channel_id=1, source_target_pairs={{0,6},{1,7},{2,4},{3,5},{4,2},{5,3},{6,0},{7,1},{8,14},{9,15},{10,... | collective-permute-start | bytes 1277960 | tf_op jit(solution)/shard_map/ppermute | solution.py:437
  82.8 2.7 %collective-permute-start.20 = (bf16[1664,128]{1,0:T(8,128)(2,1)S(1)}, bf16[1664,128]{1,0:T(8,128)(2,1)S(1)}, u32[]{:S(2)}, u32[]{:S(2)}) collective-permute-start(bf16[1664,128]{1,0:T(8,128)(2,1)S(1)} %get-tuple-element.91), channel_id=1, source_target_pairs={{0,2},{1,3},{2,0},{3,1},{4,6},{5,7},{6,4},{7,5},{8,10},{9,11},{10,... | collective-permute-start | bytes 1277960 | tf_op jit(solution)/shard_map/ppermute | solution.py:437
  85.5 2.0 %early_images.6.early = f32[13440,128]{1,0:T(8,128)S(1)} custom-call(s32[9]{0:T(128)S(1)} %concatenate.3.refs_0_.bounds.edges_ref, s32[288]{0:T(512)S(1)} %pad.10.refs_1_.order, s32[288]{0:T(512)S(1)} %pad.11.refs_2_.rows, s32[288]{0:T(512)S(1)} %pad.12.refs_3_.cols, bf16[256,128,128]{2,1,0:T(8,128)(2,1)S(1)} %resident.1.values, ...), custom_call_target="tpu_custom_call" | custom-call | tf_op jit(solution)/shard_map/early_images/pallas_call | solution.py:132
  95.1 6.6 %collective-permute-done.19.refs_3_ = bf16[1664,128]{1,0:T(8,128)(2,1)S(1)} collective-permute-done((bf16[1664,128]{1,0:T(8,128)(2,1)S(1)}, bf16[1664,128]{1,0:T(8,128)(2,1)S(1)}, u32[]{:S(2)}, u32[]{:S(2)}) %collective-permute-start.19) | collective-permute-done | bytes 426016 | tf_op jit(solution)/shard_map/ppermute | solution.py:437
  103.6 2.6 %middle_images.7.early = f32[13440,128]{1,0:T(8,128)S(1)} custom-call(s32[9]{0:T(128)S(1)} %concatenate.3.refs_0_.bounds.edges_ref, s32[288]{0:T(512)S(1)} %pad.10.refs_1_.order, s32[288]{0:T(512)S(1)} %pad.11.refs_2_.rows, s32[288]{0:T(512)S(1)} %pad.12.refs_3_.cols, bf16[256,128,128]{2,1,0:T(8,128)(2,1)S(1)} %resident.1.values, ...), custom_call_target="tpu_custom_call", output_to_operand_aliasing={{}: (5, {})} | custom-call | tf_op jit(solution)/shard_map/middle_images/pallas_call | solution.py:152
  106.2 2.6 %last_images.6 = (f32[13440,128]{1,0:T(8,128)S(1)}, bf16[1664,128]{1,0:T(8,128)(2,1)S(1)}, bf16[1664,128]{1,0:T(8,128)(2,1)S(1)}, bf16[4992,128]{1,0:T(8,128)(2,1)S(1)}, bf16[4992,128]{1,0:T(8,128)(2,1)S(1)}) custom-call(s32[9]{0:T(128)S(1)} %concatenate.3.refs_0_.bounds.edges_ref, s32[288]{0:T(512)S(1)} %pad.10.refs_1_.order, ...), custom_call_target="tpu_custom_call", output_to_operand_aliasing={{0}: (5, {})} | custom-call | tf_op jit(solution)/shard_map/last_images/pallas_call | solution.py:189
  113.3 2.7 %collective-permute-start.31 = (bf16[1664,128]{1,0:T(8,128)(2,1)S(1)}, bf16[1664,128]{1,0:T(8,128)(2,1)S(1)}, u32[]{:S(2)}, u32[]{:S(2)}) collective-permute-start(bf16[1664,128]{1,0:T(8,128)(2,1)S(1)} %summed.14), channel_id=1, source_target_pairs={{0,6},{1,7},{2,4},{3,5},{4,2},{5,3},{6,0},{7,1},{8,14},{9,15},{10,... | collective-permute-start | bytes 1277960 | tf_op jit(solution)/shard_map/ppermute | solution.py:437
  116.3 2.2 %collective-permute-start.33 = (bf16[1664,128]{1,0:T(8,128)(2,1)S(1)}, bf16[1664,128]{1,0:T(8,128)(2,1)S(1)}, u32[]{:S(2)}, u32[]{:S(2)}) collective-permute-start(bf16[1664,128]{1,0:T(8,128)(2,1)S(1)} %get-tuple-element.104), channel_id=1, source_target_pairs={{0,2},{1,3},{2,0},{3,1},{4,6},{5,7},{6,4},{7,5},{8,10},{9,11},{10,... | collective-permute-start | bytes 1277960 | tf_op jit(solution)/shard_map/ppermute | solution.py:437
  118.7 5.7 %collective-permute-done.23.refs_2_.array_ref = bf16[1664,128]{1,0:T(8,128)(2,1)S(1)} collective-permute-done((bf16[1664,128]{1,0:T(8,128)(2,1)S(1)}, bf16[1664,128]{1,0:T(8,128)(2,1)S(1)}, u32[]{:S(2)}, u32[]{:S(2)}) %collective-permute-start.23) | collective-permute-done | bytes 426016 | tf_op jit(solution)/shard_map/ppermute | solution.py:447
  126.3 3.5 %collective-permute-done.22.refs_1_ = bf16[832,128]{1,0:T(8,128)(2,1)S(1)} collective-permute-done((bf16[832,128]{1,0:T(8,128)(2,1)S(1)}, bf16[832,128]{1,0:T(8,128)(2,1)S(1)}, u32[]{:S(2)}, u32[]{:S(2)}) %collective-permute-start.22) | collective-permute-done | bytes 213024 | tf_op jit(solution)/shard_map/ppermute | solution.py:446
  130.9 2.0 %early_images.7.early = f32[13440,128]{1,0:T(8,128)S(1)} custom-call(s32[9]{0:T(128)S(1)} %concatenate.3.refs_0_.bounds.edges_ref, s32[288]{0:T(512)S(1)} %pad.10.refs_1_.order, s32[288]{0:T(512)S(1)} %pad.11.refs_2_.rows, s32[288]{0:T(512)S(1)} %pad.12.refs_3_.cols, bf16[256,128,128]{2,1,0:T(8,128)(2,1)S(1)} %resident.1.values, ...), custom_call_target="tpu_custom_call" | custom-call | tf_op jit(solution)/shard_map/early_images/pallas_call | solution.py:132
  132.9 2.6 %middle_images.6.early = f32[13440,128]{1,0:T(8,128)S(1)} custom-call(s32[9]{0:T(128)S(1)} %concatenate.3.refs_0_.bounds.edges_ref, s32[288]{0:T(512)S(1)} %pad.10.refs_1_.order, s32[288]{0:T(512)S(1)} %pad.11.refs_2_.rows, s32[288]{0:T(512)S(1)} %pad.12.refs_3_.cols, bf16[256,128,128]{2,1,0:T(8,128)(2,1)S(1)} %resident.1.values, ...), custom_call_target="tpu_custom_call", output_to_operand_aliasing={{}: (5, {})} | custom-call | tf_op jit(solution)/shard_map/middle_images/pallas_call | solution.py:152
  138.8 2.4 %last_images.7 = (f32[13440,128]{1,0:T(8,128)S(1)}, bf16[1664,128]{1,0:T(8,128)(2,1)S(1)}, bf16[1664,128]{1,0:T(8,128)(2,1)S(1)}, bf16[4992,128]{1,0:T(8,128)(2,1)S(1)}, bf16[4992,128]{1,0:T(8,128)(2,1)S(1)}) custom-call(s32[9]{0:T(128)S(1)} %concatenate.3.refs_0_.bounds.edges_ref, s32[288]{0:T(512)S(1)} %pad.10.refs_1_.order, ...), custom_call_target="tpu_custom_call", output_to_operand_aliasing={{0}: (5, {})} | custom-call | tf_op jit(solution)/shard_map/last_images/pallas_call | solution.py:189
  143.4 2.7 %collective-permute-done.37.refs_1_.refs_3_.refs_4_.refs_5_ = bf16[4992,128]{1,0:T(8,128)(2,1)S(1)} collective-permute-done((bf16[4992,128]{1,0:T(8,128)(2,1)S(1)}, bf16[4992,128]{1,0:T(8,128)(2,1)S(1)}, u32[]{:S(2)}, u32[]{:S(2)}) %collective-permute-start.37) | collective-permute-done | bytes 1277984 | tf_op jit(solution)/shard_map/ppermute | solution.py:434
  149.2 2.2 %collective-permute-done.39.refs_2_ = bf16[832,128]{1,0:T(8,128)(2,1)S(1)} collective-permute-done((bf16[832,128]{1,0:T(8,128)(2,1)S(1)}, bf16[832,128]{1,0:T(8,128)(2,1)S(1)}, u32[]{:S(2)}, u32[]{:S(2)}) %collective-permute-start.39) | collective-permute-done | bytes 213024 | tf_op jit(solution)/shard_map/ppermute | solution.py:437
  151.3 3.0 %collective-permute-done.38.refs_2_ = bf16[832,128]{1,0:T(8,128)(2,1)S(1)} collective-permute-done((bf16[832,128]{1,0:T(8,128)(2,1)S(1)}, bf16[832,128]{1,0:T(8,128)(2,1)S(1)}, u32[]{:S(2)}, u32[]{:S(2)}) %collective-permute-start.38) | collective-permute-done | bytes 213024 | tf_op jit(solution)/shard_map/ppermute | solution.py:437
  154.3 3.8 %collective-permute-done.40.refs_5_ = bf16[832,128]{1,0:T(8,128)(2,1)S(1)} collective-permute-done((bf16[832,128]{1,0:T(8,128)(2,1)S(1)}, bf16[832,128]{1,0:T(8,128)(2,1)S(1)}, u32[]{:S(2)}, u32[]{:S(2)}) %collective-permute-start.40) | collective-permute-done | bytes 213024 | tf_op jit(solution)/shard_map/ppermute | solution.py:437
  (116 shorter events, 68.3 us)
Async XLA Ops:
  1.2 24.8 %collective-permute-start.2 = (bf16[1664,128]{1,0:T(8,128)(2,1)S(1)}, bf16[1664,128]{1,0:T(8,128)(2,1)S(1)}, u32[]{:S(2)}, u32[]{:S(2)}) collective-permute-start(bf16[1664,128]{1,0:T(8,128)(2,1)S(1)} %columns_of.6.refs_0_), channel_id=1, source_target_pairs={{8,0},{24,8},{16,24},{0,16},{9,1},{25,9},{17,25},{1,17},{10,2},{26... | collective-permute-start | bytes 1277960 | tf_op jit(solution)/shard_map/ppermute | solution.py:447
  6.6 15.2 %collective-permute-start.1 = (bf16[832,128]{1,0:T(8,128)(2,1)S(1)}, bf16[832,128]{1,0:T(8,128)(2,1)S(1)}, u32[]{:S(2)}, u32[]{:S(2)}) collective-permute-start(bf16[832,128]{1,0:T(8,128)(2,1)S(1)} %columns_of.8), channel_id=1, source_target_pairs={{0,8},{8,24},{24,16},{16,0},{1,9},{9,25},{25,17},{17,1},{2,10},{10... | collective-permute-start | bytes 638984 | tf_op jit(solution)/shard_map/ppermute | solution.py:446
  6.7 18.7 %collective-permute-start = (bf16[832,128]{1,0:T(8,128)(2,1)S(1)}, bf16[832,128]{1,0:T(8,128)(2,1)S(1)}, u32[]{:S(2)}, u32[]{:S(2)}) collective-permute-start(bf16[832,128]{1,0:T(8,128)(2,1)S(1)} %columns_of.7), channel_id=1, source_target_pairs={{0,8},{8,24},{24,16},{16,0},{1,9},{9,25},{25,17},{17,1},{2,10},{10... | collective-permute-start | bytes 638984 | tf_op jit(solution)/shard_map/ppermute | solution.py:446
  25.3 12.3 %collective-permute-start.6 = (bf16[832,128]{1,0:T(8,128)(2,1)S(1)}, bf16[832,128]{1,0:T(8,128)(2,1)S(1)}, u32[]{:S(2)}, u32[]{:S(2)}) collective-permute-start(bf16[832,128]{1,0:T(8,128)(2,1)S(1)} %collective-permute-done.refs_0_), channel_id=1, source_target_pairs={{0,8},{8,24},{24,16},{16,0},{1,9},{9,25},{25,17},{17,1},{2,10},{10... | collective-permute-start | bytes 638984 | tf_op jit(solution)/shard_map/ppermute | solution.py:463
  26.1 12.3 %collective-permute-start.7 = (bf16[832,128]{1,0:T(8,128)(2,1)S(1)}, bf16[832,128]{1,0:T(8,128)(2,1)S(1)}, u32[]{:S(2)}, u32[]{:S(2)}) collective-permute-start(bf16[832,128]{1,0:T(8,128)(2,1)S(1)} %rows_of.4), channel_id=1, source_target_pairs={{8,0},{24,8},{16,24},{0,16},{9,1},{25,9},{17,25},{1,17},{10,2},{26... | collective-permute-start | bytes 638984 | tf_op jit(solution)/shard_map/ppermute | solution.py:464
  31.0 11.6 %collective-permute-start.3 = (bf16[832,128]{1,0:T(8,128)(2,1)S(1)}, bf16[832,128]{1,0:T(8,128)(2,1)S(1)}, u32[]{:S(2)}, u32[]{:S(2)}) collective-permute-start(bf16[832,128]{1,0:T(8,128)(2,1)S(1)} %columns_of.10), channel_id=1, source_target_pairs={{0,8},{8,24},{24,16},{16,0},{1,9},{9,25},{25,17},{17,1},{2,10},{10... | collective-permute-start | bytes 638984 | tf_op jit(solution)/shard_map/ppermute | solution.py:446
  44.5 12.1 %collective-permute-start.5 = (bf16[1664,128]{1,0:T(8,128)(2,1)S(1)}, bf16[1664,128]{1,0:T(8,128)(2,1)S(1)}, u32[]{:S(2)}, u32[]{:S(2)}) collective-permute-start(bf16[1664,128]{1,0:T(8,128)(2,1)S(1)} %columns_of.9.refs_0_), channel_id=1, source_target_pairs={{8,0},{24,8},{16,24},{0,16},{9,1},{25,9},{17,25},{1,17},{10,2},{26... | collective-permute-start | bytes 1277960 | tf_op jit(solution)/shard_map/ppermute | solution.py:447
  45.0 13.7 %collective-permute-start.11 = (bf16[1664,128]{1,0:T(8,128)(2,1)S(1)}, bf16[1664,128]{1,0:T(8,128)(2,1)S(1)}, u32[]{:S(2)}, u32[]{:S(2)}) collective-permute-start(bf16[1664,128]{1,0:T(8,128)(2,1)S(1)} %summed.10), channel_id=1, source_target_pairs={{0,6},{1,7},{2,4},{3,5},{4,2},{5,3},{6,0},{7,1},{8,14},{9,15},{10,... | collective-permute-start | bytes 1277960 | tf_op jit(solution)/shard_map/ppermute | solution.py:437
  47.7 19.2 %collective-permute-start.12 = (bf16[1664,128]{1,0:T(8,128)(2,1)S(1)}, bf16[1664,128]{1,0:T(8,128)(2,1)S(1)}, u32[]{:S(2)}, u32[]{:S(2)}) collective-permute-start(bf16[1664,128]{1,0:T(8,128)(2,1)S(1)} %get-tuple-element.73), channel_id=1, source_target_pairs={{0,4},{1,5},{2,6},{3,7},{4,0},{5,1},{6,2},{7,3},{8,12},{9,13},{10,... | collective-permute-start | bytes 1277960 | tf_op jit(solution)/shard_map/ppermute | solution.py:437
  49.1 17.9 %collective-permute-start.13 = (bf16[1664,128]{1,0:T(8,128)(2,1)S(1)}, bf16[1664,128]{1,0:T(8,128)(2,1)S(1)}, u32[]{:S(2)}, u32[]{:S(2)}) collective-permute-start(bf16[1664,128]{1,0:T(8,128)(2,1)S(1)} %get-tuple-element.74), channel_id=1, source_target_pairs={{0,2},{1,3},{2,0},{3,1},{4,6},{5,7},{6,4},{7,5},{8,10},{9,11},{10,... | collective-permute-start | bytes 1277960 | tf_op jit(solution)/shard_map/ppermute | solution.py:437
  54.0 15.1 %collective-permute-start.4 = (bf16[832,128]{1,0:T(8,128)(2,1)S(1)}, bf16[832,128]{1,0:T(8,128)(2,1)S(1)}, u32[]{:S(2)}, u32[]{:S(2)}) collective-permute-start(bf16[832,128]{1,0:T(8,128)(2,1)S(1)} %columns_of.11), channel_id=1, source_target_pairs={{0,8},{8,24},{24,16},{16,0},{1,9},{9,25},{25,17},{17,1},{2,10},{10... | collective-permute-start | bytes 638984 | tf_op jit(solution)/shard_map/ppermute | solution.py:446
  56.6 15.1 %collective-permute-start.10 = (bf16[832,128]{1,0:T(8,128)(2,1)S(1)}, bf16[832,128]{1,0:T(8,128)(2,1)S(1)}, u32[]{:S(2)}, u32[]{:S(2)}) collective-permute-start(bf16[832,128]{1,0:T(8,128)(2,1)S(1)} %collective-permute-done.3.refs_0_), channel_id=1, source_target_pairs={{0,8},{8,24},{24,16},{16,0},{1,9},{9,25},{25,17},{17,1},{2,10},{10... | collective-permute-start | bytes 638984 | tf_op jit(solution)/shard_map/ppermute | solution.py:463
  58.7 13.0 %collective-permute-start.14 = (bf16[832,128]{1,0:T(8,128)(2,1)S(1)}, bf16[832,128]{1,0:T(8,128)(2,1)S(1)}, u32[]{:S(2)}, u32[]{:S(2)}) collective-permute-start(bf16[832,128]{1,0:T(8,128)(2,1)S(1)} %rows_of.5), channel_id=1, source_target_pairs={{8,0},{24,8},{16,24},{0,16},{9,1},{25,9},{17,25},{1,17},{10,2},{26... | collective-permute-start | bytes 638984 | tf_op jit(solution)/shard_map/ppermute | solution.py:464
  67.4 8.3 %collective-permute-start.15 = (bf16[832,128]{1,0:T(8,128)(2,1)S(1)}, bf16[832,128]{1,0:T(8,128)(2,1)S(1)}, u32[]{:S(2)}, u32[]{:S(2)}) collective-permute-start(bf16[832,128]{1,0:T(8,128)(2,1)S(1)} %get-tuple-element.79), channel_id=1, source_target_pairs={{0,8},{8,24},{24,16},{16,0},{1,9},{9,25},{25,17},{17,1},{2,10},{10... | collective-permute-start | bytes 638984 | tf_op jit(solution)/shard_map/ppermute | solution.py:446
  77.6 12.1 %collective-permute-start.25 = (bf16[1664,128]{1,0:T(8,128)(2,1)S(1)}, bf16[1664,128]{1,0:T(8,128)(2,1)S(1)}, u32[]{:S(2)}, u32[]{:S(2)}) collective-permute-start(bf16[1664,128]{1,0:T(8,128)(2,1)S(1)} %get-tuple-element.78.refs_0_.refs_5_), channel_id=1, source_target_pairs={{8,0},{24,8},{16,24},{0,16},{9,1},{25,9},{17,25},{1,17},{10,2},{26... | collective-permute-start | bytes 1277960 | tf_op jit(solution)/shard_map/ppermute | solution.py:447
  79.2 14.0 %collective-permute-start.18 = (bf16[1664,128]{1,0:T(8,128)(2,1)S(1)}, bf16[1664,128]{1,0:T(8,128)(2,1)S(1)}, u32[]{:S(2)}, u32[]{:S(2)}) collective-permute-start(bf16[1664,128]{1,0:T(8,128)(2,1)S(1)} %summed.11), channel_id=1, source_target_pairs={{0,6},{1,7},{2,4},{3,5},{4,2},{5,3},{6,0},{7,1},{8,14},{9,15},{10,... | collective-permute-start | bytes 1277960 | tf_op jit(solution)/shard_map/ppermute | solution.py:437
  82.7 19.0 %collective-permute-start.19 = (bf16[1664,128]{1,0:T(8,128)(2,1)S(1)}, bf16[1664,128]{1,0:T(8,128)(2,1)S(1)}, u32[]{:S(2)}, u32[]{:S(2)}) collective-permute-start(bf16[1664,128]{1,0:T(8,128)(2,1)S(1)} %get-tuple-element.90), channel_id=1, source_target_pairs={{0,4},{1,5},{2,6},{3,7},{4,0},{5,1},{6,2},{7,3},{8,12},{9,13},{10,... | collective-permute-start | bytes 1277960 | tf_op jit(solution)/shard_map/ppermute | solution.py:437
  82.8 18.9 %collective-permute-start.20 = (bf16[1664,128]{1,0:T(8,128)(2,1)S(1)}, bf16[1664,128]{1,0:T(8,128)(2,1)S(1)}, u32[]{:S(2)}, u32[]{:S(2)}) collective-permute-start(bf16[1664,128]{1,0:T(8,128)(2,1)S(1)} %get-tuple-element.91), channel_id=1, source_target_pairs={{0,2},{1,3},{2,0},{3,1},{4,6},{5,7},{6,4},{7,5},{8,10},{9,11},{10,... | collective-permute-start | bytes 1277960 | tf_op jit(solution)/shard_map/ppermute | solution.py:437
  87.5 16.1 %collective-permute-start.24 = (bf16[832,128]{1,0:T(8,128)(2,1)S(1)}, bf16[832,128]{1,0:T(8,128)(2,1)S(1)}, u32[]{:S(2)}, u32[]{:S(2)}) collective-permute-start(bf16[832,128]{1,0:T(8,128)(2,1)S(1)} %get-tuple-element.80), channel_id=1, source_target_pairs={{0,8},{8,24},{24,16},{16,0},{1,9},{9,25},{25,17},{17,1},{2,10},{10... | collective-permute-start | bytes 638984 | tf_op jit(solution)/shard_map/ppermute | solution.py:446
  89.7 16.5 %collective-permute-start.26 = (bf16[832,128]{1,0:T(8,128)(2,1)S(1)}, bf16[832,128]{1,0:T(8,128)(2,1)S(1)}, u32[]{:S(2)}, u32[]{:S(2)}) collective-permute-start(bf16[832,128]{1,0:T(8,128)(2,1)S(1)} %collective-permute-done.15.refs_0_), channel_id=1, source_target_pairs={{0,8},{8,24},{24,16},{16,0},{1,9},{9,25},{25,17},{17,1},{2,10},{10... | collective-permute-start | bytes 638984 | tf_op jit(solution)/shard_map/ppermute | solution.py:463
  93.2 13.0 %collective-permute-start.27 = (bf16[832,128]{1,0:T(8,128)(2,1)S(1)}, bf16[832,128]{1,0:T(8,128)(2,1)S(1)}, u32[]{:S(2)}, u32[]{:S(2)}) collective-permute-start(bf16[832,128]{1,0:T(8,128)(2,1)S(1)} %rows_of.6), channel_id=1, source_target_pairs={{8,0},{24,8},{16,24},{0,16},{9,1},{25,9},{17,25},{1,17},{10,2},{26... | collective-permute-start | bytes 638984 | tf_op jit(solution)/shard_map/ppermute | solution.py:464
  102.1 8.1 %collective-permute-start.21 = (bf16[832,128]{1,0:T(8,128)(2,1)S(1)}, bf16[832,128]{1,0:T(8,128)(2,1)S(1)}, u32[]{:S(2)}, u32[]{:S(2)}) collective-permute-start(bf16[832,128]{1,0:T(8,128)(2,1)S(1)} %get-tuple-element.93.refs_8_), channel_id=1, source_target_pairs={{0,8},{8,24},{24,16},{16,0},{1,9},{9,25},{25,17},{17,1},{2,10},{10... | collective-permute-start | bytes 638984 | tf_op jit(solution)/shard_map/ppermute | solution.py:446
  112.1 12.2 %collective-permute-start.23 = (bf16[1664,128]{1,0:T(8,128)(2,1)S(1)}, bf16[1664,128]{1,0:T(8,128)(2,1)S(1)}, u32[]{:S(2)}, u32[]{:S(2)}) collective-permute-start(bf16[1664,128]{1,0:T(8,128)(2,1)S(1)} %get-tuple-element.92.refs_0_), channel_id=1, source_target_pairs={{8,0},{24,8},{16,24},{0,16},{9,1},{25,9},{17,25},{1,17},{10,2},{26... | collective-permute-start | bytes 1277960 | tf_op jit(solution)/shard_map/ppermute | solution.py:447
  113.3 22.2 %collective-permute-start.31 = (bf16[1664,128]{1,0:T(8,128)(2,1)S(1)}, bf16[1664,128]{1,0:T(8,128)(2,1)S(1)}, u32[]{:S(2)}, u32[]{:S(2)}) collective-permute-start(bf16[1664,128]{1,0:T(8,128)(2,1)S(1)} %summed.14), channel_id=1, source_target_pairs={{0,6},{1,7},{2,4},{3,5},{4,2},{5,3},{6,0},{7,1},{8,14},{9,15},{10,... | collective-permute-start | bytes 1277960 | tf_op jit(solution)/shard_map/ppermute | solution.py:437
  116.2 19.3 %collective-permute-start.32 = (bf16[1664,128]{1,0:T(8,128)(2,1)S(1)}, bf16[1664,128]{1,0:T(8,128)(2,1)S(1)}, u32[]{:S(2)}, u32[]{:S(2)}) collective-permute-start(bf16[1664,128]{1,0:T(8,128)(2,1)S(1)} %get-tuple-element.103), channel_id=1, source_target_pairs={{0,4},{1,5},{2,6},{3,7},{4,0},{5,1},{6,2},{7,3},{8,12},{9,13},{10,... | collective-permute-start | bytes 1277960 | tf_op jit(solution)/shard_map/ppermute | solution.py:437
  116.3 19.3 %collective-permute-start.33 = (bf16[1664,128]{1,0:T(8,128)(2,1)S(1)}, bf16[1664,128]{1,0:T(8,128)(2,1)S(1)}, u32[]{:S(2)}, u32[]{:S(2)}) collective-permute-start(bf16[1664,128]{1,0:T(8,128)(2,1)S(1)} %get-tuple-element.104), channel_id=1, source_target_pairs={{0,2},{1,3},{2,0},{3,1},{4,6},{5,7},{6,4},{7,5},{8,10},{9,11},{10,... | collective-permute-start | bytes 1277960 | tf_op jit(solution)/shard_map/ppermute | solution.py:437
  118.5 11.3 %collective-permute-start.22 = (bf16[832,128]{1,0:T(8,128)(2,1)S(1)}, bf16[832,128]{1,0:T(8,128)(2,1)S(1)}, u32[]{:S(2)}, u32[]{:S(2)}) collective-permute-start(bf16[832,128]{1,0:T(8,128)(2,1)S(1)} %get-tuple-element.94.refs_9_), channel_id=1, source_target_pairs={{0,8},{8,24},{24,16},{16,0},{1,9},{9,25},{25,17},{17,1},{2,10},{10... | collective-permute-start | bytes 638984 | tf_op jit(solution)/shard_map/ppermute | solution.py:446
  124.3 12.6 %collective-permute-start.30 = (bf16[832,128]{1,0:T(8,128)(2,1)S(1)}, bf16[832,128]{1,0:T(8,128)(2,1)S(1)}, u32[]{:S(2)}, u32[]{:S(2)}) collective-permute-start(bf16[832,128]{1,0:T(8,128)(2,1)S(1)} %collective-permute-done.21.refs_0_), channel_id=1, source_target_pairs={{0,8},{8,24},{24,16},{16,0},{1,9},{9,25},{25,17},{17,1},{2,10},{10... | collective-permute-start | bytes 638984 | tf_op jit(solution)/shard_map/ppermute | solution.py:463
  129.8 9.0 %collective-permute-start.34 = (bf16[832,128]{1,0:T(8,128)(2,1)S(1)}, bf16[832,128]{1,0:T(8,128)(2,1)S(1)}, u32[]{:S(2)}, u32[]{:S(2)}) collective-permute-start(bf16[832,128]{1,0:T(8,128)(2,1)S(1)} %rows_of.7), channel_id=1, source_target_pairs={{8,0},{24,8},{16,24},{0,16},{9,1},{25,9},{17,25},{1,17},{10,2},{26... | collective-permute-start | bytes 638984 | tf_op jit(solution)/shard_map/ppermute | solution.py:464
  146.2 8.2 %collective-permute-start.38 = (bf16[832,128]{1,0:T(8,128)(2,1)S(1)}, bf16[832,128]{1,0:T(8,128)(2,1)S(1)}, u32[]{:S(2)}, u32[]{:S(2)}) collective-permute-start(bf16[832,128]{1,0:T(8,128)(2,1)S(1)} %get-tuple-element.117), channel_id=1, source_target_pairs={{0,2},{1,3},{2,0},{3,1},{4,6},{5,7},{6,4},{7,5},{8,10},{9,11},{10,... | collective-permute-start | bytes 638984 | tf_op jit(solution)/shard_map/ppermute | solution.py:437
  147.2 10.9 %collective-permute-start.40 = (bf16[832,128]{1,0:T(8,128)(2,1)S(1)}, bf16[832,128]{1,0:T(8,128)(2,1)S(1)}, u32[]{:S(2)}, u32[]{:S(2)}) collective-permute-start(bf16[832,128]{1,0:T(8,128)(2,1)S(1)} %get-tuple-element.121), channel_id=1, source_target_pairs={{0,2},{1,3},{2,0},{3,1},{4,6},{5,7},{6,4},{7,5},{8,10},{9,11},{10,... | collective-permute-start | bytes 638984 | tf_op jit(solution)/shard_map/ppermute | solution.py:437
  148.3 16.1 %collective-permute-start.43 = (bf16[832,128]{1,0:T(8,128)(2,1)S(1)}, bf16[832,128]{1,0:T(8,128)(2,1)S(1)}, u32[]{:S(2)}, u32[]{:S(2)}) collective-permute-start(bf16[832,128]{1,0:T(8,128)(2,1)S(1)} %get-tuple-element.124), channel_id=1, source_target_pairs={{0,4},{1,5},{2,6},{3,7},{4,0},{5,1},{6,2},{7,3},{8,12},{9,13},{10,... | collective-permute-start | bytes 638984 | tf_op jit(solution)/shard_map/ppermute | solution.py:437
  (17 other events, 56.9 us)

commit v8 on v6

--- a/solution.py
+++ b/solution.py
@@ -308,7 +308,16 @@
     given = [] if relaid is None else [relaid]
 
     def kernel(edges_ref, second_ref, partner_ref, *refs):
-        out_ref, window, block_rows, sem = refs[-4:]
+        out_ref, window, block_rows, sems = refs[-4:]
+        split = capacity // 2
+        copies = []
+        for index, (first, end) in enumerate([(0, split), (split, capacity)]):
+            span = pl.ds(first * orbitals, (end - first) * orbitals)
+            copies.append(
+                pltpu.make_async_copy(
+                    block_rows.at[span], out_ref.at[span, pl.ds(low, width)], sems.at[index]
+                )
+            )
         window[pl.ds(pl.multiple_of(edges_ref[1], 16), own * orbitals), :] = second_ref[...]
         window[pl.ds(pl.multiple_of(edges_ref[2], 16), edge_size), :] = partner_ref[...]
         for block in range(capacity):
@@ -323,9 +332,12 @@
             def _():
                 block_rows[span, :] = jnp.zeros((orbitals, width), block_rows.dtype)
 
-        copy = pltpu.make_async_copy(block_rows, out_ref.at[:, pl.ds(low, width)], sem)
-        copy.start()
-        copy.wait()
+            if block == split - 1:
+                copies[0].start()
+
+        copies[1].start()
+        for copy in copies:
+            copy.wait()
 
     out = jax.ShapeDtypeStruct(shape, jnp.bfloat16)
     return pl.pallas_call(
@@ -336,7 +348,7 @@
         scratch_shapes=[
             pltpu.VMEM((own * orbitals + edge_size, width), jnp.bfloat16),
             pltpu.VMEM((shape[0], width), jnp.bfloat16),
-            pltpu.SemaphoreType.DMA,
+            pltpu.SemaphoreType.DMA((2,)),
         ],
         input_output_aliases={3: 0} if given else {},
         compiler_params=params(bytes_of(out) + 2 * bytes_of(second)),

time: 168 us -> 168 us (level)
  Pallas kernels: 37.4 us -> 39.2 us
    pallas_call x4, Pallas kernels: 10.3 us -> 12.2 us  [middle_images(): pl.pallas_call(kernel, out_shape=pltpu.VMEM(early.shape, jnp.float32), in...]
  transfers between devices with their start and end apart: 45 -> 45, of which waited for: 27 -> 27; matrix products, arithmetic and copies ran while one was open for 3% -> 3% of each run, Pallas kernels for 19% -> 20%
where the time goes in v8:
time: 168 us
  waiting for transfers between devices  63.4 us (38%)
  starting transfers between devices  50.4 us (30%)
  Pallas kernels  39.2 us (23%)
  local copies, waits for them, and re-layouts  8.29 us (5%)
  other arithmetic  3.23 us (2%)
  between operations  3.2 us (2%)
    ppermute x15, waiting for transfers between devices, to_chip(): lax.ppermute(array, 'col', [(i, i ^ 2 * chip) for i in range(col_count)])  24.2 us
    ppermute x15, starting transfers between devices, to_chip(): lax.ppermute(array, 'col', [(i, i ^ 2 * chip) for i in range(col_count)])  23.6 us
    pallas_call x4, Pallas kernels, middle_images(): pl.pallas_call(kernel, out_shape=pltpu.VMEM(early.shape, jnp.float32), in...  12.2 us
    ppermute x8, waiting for transfers between devices, __init__(): upper, lower = (lax.ppermute(half, 'row', route) for half in (upper, lower))  12 us
    pallas_call x4, Pallas kernels, early_images(): pl.pallas_call(kernel, out_shape=pltpu.VMEM(total, jnp.float32), in_specs...  10 us
    ppermute x10, waiting for transfers between devices, to_core(): return lax.ppermute(array, 'col', other_core)  9.87 us
    ppermute x4, waiting for transfers between devices, __init__(): self.early = [part, upper, lower, lax.ppermute(part, 'row', back_route)]  9.61 us
    pallas_call x4, Pallas kernels, last_images(): pl.pallas_call(kernel, out_shape=[pltpu.VMEM(early.shape, jnp.float32), *...  7.91 us
  transfers between devices with their start and end apart: 45, of which 27 were waited for; matrix products, arithmetic and copies ran while one was open for 3% of the time, Pallas kernels for 20%

profile of v8, /device:TPU:0, one launch (start us, length us, event | category | flops | bytes accessed | tf_op | source)
XLA Modules:
  0.0 167.7 jit_solution(4809653845946873825)
XLA Ops:
  1.2 4.1 %collective-permute-start.2 = (bf16[1664,128]{1,0:T(8,128)(2,1)S(1)}, bf16[1664,128]{1,0:T(8,128)(2,1)S(1)}, u32[]{:S(2)}, u32[]{:S(2)}) collective-permute-start(bf16[1664,128]{1,0:T(8,128)(2,1)S(1)} %columns_of.6.refs_0_), channel_id=1, source_target_pairs={{8,0},{24,8},{16,24},{0,16},{9,1},{25,9},{17,25},{1,17},{10,2},{26... | collective-permute-start | bytes 1277960 | tf_op jit(solution)/shard_map/ppermute | solution.py:459
  6.7 1.9 %collective-permute-start = (bf16[832,128]{1,0:T(8,128)(2,1)S(1)}, bf16[832,128]{1,0:T(8,128)(2,1)S(1)}, u32[]{:S(2)}, u32[]{:S(2)}) collective-permute-start(bf16[832,128]{1,0:T(8,128)(2,1)S(1)} %columns_of.7), channel_id=1, source_target_pairs={{0,8},{8,24},{24,16},{16,0},{1,9},{9,25},{25,17},{17,1},{2,10},{10... | collective-permute-start | bytes 638984 | tf_op jit(solution)/shard_map/ppermute | solution.py:458
  15.8 3.4 %copy-done.3 = bf16[1,1,256,128,128]{4,3,2,1,0:T(8,128)(2,1)S(1)} copy-done((bf16[1,1,256,128,128]{4,3,2,1,0:T(8,128)(2,1)S(1)}, bf16[1,1,256,128,128]{4,3,2,1,0:T(8,128)(2,1)}, u32[]{:S(2)}) %copy-start.3) | copy-done | bytes 8388632
  19.7 2.5 %early_images.4.early = f32[13440,128]{1,0:T(8,128)S(1)} custom-call(s32[9]{0:T(128)S(1)} %concatenate.3.refs_0_.bounds.edges_ref, s32[288]{0:T(512)S(1)} %pad.10.refs_1_.order, s32[288]{0:T(512)S(1)} %pad.11.refs_2_.rows, s32[288]{0:T(512)S(1)} %pad.12.refs_3_.cols, bf16[256,128,128]{2,1,0:T(8,128)(2,1)S(1)} %resident.1.values, ...), custom_call_target="tpu_custom_call" | custom-call | tf_op jit(solution)/shard_map/early_images/pallas_call | solution.py:132
  22.3 3.1 %collective-permute-done.refs_0_ = bf16[832,128]{1,0:T(8,128)(2,1)S(1)} collective-permute-done((bf16[832,128]{1,0:T(8,128)(2,1)S(1)}, bf16[832,128]{1,0:T(8,128)(2,1)S(1)}, u32[]{:S(2)}, u32[]{:S(2)}) %collective-permute-start) | collective-permute-done | bytes 213024 | tf_op jit(solution)/shard_map/ppermute | solution.py:458
  26.1 2.3 %collective-permute-start.7 = (bf16[832,128]{1,0:T(8,128)(2,1)S(1)}, bf16[832,128]{1,0:T(8,128)(2,1)S(1)}, u32[]{:S(2)}, u32[]{:S(2)}) collective-permute-start(bf16[832,128]{1,0:T(8,128)(2,1)S(1)} %rows_of.4), channel_id=1, source_target_pairs={{8,0},{24,8},{16,24},{0,16},{9,1},{25,9},{17,25},{1,17},{10,2},{26... | collective-permute-start | bytes 638984 | tf_op jit(solution)/shard_map/ppermute | solution.py:476
  28.4 3.1 %middle_images.4.refs_0_.early = f32[13440,128]{1,0:T(8,128)S(1)} custom-call(s32[9]{0:T(128)S(1)} %concatenate.3.refs_0_.bounds.edges_ref, s32[288]{0:T(512)S(1)} %pad.10.refs_1_.order, s32[288]{0:T(512)S(1)} %pad.11.refs_2_.rows, s32[288]{0:T(512)S(1)} %pad.12.refs_3_.cols, ...), custom_call_target="tpu_custom_call", output_to_operand_aliasing={{}: (5, {})} | custom-call | tf_op jit(solution)/shard_map/middle_images/pallas_call | solution.py:152
  31.7 5.9 %collective-permute-done.6.refs_0_ = bf16[832,128]{1,0:T(8,128)(2,1)S(1)} collective-permute-done((bf16[832,128]{1,0:T(8,128)(2,1)S(1)}, bf16[832,128]{1,0:T(8,128)(2,1)S(1)}, u32[]{:S(2)}, u32[]{:S(2)}) %collective-permute-start.6) | collective-permute-done | bytes 213024 | tf_op jit(solution)/shard_map/ppermute | solution.py:475
  40.3 2.3 %collective-permute-done.3.refs_0_ = bf16[832,128]{1,0:T(8,128)(2,1)S(1)} collective-permute-done((bf16[832,128]{1,0:T(8,128)(2,1)S(1)}, bf16[832,128]{1,0:T(8,128)(2,1)S(1)}, u32[]{:S(2)}, u32[]{:S(2)}) %collective-permute-start.3) | collective-permute-done | bytes 213024 | tf_op jit(solution)/shard_map/ppermute | solution.py:458
  45.0 2.5 %collective-permute-start.11 = (bf16[1664,128]{1,0:T(8,128)(2,1)S(1)}, bf16[1664,128]{1,0:T(8,128)(2,1)S(1)}, u32[]{:S(2)}, u32[]{:S(2)}) collective-permute-start(bf16[1664,128]{1,0:T(8,128)(2,1)S(1)} %summed.10), channel_id=1, source_target_pairs={{0,6},{1,7},{2,4},{3,5},{4,2},{5,3},{6,0},{7,1},{8,14},{9,15},{10,... | collective-permute-start | bytes 1277960 | tf_op jit(solution)/shard_map/ppermute | solution.py:449
  51.9 2.5 %early_images.5.early = f32[13440,128]{1,0:T(8,128)S(1)} custom-call(s32[9]{0:T(128)S(1)} %concatenate.3.refs_0_.bounds.edges_ref, s32[288]{0:T(512)S(1)} %pad.10.refs_1_.order, s32[288]{0:T(512)S(1)} %pad.11.refs_2_.rows, s32[288]{0:T(512)S(1)} %pad.12.refs_3_.cols, bf16[256,128,128]{2,1,0:T(8,128)(2,1)S(1)} %resident.1.values, ...), custom_call_target="tpu_custom_call" | custom-call | tf_op jit(solution)/shard_map/early_images/pallas_call | solution.py:132
  54.5 2.1 %collective-permute-done.5.refs_2_.array_ref = bf16[1664,128]{1,0:T(8,128)(2,1)S(1)} collective-permute-done((bf16[1664,128]{1,0:T(8,128)(2,1)S(1)}, bf16[1664,128]{1,0:T(8,128)(2,1)S(1)}, u32[]{:S(2)}, u32[]{:S(2)}) %collective-permute-start.5) | collective-permute-done | bytes 426016 | tf_op jit(solution)/shard_map/ppermute | solution.py:459
  58.7 2.6 %collective-permute-start.14 = (bf16[832,128]{1,0:T(8,128)(2,1)S(1)}, bf16[832,128]{1,0:T(8,128)(2,1)S(1)}, u32[]{:S(2)}, u32[]{:S(2)}) collective-permute-start(bf16[832,128]{1,0:T(8,128)(2,1)S(1)} %rows_of.5), channel_id=1, source_target_pairs={{8,0},{24,8},{16,24},{0,16},{9,1},{25,9},{17,25},{1,17},{10,2},{26... | collective-permute-start | bytes 638984 | tf_op jit(solution)/shard_map/ppermute | solution.py:476
  61.3 5.6 %collective-permute-done.12.refs_3_ = bf16[1664,128]{1,0:T(8,128)(2,1)S(1)} collective-permute-done((bf16[1664,128]{1,0:T(8,128)(2,1)S(1)}, bf16[1664,128]{1,0:T(8,128)(2,1)S(1)}, u32[]{:S(2)}, u32[]{:S(2)}) %collective-permute-start.12) | collective-permute-done | bytes 426016 | tf_op jit(solution)/shard_map/ppermute | solution.py:449
  69.1 3.0 %middle_images.5.early = f32[13440,128]{1,0:T(8,128)S(1)} custom-call(s32[9]{0:T(128)S(1)} %concatenate.3.refs_0_.bounds.edges_ref, s32[288]{0:T(512)S(1)} %pad.10.refs_1_.order, s32[288]{0:T(512)S(1)} %pad.11.refs_2_.rows, s32[288]{0:T(512)S(1)} %pad.12.refs_3_.cols, bf16[256,128,128]{2,1,0:T(8,128)(2,1)S(1)} %resident.1.values, ...), custom_call_target="tpu_custom_call", output_to_operand_aliasing={{}: (5, {})} | custom-call | tf_op jit(solution)/shard_map/middle_images/pallas_call | solution.py:152
  72.2 1.9 %last_images.5 = (f32[13440,128]{1,0:T(8,128)S(1)}, bf16[1664,128]{1,0:T(8,128)(2,1)S(1)}, bf16[1664,128]{1,0:T(8,128)(2,1)S(1)}, bf16[4992,128]{1,0:T(8,128)(2,1)S(1)}, bf16[4992,128]{1,0:T(8,128)(2,1)S(1)}) custom-call(s32[9]{0:T(128)S(1)} %concatenate.3.refs_0_.bounds.edges_ref, s32[288]{0:T(512)S(1)} %pad.10.refs_1_.order, ...), custom_call_target="tpu_custom_call", output_to_operand_aliasing={{0}: (5, {})} | custom-call | tf_op jit(solution)/shard_map/last_images/pallas_call | solution.py:189
  79.2 3.3 %collective-permute-start.18 = (bf16[1664,128]{1,0:T(8,128)(2,1)S(1)}, bf16[1664,128]{1,0:T(8,128)(2,1)S(1)}, u32[]{:S(2)}, u32[]{:S(2)}) collective-permute-start(bf16[1664,128]{1,0:T(8,128)(2,1)S(1)} %summed.11), channel_id=1, source_target_pairs={{0,6},{1,7},{2,4},{3,5},{4,2},{5,3},{6,0},{7,1},{8,14},{9,15},{10,... | collective-permute-start | bytes 1277960 | tf_op jit(solution)/shard_map/ppermute | solution.py:449
  82.8 2.7 %collective-permute-start.20 = (bf16[1664,128]{1,0:T(8,128)(2,1)S(1)}, bf16[1664,128]{1,0:T(8,128)(2,1)S(1)}, u32[]{:S(2)}, u32[]{:S(2)}) collective-permute-start(bf16[1664,128]{1,0:T(8,128)(2,1)S(1)} %get-tuple-element.90), channel_id=1, source_target_pairs={{0,2},{1,3},{2,0},{3,1},{4,6},{5,7},{6,4},{7,5},{8,10},{9,11},{10,... | collective-permute-start | bytes 1277960 | tf_op jit(solution)/shard_map/ppermute | solution.py:449
  85.5 2.5 %early_images.6.early = f32[13440,128]{1,0:T(8,128)S(1)} custom-call(s32[9]{0:T(128)S(1)} %concatenate.3.refs_0_.bounds.edges_ref, s32[288]{0:T(512)S(1)} %pad.10.refs_1_.order, s32[288]{0:T(512)S(1)} %pad.11.refs_2_.rows, s32[288]{0:T(512)S(1)} %pad.12.refs_3_.cols, bf16[256,128,128]{2,1,0:T(8,128)(2,1)S(1)} %resident.1.values, ...), custom_call_target="tpu_custom_call" | custom-call | tf_op jit(solution)/shard_map/early_images/pallas_call | solution.py:132
  95.1 6.6 %collective-permute-done.19.refs_3_ = bf16[1664,128]{1,0:T(8,128)(2,1)S(1)} collective-permute-done((bf16[1664,128]{1,0:T(8,128)(2,1)S(1)}, bf16[1664,128]{1,0:T(8,128)(2,1)S(1)}, u32[]{:S(2)}, u32[]{:S(2)}) %collective-permute-start.19) | collective-permute-done | bytes 426016 | tf_op jit(solution)/shard_map/ppermute | solution.py:449
  103.6 3.1 %middle_images.7.early = f32[13440,128]{1,0:T(8,128)S(1)} custom-call(s32[9]{0:T(128)S(1)} %concatenate.3.refs_0_.bounds.edges_ref, s32[288]{0:T(512)S(1)} %pad.10.refs_1_.order, s32[288]{0:T(512)S(1)} %pad.11.refs_2_.rows, s32[288]{0:T(512)S(1)} %pad.12.refs_3_.cols, bf16[256,128,128]{2,1,0:T(8,128)(2,1)S(1)} %resident.1.values, ...), custom_call_target="tpu_custom_call", output_to_operand_aliasing={{}: (5, {})} | custom-call | tf_op jit(solution)/shard_map/middle_images/pallas_call | solution.py:152
  106.7 2.1 %last_images.6 = (f32[13440,128]{1,0:T(8,128)S(1)}, bf16[1664,128]{1,0:T(8,128)(2,1)S(1)}, bf16[1664,128]{1,0:T(8,128)(2,1)S(1)}, bf16[4992,128]{1,0:T(8,128)(2,1)S(1)}, bf16[4992,128]{1,0:T(8,128)(2,1)S(1)}) custom-call(s32[9]{0:T(128)S(1)} %concatenate.3.refs_0_.bounds.edges_ref, s32[288]{0:T(512)S(1)} %pad.10.refs_1_.order, ...), custom_call_target="tpu_custom_call", output_to_operand_aliasing={{0}: (5, {})} | custom-call | tf_op jit(solution)/shard_map/last_images/pallas_call | solution.py:189
  113.3 2.7 %collective-permute-start.31 = (bf16[1664,128]{1,0:T(8,128)(2,1)S(1)}, bf16[1664,128]{1,0:T(8,128)(2,1)S(1)}, u32[]{:S(2)}, u32[]{:S(2)}) collective-permute-start(bf16[1664,128]{1,0:T(8,128)(2,1)S(1)} %summed.14), channel_id=1, source_target_pairs={{0,6},{1,7},{2,4},{3,5},{4,2},{5,3},{6,0},{7,1},{8,14},{9,15},{10,... | collective-permute-start | bytes 1277960 | tf_op jit(solution)/shard_map/ppermute | solution.py:449
  116.3 2.2 %collective-permute-start.33 = (bf16[1664,128]{1,0:T(8,128)(2,1)S(1)}, bf16[1664,128]{1,0:T(8,128)(2,1)S(1)}, u32[]{:S(2)}, u32[]{:S(2)}) collective-permute-start(bf16[1664,128]{1,0:T(8,128)(2,1)S(1)} %get-tuple-element.103), channel_id=1, source_target_pairs={{0,2},{1,3},{2,0},{3,1},{4,6},{5,7},{6,4},{7,5},{8,10},{9,11},{10,... | collective-permute-start | bytes 1277960 | tf_op jit(solution)/shard_map/ppermute | solution.py:449
  118.7 5.6 %collective-permute-done.23.refs_2_.array_ref = bf16[1664,128]{1,0:T(8,128)(2,1)S(1)} collective-permute-done((bf16[1664,128]{1,0:T(8,128)(2,1)S(1)}, bf16[1664,128]{1,0:T(8,128)(2,1)S(1)}, u32[]{:S(2)}, u32[]{:S(2)}) %collective-permute-start.23) | collective-permute-done | bytes 426016 | tf_op jit(solution)/shard_map/ppermute | solution.py:459
  124.3 2.0 %collective-permute-start.30 = (bf16[832,128]{1,0:T(8,128)(2,1)S(1)}, bf16[832,128]{1,0:T(8,128)(2,1)S(1)}, u32[]{:S(2)}, u32[]{:S(2)}) collective-permute-start(bf16[832,128]{1,0:T(8,128)(2,1)S(1)} %collective-permute-done.21.refs_0_), channel_id=1, source_target_pairs={{0,8},{8,24},{24,16},{16,0},{1,9},{9,25},{25,17},{17,1},{2,10},{10... | collective-permute-start | bytes 638984 | tf_op jit(solution)/shard_map/ppermute | solution.py:475
  126.3 3.5 %collective-permute-done.22.refs_1_ = bf16[832,128]{1,0:T(8,128)(2,1)S(1)} collective-permute-done((bf16[832,128]{1,0:T(8,128)(2,1)S(1)}, bf16[832,128]{1,0:T(8,128)(2,1)S(1)}, u32[]{:S(2)}, u32[]{:S(2)}) %collective-permute-start.22) | collective-permute-done | bytes 213024 | tf_op jit(solution)/shard_map/ppermute | solution.py:458
  130.9 2.5 %early_images.7.early = f32[13440,128]{1,0:T(8,128)S(1)} custom-call(s32[9]{0:T(128)S(1)} %concatenate.3.refs_0_.bounds.edges_ref, s32[288]{0:T(512)S(1)} %pad.10.refs_1_.order, s32[288]{0:T(512)S(1)} %pad.11.refs_2_.rows, s32[288]{0:T(512)S(1)} %pad.12.refs_3_.cols, bf16[256,128,128]{2,1,0:T(8,128)(2,1)S(1)} %resident.1.values, ...), custom_call_target="tpu_custom_call" | custom-call | tf_op jit(solution)/shard_map/early_images/pallas_call | solution.py:132
  133.4 3.1 %middle_images.6.early = f32[13440,128]{1,0:T(8,128)S(1)} custom-call(s32[9]{0:T(128)S(1)} %concatenate.3.refs_0_.bounds.edges_ref, s32[288]{0:T(512)S(1)} %pad.10.refs_1_.order, s32[288]{0:T(512)S(1)} %pad.11.refs_2_.rows, s32[288]{0:T(512)S(1)} %pad.12.refs_3_.cols, bf16[256,128,128]{2,1,0:T(8,128)(2,1)S(1)} %resident.1.values, ...), custom_call_target="tpu_custom_call", output_to_operand_aliasing={{}: (5, {})} | custom-call | tf_op jit(solution)/shard_map/middle_images/pallas_call | solution.py:152
  143.4 2.4 %collective-permute-start.40 = (bf16[832,128]{1,0:T(8,128)(2,1)S(1)}, bf16[832,128]{1,0:T(8,128)(2,1)S(1)}, u32[]{:S(2)}, u32[]{:S(2)}) collective-permute-start(bf16[832,128]{1,0:T(8,128)(2,1)S(1)} %get-tuple-element.119), channel_id=1, source_target_pairs={{0,2},{1,3},{2,0},{3,1},{4,6},{5,7},{6,4},{7,5},{8,10},{9,11},{10,... | collective-permute-start | bytes 638984 | tf_op jit(solution)/shard_map/ppermute | solution.py:449
  145.8 4.7 %collective-permute-done.39.refs_2_ = bf16[832,128]{1,0:T(8,128)(2,1)S(1)} collective-permute-done((bf16[832,128]{1,0:T(8,128)(2,1)S(1)}, bf16[832,128]{1,0:T(8,128)(2,1)S(1)}, u32[]{:S(2)}, u32[]{:S(2)}) %collective-permute-start.39) | collective-permute-done | bytes 213024 | tf_op jit(solution)/shard_map/ppermute | solution.py:449
  160.6 2.5 %collective-permute-done.38.refs_2_ = bf16[832,128]{1,0:T(8,128)(2,1)S(1)} collective-permute-done((bf16[832,128]{1,0:T(8,128)(2,1)S(1)}, bf16[832,128]{1,0:T(8,128)(2,1)S(1)}, u32[]{:S(2)}, u32[]{:S(2)}) %collective-permute-start.38) | collective-permute-done | bytes 213024 | tf_op jit(solution)/shard_map/ppermute | solution.py:449
  (116 shorter events, 64.3 us)
Async XLA Ops:
  1.2 24.8 %collective-permute-start.2 = (bf16[1664,128]{1,0:T(8,128)(2,1)S(1)}, bf16[1664,128]{1,0:T(8,128)(2,1)S(1)}, u32[]{:S(2)}, u32[]{:S(2)}) collective-permute-start(bf16[1664,128]{1,0:T(8,128)(2,1)S(1)} %columns_of.6.refs_0_), channel_id=1, source_target_pairs={{8,0},{24,8},{16,24},{0,16},{9,1},{25,9},{17,25},{1,17},{10,2},{26... | collective-permute-start | bytes 1277960 | tf_op jit(solution)/shard_map/ppermute | solution.py:459
  6.6 15.7 %collective-permute-start.1 = (bf16[832,128]{1,0:T(8,128)(2,1)S(1)}, bf16[832,128]{1,0:T(8,128)(2,1)S(1)}, u32[]{:S(2)}, u32[]{:S(2)}) collective-permute-start(bf16[832,128]{1,0:T(8,128)(2,1)S(1)} %columns_of.8), channel_id=1, source_target_pairs={{0,8},{8,24},{24,16},{16,0},{1,9},{9,25},{25,17},{17,1},{2,10},{10... | collective-permute-start | bytes 638984 | tf_op jit(solution)/shard_map/ppermute | solution.py:458
  6.7 18.7 %collective-permute-start = (bf16[832,128]{1,0:T(8,128)(2,1)S(1)}, bf16[832,128]{1,0:T(8,128)(2,1)S(1)}, u32[]{:S(2)}, u32[]{:S(2)}) collective-permute-start(bf16[832,128]{1,0:T(8,128)(2,1)S(1)} %columns_of.7), channel_id=1, source_target_pairs={{0,8},{8,24},{24,16},{16,0},{1,9},{9,25},{25,17},{17,1},{2,10},{10... | collective-permute-start | bytes 638984 | tf_op jit(solution)/shard_map/ppermute | solution.py:458
  25.3 12.3 %collective-permute-start.6 = (bf16[832,128]{1,0:T(8,128)(2,1)S(1)}, bf16[832,128]{1,0:T(8,128)(2,1)S(1)}, u32[]{:S(2)}, u32[]{:S(2)}) collective-permute-start(bf16[832,128]{1,0:T(8,128)(2,1)S(1)} %collective-permute-done.refs_0_), channel_id=1, source_target_pairs={{0,8},{8,24},{24,16},{16,0},{1,9},{9,25},{25,17},{17,1},{2,10},{10... | collective-permute-start | bytes 638984 | tf_op jit(solution)/shard_map/ppermute | solution.py:475
  26.1 12.3 %collective-permute-start.7 = (bf16[832,128]{1,0:T(8,128)(2,1)S(1)}, bf16[832,128]{1,0:T(8,128)(2,1)S(1)}, u32[]{:S(2)}, u32[]{:S(2)}) collective-permute-start(bf16[832,128]{1,0:T(8,128)(2,1)S(1)} %rows_of.4), channel_id=1, source_target_pairs={{8,0},{24,8},{16,24},{0,16},{9,1},{25,9},{17,25},{1,17},{10,2},{26... | collective-permute-start | bytes 638984 | tf_op jit(solution)/shard_map/ppermute | solution.py:476
  31.5 11.1 %collective-permute-start.3 = (bf16[832,128]{1,0:T(8,128)(2,1)S(1)}, bf16[832,128]{1,0:T(8,128)(2,1)S(1)}, u32[]{:S(2)}, u32[]{:S(2)}) collective-permute-start(bf16[832,128]{1,0:T(8,128)(2,1)S(1)} %columns_of.10), channel_id=1, source_target_pairs={{0,8},{8,24},{24,16},{16,0},{1,9},{9,25},{25,17},{17,1},{2,10},{10... | collective-permute-start | bytes 638984 | tf_op jit(solution)/shard_map/ppermute | solution.py:458
  44.5 12.1 %collective-permute-start.5 = (bf16[1664,128]{1,0:T(8,128)(2,1)S(1)}, bf16[1664,128]{1,0:T(8,128)(2,1)S(1)}, u32[]{:S(2)}, u32[]{:S(2)}) collective-permute-start(bf16[1664,128]{1,0:T(8,128)(2,1)S(1)} %columns_of.9.refs_0_), channel_id=1, source_target_pairs={{8,0},{24,8},{16,24},{0,16},{9,1},{25,9},{17,25},{1,17},{10,2},{26... | collective-permute-start | bytes 1277960 | tf_op jit(solution)/shard_map/ppermute | solution.py:459
  45.0 13.7 %collective-permute-start.11 = (bf16[1664,128]{1,0:T(8,128)(2,1)S(1)}, bf16[1664,128]{1,0:T(8,128)(2,1)S(1)}, u32[]{:S(2)}, u32[]{:S(2)}) collective-permute-start(bf16[1664,128]{1,0:T(8,128)(2,1)S(1)} %summed.10), channel_id=1, source_target_pairs={{0,6},{1,7},{2,4},{3,5},{4,2},{5,3},{6,0},{7,1},{8,14},{9,15},{10,... | collective-permute-start | bytes 1277960 | tf_op jit(solution)/shard_map/ppermute | solution.py:449
  47.7 19.2 %collective-permute-start.12 = (bf16[1664,128]{1,0:T(8,128)(2,1)S(1)}, bf16[1664,128]{1,0:T(8,128)(2,1)S(1)}, u32[]{:S(2)}, u32[]{:S(2)}) collective-permute-start(bf16[1664,128]{1,0:T(8,128)(2,1)S(1)} %get-tuple-element.72), channel_id=1, source_target_pairs={{0,4},{1,5},{2,6},{3,7},{4,0},{5,1},{6,2},{7,3},{8,12},{9,13},{10,... | collective-permute-start | bytes 1277960 | tf_op jit(solution)/shard_map/ppermute | solution.py:449
  49.1 17.9 %collective-permute-start.13 = (bf16[1664,128]{1,0:T(8,128)(2,1)S(1)}, bf16[1664,128]{1,0:T(8,128)(2,1)S(1)}, u32[]{:S(2)}, u32[]{:S(2)}) collective-permute-start(bf16[1664,128]{1,0:T(8,128)(2,1)S(1)} %get-tuple-element.73), channel_id=1, source_target_pairs={{0,2},{1,3},{2,0},{3,1},{4,6},{5,7},{6,4},{7,5},{8,10},{9,11},{10,... | collective-permute-start | bytes 1277960 | tf_op jit(solution)/shard_map/ppermute | solution.py:449
  54.5 14.6 %collective-permute-start.4 = (bf16[832,128]{1,0:T(8,128)(2,1)S(1)}, bf16[832,128]{1,0:T(8,128)(2,1)S(1)}, u32[]{:S(2)}, u32[]{:S(2)}) collective-permute-start(bf16[832,128]{1,0:T(8,128)(2,1)S(1)} %columns_of.11), channel_id=1, source_target_pairs={{0,8},{8,24},{24,16},{16,0},{1,9},{9,25},{25,17},{17,1},{2,10},{10... | collective-permute-start | bytes 638984 | tf_op jit(solution)/shard_map/ppermute | solution.py:458
  56.6 15.5 %collective-permute-start.10 = (bf16[832,128]{1,0:T(8,128)(2,1)S(1)}, bf16[832,128]{1,0:T(8,128)(2,1)S(1)}, u32[]{:S(2)}, u32[]{:S(2)}) collective-permute-start(bf16[832,128]{1,0:T(8,128)(2,1)S(1)} %collective-permute-done.3.refs_0_), channel_id=1, source_target_pairs={{0,8},{8,24},{24,16},{16,0},{1,9},{9,25},{25,17},{17,1},{2,10},{10... | collective-permute-start | bytes 638984 | tf_op jit(solution)/shard_map/ppermute | solution.py:475
  58.7 13.5 %collective-permute-start.14 = (bf16[832,128]{1,0:T(8,128)(2,1)S(1)}, bf16[832,128]{1,0:T(8,128)(2,1)S(1)}, u32[]{:S(2)}, u32[]{:S(2)}) collective-permute-start(bf16[832,128]{1,0:T(8,128)(2,1)S(1)} %rows_of.5), channel_id=1, source_target_pairs={{8,0},{24,8},{16,24},{0,16},{9,1},{25,9},{17,25},{1,17},{10,2},{26... | collective-permute-start | bytes 638984 | tf_op jit(solution)/shard_map/ppermute | solution.py:476
  67.4 8.5 %collective-permute-start.15 = (bf16[832,128]{1,0:T(8,128)(2,1)S(1)}, bf16[832,128]{1,0:T(8,128)(2,1)S(1)}, u32[]{:S(2)}, u32[]{:S(2)}) collective-permute-start(bf16[832,128]{1,0:T(8,128)(2,1)S(1)} %get-tuple-element.78), channel_id=1, source_target_pairs={{0,8},{8,24},{24,16},{16,0},{1,9},{9,25},{25,17},{17,1},{2,10},{10... | collective-permute-start | bytes 638984 | tf_op jit(solution)/shard_map/ppermute | solution.py:458
  77.8 12.1 %collective-permute-start.25 = (bf16[1664,128]{1,0:T(8,128)(2,1)S(1)}, bf16[1664,128]{1,0:T(8,128)(2,1)S(1)}, u32[]{:S(2)}, u32[]{:S(2)}) collective-permute-start(bf16[1664,128]{1,0:T(8,128)(2,1)S(1)} %get-tuple-element.77.refs_0_.refs_5_), channel_id=1, source_target_pairs={{8,0},{24,8},{16,24},{0,16},{9,1},{25,9},{17,25},{1,17},{10,2},{26... | collective-permute-start | bytes 1277960 | tf_op jit(solution)/shard_map/ppermute | solution.py:459
  79.2 14.0 %collective-permute-start.18 = (bf16[1664,128]{1,0:T(8,128)(2,1)S(1)}, bf16[1664,128]{1,0:T(8,128)(2,1)S(1)}, u32[]{:S(2)}, u32[]{:S(2)}) collective-permute-start(bf16[1664,128]{1,0:T(8,128)(2,1)S(1)} %summed.11), channel_id=1, source_target_pairs={{0,6},{1,7},{2,4},{3,5},{4,2},{5,3},{6,0},{7,1},{8,14},{9,15},{10,... | collective-permute-start | bytes 1277960 | tf_op jit(solution)/shard_map/ppermute | solution.py:449
  82.7 19.0 %collective-permute-start.19 = (bf16[1664,128]{1,0:T(8,128)(2,1)S(1)}, bf16[1664,128]{1,0:T(8,128)(2,1)S(1)}, u32[]{:S(2)}, u32[]{:S(2)}) collective-permute-start(bf16[1664,128]{1,0:T(8,128)(2,1)S(1)} %get-tuple-element.89), channel_id=1, source_target_pairs={{0,4},{1,5},{2,6},{3,7},{4,0},{5,1},{6,2},{7,3},{8,12},{9,13},{10,... | collective-permute-start | bytes 1277960 | tf_op jit(solution)/shard_map/ppermute | solution.py:449
  82.8 18.9 %collective-permute-start.20 = (bf16[1664,128]{1,0:T(8,128)(2,1)S(1)}, bf16[1664,128]{1,0:T(8,128)(2,1)S(1)}, u32[]{:S(2)}, u32[]{:S(2)}) collective-permute-start(bf16[1664,128]{1,0:T(8,128)(2,1)S(1)} %get-tuple-element.90), channel_id=1, source_target_pairs={{0,2},{1,3},{2,0},{3,1},{4,6},{5,7},{6,4},{7,5},{8,10},{9,11},{10,... | collective-permute-start | bytes 1277960 | tf_op jit(solution)/shard_map/ppermute | solution.py:449
  88.0 15.7 %collective-permute-start.24 = (bf16[832,128]{1,0:T(8,128)(2,1)S(1)}, bf16[832,128]{1,0:T(8,128)(2,1)S(1)}, u32[]{:S(2)}, u32[]{:S(2)}) collective-permute-start(bf16[832,128]{1,0:T(8,128)(2,1)S(1)} %get-tuple-element.79), channel_id=1, source_target_pairs={{0,8},{8,24},{24,16},{16,0},{1,9},{9,25},{25,17},{17,1},{2,10},{10... | collective-permute-start | bytes 638984 | tf_op jit(solution)/shard_map/ppermute | solution.py:458
  89.9 16.8 %collective-permute-start.26 = (bf16[832,128]{1,0:T(8,128)(2,1)S(1)}, bf16[832,128]{1,0:T(8,128)(2,1)S(1)}, u32[]{:S(2)}, u32[]{:S(2)}) collective-permute-start(bf16[832,128]{1,0:T(8,128)(2,1)S(1)} %collective-permute-done.15.refs_0_), channel_id=1, source_target_pairs={{0,8},{8,24},{24,16},{16,0},{1,9},{9,25},{25,17},{17,1},{2,10},{10... | collective-permute-start | bytes 638984 | tf_op jit(solution)/shard_map/ppermute | solution.py:475
  93.2 13.5 %collective-permute-start.27 = (bf16[832,128]{1,0:T(8,128)(2,1)S(1)}, bf16[832,128]{1,0:T(8,128)(2,1)S(1)}, u32[]{:S(2)}, u32[]{:S(2)}) collective-permute-start(bf16[832,128]{1,0:T(8,128)(2,1)S(1)} %rows_of.6), channel_id=1, source_target_pairs={{8,0},{24,8},{16,24},{0,16},{9,1},{25,9},{17,25},{1,17},{10,2},{26... | collective-permute-start | bytes 638984 | tf_op jit(solution)/shard_map/ppermute | solution.py:476
  112.1 12.2 %collective-permute-start.23 = (bf16[1664,128]{1,0:T(8,128)(2,1)S(1)}, bf16[1664,128]{1,0:T(8,128)(2,1)S(1)}, u32[]{:S(2)}, u32[]{:S(2)}) collective-permute-start(bf16[1664,128]{1,0:T(8,128)(2,1)S(1)} %get-tuple-element.91.refs_0_), channel_id=1, source_target_pairs={{8,0},{24,8},{16,24},{0,16},{9,1},{25,9},{17,25},{1,17},{10,2},{26... | collective-permute-start | bytes 1277960 | tf_op jit(solution)/shard_map/ppermute | solution.py:459
  113.3 23.2 %collective-permute-start.31 = (bf16[1664,128]{1,0:T(8,128)(2,1)S(1)}, bf16[1664,128]{1,0:T(8,128)(2,1)S(1)}, u32[]{:S(2)}, u32[]{:S(2)}) collective-permute-start(bf16[1664,128]{1,0:T(8,128)(2,1)S(1)} %summed.14), channel_id=1, source_target_pairs={{0,6},{1,7},{2,4},{3,5},{4,2},{5,3},{6,0},{7,1},{8,14},{9,15},{10,... | collective-permute-start | bytes 1277960 | tf_op jit(solution)/shard_map/ppermute | solution.py:449
  116.2 20.3 %collective-permute-start.32 = (bf16[1664,128]{1,0:T(8,128)(2,1)S(1)}, bf16[1664,128]{1,0:T(8,128)(2,1)S(1)}, u32[]{:S(2)}, u32[]{:S(2)}) collective-permute-start(bf16[1664,128]{1,0:T(8,128)(2,1)S(1)} %get-tuple-element.102), channel_id=1, source_target_pairs={{0,4},{1,5},{2,6},{3,7},{4,0},{5,1},{6,2},{7,3},{8,12},{9,13},{10,... | collective-permute-start | bytes 1277960 | tf_op jit(solution)/shard_map/ppermute | solution.py:449
  116.3 20.2 %collective-permute-start.33 = (bf16[1664,128]{1,0:T(8,128)(2,1)S(1)}, bf16[1664,128]{1,0:T(8,128)(2,1)S(1)}, u32[]{:S(2)}, u32[]{:S(2)}) collective-permute-start(bf16[1664,128]{1,0:T(8,128)(2,1)S(1)} %get-tuple-element.103), channel_id=1, source_target_pairs={{0,2},{1,3},{2,0},{3,1},{4,6},{5,7},{6,4},{7,5},{8,10},{9,11},{10,... | collective-permute-start | bytes 1277960 | tf_op jit(solution)/shard_map/ppermute | solution.py:449
  118.5 11.3 %collective-permute-start.22 = (bf16[832,128]{1,0:T(8,128)(2,1)S(1)}, bf16[832,128]{1,0:T(8,128)(2,1)S(1)}, u32[]{:S(2)}, u32[]{:S(2)}) collective-permute-start(bf16[832,128]{1,0:T(8,128)(2,1)S(1)} %get-tuple-element.93.refs_9_), channel_id=1, source_target_pairs={{0,8},{8,24},{24,16},{16,0},{1,9},{9,25},{25,17},{17,1},{2,10},{10... | collective-permute-start | bytes 638984 | tf_op jit(solution)/shard_map/ppermute | solution.py:458
  124.3 13.5 %collective-permute-start.30 = (bf16[832,128]{1,0:T(8,128)(2,1)S(1)}, bf16[832,128]{1,0:T(8,128)(2,1)S(1)}, u32[]{:S(2)}, u32[]{:S(2)}) collective-permute-start(bf16[832,128]{1,0:T(8,128)(2,1)S(1)} %collective-permute-done.21.refs_0_), channel_id=1, source_target_pairs={{0,8},{8,24},{24,16},{16,0},{1,9},{9,25},{25,17},{17,1},{2,10},{10... | collective-permute-start | bytes 638984 | tf_op jit(solution)/shard_map/ppermute | solution.py:475
  129.8 9.0 %collective-permute-start.34 = (bf16[832,128]{1,0:T(8,128)(2,1)S(1)}, bf16[832,128]{1,0:T(8,128)(2,1)S(1)}, u32[]{:S(2)}, u32[]{:S(2)}) collective-permute-start(bf16[832,128]{1,0:T(8,128)(2,1)S(1)} %rows_of.7), channel_id=1, source_target_pairs={{8,0},{24,8},{16,24},{0,16},{9,1},{25,9},{17,25},{1,17},{10,2},{26... | collective-permute-start | bytes 638984 | tf_op jit(solution)/shard_map/ppermute | solution.py:476
  142.6 8.7 %collective-permute-start.37 = (bf16[4992,128]{1,0:T(8,128)(2,1)S(1)}, bf16[4992,128]{1,0:T(8,128)(2,1)S(1)}, u32[]{:S(2)}, u32[]{:S(2)}) collective-permute-start(bf16[4992,128]{1,0:T(8,128)(2,1)S(1)} %get-tuple-element.115), channel_id=1, source_target_pairs={{0,1},{1,0},{2,3},{3,2},{4,5},{5,4},{6,7},{7,6},{8,9},{9,8},{10,11... | collective-permute-start | bytes 3833864 | tf_op jit(solution)/shard_map/ppermute | solution.py:446
  151.5 8.2 %collective-permute-start.41 = (bf16[832,128]{1,0:T(8,128)(2,1)S(1)}, bf16[832,128]{1,0:T(8,128)(2,1)S(1)}, u32[]{:S(2)}, u32[]{:S(2)}) collective-permute-start(bf16[832,128]{1,0:T(8,128)(2,1)S(1)} %get-tuple-element.120), channel_id=1, source_target_pairs={{0,4},{1,5},{2,6},{3,7},{4,0},{5,1},{6,2},{7,3},{8,12},{9,13},{10,... | collective-permute-start | bytes 638984 | tf_op jit(solution)/shard_map/ppermute | solution.py:449
  153.7 9.4 %collective-permute-start.38 = (bf16[832,128]{1,0:T(8,128)(2,1)S(1)}, bf16[832,128]{1,0:T(8,128)(2,1)S(1)}, u32[]{:S(2)}, u32[]{:S(2)}) collective-permute-start(bf16[832,128]{1,0:T(8,128)(2,1)S(1)} %get-tuple-element.116), channel_id=1, source_target_pairs={{0,2},{1,3},{2,0},{3,1},{4,6},{5,7},{6,4},{7,5},{8,10},{9,11},{10,... | collective-permute-start | bytes 638984 | tf_op jit(solution)/shard_map/ppermute | solution.py:449
  154.6 8.5 %collective-permute-start.43 = (bf16[832,128]{1,0:T(8,128)(2,1)S(1)}, bf16[832,128]{1,0:T(8,128)(2,1)S(1)}, u32[]{:S(2)}, u32[]{:S(2)}) collective-permute-start(bf16[832,128]{1,0:T(8,128)(2,1)S(1)} %get-tuple-element.122), channel_id=1, source_target_pairs={{0,4},{1,5},{2,6},{3,7},{4,0},{5,1},{6,2},{7,3},{8,12},{9,13},{10,... | collective-permute-start | bytes 638984 | tf_op jit(solution)/shard_map/ppermute | solution.py:449
  (17 other events, 64.9 us)
